TPU v7x, 32 devices: a whole 2x2x4 slice. The times are simulated.
32 devices in a mesh: seq: 8 (over z, x), head: 4 (over y, core).
Axes of the slice: x: 2, y: 2, z: 4, core: 2. Of those that a mesh axis runs over, the one named last changes fastest.
Arguments:
- hidden_in: bfloat16 [4096, 1536], P('seq'), may hold values from -6 to 6
- seg_ids: int32 [4096], P('seq'), may hold values from 0 to 1, as said below
- out_cotangent: bfloat16 [4096, 1536], P('seq'), may hold values from -6 to 6
- norm_gain: float32 [2, 1536], replicated, may hold values from 0.1 to 1.9
- w_zx: bfloat16 [2, 1536, 2, 3072], P(None, None, None, 'head'), may hold values from -0.15625 to 0.15625
- w_bc: bfloat16 [2, 1536, 256], replicated, may hold values from -0.15625 to 0.15625
- w_dt: bfloat16 [2, 1536, 48], P(None, None, 'head'), may hold values from -0.15625 to 0.15625
- conv_x: float32 [2, 5, 3072], P(None, None, 'head'), may hold values from -3 to 3
- conv_bc: float32 [2, 5, 256], replicated, may hold values from -3 to 3
- dt_bias: float32 [2, 48], P(None, 'head'), may hold values from -8 to 0
- a_log: float32 [2, 48], P(None, 'head'), may hold values from -9 to 0
- skip_d: float32 [2, 48], P(None, 'head'), may hold values from 0.5 to 2
- gate_gain: float32 [2, 3072], P(None, 'head'), may hold values from 0.1 to 1.9
- w_out: bfloat16 [2, 3072, 1536], P(None, 'head'), may hold values from -0.109375 to 0.109375
Outputs:
- hidden_out: bfloat16 [4096, 1536], P('seq')
- grad_in: float32 [4096, 1536], P('seq')
- g_norm_gain: float32 [2, 1536], P(None, 'seq')
- g_w_zx: float32 [2, 1536, 2, 3072], P(None, 'seq', None, 'head')
- g_w_bc: float32 [2, 1536, 256], P(None, 'seq', 'head')
- g_w_dt: float32 [2, 1536, 48], P(None, 'seq', 'head')
- g_conv_x: float32 [2, 5, 3072], P(None, None, 'head')
- g_conv_bc: float32 [2, 5, 256], replicated
- g_dt_bias: float32 [2, 48], P(None, 'head')
- g_a_log: float32 [2, 48], P(None, 'head')
- g_skip_d: float32 [2, 48], P(None, 'head')
- g_gate_gain: float32 [2, 3072], P(None, 'head')
- g_w_out: float32 [2, 3072, 1536], P(None, 'head', 'seq')
Inputs may be any that keep to these rules, and one draw needn't show every extreme that they name: `seg_ids`: 0 for the tokens of the first sequence and 1 for those of the second; never falling; the first token of the second sequence lies within the first or the last 512 tokens, at a place whose remainder modulo 512 is 3 to 509.
All inputs are finite; a program needn't handle non-finite values.
Results may differ from a plain program's by a relative error of at most 0.03.
The roundings to bfloat16 on the way count: a program that leaves them out, or rounds other values in their place, can miss the bound.
Values may be sent and summed in bfloat16 or wider, within the bound.
A program may use at most 256 MiB of HBM per device.

v0:
```python
from functools import partial

import jax
import jax.numpy as jnp
from jax import lax
from jax.sharding import PartitionSpec as P

DI = 3072
CONV = 4
BLOCK = 256
LAYERS = 2


EPS = 1e-05
HIGH = lax.Precision.HIGHEST


def entering_2(part, axis, combine, identity, reverse):
    count = lax.axis_size(axis)
    place = lax.axis_index(axis)
    ahead = count - 1 - place if reverse else place
    gathered = jax.tree.map(lambda a: lax.all_gather(a, axis), part)
    state = jax.tree.map(lambda a, e: jnp.zeros_like(a) + jnp.asarray(e, a.dtype), part, identity)

    def one(hop, state):
        source = count - 1 - hop if reverse else hop
        return combine(
            state, jax.tree.map(lambda a: lax.dynamic_index_in_dim(a, source, 0, False), gathered)
        )

    return lax.fori_loop(0, ahead, one, state)


def from_behind(block, axis, distance):
    devices = range(lax.axis_size(axis))
    route = [(i - distance, i) for i in devices if i - distance in devices]
    return lax.ppermute(block, axis, route)


def silu_slope(inputs):
    sigmoid_part = jax.nn.sigmoid(inputs)
    return sigmoid_part * (1.0 + inputs * (1.0 - sigmoid_part))


def token_totals(partial_sums):
    return lax.psum(partial_sums, "head")


def combine_states(earlier, later):
    return (earlier[0] * later[0], later[0][:, None, None] * earlier[1] + later[1])


def carry_states(decay, carry_state):
    identity_pair = (jnp.ones_like(decay), jnp.zeros_like(carry_state))
    prefix = entering_2((decay, carry_state), "seq", combine_states, identity_pair, False)
    return (prefix[1], decay)


def carry_grads(kept_decay, grad_local):
    identity_pair = (jnp.ones_like(kept_decay), jnp.zeros_like(grad_local))
    suffix = entering_2((kept_decay, grad_local), "seq", combine_states, identity_pair, True)
    return suffix[1]


def ssd_device(values, keys_b, reads_c, step_sizes, decay_rates, segments, seg_before):
    token_count, head_count, head_size = values.shape
    blocks = token_count // BLOCK
    log_decay = (step_sizes * decay_rates[None, :]).reshape(blocks, BLOCK, head_count)
    cumulative = jnp.cumsum(log_decay, axis=1)
    cumul_heads = jnp.transpose(cumulative, (0, 2, 1))
    seg_blocks = segments.reshape(blocks, BLOCK)
    values_blk = values.reshape(blocks, BLOCK, head_count, head_size)
    keys_blk = keys_b.reshape(blocks, BLOCK, -1)
    reads_blk = reads_c.reshape(blocks, BLOCK, -1)
    steps_blk = step_sizes.reshape(blocks, BLOCK, head_count)
    steps_heads = jnp.transpose(steps_blk, (0, 2, 1))
    places = jnp.arange(BLOCK)
    causal = places[:, None] >= places[None, :]
    keep_mask = causal[None] & (seg_blocks[:, :, None] == seg_blocks[:, None, :])
    gram_block = jnp.einsum("cqn,csn->cqs", reads_blk, keys_blk, precision=HIGH)
    spread = cumul_heads[:, :, :, None] - cumul_heads[:, :, None, :]
    kernel = jnp.where(keep_mask[:, None], jnp.exp(jnp.minimum(spread, 0.0)), 0.0)
    mixing = kernel * gram_block[:, None] * steps_heads[:, :, None, :]
    inside_y = jnp.einsum("chqs,cshp->cqhp", mixing, values_blk, precision=HIGH)
    last_seg = seg_blocks[:, -1]
    tail_weight = (
        jnp.where(
            (seg_blocks == last_seg[:, None])[:, :, None],
            jnp.exp(cumulative[:, -1:, :] - cumulative),
            0.0,
        )
        * steps_blk
    )
    block_states = jnp.einsum(
        "csh,cshp,csn->chpn", tail_weight, values_blk, keys_blk, precision=HIGH
    )
    befores = jnp.concatenate([jnp.reshape(seg_before, (1,)), last_seg[:-1]], axis=0)
    block_decay = jnp.where((last_seg == befores)[:, None], jnp.exp(cumulative[:, -1, :]), 0.0)
    entry_weight = jnp.where((seg_blocks == befores[:, None])[:, :, None], jnp.exp(cumulative), 0.0)

    def advance(carry_state, block_piece):
        return (block_piece[0][:, None, None] * carry_state + block_piece[1], carry_state)

    start_state = jnp.zeros(block_states.shape[1:], jnp.float32)
    final_state, entering = lax.scan(advance, start_state, (block_decay, block_states))
    carried_y = (
        jnp.einsum("chpn,cqn->cqhp", entering, reads_blk, precision=HIGH)
        * entry_weight[:, :, :, None]
    )
    local_y = (inside_y + carried_y).reshape(token_count, head_count, head_size)
    return (local_y, final_state, jnp.prod(block_decay, axis=0))


def ssd_incoming(reads_c, step_sizes, decay_rates, incoming, segments, seg_before):
    cumulative = jnp.cumsum(step_sizes * decay_rates[None, :], axis=0)
    entry_weight = jnp.where((segments == seg_before)[:, None], jnp.exp(cumulative), 0.0)
    return jnp.einsum("hpn,tn->thp", incoming, reads_c, precision=HIGH) * entry_weight[:, :, None]


def conv_taps(extended, seg_ext, taps, row_count):
    seg_own = seg_ext[CONV - 1 :]
    mixed = jnp.broadcast_to(taps[CONV][None, :], (row_count, taps.shape[1]))
    masks = []
    for shift_back in range(CONV):
        begin_at = CONV - 1 - shift_back
        matching = (seg_ext[begin_at : begin_at + row_count] == seg_own)[:, None]
        masks.append(matching)
        mixed = mixed + jnp.where(
            matching, extended[begin_at : begin_at + row_count] * taps[shift_back][None, :], 0.0
        )
    return (mixed, masks)


def forward_layer(residual, params, segment_info):
    seg_ids, seg_ext, seg_before = segment_info
    (
        norm_scale,
        zx_weight,
        bc_weight,
        dt_weight,
        taps_x,
        taps_bc,
        dt_shift,
        log_rate,
        skip_gain,
        out_gain,
        out_weight,
    ) = params
    row_count = residual.shape[0]
    inner_local = zx_weight.shape[2]
    head_count = dt_weight.shape[1]
    state_size = bc_weight.shape[1] // 2
    inv_rms = lax.rsqrt(jnp.mean(residual * residual, axis=1, keepdims=True) + EPS)
    normed = (residual * inv_rms * norm_scale[None, :]).astype(jnp.bfloat16)
    proj_zx = jnp.einsum(
        "td,dke->tke", normed, zx_weight, preferred_element_type=jnp.float32
    ).astype(jnp.bfloat16)
    proj_bc = jnp.dot(normed, bc_weight, preferred_element_type=jnp.float32).astype(jnp.bfloat16)
    proj_dt = jnp.dot(normed, dt_weight, preferred_element_type=jnp.float32).astype(jnp.bfloat16)
    conv_in = jnp.concatenate([proj_zx[:, 1, :], proj_bc], axis=1)
    edge_rows = from_behind(conv_in[row_count - CONV + 1 :], "seq", 1)
    extended = jnp.concatenate([edge_rows, conv_in], axis=0).astype(jnp.float32)
    taps = jnp.concatenate([taps_x, taps_bc], axis=1)
    mixed, masks = conv_taps(extended, seg_ext, taps, row_count)
    conv_out = jax.nn.silu(mixed)
    values = conv_out[:, :inner_local].reshape(row_count, head_count, inner_local // head_count)
    keys_b = conv_out[:, inner_local : inner_local + state_size]
    reads_c = conv_out[:, inner_local + state_size :]
    step_sizes = jax.nn.softplus(proj_dt.astype(jnp.float32) + dt_shift[None, :])
    decay_rates = -jnp.exp(log_rate)
    local_fn = partial(ssd_device, segments=seg_ids, seg_before=seg_before)
    local_out, local_pull = jax.vjp(local_fn, values, keys_b, reads_c, step_sizes, decay_rates)
    local_y, local_state, local_decay = local_out
    incoming, kept_decay = carry_states(local_decay, local_state)
    incoming_fn = partial(ssd_incoming, segments=seg_ids, seg_before=seg_before)
    state_y, incoming_pull = jax.vjp(incoming_fn, reads_c, step_sizes, decay_rates, incoming)
    ssd_y = local_y + state_y + skip_gain[None, :, None] * values
    flat_y = ssd_y.reshape(row_count, inner_local)
    gate_z = proj_zx[:, 0, :].astype(jnp.float32)
    gated = flat_y * jax.nn.silu(gate_z)
    squares = token_totals(jnp.sum(gated * gated, axis=1))
    inv_gate = lax.rsqrt(squares / DI + EPS)
    scaled = (gated * inv_gate[:, None] * out_gain[None, :]).astype(jnp.bfloat16)
    head_out = jnp.dot(scaled, out_weight, preferred_element_type=jnp.float32)
    branch = lax.psum(head_out, "head")
    stored = dict(
        residual=residual,
        inv_rms=inv_rms,
        normed=normed,
        proj_dt=proj_dt,
        extended=extended,
        masks=masks,
        mixed=mixed,
        values=values,
        local_pull=local_pull,
        incoming_pull=incoming_pull,
        incoming=incoming,
        kept_decay=kept_decay,
        flat_y=flat_y,
        gate_z=gate_z,
        gated=gated,
        inv_gate=inv_gate,
        scaled=scaled,
        taps=taps,
    )
    return (residual + branch, stored)


def backward_layer(gradient, grad_low, stored, params, head_rank):
    (
        norm_scale,
        zx_weight,
        bc_weight,
        dt_weight,
        taps_x,
        taps_bc,
        dt_shift,
        log_rate,
        skip_gain,
        out_gain,
        out_weight,
    ) = params
    row_count = grad_low.shape[0]
    model_width = norm_scale.shape[0]
    values = stored["values"]
    inner_local = values.shape[1] * values.shape[2]
    grad_out_w = jnp.einsum(
        "tk,td->kd", stored["scaled"], grad_low, preferred_element_type=jnp.float32
    )
    grad_scaled = jnp.einsum("td,kd->tk", grad_low, out_weight, preferred_element_type=jnp.float32)
    gated = stored["gated"]
    inv_gate = stored["inv_gate"]
    grad_out_gain = jnp.sum(grad_scaled * gated * inv_gate[:, None], axis=0)
    inner_sum = token_totals(jnp.sum(grad_scaled * out_gain[None, :] * gated, axis=1))
    grad_gated = (
        inv_gate[:, None] * out_gain[None, :] * grad_scaled
        - gated * (inv_gate * inv_gate * inv_gate * inner_sum / DI)[:, None]
    )
    gate_z = stored["gate_z"]
    grad_y = (grad_gated * jax.nn.silu(gate_z)).reshape(values.shape)
    grad_z = grad_gated * stored["flat_y"] * silu_slope(gate_z)
    grad_skip = jnp.sum(grad_y * values, axis=(0, 2))
    grad_reads_in, grad_steps_in, grad_rates_in, grad_incoming = stored["incoming_pull"](grad_y)
    later_grad = carry_grads(stored["kept_decay"], grad_incoming)
    grad_decay = jnp.sum(later_grad * stored["incoming"], axis=(1, 2))
    grad_values, grad_keys, grad_reads, grad_steps, grad_rates = stored["local_pull"](
        (grad_y, later_grad, grad_decay)
    )
    grad_values = grad_values + grad_y * skip_gain[None, :, None]
    grad_bc = lax.psum(jnp.concatenate([grad_keys, grad_reads + grad_reads_in], axis=1), "head")
    grad_steps = grad_steps + grad_steps_in
    grad_log_rate = (grad_rates + grad_rates_in) * -jnp.exp(log_rate)
    grad_dt_proj = grad_steps * jax.nn.sigmoid(
        stored["proj_dt"].astype(jnp.float32) + dt_shift[None, :]
    )
    grad_dt_shift = jnp.sum(grad_dt_proj, axis=0)
    grad_conv_out = jnp.concatenate([grad_values.reshape(row_count, inner_local), grad_bc], axis=1)
    grad_mixed = grad_conv_out * silu_slope(stored["mixed"])
    extended = stored["extended"]
    taps = stored["taps"]
    grad_ext = jnp.zeros_like(extended)
    tap_rows = []
    for shift_back in range(CONV):
        begin_at = CONV - 1 - shift_back
        window = extended[begin_at : begin_at + row_count]
        masked = jnp.where(stored["masks"][shift_back], grad_mixed, 0.0)
        tap_rows.append(jnp.sum(masked * window, axis=0))
        grad_ext = grad_ext + jnp.pad(
            masked * taps[shift_back][None, :], ((begin_at, CONV - 1 - begin_at), (0, 0))
        )
    tap_rows.append(jnp.sum(grad_mixed, axis=0))
    grad_taps = jnp.stack(tap_rows, axis=0)
    from_next = from_behind(grad_ext[: CONV - 1], "seq", -1)
    grad_conv_in = grad_ext[CONV - 1 :] + jnp.pad(from_next, ((row_count - CONV + 1, 0), (0, 0)))
    grad_x_low = grad_conv_in[:, :inner_local].astype(jnp.bfloat16)
    grad_bc_low = grad_conv_in[:, inner_local:].astype(jnp.bfloat16)
    grad_zx_low = jnp.stack([grad_z.astype(jnp.bfloat16), grad_x_low], axis=1)
    grad_dt_low = grad_dt_proj.astype(jnp.bfloat16)
    bc_share = bc_weight.shape[1] // lax.axis_size("head")
    grad_bc_mine = lax.dynamic_slice_in_dim(grad_bc_low, head_rank * bc_share, bc_share, 1)
    bc_weight_mine = lax.dynamic_slice_in_dim(bc_weight, head_rank * bc_share, bc_share, 1)
    normed = stored["normed"]
    grad_zx_w = jnp.einsum("td,tke->dke", normed, grad_zx_low, preferred_element_type=jnp.float32)
    grad_bc_w = jnp.einsum("td,tk->dk", normed, grad_bc_mine, preferred_element_type=jnp.float32)
    grad_dt_w = jnp.einsum("td,th->dh", normed, grad_dt_low, preferred_element_type=jnp.float32)
    grad_normed = jnp.einsum(
        "tke,dke->td", grad_zx_low, zx_weight, preferred_element_type=jnp.float32
    )
    grad_normed = grad_normed + jnp.einsum(
        "tk,dk->td", grad_bc_mine, bc_weight_mine, preferred_element_type=jnp.float32
    )
    grad_normed = grad_normed + jnp.einsum(
        "th,dh->td", grad_dt_low, dt_weight, preferred_element_type=jnp.float32
    )
    residual = stored["residual"]
    inv_rms = stored["inv_rms"]
    grad_normed = lax.psum(grad_normed, "head")
    grad_norm_scale = jnp.sum(grad_normed * residual * inv_rms, axis=0)
    inner_norm = jnp.sum(grad_normed * norm_scale[None, :] * residual, axis=1, keepdims=True)
    gain_use = norm_scale[None, :]
    grad_residual = (
        gradient
        + inv_rms * gain_use * grad_normed
        - residual * (inv_rms * inv_rms * inv_rms) * inner_norm / model_width
    )
    large_grads = (grad_norm_scale, grad_zx_w, grad_bc_w, grad_dt_w, grad_out_w)
    small_grads = (
        grad_taps[:, :inner_local],
        grad_taps[:, inner_local:],
        grad_dt_shift,
        grad_log_rate,
        grad_skip,
        grad_out_gain,
    )
    return (grad_residual, large_grads, small_grads)


def stack_layers(collected, position):
    return jnp.stack([member[position] for member in collected], axis=0)


def local(
    hidden_in,
    seg_ids,
    out_cotangent,
    norm_gain,
    w_zx,
    w_bc,
    w_dt,
    conv_x,
    conv_bc,
    dt_bias,
    a_log,
    skip_d,
    gate_gain,
    w_out,
):
    head_rank = lax.axis_index("head")
    prior_ids = jnp.full((CONV - 1,), seg_ids[0], jnp.int32)
    segment_info = (seg_ids, jnp.concatenate([prior_ids, seg_ids], axis=0), prior_ids[CONV - 2])
    weights_all = (
        norm_gain,
        w_zx,
        w_bc,
        w_dt,
        conv_x,
        conv_bc,
        dt_bias,
        a_log,
        skip_d,
        gate_gain,
        w_out,
    )
    residual = hidden_in.astype(jnp.float32)
    stored_list = []
    for layer_index in range(LAYERS):
        params = tuple((weight[layer_index] for weight in weights_all))
        residual, stored = forward_layer(residual, params, segment_info)
        stored_list.append(stored)
    hidden_out = residual.astype(jnp.bfloat16)
    gradient = out_cotangent.astype(jnp.float32)
    grad_low = out_cotangent
    large_list = []
    small_list = []
    for layer_index in reversed(range(LAYERS)):
        params = tuple((weight[layer_index] for weight in weights_all))
        gradient, large_grads, small_grads = backward_layer(
            gradient, grad_low, stored_list[layer_index], params, head_rank
        )
        large_list.insert(0, large_grads)
        small_list.insert(0, small_grads)
        if layer_index > 0:
            grad_low = gradient.astype(jnp.bfloat16)
    summed_large = (
        lax.psum_scatter(stack_layers(large_list, 0), "seq", scatter_dimension=1, tiled=True),
        lax.psum_scatter(stack_layers(large_list, 1), "seq", scatter_dimension=1, tiled=True),
        lax.psum_scatter(stack_layers(large_list, 2), "seq", scatter_dimension=1, tiled=True),
        lax.psum_scatter(stack_layers(large_list, 3), "seq", scatter_dimension=1, tiled=True),
        lax.psum_scatter(stack_layers(large_list, 4), "seq", scatter_dimension=2, tiled=True),
    )
    summed_small = lax.psum(
        (
            stack_layers(small_list, 0),
            stack_layers(small_list, 1),
            stack_layers(small_list, 2),
            stack_layers(small_list, 3),
            stack_layers(small_list, 4),
            stack_layers(small_list, 5),
        ),
        "seq",
    )
    return (
        hidden_out,
        gradient,
        summed_large[0],
        summed_large[1],
        summed_large[2],
        summed_large[3],
        summed_small[0],
        summed_small[1],
        summed_small[2],
        summed_small[3],
        summed_small[4],
        summed_small[5],
        summed_large[4],
    )


def solution(mesh):
    placed = (
        P("seq", None),
        P("seq"),
        P("seq", None),
        P(),
        P(None, None, None, "head"),
        P(),
        P(None, None, "head"),
        P(None, None, "head"),
        P(),
        P(None, "head"),
        P(None, "head"),
        P(None, "head"),
        P(None, "head"),
        P(None, "head", None),
    )
    return jax.shard_map(
        local,
        mesh=mesh,
        in_specs=placed,
        out_specs=(
            P("seq", None),
            P("seq", None),
            P(None, "seq"),
            P(None, "seq", None, "head"),
            P(None, "seq", "head"),
            P(None, "seq", "head"),
            P(None, None, "head"),
            P(),
            P(None, "head"),
            P(None, "head"),
            P(None, "head"),
            P(None, "head"),
            P(None, "head", "seq"),
        ),
        check_vma=False,
    )
```

profile of v0, /device:TPU:0, one launch (start us, length us, event | category | flops | bytes accessed | tf_op | source)
XLA Modules:
  0.0 1757.3 jit_solution(9922414797372557797)
XLA Ops:
  10.4 8.9 fusion.292
  25.5 4.8 collective-permute-start
  62.0 19.2 %all-gather.4 = f32[8,1,12]{2,1,0:T(1,128)} all-gather(f32[1,1,12]{2,1,0:T(1,128)S(1)} %multiply_bitcast_fusion.3), channel_id=1, replica_groups=mesh['seq'=8,'head'=4] {'seq'}, dimensions={0}, use_global_device_ids=true | all-gather | bytes 432 | tf_op jit(solution)/shard_map/all_gather | solution.py:22
  84.1 7.5 fusion.108
  93.0 23.8 %all-gather.11.cloned.1.call-done = f32[96,64,128]{2,1,0:T(8,128)} async-done(((f32[12,64,128]{2,1,0:T(8,128)}), f32[96,64,128]{2,1,0:T(8,128)}) %all-gather.11.cloned.1.call-update) | async-done | bytes 3145744 | tf_op jit(solution)/shard_map/all_gather | solution.py:22
  118.4 6.0 multiply_reduce_fusion.24
  124.5 5.7 psum.112
  131.8 4.7 fusion.79
  138.0 77.7 %all-reduce.29.cloned.1.call-done = f32[512,1536]{1,0:T(8,128)} async-done(((f32[512,1536]{1,0:T(8,128)}), f32[512,1536]{1,0:T(8,128)}) %all-reduce.29.cloned.1.call-update) | async-done | bytes 3145744 | tf_op jit(solution)/shard_map/psum | solution.py:185
  239.9 5.4 fusion.89
  246.9 3.4 collective-permute-start.1
  263.9 3.8 fusion.135
  269.3 7.5 while.125
  283.9 22.3 %all-gather.5 = f32[8,1,12]{2,1,0:T(1,128)} all-gather(f32[1,1,12]{2,1,0:T(1,128)S(1)} %multiply_bitcast_fusion.2), channel_id=1, replica_groups=mesh['seq'=8,'head'=4] {'seq'}, dimensions={0}, use_global_device_ids=true | all-gather | bytes 432 | tf_op jit(solution)/shard_map/all_gather | solution.py:22
  311.2 7.5 fusion.105
  320.1 19.0 %all-gather.13.cloned.1.call-done = f32[96,64,128]{2,1,0:T(8,128)} async-done(((f32[12,64,128]{2,1,0:T(8,128)}), f32[96,64,128]{2,1,0:T(8,128)}) %all-gather.13.cloned.1.call-update) | async-done | bytes 3145744 | tf_op jit(solution)/shard_map/all_gather | solution.py:22
  339.2 7.2 multiply_reduce_fusion.23
  349.5 6.4 psum.114
  356.6 6.2 multiply_reduce_fusion.13
  362.8 7.4 psum.116
  371.0 5.7 multiply_reduce_fusion.15
  379.7 3.6 fusion.131
  396.7 6.2 reduce-window.70
  406.7 4.3 fusion.154
  413.5 13.0 fusion.202
  427.2 3.4 fusion.170
  433.0 21.9 %all-gather.15.cloned.1.call-done = f32[96,64,128]{2,1,0:T(8,128)} async-done(((f32[12,64,128]{2,1,0:T(8,128)}), f32[96,64,128]{2,1,0:T(8,128)}) %all-gather.15.cloned.1.call-update) | async-done | bytes 3145744 | tf_op jit(solution)/shard_map/all_gather | solution.py:22
  455.0 12.9 while.120
  471.1 8.0 while.121
  483.5 6.7 bitcast_add_fusion.9
  490.3 3.4 fusion.158
  494.5 5.1 reduce-window.66
  515.1 26.3 %all-reduce.31.cloned.1.call-done = f32[512,256]{1,0:T(8,128)} async-done(((f32[512,256]{1,0:T(8,128)}), f32[512,256]{1,0:T(8,128)}) %all-reduce.31.cloned.1.call-update) | async-done | bytes 524304 | tf_op jit(solution)/shard_map/psum | solution.py:250
  561.4 65.2 %all-reduce.33.cloned.1.call-done = f32[512,1536]{1,0:T(8,128)} async-done(((f32[512,1536]{1,0:T(8,128)}), f32[512,1536]{1,0:T(8,128)}) %all-reduce.33.cloned.1.call-update) | async-done | bytes 3145744 | tf_op jit(solution)/shard_map/psum | solution.py:297
  626.6 3.4 multiply_reduce_fusion
  632.8 3.5 multiply_reduce_fusion.14
  636.3 5.8 psum.119
  642.1 5.2 multiply_reduce_fusion.16
  653.9 4.8 fusion.75
  662.3 5.0 reduce-window.76
  668.2 3.8 fusion.153
  673.6 13.4 fusion.204
  692.6 20.9 %all-gather.17.cloned.1.call-done = f32[96,64,128]{2,1,0:T(8,128)} async-done(((f32[12,64,128]{2,1,0:T(8,128)}), f32[96,64,128]{2,1,0:T(8,128)}) %all-gather.17.cloned.1.call-update) | async-done | bytes 3145744 | tf_op jit(solution)/shard_map/all_gather | solution.py:22
  713.6 12.9 while.122
  734.6 6.7 bitcast_add_fusion.8
  741.3 4.6 fusion.155
  748.8 5.2 reduce-window.74
  763.5 26.1 %all-reduce.35.cloned.1.call-done = f32[512,256]{1,0:T(8,128)} async-done(((f32[512,256]{1,0:T(8,128)}), f32[512,256]{1,0:T(8,128)}) %all-reduce.35.cloned.1.call-update) | async-done | bytes 524304 | tf_op jit(solution)/shard_map/psum | solution.py:250
  789.7 8.6 multiply_reduce_fusion.3
  815.8 3.4 copy.603
  831.3 6.1 convolution_bitcast_fusion.2
  837.5 3.8 convolution_bitcast_fusion.3
  841.2 90.0 %all-reduce.39.cloned.1.call-done = (f32[512,1536]{1,0:T(8,128)}, f32[512,1536]{1,0:T(8,128)}) async-done(((f32[512,1536]{1,0:T(8,128)}, f32[512,1536]{1,0:T(8,128)}), (f32[512,1536]{1,0:T(8,128)}, f32[512,1536]{1,0:T(8,128)})) %all-reduce.39.cloned.1.call-update) | async-done | bytes 6291472 | tf_op jit(solution)/shard_map/psum | solution.py:185
  935.5 8.3 pad_maximum_fusion.1
  943.8 14.9 copy.555
  958.9 4.1 convolution_bitcast_fusion
  965.8 6.7 pad_maximum_fusion
  975.3 38.8 %all-reduce.20 = (f32[2,5,768]{2,1,0:T(8,128)S(1)}, f32[2,5,256]{2,1,0:T(8,128)S(1)}, f32[2,12]{1,0:T(2,128)}, f32[2,12]{1,0:T(2,128)}, f32[2,12]{1,0:T(2,128)}, /*index=5*/f32[2,768]{1,0:T(2,128)}) all-reduce(f32[2,5,768]{2,1,0:T(8,128)S(1)} %pad_maximum_fusion.12, ...), channel_id=1, replica_groups=mesh['seq'=8,'head'=4] {'seq'}, use_global_device_ids=true, to_apply=%region_84.85 | all-reduce | flops 11848 | bytes 94784 | tf_op jit(solution)/shard_map/psum | solution.py:381
  1017.2 45.3 %reduce-scatter.15.cloned.1.call-done = f32[192,128]{1,0:T(8,128)} async-done(((f32[1536,128]{1,0:T(8,128)}), f32[192,128]{1,0:T(8,128)}) %reduce-scatter.15.cloned.1.call-update) | async-done | bytes 98320
  1064.3 3.6 add_convert_fusion
  1071.8 55.9 %reduce-scatter.13.cloned.1.call-done = f32[192,2]{1,0:T(8,128)} async-done(((f32[1536,2]{1,0:T(8,128)}), f32[192,2]{1,0:T(8,128)}) %reduce-scatter.13.cloned.1.call-update) | async-done | bytes 1552
  1129.2 299.9 %all-reduce.37.cloned.1.call-done = f32[2,768,1536]{1,0,2:T(2,128)} async-done(((f32[2,768,1536]{1,0,2:T(2,128)}), f32[2,768,1536]{1,0,2:T(2,128)}) %all-reduce.37.cloned.1.call-update) | async-done | bytes 9437200
  1431.9 313.8 %reduce-scatter.11.cloned.1.call-done = f32[2,192,2,768]{3,1,2,0:T(8,128)} async-done(((f32[2,1536,2,768]{3,1,2,0:T(8,128)}), f32[2,192,2,768]{3,1,2,0:T(8,128)}) %reduce-scatter.11.cloned.1.call-update) | async-done | bytes 2359312 | tf_op jit(solution)/shard_map/reduce_scatter | solution.py:376
  1745.7 4.9 copy.556
  (930 shorter events, 313.9 us)
Async XLA Ops:
  7.2 109.7 %all-gather.11.cloned.1.call-start = ((), (), s32[]{:S(2)}) async-start(), calls=%async_computation.9 | async-start | bytes 3538944 | tf_op jit(solution)/shard_map/all_gather | solution.py:22
  8.0 24.9 %copy-start.128 = (f32[1536]{0:T(1024)}, f32[1536]{0:T(1024)S(1)}, u32[]{:S(2)}) copy-start(f32[1536]{0:T(1024)S(1)} %get-tuple-element.786) | copy-start | bytes 18436
  10.4 22.5 %copy-start.189 = (f32[512]{0:T(512)}, f32[512]{0:T(512)S(1)}, u32[]{:S(2)}) copy-start(f32[512]{0:T(512)S(1)} %get-tuple-element.975) | copy-start | bytes 6148
  25.5 15.1 collective-permute-start
  32.9 23.2 %copy-start.228 = (f32[12]{0:T(128)}, f32[12]{0:T(128)S(1)}, u32[]{:S(2)}) copy-start(f32[12]{0:T(128)S(1)} %get-tuple-element.1006) | copy-start | bytes 148
  33.5 22.5 %copy-start.123 = (f32[512,12]{0,1:T(8,128)}, f32[512,12]{0,1:T(8,128)S(1)}, u32[]{:S(2)}) copy-start(f32[512,12]{0,1:T(8,128)S(1)} %get-tuple-element.996) | copy-start | bytes 73732
  35.1 49.0 %copy-start.78 = (f32[2,12,256]{2,1,0:T(8,128)}, f32[2,12,256]{2,1,0:T(8,128)S(1)}, u32[]{:S(2)}) copy-start(f32[2,12,256]{2,1,0:T(8,128)S(1)} %reshape.575) | copy-start | bytes 73732
  35.3 20.7 %copy-start.84 = (f32[2,256,12]{1,0,2:T(2,128)}, f32[2,256,12]{1,0,2:T(2,128)S(1)}, u32[]{:S(2)}) copy-start(f32[2,256,12]{1,0,2:T(2,128)S(1)} %reshape.491) | copy-start | bytes 73732
  37.5 44.3 %copy-start.213 = (pred[512]{0:T(512)(128)(4,1)}, pred[512]{0:T(512)(128)(4,1)S(1)}, u32[]{:S(2)}) copy-start(pred[512]{0:T(512)(128)(4,1)S(1)} %get-tuple-element.978) | copy-start | bytes 1540
  39.1 455.2 %copy-start.132 = (pred[2,256]{1,0:T(4,128)(4,1)}, pred[2,256]{1,0:T(4,128)(4,1)S(1)}, u32[]{:S(2)}) copy-start(pred[2,256]{1,0:T(4,128)(4,1)S(1)} %get-tuple-element.983) | copy-start | bytes 1540
  40.5 43.6 %copy-start.108 = (f32[2,256,12]{1,2,0:T(8,128)}, f32[2,256,12]{1,2,0:T(8,128)S(1)}, u32[]{:S(2)}) copy-start(f32[2,256,12]{1,2,0:T(8,128)S(1)} %get-tuple-element.961) | copy-start | bytes 73732
  46.4 35.6 %copy-start.43 = (f32[512,128]{1,0:T(8,128)}, f32[512,128]{1,0:T(8,128)S(1)}, u32[]{:S(2)}) copy-start(f32[512,128]{1,0:T(8,128)S(1)} %get-tuple-element.934) | copy-start | bytes 786436
  46.4 36.3 %copy-start.41 = (f32[512,128]{1,0:T(8,128)}, f32[512,128]{1,0:T(8,128)S(1)}, u32[]{:S(2)}) copy-start(f32[512,128]{1,0:T(8,128)S(1)} %get-tuple-element.935) | copy-start | bytes 786436
  50.3 33.8 %copy-start.16 = (f32[2,256,12,64]{1,0,3,2:T(2,128)}, f32[2,256,12,64]{1,0,3,2:T(2,128)S(1)}, u32[]{:S(2)}) copy-start(f32[2,256,12,64]{1,0,3,2:T(2,128)S(1)} %reshape_reshape.12) | copy-start | bytes 4718596
  55.2 26.0 %copy-start.235 = (f32[2,12]{1,0:T(2,128)}, f32[2,12]{1,0:T(2,128)S(1)}, u32[]{:S(2)}) copy-start(f32[2,12]{1,0:T(2,128)S(1)} %get-tuple-element.1588) | copy-start | bytes 292
  55.2 27.4 %copy-start.27 = (f32[2,12,64,128]{3,2,1,0:T(8,128)}, f32[2,12,64,128]{3,2,1,0:T(8,128)S(1)}, u32[]{:S(2)}) copy-start(f32[2,12,64,128]{3,2,1,0:T(8,128)S(1)} %get-tuple-element.1495) | copy-start | bytes 2359300
  55.7 25.5 %copy-start.250 = (f32[2,12]{1,0:T(2,128)S(1)}, f32[2,12]{1,0:T(2,128)}, u32[]{:S(2)}) copy-start(f32[2,12]{1,0:T(2,128)} %param.41) | copy-start | bytes 292
  56.0 159.7 %all-reduce.29.cloned.1.call-start = ((), (), s32[]{:S(2)}) async-start(), calls=%async_computation.4 | async-start | bytes 6291456 | tf_op jit(solution)/shard_map/psum | solution.py:185
  56.1 28.1 %copy-start.166 = (f32[2,12,256]{2,1,0:T(8,128)}, f32[2,12,256]{2,1,0:T(8,128)S(1)}, u32[]{:S(2)}) copy-start(f32[2,12,256]{2,1,0:T(8,128)S(1)} %copy.475) | copy-start | bytes 73732
  57.7 24.9 %copy-start.100 = (f32[2,8,4,128]{3,1,2,0:T(8,128)}, f32[2,8,4,128]{3,1,2,0:T(8,128)S(1)}, u32[]{:S(2)}) copy-start(f32[2,8,4,128]{3,1,2,0:T(8,128)S(1)} %copy.622) | copy-start | bytes 98308
  61.4 20.5 %copy-start.153 = (f32[768]{0:T(1024)}, f32[768]{0:T(1024)S(1)}, u32[]{:S(2)}) copy-start(f32[768]{0:T(1024)S(1)} %get-tuple-element.788) | copy-start | bytes 9220
  81.8 35.1 %copy-start.89 = (f32[512,12]{0,1:T(8,128)}, f32[512,12]{0,1:T(8,128)S(1)}, u32[]{:S(2)}) copy-start(f32[512,12]{0,1:T(8,128)S(1)} %select_bitcast_fusion.1) | copy-start | bytes 73732
  136.6 202.5 %all-gather.13.cloned.1.call-start = ((), (), s32[]{:S(2)}) async-start(), calls=%async_computation.10 | async-start | bytes 3538944 | tf_op jit(solution)/shard_map/all_gather | solution.py:22
  138.0 114.0 %copy-start.133 = (f32[1,1024]{1,0:T(1,128)}, f32[1,1024]{1,0:T(1,128)S(1)}, u32[]{:S(2)}) copy-start(f32[1,1024]{1,0:T(1,128)S(1)} %get-tuple-element.957) | copy-start | bytes 12292
  218.5 411.5 %copy-start.3 = (f32[512,1536]{1,0:T(8,128)}, f32[512,1536]{1,0:T(8,128)S(1)}, u32[]{:S(2)}) copy-start(f32[512,1536]{1,0:T(8,128)S(1)} %get-tuple-element.911) | copy-start | bytes 9437188
  246.9 4.7 collective-permute-start.1
  276.8 29.3 %copy-start.214 = (pred[512]{0:T(512)(128)(4,1)S(1)}, pred[512]{0:T(512)(128)(4,1)}, u32[]{:S(2)}) copy-start(pred[512]{0:T(512)(128)(4,1)} %copy-done.213) | copy-start | bytes 1540
  277.6 29.2 %copy-start.45 = (f32[512,128]{1,0:T(8,128)S(1)}, f32[512,128]{1,0:T(8,128)}, u32[]{:S(2)}) copy-start(f32[512,128]{1,0:T(8,128)} %get-tuple-element.933) | copy-start | bytes 786436
  277.6 177.3 %all-gather.15.cloned.1.call-start = ((), (), s32[]{:S(2)}) async-start(), calls=%async_computation.11 | async-start | bytes 3538944 | tf_op jit(solution)/shard_map/all_gather | solution.py:22
  280.1 28.2 %copy-start.102 = (f32[2,8,4,128]{3,1,2,0:T(8,128)}, f32[2,8,4,128]{3,1,2,0:T(8,128)S(1)}, u32[]{:S(2)}) copy-start(f32[2,8,4,128]{3,1,2,0:T(8,128)S(1)} %copy.623) | copy-start | bytes 98308
  280.8 30.3 %copy-start.169 = (f32[2,12,256]{2,1,0:T(8,128)}, f32[2,12,256]{2,1,0:T(8,128)S(1)}, u32[]{:S(2)}) copy-start(f32[2,12,256]{2,1,0:T(8,128)S(1)} %copy.495) | copy-start | bytes 73732
  283.9 27.3 %copy-start.19 = (f32[2,256,12,64]{1,0,3,2:T(2,128)S(1)}, f32[2,256,12,64]{1,0,3,2:T(2,128)}, u32[]{:S(2)}) copy-start(f32[2,256,12,64]{1,0,3,2:T(2,128)} %reshape_reshape.13) | copy-start | bytes 4718596
  283.9 27.3 %copy-start.81 = (f32[2,12,256]{2,1,0:T(8,128)S(1)}, f32[2,12,256]{2,1,0:T(8,128)}, u32[]{:S(2)}) copy-start(f32[2,12,256]{2,1,0:T(8,128)} %reshape.576) | copy-start | bytes 73732
  283.9 27.3 %copy-start.111 = (f32[2,256,12]{1,2,0:T(8,128)S(1)}, f32[2,256,12]{1,2,0:T(8,128)}, u32[]{:S(2)}) copy-start(f32[2,256,12]{1,2,0:T(8,128)} %get-tuple-element.952) | copy-start | bytes 73732
  283.9 27.3 %copy-start.118 = (pred[2,256,256]{2,1,0:T(8,128)(4,1)S(1)}, pred[2,256,256]{2,1,0:T(8,128)(4,1)}, u32[]{:S(2)}) copy-start(pred[2,256,256]{2,1,0:T(8,128)(4,1)} %copy-done.117) | copy-start | bytes 393220
  339.2 88.0 %copy-start.10 = (f32[12,64,128]{2,1,0:T(8,128)}, f32[12,64,128]{2,1,0:T(8,128)S(1)}, u32[]{:S(2)}) copy-start(f32[12,64,128]{2,1,0:T(8,128)S(1)} %get-tuple-element.626) | copy-start | bytes 1179652
  383.3 158.1 %all-reduce.31.cloned.1.call-start = ((), (), s32[]{:S(2)}) async-start(), calls=%async_computation.5 | async-start | bytes 1048576 | tf_op jit(solution)/shard_map/psum | solution.py:250
  413.5 13.1 copy-start.48
  413.5 13.7 copy-start.7
  413.5 13.7 copy-start.91
  510.8 30.5 %copy-start.148 = (f32[1,1024]{1,0:T(1,128)S(1)}, f32[1,1024]{1,0:T(1,128)}, u32[]{:S(2)}) copy-start(f32[1,1024]{1,0:T(1,128)} %get-tuple-element.959) | copy-start | bytes 12292
  510.8 115.8 %all-reduce.33.cloned.1.call-start = ((), (), s32[]{:S(2)}) async-start(), calls=%async_computation.6 | async-start | bytes 6291456 | tf_op jit(solution)/shard_map/psum | solution.py:297
  545.9 5.9 collective-permute-start.2
  558.1 68.6 %copy-start.160 = (f32[512]{0:T(512)S(1)}, f32[512]{0:T(512)}, u32[]{:S(2)}) copy-start(f32[512]{0:T(512)} %copy-done.159) | copy-start | bytes 6148
  558.1 155.5 %all-gather.17.cloned.1.call-start = ((), (), s32[]{:S(2)}) async-start(), calls=%async_computation.12 | async-start | bytes 3538944 | tf_op jit(solution)/shard_map/all_gather | solution.py:22
  561.4 68.7 %copy-start.225 = (f32[512]{0:T(512)S(1)}, f32[512]{0:T(512)}, u32[]{:S(2)}) copy-start(f32[512]{0:T(512)} %get-tuple-element.976) | copy-start | bytes 6148
  652.4 137.2 %all-reduce.35.cloned.1.call-start = ((), (), s32[]{:S(2)}) async-start(), calls=%async_computation.7 | async-start | bytes 1048576 | tf_op jit(solution)/shard_map/psum | solution.py:250
  673.6 13.5 copy-start.44
  673.6 14.2 copy-start.9
  713.6 14.7 copy-start.28
  713.6 14.7 copy-start.256
  759.1 30.5 %copy-start.1 = (f32[515,1024]{1,0:T(8,128)S(1)}, f32[515,1024]{1,0:T(8,128)}, u32[]{:S(2)}) copy-start(f32[515,1024]{1,0:T(8,128)} %copy-done) | copy-start | bytes 6328324
  759.1 30.5 %copy-start.180 = (pred[512]{0:T(512)(128)(4,1)S(1)}, pred[512]{0:T(512)(128)(4,1)}, u32[]{:S(2)}) copy-start(pred[512]{0:T(512)(128)(4,1)} %copy-done.177) | copy-start | bytes 1540
  759.1 30.5 %copy-start.184 = (pred[512]{0:T(512)(128)(4,1)S(1)}, pred[512]{0:T(512)(128)(4,1)}, u32[]{:S(2)}) copy-start(pred[512]{0:T(512)(128)(4,1)} %copy-done.181) | copy-start | bytes 1540
  759.1 30.5 %copy-start.188 = (pred[512]{0:T(512)(128)(4,1)S(1)}, pred[512]{0:T(512)(128)(4,1)}, u32[]{:S(2)}) copy-start(pred[512]{0:T(512)(128)(4,1)} %copy-done.185) | copy-start | bytes 1540
  759.1 172.1 %all-reduce.39.cloned.1.call-start = ((), (), s32[]{:S(2)}) async-start(), calls=%async_computation.17 | async-start | bytes 12582912 | tf_op jit(solution)/shard_map/psum | solution.py:185
  763.5 45.4 %copy-start.130 = (bf16[512,12]{0,1:T(8,128)(2,1)}, bf16[512,12]{0,1:T(8,128)(2,1)S(1)}, u32[]{:S(2)}) copy-start(bf16[512,12]{0,1:T(8,128)(2,1)S(1)} %get-tuple-element.943) | copy-start | bytes 36868
  799.2 5.9 collective-permute-start.3
  811.4 204.0 %reduce-scatter.17.cloned.1.call-start = ((), (), s32[]{:S(2)}) async-start(), calls=%async_computation.15 | async-start | bytes 884736
  822.2 240.2 %reduce-scatter.15.cloned.1.call-start = ((), (), s32[]{:S(2)}) async-start(), calls=%async_computation.14 | async-start | bytes 884736
  831.2 296.5 %reduce-scatter.13.cloned.1.call-start = ((), (), s32[]{:S(2)}) async-start(), calls=%async_computation.13 | async-start | bytes 884736
  935.4 493.7 %all-reduce.37.cloned.1.call-start = ((), (), s32[]{:S(2)}) async-start(), calls=%async_computation.16 | async-start | bytes 18874368
  958.7 787.0 %reduce-scatter.11.cloned.1.call-start = ((), (), s32[]{:S(2)}) async-start(), calls=%async_computation.8 | async-start | bytes 21233664 | tf_op jit(solution)/shard_map/reduce_scatter | solution.py:376
  972.8 91.5 %copy-start.4 = (f32[512,1536]{1,0:T(8,128)S(1)}, f32[512,1536]{1,0:T(8,128)}, u32[]{:S(2)}) copy-start(f32[512,1536]{1,0:T(8,128)} %copy-done.3) | copy-start | bytes 9437188
  (218 other events, 866.5 us)
Sparse Core Ops, SparseCore 0:
  56.1 60.7 all-gather.10
  136.7 78.8 all-reduce.28
  277.7 61.3 all-gather.12
  383.4 71.5 all-gather.14
  510.9 30.4 all-reduce.30
  558.2 68.4 all-reduce.32
  652.6 60.9 all-gather.16
  759.2 30.3 all-reduce.34
  811.5 119.7 all-reduce.38
  934.4 62.7 reduce-scatter.16
  1000.9 61.4 reduce-scatter.14
  1066.2 61.4 reduce-scatter.12
  1131.9 297.1 all-reduce.36
  1433.4 312.2 reduce-scatter.10
where the time goes:
time: 1770 us; the launch traced here: 1760 us
  waiting for transfers between devices  1090 us (62%)
  matrix products  187 us (11%)
  other arithmetic  171 us (10%)
  local copies, waits for them, and re-layouts  170 us (10%)
  blocking collectives  106 us (6%)
  between operations  18.6 us (1%)
    unnamed x18, waiting for transfers between devices  401 us
    reduce_scatter x1, waiting for transfers between devices, local(): lax.psum_scatter(stack_layers(large_list, 1), 'seq', scatter_dimension=1,...  314 us
    psum x2, waiting for transfers between devices, forward_layer(): branch = lax.psum(head_out, 'head')  168 us
    all_gather x4, waiting for transfers between devices, entering_2(): gathered = jax.tree.map(lambda a: lax.all_gather(a, axis), part)  85.7 us
    psum x1, waiting for transfers between devices, backward_layer(): grad_normed = lax.psum(grad_normed, 'head')  65.2 us
    dot_general x6, matrix products, ssd_device(): inside_y = jnp.einsum('chqs,cshp->cqhp', mixing, values_blk, precision=HIGH)  54.9 us
    psum x2, waiting for transfers between devices, backward_layer(): lax.psum(jnp.concatenate([grad_keys, grad_reads + grad_reads_in], axis=1)...  52.4 us
    unnamed x564, local copies, waits for them, and re-layouts  46.2 us
  transfers between devices with their start and end apart: 18, of which 15 were waited for; matrix products, arithmetic and copies ran while one was open for 13% of the time, Pallas kernels for 0%

commit v1 on v0

v1 whole, which is shorter than its diff:
```python
from functools import partial

import jax
import jax.numpy as jnp
from jax import lax
from jax.experimental import pallas as pl
from jax.experimental.pallas import tpu as pltpu
from jax.sharding import PartitionSpec as P

CONV = 4
LAYERS = 2
EPS = 1e-05
F32 = jnp.float32
BF16 = jnp.bfloat16


def dot(a, b, dims):
    return lax.dot_general(a.astype(BF16), b.astype(BF16), (dims, ((), ())), preferred_element_type=F32)


def mm(a, b):
    return dot(a, b, ((1,), (0,)))


def mm_nt(a, b):
    return dot(a, b, ((1,), (1,)))


def mm_tn(a, b):
    return dot(a, b, ((0,), (0,)))


def swap(x, axis, bit):
    n = lax.axis_size(axis)
    return lax.ppermute(x, axis, [(i, i ^ bit) for i in range(n)])


def shift(x, axis, by):
    n = lax.axis_size(axis)
    return lax.ppermute(x, axis, [(i, i + by) for i in range(n) if 0 <= i + by < n])


def bits_of(axis):
    n = lax.axis_size(axis)
    bits = []
    b = 1
    while b < n:
        bits.append(b)
        b *= 2
    return bits


def my_bit(axis, bit):
    return (lax.axis_index(axis) // bit) % 2


def take(x, dim, index):
    return lax.dynamic_index_in_dim(x, index, dim, keepdims=False)


def head_scatter(x):
    for bit in bits_of("head"):
        me = my_bit("head", bit)
        halves = x.reshape((2, x.shape[0] // 2) + x.shape[1:])
        got = swap(take(halves, 0, 1 - me).astype(BF16), "head", bit)
        x = take(halves, 0, me).astype(F32) + got.astype(F32)
    return x


def head_scatter_exact(x):
    for bit in bits_of("head"):
        me = my_bit("head", bit)
        halves = x.reshape((2, x.shape[0] // 2) + x.shape[1:])
        x = take(halves, 0, me) + swap(take(halves, 0, 1 - me), "head", bit)
    return x


def head_gather(x):
    for bit in reversed(bits_of("head")):
        me = my_bit("head", bit)
        got = swap(x, "head", bit)
        x = jnp.where(me == 0, jnp.concatenate([x, got], 0), jnp.concatenate([got, x], 0))
    return x


def own_rows(x):
    for bit in bits_of("head"):
        x = take(x.reshape((2, x.shape[0] // 2) + x.shape[1:]), 0, my_bit("head", bit))
    return x


def carry_scan(state, decay, reverse):
    total, total_d = state, decay
    entering = jnp.zeros_like(state)
    enter_d = jnp.ones_like(decay)
    for bit in bits_of("seq"):
        me = my_bit("seq", bit)
        other = swap(total.astype(BF16), "seq", bit).astype(F32)
        other_d = swap(total_d, "seq", bit)
        second = (me == 0) if reverse else (me == 1)
        entering = jnp.where(second, entering + enter_d[:, None, None] * other, entering)
        enter_d = jnp.where(second, enter_d * other_d, enter_d)
        total = jnp.where(
            second, total_d[:, None, None] * other + total, other_d[:, None, None] * total + other
        )
        total_d = total_d * other_d
    return entering


def silu_slope(v):
    s = jax.nn.sigmoid(v)
    return s * (1.0 + v * (1.0 - s))


def scatter_rows(x):
    bits = bits_of("seq")
    k = len(bits)
    n = lax.axis_size("seq")
    x = x.reshape((2,) * k + (x.shape[0] // n, x.shape[1]))
    for b in range(k):
        axis = k - 1 - b
        me = my_bit("seq", bits[b])
        got = swap(take(x, axis, 1 - me).astype(BF16), "seq", bits[b])
        x = take(x, axis, me).astype(F32) + got.astype(F32)
    return x


HALO = 16
LANE = 128
NT = ((1,), (1,))
NN = ((1,), (0,))
TN = ((0,), (0,))


def bdot(a, b, dims):
    return lax.dot_general(a.astype(BF16), b.astype(BF16), (dims, ((), ())), preferred_element_type=F32)


def hdot(a, b, dims):
    return lax.dot_general(a, b, (dims, ((), ())), precision=lax.Precision.HIGHEST, preferred_element_type=F32)


def sig(v):
    return 0.5 * jnp.tanh(0.5 * v) + 0.5


def softplus(v):
    e = jnp.exp(-jnp.abs(v))
    s = e / (2.0 + e)
    q = s * s
    series = 1.0 / 13.0
    for k in (11, 9, 7, 5, 3, 1):
        series = series * q + 1.0 / k
    return jnp.maximum(v, 0.0) + 2.0 * s * series


def mix_taps(us, taps, aux, width):
    tokens = aux.shape[1]
    wide = lambda m: m if width == LANE else jnp.concatenate([m] * (width // LANE), axis=1)
    acc = us[pl.ds(HALO, tokens), :] * taps[0:1, :] + taps[CONV : CONV + 1, :]
    for j in range(1, CONV):
        acc = acc + us[pl.ds(HALO - j, tokens), :] * wide(aux[j - 1]) * taps[j : j + 1, :]
    return acc


def pick_lane(values, h, lanes):
    return jnp.sum(jnp.where(lanes == h, values, 0.0), axis=1, keepdims=True)


def fwd_mix_body(heads, size, nx, wzx, wbc, wdt, tapx, tapbc, dtb, lograte, skip, aux, segrow,
                 gate, ux, ubc, krs, pdt, steps_o, cum_o, cT, gram, mixed_o, ypart, entry_o, state, dec, decl,
                 us, usbc, cb):
    p = pl.program_id(0)
    tokens = aux.shape[1]
    states = wbc.shape[1] // 2
    lanes = lax.broadcasted_iota(jnp.int32, (tokens, LANE), 1)
    half = lanes < size

    @pl.when(p == 0)
    def _():
        bc = bdot(nx[...], wbc[...], NN).astype(BF16)
        ubc[...] = bc
        usbc[...] = bc.astype(F32)
        m = mix_taps(usbc, tapbc, aux, 2 * states)
        act = (m * sig(m)).astype(BF16)
        krs[...] = act
        g = bdot(act[:, states:], act[:, :states], NT)
        ii = lax.broadcasted_iota(jnp.int32, (tokens, tokens), 0)
        jj = lax.broadcasted_iota(jnp.int32, (tokens, tokens), 1)
        segc = jnp.concatenate([aux[5]] * (tokens // LANE), axis=1)
        keep = (ii >= jj) & (segc == segrow[...])
        gram[...] = jnp.where(keep, g, 0.0)
        pd = bdot(nx[pl.ds(HALO, tokens), :], wdt[...], NN).astype(BF16)
        pdt[...] = pd
        st = softplus(pd.astype(F32) + dtb[...])
        steps_o[...] = st
        log = st * -jnp.exp(lograte[...])
        cum = hdot(jnp.where(ii >= jj, 1.0, 0.0), log, NN)
        cum_o[...] = cum
        cT[...] = cum.T
        keeps = aux[3, tokens - 1 : tokens, :]
        decl[...] = jnp.broadcast_to(jnp.exp(cum[tokens - 1 : tokens, :]) * keeps, (8, LANE))
        dec[...] = jnp.exp(jnp.broadcast_to(cT[0:16, tokens - 1 : tokens], (16, LANE))) * keeps

    gate[...] = bdot(nx[pl.ds(HALO, tokens), :], wzx[0], NN).astype(BF16)
    u = bdot(nx[...], wzx[1], NN).astype(BF16)
    ux[...] = u
    us[...] = u.astype(F32)
    m = mix_taps(us, tapx, aux, LANE)
    mixed_o[...] = m
    v = m * sig(m)
    cum = cum_o[...]
    st = steps_o[...]
    h0 = p * (LANE // size)
    dd = jnp.where(half, pick_lane(st, h0, lanes), pick_lane(st, h0 + 1, lanes))
    vd = v * dd
    vdb = vd.astype(BF16)
    ys = []
    for k in range(LANE // size):
        h = h0 + k
        cb[k] = jnp.broadcast_to(pick_lane(cum, h, lanes), (tokens, LANE))
        row = cT[pl.ds(h, 1), :]
        parts = []
        for ib in range(tokens // LANE):
            tiles = []
            ci = cb[k, pl.ds(ib * LANE, LANE), :]
            for jb in range(ib + 1):
                spread = ci - row[:, jb * LANE : (jb + 1) * LANE]
                if jb == ib:
                    spread = jnp.minimum(spread, 0.0)
                tiles.append((jnp.exp(spread) * gram[pl.ds(ib * LANE, LANE), pl.ds(jb * LANE, LANE)]).astype(BF16))
            w = tiles[0] if ib == 0 else jnp.concatenate(tiles, axis=1)
            parts.append(bdot(w, vdb[: (ib + 1) * LANE], NN))
        ys.append(jnp.concatenate(parts, axis=0))
    y = jnp.where(half, ys[0], ys[1])
    ypart[...] = y + skip[...] * v
    ct = jnp.where(half, cb[0], cb[1])
    entry_o[...] = jnp.exp(ct) * aux[3]
    tail = jnp.exp(ct[tokens - 1 : tokens, :] - ct) * aux[4]
    state[...] = bdot(vd * tail, krs[:, :states], TN)


def full(shape):
    n = len(shape)
    return pl.BlockSpec(shape, lambda p: (0,) * n)


def cols(rows):
    return pl.BlockSpec((rows, LANE), lambda p: (0, p))


def rowsb(width):
    return pl.BlockSpec((LANE, width), lambda p: (p, 0))


VMEM_LIMIT = 56 * 1024 * 1024


def fwd_mix(heads, size, nx, wzx, wbc, wdt, tapx, tapbc, dtb, lograte, skip, aux, segrow):
    tokens = aux.shape[1]
    ext, d = nx.shape
    inner = wzx.shape[2]
    two = wbc.shape[1]
    S = jax.ShapeDtypeStruct
    return pl.pallas_call(
        partial(fwd_mix_body, heads, size),
        name="fwd_mix",
        grid=(inner // LANE,),
        in_specs=[full(nx.shape), pl.BlockSpec((2, d, LANE), lambda p: (0, 0, p)), full(wbc.shape), full(wdt.shape),
                  cols(tapx.shape[0]), full(tapbc.shape), full(dtb.shape), full(lograte.shape), cols(1),
                  full(aux.shape), full(segrow.shape)],
        out_specs=[cols(tokens), cols(ext), full((ext, two)), full((tokens, two)), full((tokens, LANE)), full((tokens, LANE)),
                   full((tokens, LANE)), full((LANE, tokens)), full((tokens, tokens)), cols(tokens), cols(tokens),
                   cols(tokens), rowsb(two // 2), full((16, LANE)), full((8, LANE))],
        out_shape=[S((tokens, inner), BF16), S((ext, inner), BF16), S((ext, two), BF16), S((tokens, two), BF16),
                   S((tokens, LANE), BF16), S((tokens, LANE), F32), S((tokens, LANE), F32), S((LANE, tokens), F32),
                   S((tokens, tokens), F32), S((tokens, inner), F32), S((tokens, inner), F32), S((tokens, inner), F32),
                   S((inner, two // 2), F32), S((16, LANE), F32), S((8, LANE), F32)],
        scratch_shapes=[pltpu.VMEM((ext, LANE), F32), pltpu.VMEM((ext, two), F32), pltpu.VMEM((2, tokens, LANE), F32)],
        compiler_params=pltpu.CompilerParams(vmem_limit_bytes=VMEM_LIMIT),
        cost_estimate=pl.CostEstimate(flops=2 * ext * d * (2 * inner + two) + 6 * tokens * tokens * inner,
                                      bytes_accessed=4 * d * inner + 16 * tokens * inner, transcendentals=tokens * tokens * heads),
    )(nx, wzx, wbc, wdt, tapx, tapbc, dtb, lograte, skip, aux, segrow)


def fwd_gate_body(ypart, entry, gate, krs, enter, y, carr, gated, sq, sqacc):
    p = pl.program_id(0)
    states = krs.shape[1] // 2
    c = bdot(krs[:, states:], enter[...], NT) * entry[...]
    carr[...] = c
    yy = ypart[...] + c
    y[...] = yy
    z = gate[...].astype(F32)
    g = yy * (z * sig(z))
    gated[...] = g

    @pl.when(p == 0)
    def _():
        sqacc[...] = g * g

    @pl.when(p > 0)
    def _():
        sqacc[...] += g * g

    @pl.when(p == pl.num_programs(0) - 1)
    def _():
        sq[...] = jnp.broadcast_to(jnp.sum(jnp.transpose(sqacc[...]), axis=0, keepdims=True), sq.shape)


def fwd_gate(ypart, entry, gate, krs, enter):
    tokens, inner = ypart.shape
    S = jax.ShapeDtypeStruct
    return pl.pallas_call(
        fwd_gate_body,
        name="fwd_gate",
        grid=(inner // LANE,),
        in_specs=[cols(tokens), cols(tokens), cols(tokens), full(krs.shape), rowsb(enter.shape[1])],
        out_specs=[cols(tokens), cols(tokens), cols(tokens), full((8, tokens))],
        scratch_shapes=[pltpu.VMEM((tokens, LANE), F32)],
        out_shape=[S((tokens, inner), F32)] * 3 + [S((8, tokens), F32)],
        compiler_params=pltpu.CompilerParams(vmem_limit_bytes=VMEM_LIMIT),
        cost_estimate=pl.CostEstimate(flops=2 * tokens * inner * LANE, bytes_accessed=26 * tokens * inner, transcendentals=tokens * inner),
    )(ypart, entry, gate, krs, enter)


def bwd_gate_body(gb, wout, gate, y, mixed, entry, krs, r2b, krb, gain, gy_o, gz_o, scaled_o, qloc, ggate, gskip):
    states = krs.shape[1] // 2
    gs = bdot(gb[...], wout[...], NT)
    z = gate[...].astype(F32)
    s = sig(z)
    sil = z * s
    yy = y[...]
    gated = yy * sil
    r2 = r2b[...]
    gr = gated * r2
    ggate[...] = jnp.sum(gs * gr, axis=0, keepdims=True)
    scaled_o[...] = (gr * gain[...]).astype(BF16)
    gg = r2 * gain[...] * gs - gated * krb[...]
    gy = gg * sil
    gy_o[...] = gy
    gz_o[...] = (gg * yy * (s * (1.0 + z * (1.0 - s)))).astype(BF16)
    m = mixed[...]
    gskip[...] = jnp.sum(gy * (m * sig(m)), axis=0, keepdims=True)
    qloc[...] = bdot(gy * entry[...], krs[:, states:], TN)


def bwd_gate(gb, wout, gate, y, mixed, entry, krs, r2b, krb, gain):
    tokens, inner = y.shape
    d = gb.shape[1]
    states = krs.shape[1] // 2
    S = jax.ShapeDtypeStruct
    return pl.pallas_call(
        bwd_gate_body,
        name="bwd_gate",
        grid=(inner // LANE,),
        in_specs=[full(gb.shape), rowsb(d), cols(tokens), cols(tokens), cols(tokens), cols(tokens), full(krs.shape),
                  full(r2b.shape), full(krb.shape), cols(1)],
        out_specs=[cols(tokens), cols(tokens), cols(tokens), rowsb(states), cols(1), cols(1)],
        out_shape=[S((tokens, inner), F32), S((tokens, inner), BF16), S((tokens, inner), BF16), S((inner, states), F32),
                   S((1, inner), F32), S((1, inner), F32)],
        compiler_params=pltpu.CompilerParams(vmem_limit_bytes=VMEM_LIMIT),
        cost_estimate=pl.CostEstimate(flops=2 * tokens * inner * d, bytes_accessed=26 * tokens * inner + 2 * d * inner, transcendentals=2 * tokens * inner),
    )(gb, wout, gate, y, mixed, entry, krs, r2b, krb, gain)


def bwd_local_body(size, gy_r, mixed, krs, cum, steps, cT, gram, entry, enter, segc, segrow,
                   dvd, dd_o, rowT, dkr, cb, db, gramT, dgT, vb, gk):
    p = pl.program_id(0)
    tokens = gy_r.shape[0]
    states = krs.shape[1] // 2
    lanes = lax.broadcasted_iota(jnp.int32, (tokens, LANE), 1)
    half = lanes < size

    @pl.when(p == 0)
    def _():
        gramT[...] = gram[...].T
        dgT[...] = jnp.zeros_like(dgT)
        dd_o[...] = jnp.zeros_like(dd_o)
        rowT[...] = jnp.zeros_like(rowT)
        dkr[...] = jnp.zeros_like(dkr)

    m = mixed[...]
    vb[...] = (m * sig(m)).astype(BF16)
    gy = gy_r[...]
    gyb = gy.astype(BF16)
    h0 = p * (LANE // size)
    outs = []
    for k in range(LANE // size):
        h = h0 + k
        gk[...] = jnp.where(half if k == 0 else jnp.logical_not(half), gy, 0.0).astype(BF16)
        cb[...] = jnp.broadcast_to(pick_lane(cum[...], h, lanes), (tokens, LANE))
        db[...] = jnp.broadcast_to(pick_lane(steps[...], h, lanes), (tokens, LANE))
        row = cT[pl.ds(h, 1), :]
        parts = []
        dds = []
        rows_acc = [jnp.zeros((8, LANE), F32) for _ in range(tokens // LANE)]
        for jb in range(tokens // LANE):
            js = pl.ds(jb * LANE, LANE)
            cj = cb[js, :]
            dj = db[js, :]
            pt = bdot(vb[js, :], gk[pl.ds(jb * LANE, tokens - jb * LANE), :], NT)
            ws = []
            dsum = None
            for ib in range(jb, tokens // LANE):
                sl = pl.ds(ib * LANE, LANE)
                spread = row[:, ib * LANE : (ib + 1) * LANE] - cj
                if jb == ib:
                    spread = jnp.minimum(spread, 0.0)
                e = jnp.exp(spread)
                w = e * gramT[js, sl]
                ws.append(w.astype(BF16))
                pp = pt[:, (ib - jb) * LANE : (ib - jb + 1) * LANE]
                wp = w * pp
                dgT[js, sl] += e * (pp * dj)
                x = wp * dj
                rows_acc[ib] = rows_acc[ib] + jnp.sum(x.reshape(LANE // 8, 8, LANE), axis=0)
                dsum = wp if dsum is None else dsum + wp
            dds.append(jnp.sum(dsum, axis=1, keepdims=True))
            w = ws[0] if len(ws) == 1 else jnp.concatenate(ws, axis=1)
            parts.append(bdot(w, gyb[jb * LANE :], NN))
        outs.append(jnp.concatenate(parts, axis=0))
        dd_o[...] += jnp.where(lanes == h, jnp.concatenate(dds, axis=0), 0.0)
        rowT[pl.ds(h, 1), :] = jnp.concatenate([jnp.sum(r, axis=0, keepdims=True) for r in rows_acc], axis=1)
    dvd[...] = jnp.where(half, outs[0], outs[1])
    dkr[:, states:] += bdot(gy * entry[...], enter[...], NN)

    @pl.when(p == pl.num_programs(0) - 1)
    def _():
        jj = lax.broadcasted_iota(jnp.int32, (tokens, tokens), 0)
        ii = lax.broadcasted_iota(jnp.int32, (tokens, tokens), 1)
        segs = jnp.concatenate([segc[...]] * (tokens // LANE), axis=1)
        g = jnp.where((ii >= jj) & (segs == segrow[...]), dgT[...], 0.0)
        dkr[:, :states] += bdot(g, krs[:, states:], NN)
        dkr[:, states:] += bdot(g, krs[:, :states], TN)


def bwd_local(size, gy, mixed, krs, cum, steps, cT, gram, entry, enter, segc, segrow):
    tokens, inner = gy.shape
    two = krs.shape[1]
    S = jax.ShapeDtypeStruct
    return pl.pallas_call(
        partial(bwd_local_body, size),
        name="bwd_local",
        grid=(inner // LANE,),
        in_specs=[cols(tokens), cols(tokens), full(krs.shape), full(cum.shape), full(steps.shape), full(cT.shape), full(gram.shape),
                  cols(tokens), rowsb(two // 2), full(segc.shape), full(segrow.shape)],
        out_specs=[cols(tokens), full((tokens, LANE)), full((LANE, tokens)), full((tokens, two))],
        out_shape=[S((tokens, inner), F32), S((tokens, LANE), F32), S((LANE, tokens), F32), S((tokens, two), F32)],
        scratch_shapes=[pltpu.VMEM((tokens, LANE), F32), pltpu.VMEM((tokens, LANE), F32), pltpu.VMEM((tokens, tokens), F32),
                        pltpu.VMEM((tokens, tokens), F32), pltpu.VMEM((tokens, LANE), BF16), pltpu.VMEM((tokens, LANE), BF16)],
        compiler_params=pltpu.CompilerParams(vmem_limit_bytes=VMEM_LIMIT),
        cost_estimate=pl.CostEstimate(flops=12 * tokens * tokens * inner, bytes_accessed=20 * tokens * inner, transcendentals=tokens * tokens * inner // size),
    )(gy, mixed, krs, cum, steps, cT, gram, entry, enter, segc, segrow)


def bwd_carry_body(size, gy_r, dvd_r, mixed, carr, entry, krs, cum, steps, pdt, dtb, lograte, skip, ux, tapx, aux, later, enter,
                   dd_r, rowT, dkr_r, decay,
                   gm_o, gu_o, gtail_o, gtaps, gdt_o, gvec, dkr, us, ms, ddacc, dcum, last):
    p = pl.program_id(0)
    tokens = gy_r.shape[0]
    states = krs.shape[1] // 2
    lanes = lax.broadcasted_iota(jnp.int32, (tokens, LANE), 1)
    lane1 = lax.broadcasted_iota(jnp.int32, (1, LANE), 1)
    half = lanes < size

    @pl.when(p == 0)
    def _():
        ddacc[...] = dd_r[...]
        dcum[...] = jnp.transpose(rowT[...]) - dd_r[...] * steps[...]
        last[...] = jnp.zeros_like(last)
        dkr[...] = dkr_r[...]

    h0 = p * (LANE // size)
    st = steps[...]
    cu = cum[...]
    cc = [pick_lane(cu, h0 + k, lanes) for k in range(2)]
    dcol = [pick_lane(st, h0 + k, lanes) for k in range(2)]
    ct = jnp.where(half, cc[0], cc[1])
    dpair = jnp.where(half, dcol[0], dcol[1])
    tail = jnp.exp(ct[tokens - 1 : tokens, :] - ct) * aux[4]
    m = mixed[...]
    s = sig(m)
    v = m * s
    gy = gy_r[...]
    qk = bdot(krs[:, :states], later[...], NT) * tail
    dvd = dvd_r[...] + qk
    dkr[:, :states] += bdot(v * dpair * tail, later[...], NN)
    tq = v * qk
    eq = gy * carr[...]
    qs = later[...] * enter[...]
    for k in range(2):
        h = h0 + k
        mine = half if k == 0 else jnp.logical_not(half)
        td = jnp.sum(jnp.where(mine, tq, 0.0), axis=1, keepdims=True)
        ec = jnp.sum(jnp.where(mine, eq, 0.0), axis=1, keepdims=True)
        tdd = td * dcol[k]
        ddacc[...] += jnp.where(lanes == h, td, 0.0)
        dcum[...] += jnp.where(lanes == h, ec - tdd, 0.0)
        dot_qs = jnp.sum(jnp.sum(qs[k * size : (k + 1) * size, :], axis=0, keepdims=True), axis=1, keepdims=True)
        last[...] += jnp.where(lane1 == h, jnp.sum(tdd, axis=0, keepdims=True) + dot_qs * decay[...], 0.0)
    dv = dvd * dpair + skip[...] * gy
    gm = dv * (s * (1.0 + m * (1.0 - s)))
    gm_o[...] = gm[:8]
    us[...] = ux[...].astype(F32)
    acc = gm * tapx[0:1, :]
    gtaps[0:1, :] = jnp.sum(gm * us[pl.ds(HALO, tokens), :], axis=0, keepdims=True)
    gtaps[CONV : CONV + 1, :] = jnp.sum(gm, axis=0, keepdims=True)
    ms[pl.ds(tokens, 8), :] = jnp.zeros((8, LANE), F32)
    for j in range(1, CONV):
        gmj = gm * aux[j - 1]
        gtaps[j : j + 1, :] = jnp.sum(gmj * us[pl.ds(HALO - j, tokens), :], axis=0, keepdims=True)
        ms[pl.ds(0, tokens), :] = gmj
        acc = acc + ms[pl.ds(j, tokens), :] * tapx[j : j + 1, :]
    gu_o[...] = acc.astype(BF16)
    gtail_o[...] = acc[tokens - 16 :]

    @pl.when(p == pl.num_programs(0) - 1)
    def _():
        ii = lax.broadcasted_iota(jnp.int32, (tokens, tokens), 0)
        jj = lax.broadcasted_iota(jnp.int32, (tokens, tokens), 1)
        dlog = hdot(jnp.where(jj >= ii, 1.0, 0.0), dcum[...], NN) + last[...]
        rates = -jnp.exp(lograte[...])
        dsteps = ddacc[...] + rates * dlog
        gdt = dsteps * sig(pdt[...].astype(F32) + dtb[...])
        gdt_o[...] = gdt.astype(BF16)
        gvec[0:1, :] = jnp.sum(gdt, axis=0, keepdims=True)
        gvec[1:2, :] = jnp.sum(st * dlog, axis=0, keepdims=True) * rates


def bwd_carry(size, gy, dvd, mixed, carr, entry, krs, cum, steps, pdt, dtb, lograte, skip, ux, tapx, aux, later, enter, dd, rowT, dkr, decay):
    tokens, inner = gy.shape
    ext = ux.shape[0]
    two = krs.shape[1]
    S = jax.ShapeDtypeStruct
    return pl.pallas_call(
        partial(bwd_carry_body, size),
        name="bwd_carry",
        grid=(inner // LANE,),
        in_specs=[cols(tokens), cols(tokens), cols(tokens), cols(tokens), cols(tokens), full(krs.shape), full(cum.shape), full(steps.shape),
                  full(pdt.shape), full(dtb.shape), full(lograte.shape), cols(1), cols(ext), cols(tapx.shape[0]), full(aux.shape),
                  rowsb(two // 2), rowsb(two // 2), full(dd.shape), full(rowT.shape), full(dkr.shape), full(decay.shape)],
        out_specs=[cols(8), cols(tokens), cols(16), cols(8), full((tokens, LANE)), full((8, LANE)), full((tokens, two))],
        out_shape=[S((8, inner), F32), S((tokens, inner), BF16), S((16, inner), F32), S((8, inner), F32), S((tokens, LANE), BF16),
                   S((8, LANE), F32), S((tokens, two), F32)],
        scratch_shapes=[pltpu.VMEM((ext, LANE), F32), pltpu.VMEM((tokens + 8, LANE), F32), pltpu.VMEM((tokens, LANE), F32),
                        pltpu.VMEM((tokens, LANE), F32), pltpu.VMEM((1, LANE), F32)],
        compiler_params=pltpu.CompilerParams(vmem_limit_bytes=VMEM_LIMIT),
        cost_estimate=pl.CostEstimate(flops=4 * tokens * inner * LANE, bytes_accessed=24 * tokens * inner, transcendentals=2 * tokens * inner),
    )(gy, dvd, mixed, carr, entry, krs, cum, steps, pdt, dtb, lograte, skip, ux, tapx, aux, later, enter, dd, rowT, dkr, decay)


MESH = pl.DeviceIdType.MESH
SUBS = 2


def greet(partners):
    barrier = pltpu.get_barrier_semaphore()
    for where in partners:
        pl.semaphore_signal(barrier, inc=1, device_id=where, device_id_type=MESH)
    pl.semaphore_wait(barrier, len(partners))


def send(src, dst, sems, where):
    copy = pltpu.make_async_remote_copy(
        src_ref=src, dst_ref=dst, send_sem=sems[0], recv_sem=sems[1], device_id=where, device_id_type=MESH)
    copy.start()
    return copy


def flip(me, bit):
    return me + bit * (1 - 2 * ((me // bit) % 2))


def carry_body(bits, reverse, heads, size, st, dec, out, tx, rx, dtx, drx, tot, ssem, rsem):
    me = lax.axis_index("seq")
    wheres = [{"seq": flip(me, b)} for b in bits]
    greet(wheres)
    enter_d = jnp.ones_like(dec[...])
    total_d = dec[...]
    for i, b in enumerate(bits):
        src = st if i == 0 else tot
        tx[...] = src[...].astype(BF16)
        dtx[...] = total_d
        one = send(tx, rx.at[i], (ssem.at[2 * i], rsem.at[2 * i]), wheres[i])
        two = send(dtx, drx.at[i], (ssem.at[2 * i + 1], rsem.at[2 * i + 1]), wheres[i])
        bit = (me // b) % 2
        second = (1 - bit) if reverse else bit
        two.wait()
        other_d = drx[i]
        one.wait()
        keep = second.astype(F32)
        for h in range(heads):
            rows = pl.ds(h * size, size)
            other = rx[i, rows, :].astype(F32)
            add = other * (enter_d[h : h + 1] * keep)
            if i == 0:
                out[rows, :] = add
            else:
                out[rows, :] += add
            if i + 1 < len(bits):
                mine = src[rows, :]
                a = jnp.where(second == 1, total_d[h : h + 1], 1.0)
                c = jnp.where(second == 1, 1.0, other_d[h : h + 1])
                tot[rows, :] = a * other + c * mine
        enter_d = jnp.where(second == 1, enter_d * other_d, enter_d)
        total_d = total_d * other_d


def carry_kernel(state, dec, heads, size, reverse, cid):
    bits = bits_of("seq")
    rows, states = state.shape
    n = len(bits)
    return pl.pallas_call(
        partial(carry_body, bits, reverse, heads, size),
        name="carry_back" if reverse else "carry_on",
        in_specs=[pl.BlockSpec(memory_space=pltpu.VMEM)] * 2,
        out_specs=pl.BlockSpec(memory_space=pltpu.VMEM),
        out_shape=jax.ShapeDtypeStruct((rows, states), F32),
        scratch_shapes=[pltpu.VMEM((rows, states), BF16), pltpu.VMEM((n, rows, states), BF16), pltpu.VMEM(dec.shape, F32),
                        pltpu.VMEM((n,) + dec.shape, F32), pltpu.VMEM((rows, states), F32),
                        pltpu.SemaphoreType.DMA((2 * n,)), pltpu.SemaphoreType.DMA((2 * n,))],
        compiler_params=pltpu.CompilerParams(collective_id=cid, has_side_effects=True, vmem_limit_bytes=VMEM_LIMIT),
    )(state, dec)


def head_core(tokens, part, middle, nx, off, side, tx0, rx0, tx1, rx1, acc, ssem, rsem, me, core_at, y_at):
    quarter = tokens // 4
    sub = quarter // SUBS
    c = me % 2
    y = me // 2
    half = 2 * quarter
    other_y = pl.multiple_of((1 - y) * quarter, quarter)
    own_y = pl.multiple_of(y * quarter, quarter)
    n = 0
    sends = []

    def go(src, dst, where):
        nonlocal n
        copy = send(src, dst, (ssem.at[n], rsem.at[n]), where)
        sends.append(copy)
        n += 1
        return copy

    acc[...] = part(pl.multiple_of((1 - c) * half, half), half)
    first = []
    for i, base in enumerate((other_y, own_y)):
        for s in range(SUBS):
            tx0[i, s] = acc[pl.ds(pl.multiple_of(base + s * sub, sub), sub), :].astype(BF16)
            first.append(go(tx0.at[i, s], rx0.at[i, s], core_at))
    acc[...] = part(pl.multiple_of(c * half, half), half)
    second = []
    for s in range(SUBS):
        first[s].wait_recv()
        tx1[s] = (acc[pl.ds(pl.multiple_of(other_y + s * sub, sub), sub), :] + rx0[0, s].astype(F32)).astype(BF16)
        second.append(go(tx1.at[s], rx1.at[s], y_at))
    own = (c * 2 + y) * quarter
    theirs = (c * 2 + 1 - y) * quarter
    to_y, to_core, onward = [], [], []
    for s in range(SUBS):
        first[SUBS + s].wait_recv()
        second[s].wait_recv()
        total = acc[pl.ds(pl.multiple_of(own_y + s * sub, sub), sub), :] + rx0[1, s].astype(F32) + rx1[s].astype(F32)
        rows = pl.ds(pl.multiple_of(off + own + s * sub, 16), sub)
        nx[rows, :] = middle(s, sub, total)
        to_y.append(go(nx.at[rows, :], nx.at[rows, :], y_at))
        to_core.append(go(nx.at[rows, :], nx.at[rows, :], core_at))
    if side is not None:
        srows = pl.ds(pl.multiple_of((c * 2 + y) * 8, 8), 8)
        to_y.append(go(side.at[srows, :], side.at[srows, :], y_at))
        to_core.append(go(side.at[srows, :], side.at[srows, :], core_at))
    for s in range(SUBS):
        to_y[s].wait_recv()
        rows = pl.ds(pl.multiple_of(off + theirs + s * sub, 16), sub)
        onward.append(go(nx.at[rows, :], nx.at[rows, :], core_at))
    if side is not None:
        to_y[SUBS].wait_recv()
        srows = pl.ds(pl.multiple_of((c * 2 + 1 - y) * 8, 8), 8)
        onward.append(go(side.at[srows, :], side.at[srows, :], core_at))
    for copy in to_core + onward:
        copy.wait_recv()
    for copy in sends:
        copy.wait_send()


HEAD_COPIES = 3 * SUBS + 3 * SUBS + 3


def head_fwd_body(tokens, last, width, gated, sq, ggain, wout, h_own, extra,
                  nx, h_new, branch, r2b, side, sqrx, tx0, rx0, tx1, rx1, acc, krc, ssem, rsem, qs, qr, hs, hr):
    me = lax.axis_index("head")
    at = lax.axis_index("seq")
    count = lax.axis_size("seq")
    peers = [lax.rem(me + k, 4) for k in (1, 2, 3)]
    barrier = pltpu.get_barrier_semaphore()
    for pr in peers:
        pl.semaphore_signal(barrier, inc=1, device_id={"head": pr}, device_id_type=MESH)
    if not last:
        @pl.when(at > 0)
        def _():
            pl.semaphore_signal(barrier, inc=1, device_id={"seq": at - 1}, device_id_type=MESH)
    if last:
        pl.semaphore_wait(barrier, 3)
    else:
        pl.semaphore_wait(barrier, 3 + (at < count - 1).astype(jnp.int32))
    copies = [send(sq, sqrx.at[2 - k], (qs.at[k], qr.at[2 - k]), {"head": pr}) for k, pr in enumerate(peers)]
    for copy in copies:
        copy.wait_send()
    for k in range(3):
        pltpu.make_async_remote_copy(src_ref=sq, dst_ref=sqrx.at[k], send_sem=qs.at[k], recv_sem=qr.at[k],
                                     device_id={"head": peers[2 - k]}, device_id_type=MESH).wait_recv()
    total_sq = ((sq[...] + sqrx[0]) + (sqrx[1] + sqrx[2]))[0:1, :]
    r2row = lax.rsqrt(total_sq / width + EPS)
    r2b[...] = jnp.transpose(jnp.broadcast_to(r2row, (LANE, tokens)))
    inner = gated.shape[1]

    def part(start, rows):
        where = pl.ds(start, rows)
        r2 = jnp.concatenate([r2b[where, :]] * (inner // LANE), axis=1)
        return bdot(gated[where, :] * r2 * ggain[...], wout[...], NN)

    d = wout.shape[1]

    def middle(s, sub, total):
        rows = pl.ds(s * sub, sub)
        branch[rows, :] = total
        h = h_own[rows, :] + total
        h_new[rows, :] = h
        if last:
            krc[rows, :] = jnp.broadcast_to(jnp.sum(extra[rows, :].astype(F32) * total, axis=1, keepdims=True), (sub, LANE))
            if s == SUBS - 1:
                mine = pl.ds(pl.multiple_of(((me % 2) * 2 + me // 2) * 8, 8), 8)
                side[mine, :] = jnp.transpose(krc[...])[0:8, :]
            return h.astype(BF16)
        r1 = lax.rsqrt(jnp.sum(h * h, axis=1, keepdims=True) / d + EPS)
        return (h * r1 * extra[...]).astype(BF16)

    off = 0 if last else HALO
    if not last:
        side[...] = jnp.zeros_like(side)
    head_core(tokens, part, middle, nx, off, side if last else None, tx0, rx0, tx1, rx1, acc, ssem, rsem, me,
              {"head": flip(me, 1)}, {"head": flip(me, 2)})
    if not last:
        src = nx.at[pl.ds(tokens, HALO), :]
        dst = nx.at[pl.ds(0, HALO), :]
        copy = pltpu.make_async_remote_copy(src_ref=src, dst_ref=dst, send_sem=hs.at[0], recv_sem=hr.at[0],
                                            device_id={"seq": lax.rem(at + 1, count)}, device_id_type=MESH)

        @pl.when(at < count - 1)
        def _():
            copy.start()
            copy.wait_send()

        @pl.when(at > 0)
        def _():
            copy.wait_recv()

        @pl.when(at == 0)
        def _():
            nx[pl.ds(0, HALO), :] = jnp.zeros((HALO, d), BF16)


def head_scratch(tokens, d):
    sub = tokens // 4 // SUBS
    return [pltpu.VMEM((2, SUBS, sub, d), BF16), pltpu.VMEM((2, SUBS, sub, d), BF16), pltpu.VMEM((SUBS, sub, d), BF16),
            pltpu.VMEM((SUBS, sub, d), BF16), pltpu.VMEM((tokens // 2, d), F32), pltpu.VMEM((tokens // 4, LANE), F32),
            pltpu.SemaphoreType.DMA((HEAD_COPIES,)), pltpu.SemaphoreType.DMA((HEAD_COPIES,))]


def head_fwd(gated, sq, ggain, wout, h_own, extra, last, width, cid):
    tokens, inner = gated.shape
    d = wout.shape[1]
    S = jax.ShapeDtypeStruct
    vm = pl.BlockSpec(memory_space=pltpu.VMEM)
    return pl.pallas_call(
        partial(head_fwd_body, tokens, last, width),
        name="head_fwd_last" if last else "head_fwd",
        in_specs=[vm] * 6,
        out_specs=[vm] * 5,
        out_shape=[S((tokens if last else tokens + HALO, d), BF16), S((tokens // 4, d), F32), S((tokens // 4, d), F32),
                   S((tokens, LANE), F32), S((32, LANE), F32)],
        scratch_shapes=[pltpu.VMEM((3, 8, tokens), F32)] + head_scratch(tokens, d)
        + [pltpu.SemaphoreType.DMA((3,)), pltpu.SemaphoreType.DMA((3,)), pltpu.SemaphoreType.DMA((1,)), pltpu.SemaphoreType.DMA((1,))],
        compiler_params=pltpu.CompilerParams(collective_id=cid, has_side_effects=True, vmem_limit_bytes=VMEM_LIMIT),
    )(gated, sq, ggain, wout, h_own, extra)


def head_bwd_body(tokens, gz, gu, small, wzx, wsmall, h_own, gain, g_own, branch,
                  gb, g_new, ggain, side, tx0, rx0, tx1, rx1, acc, krc, ssem, rsem):
    me = lax.axis_index("head")
    core_at, y_at = {"head": flip(me, 1)}, {"head": flip(me, 2)}
    greet([core_at, y_at])
    d = gain.shape[1]

    def part(start, rows):
        where = pl.ds(start, rows)
        return bdot(gz[where, :], wzx[0], NT) + bdot(gu[where, :], wzx[1], NT) + bdot(small[where, :], wsmall[...], NT)

    def middle(s, sub, total):
        rows = pl.ds(s * sub, sub)
        h = h_own[rows, :]
        r1 = lax.rsqrt(jnp.sum(h * h, axis=1, keepdims=True) / d + EPS)
        th = total * h
        gg = jnp.sum(th * r1, axis=0, keepdims=True)
        if s == 0:
            ggain[...] = gg
        else:
            ggain[...] += gg
        k1 = jnp.sum(th * gain[...], axis=1, keepdims=True)
        g = g_own[rows, :] + r1 * (gain[...] * total) - h * (r1 * r1 * r1 * (k1 / d))
        g_new[rows, :] = g
        low = g.astype(BF16)
        krc[rows, :] = jnp.broadcast_to(jnp.sum(low.astype(F32) * branch[rows, :], axis=1, keepdims=True), (sub, LANE))
        if s == SUBS - 1:
            mine = pl.ds(pl.multiple_of(((me % 2) * 2 + me // 2) * 8, 8), 8)
            side[mine, :] = jnp.transpose(krc[...])[0:8, :]
        return low

    head_core(tokens, part, middle, gb, 0, side, tx0, rx0, tx1, rx1, acc, ssem, rsem, me, core_at, y_at)


def head_bwd(gz, gu, small, wzx, wsmall, h_own, gain, g_own, branch, cid):
    tokens = gz.shape[0]
    d = gain.shape[1]
    S = jax.ShapeDtypeStruct
    vm = pl.BlockSpec(memory_space=pltpu.VMEM)
    return pl.pallas_call(
        partial(head_bwd_body, tokens),
        name="head_bwd",
        in_specs=[vm] * 9,
        out_specs=[vm] * 4,
        out_shape=[S((tokens, d), BF16), S((tokens // 4, d), F32), S((1, d), F32), S((32, LANE), F32)],
        scratch_shapes=head_scratch(tokens, d),
        compiler_params=pltpu.CompilerParams(collective_id=cid, has_side_effects=True, vmem_limit_bytes=VMEM_LIMIT),
    )(gz, gu, small, wzx, wsmall, h_own, gain, g_own, branch)


def maps_bwd_body(tokens, dkr, ubc, taps, aux, gdt, gtail, gm8, tapx,
                  small, gtaps, gtail_o, ytx, yrx, yacc, ctx, crx, us, ms, nextx, nextb, gmb, sems, semr):
    me = lax.axis_index("head")
    at = lax.axis_index("seq")
    count = lax.axis_size("seq")
    c = me % 2
    y = me // 2
    core_at, y_at = {"head": flip(me, 1)}, {"head": flip(me, 2)}
    barrier = pltpu.get_barrier_semaphore()
    for where in (core_at, y_at):
        pl.semaphore_signal(barrier, inc=1, device_id=where, device_id_type=MESH)

    @pl.when(at < count - 1)
    def _():
        pl.semaphore_signal(barrier, inc=1, device_id={"seq": at + 1}, device_id_type=MESH)
    pl.semaphore_wait(barrier, 2 + (at > 0).astype(jnp.int32))
    lanes = lax.broadcasted_iota(jnp.int32, (tokens, LANE), 1)
    before = {"seq": lax.rem(at + count - 1, count)}
    ahead_x = pltpu.make_async_remote_copy(src_ref=gm8, dst_ref=nextx, send_sem=sems.at[2], recv_sem=semr.at[2],
                                           device_id=before, device_id_type=MESH)

    @pl.when(at > 0)
    def _():
        ahead_x.start()
    low, high = dkr[:, :LANE], dkr[:, LANE:]
    ytx[...] = jnp.where(y == 0, high, low)
    one = send(ytx, yrx, (sems.at[0], semr.at[0]), y_at)
    tile = pl.ds(pl.multiple_of(y * LANE, LANE), LANE)
    us[...] = ubc[:, tile].astype(F32)
    tp = taps[:, tile]
    m = mix_taps(us, tp, aux, LANE)
    s = sig(m)
    slope = s * (1.0 + m * (1.0 - s))
    one.wait()
    ctx[...] = jnp.where(y == 0, low, high) + yrx[...]
    two = send(ctx, crx, (sems.at[1], semr.at[1]), core_at)
    two.wait()
    gm = (ctx[...] + crx[...]) * slope
    gmb[...] = gm[0:8]
    ahead_b = pltpu.make_async_remote_copy(src_ref=gmb, dst_ref=nextb, send_sem=sems.at[3], recv_sem=semr.at[3],
                                           device_id=before, device_id_type=MESH)

    @pl.when(at > 0)
    def _():
        ahead_b.start()

    @pl.when(at == count - 1)
    def _():
        nextx[...] = jnp.zeros_like(nextx)
        nextb[...] = jnp.zeros_like(nextb)
    gtaps[...] = jnp.zeros_like(gtaps)
    gtaps[0:1, :] = jnp.sum(gm * us[pl.ds(HALO, tokens), :], axis=0, keepdims=True)
    gtaps[CONV : CONV + 1, :] = jnp.sum(gm, axis=0, keepdims=True)
    for j in range(1, CONV):
        gtaps[j : j + 1, :] = jnp.sum(gm * aux[j - 1] * us[pl.ds(HALO - j, tokens), :], axis=0, keepdims=True)

    @pl.when(at < count - 1)
    def _():
        ahead_x.wait_recv()
        ahead_b.wait_recv()
    acc = gm * tp[0:1, :]
    for j in range(1, CONV):
        ms[pl.ds(0, tokens), :] = gm * aux[j - 1]
        ms[pl.ds(tokens, 8), :] = nextb[...]
        acc = acc + ms[pl.ds(j, tokens), :] * tp[j : j + 1, :]
    own = jnp.where(c == 0, lanes, LANE - 1 - lanes) < 64
    g = gdt[...].astype(F32)
    moved = jnp.concatenate([g[:, 64:], g[:, :64]], axis=1)
    small[...] = jnp.where(own, acc, jnp.where(c == 0, moved, g)).astype(BF16)
    gtail_o[...] = gtail[...].astype(BF16)
    nx = nextx[...]
    tail = gtail[...]
    rows = lax.broadcasted_iota(jnp.int32, tail.shape, 0)
    for j in range(1, CONV):
        for k in range(j):
            tail = tail + jnp.where(rows == 16 - j + k, nx[k : k + 1, :] * tapx[j : j + 1, :], 0.0)
    gtail_o[...] = tail.astype(BF16)

    @pl.when(at > 0)
    def _():
        ahead_x.wait_send()
        ahead_b.wait_send()


def maps_bwd(dkr, ubc, taps, aux, gdt, gtail, gm8, tapx, cid):
    tokens = dkr.shape[0]
    inner = tapx.shape[1]
    S = jax.ShapeDtypeStruct
    vm = pl.BlockSpec(memory_space=pltpu.VMEM)
    tile = pltpu.VMEM((tokens, LANE), F32)
    return pl.pallas_call(
        partial(maps_bwd_body, tokens),
        name="maps_bwd",
        in_specs=[vm] * 8,
        out_specs=[vm] * 3,
        out_shape=[S((tokens, LANE), BF16), S((8, LANE), F32), S((16, inner), BF16)],
        scratch_shapes=[tile, tile, tile, tile, tile, pltpu.VMEM((tokens + HALO, LANE), F32), pltpu.VMEM((tokens + 8, LANE), F32),
                        pltpu.VMEM((8, inner), F32), pltpu.VMEM((8, LANE), F32), pltpu.VMEM((8, LANE), F32),
                        pltpu.SemaphoreType.DMA((4,)), pltpu.SemaphoreType.DMA((4,))],
        compiler_params=pltpu.CompilerParams(collective_id=cid, has_side_effects=True, vmem_limit_bytes=VMEM_LIMIT),
    )(dkr, ubc, taps, aux, gdt, gtail, gm8, tapx)


def sums_body(parts, *refs):
    ins = refs[: 6 * parts]
    conv_x, conv_bc, ggate, gskip, gvec, ggain = refs[6 * parts : 6 * parts + 6]
    stage, rx, ssem, rsem = refs[6 * parts + 6 :]
    inner = stage.shape[2]
    me = lax.axis_index("head")
    tile = pl.multiple_of((me // 2) * LANE, LANE)
    steps = [("seq", b) for b in bits_of("seq")] + [("head", b) for b in bits_of("head")]
    wheres = [{axis: flip(lax.axis_index(axis), b)} for axis, b in steps]
    greet(wheres)
    stage[...] = jnp.zeros_like(stage)
    for l in range(parts):
        taps, gate, skip, vec, maps, gain = ins[6 * l : 6 * l + 6]
        stage[l, 0 : CONV + 1, :] = taps[0 : CONV + 1, :]
        stage[l, 5:6, :] = gate[...]
        stage[l, 6:7, :] = skip[...]
        stage[l, 7:8, 0:LANE] = vec[0:1, :]
        stage[l, 7:8, LANE : 2 * LANE] = vec[1:2, :]
        stage[l, 8:9, :] = gain[:, :inner]
        stage[l, 9:10, :] = gain[:, inner:]
        for r in range(CONV + 1):
            row = maps[r : r + 1, :] * 0.5
            here = [jnp.where(me // 2 == k, row, 0.0) for k in range(2)]
            stage[l, 10 + r // 3 : 11 + r // 3, (r % 3) * 2 * LANE : ((r % 3) * 2 + 2) * LANE] = jnp.concatenate(here, axis=1)
    for i, (axis, b) in enumerate(steps):
        if axis == "seq":
            copy = send(stage, rx.at[i], (ssem.at[i], rsem.at[i]), wheres[i])
            copy.wait()
            stage[...] += rx[i]
        else:
            where = pl.ds(8, 8)
            copy = send(stage.at[:, where, :], rx.at[i, :, where, :], (ssem.at[i], rsem.at[i]), wheres[i])
            copy.wait()
            stage[:, 8:16, :] += rx[i, :, 8:16, :]
    for l in range(parts):
        conv_x[l] = stage[l, 0 : CONV + 1, :]
        ggate[l : l + 1, :] = stage[l, 5:6, :]
        gskip[l : l + 1, :] = stage[l, 6:7, :]
        gvec[l : l + 1, :] = stage[l, 7:8, 0 : 2 * LANE]
        ggain[l : l + 1, :inner] = stage[l, 8:9, :]
        ggain[l : l + 1, inner:] = stage[l, 9:10, :]
        for r in range(CONV + 1):
            conv_bc[l, r : r + 1, :] = stage[l, 10 + r // 3 : 11 + r // 3, (r % 3) * 2 * LANE : ((r % 3) * 2 + 2) * LANE]


def sums_kernel(smalls, inner, d, cid):
    parts = len(smalls)
    n = len(bits_of("seq")) + len(bits_of("head"))
    vm = pl.BlockSpec(memory_space=pltpu.VMEM)
    S = jax.ShapeDtypeStruct
    return pl.pallas_call(
        partial(sums_body, parts),
        name="sums_small",
        in_specs=[vm] * (6 * parts),
        out_specs=[vm] * 6,
        out_shape=[S((parts, CONV + 1, inner), F32), S((parts, CONV + 1, 2 * LANE), F32), S((parts, inner), F32), S((parts, inner), F32),
                   S((parts, 2 * LANE), F32), S((parts, d), F32)],
        scratch_shapes=[pltpu.VMEM((parts, 16, inner), F32), pltpu.VMEM((n, parts, 16, inner), F32),
                        pltpu.SemaphoreType.DMA((n,)), pltpu.SemaphoreType.DMA((n,))],
        compiler_params=pltpu.CompilerParams(collective_id=cid, has_side_effects=True, vmem_limit_bytes=VMEM_LIMIT),
    )(*[x for part in smalls for x in part])


def pad_lanes(x, to=LANE):
    return jnp.pad(x, [(0, 0)] * (x.ndim - 1) + [(0, to - x.shape[-1])])


def forward_layer(nx, h_own, extra, q, aux, segrow, layer):
    heads, size, inner = q["heads"], q["size"], q["inner"]
    (gate, ux, ubc, krs, pdt, steps, cum, cT, gram, mixed, ypart, entry, state, dec, decl) = fwd_mix(
        heads, size, nx, q["w_zx"], q["w_bc"], q["w_dt"], q["taps_x"], q["taps_bc"], q["dt_bias"], q["a_log"], q["skip"], aux, segrow)
    enter = carry_kernel(state, dec, heads, size, False, layer)
    y, carr, gated, sq = fwd_gate(ypart, entry, gate, krs, enter)
    width = inner * lax.axis_size("head")
    nx_next, h_new, branch, r2b, side = head_fwd(gated, sq, q["gate_gain"], q["w_out"], h_own, extra, layer == LAYERS - 1, width, LAYERS + layer)
    stored = dict(nx=nx, gate=gate, ux=ux, ubc=ubc, krs=krs, pdt=pdt, steps=steps, cum=cum, cT=cT, gram=gram, mixed=mixed,
                  entry=entry, dec=dec, decl=decl, enter=enter, y=y, carr=carr, r2b=r2b, branch=branch, h_own=h_own)
    return nx_next, h_new, side, stored


def backward_layer(g_own, gb, side, s, q, aux, segrow, layer, branch_before):
    tokens = gb.shape[0]
    heads, size, inner = q["heads"], q["size"], q["inner"]
    width = inner * lax.axis_size("head")
    kr = side.reshape(4, 8, LANE)[:, 0, :].reshape(tokens)
    r2b = s["r2b"]
    krb = r2b * r2b * (kr[:, None] / width)
    gy, gz, scaled, qloc, ggate, gskip = bwd_gate(gb, q["w_out"], s["gate"], s["y"], s["mixed"], s["entry"], s["krs"], r2b, krb, q["gate_gain"])
    g_w_out = scatter_rows(mm_tn(gb, scaled))
    later = carry_kernel(qloc, s["dec"], heads, size, True, 2 * LAYERS + layer)
    dvd, dd, rowT, dkr = bwd_local(size, gy, s["mixed"], s["krs"], s["cum"], s["steps"], s["cT"], s["gram"], s["entry"], s["enter"], aux[5], segrow)
    gm8, gu, gtail, gtaps_x, gdt, gvec, dkr = bwd_carry(
        size, gy, dvd, s["mixed"], s["carr"], s["entry"], s["krs"], s["cum"], s["steps"], s["pdt"], q["dt_bias"], q["a_log"], q["skip"],
        s["ux"], q["taps_x"], aux, later, s["enter"], dd, rowT, dkr, s["decl"][:1])
    small, gtaps_bc, gtail = maps_bwd(dkr, s["ubc"], q["taps_bc"], aux, gdt, gtail, gm8, q["taps_x"], 3 * LAYERS + layer)
    gu = lax.dynamic_update_slice(gu, gtail, (tokens - 16, 0))
    normed = s["nx"][HALO:]
    g_w_zx = scatter_rows(mm_tn(normed, jnp.concatenate([gz, gu], 1)))
    g_w_small = scatter_rows(mm_tn(normed, small))
    gb, g_own, g_gain, side = head_bwd(gz, gu, small, q["w_zx"], q["w_small"], s["h_own"], q["gain"][None], g_own, branch_before, 4 * LAYERS + layer)
    return gb, g_own, side, (g_w_zx, g_w_small, g_w_out), (gtaps_x, ggate, gskip, gvec, gtaps_bc, g_gain)


def local(hidden_in, seg, cot, norm_gain, w_zx, w_bc, w_dt, conv_x, conv_bc, dt_bias, a_log, skip_d, gate_gain, w_out):
    tokens = hidden_in.shape[0]
    inner = w_zx.shape[3]
    heads = w_dt.shape[2]
    size = inner // heads
    rank = lax.axis_index("head")
    segf = seg.astype(F32)
    ext = jnp.concatenate([jnp.full((HALO,), segf[0], F32), segf], 0)
    vecs = [(ext[HALO - j : HALO - j + tokens] == segf).astype(F32) for j in range(1, CONV)]
    vecs += [(segf == segf[0]).astype(F32), (segf == segf[-1]).astype(F32), segf]
    aux = jnp.broadcast_to(jnp.stack(vecs, 0)[:, :, None], (len(vecs), tokens, LANE))
    segrow = segf[None]
    wt = jnp.transpose(w_zx, (0, 2, 1, 3))
    lanes = jnp.arange(LANE)
    own = jnp.where(rank % 2 == 0, lanes, LANE - 1 - lanes) < LANE // 2
    qs = []
    for l in range(LAYERS):
        dt_pad = pad_lanes(w_dt[l])
        tile = lax.dynamic_slice_in_dim(w_bc[l], (rank // 2) * LANE, LANE, 1)
        w_small = jnp.where(own[None], tile, jnp.where(rank % 2 == 0, jnp.roll(dt_pad, LANE // 2, axis=1), dt_pad))
        qs.append(dict(heads=heads, size=size, inner=inner, gain=norm_gain[l], w_zx=wt[l], w_bc=w_bc[l], w_dt=dt_pad, w_small=w_small,
                       taps_x=jnp.pad(conv_x[l], ((0, 3), (0, 0))), taps_bc=jnp.pad(conv_bc[l], ((0, 3), (0, 0))),
                       dt_bias=pad_lanes(dt_bias[l][None]), a_log=pad_lanes(a_log[l][None]), skip=jnp.repeat(skip_d[l], size)[None],
                       gate_gain=gate_gain[l][None], w_out=w_out[l]))
    h = hidden_in.astype(F32)
    h_own = own_rows(h)
    cot_own = own_rows(cot)
    normed = (h * lax.rsqrt(jnp.mean(h * h, axis=1, keepdims=True) + EPS) * norm_gain[0][None]).astype(BF16)
    nx = jnp.concatenate([shift(normed[tokens - HALO :], "seq", 1), normed], 0)
    stored = []
    for l in range(LAYERS):
        extra = cot_own if l == LAYERS - 1 else norm_gain[l + 1][None]
        nx, h_own, side, s = forward_layer(nx, h_own, extra, qs[l], aux, segrow, l)
        stored.append(s)
    hidden_out = nx
    gb = cot
    g_own = cot_own.astype(F32)
    larges, smalls = [], []
    for l in reversed(range(LAYERS)):
        before = stored[max(l - 1, 0)]["branch"]
        gb, g_own, side, large, small = backward_layer(g_own, gb, side, stored[l], qs[l], aux, segrow, l, before)
        larges.insert(0, large)
        smalls.insert(0, small)
    grad_in = gb.astype(F32)
    stack = lambda which, i: jnp.stack([m[i] for m in which], 0)
    g_w_zx = stack(larges, 0)
    g_w_zx = g_w_zx.reshape(g_w_zx.shape[0], g_w_zx.shape[1], 2, inner)
    g_small = stack(larges, 1)
    even = rank % 2 == 0
    g_w_bc = jnp.where(even, g_small[:, :, : LANE // 2], g_small[:, :, LANE // 2 :])
    g_w_dt = jnp.where(even, g_small[:, :, LANE // 2 : LANE // 2 + heads], g_small[:, :, :heads])
    g_w_out = jnp.transpose(stack(larges, 2), (0, 2, 1))
    g_conv_x, g_conv_bc, g_gate, g_skip, g_vec, g_gain = sums_kernel(smalls, inner, norm_gain.shape[1], 5 * LAYERS)
    g_skip = jnp.sum(g_skip.reshape(LAYERS, heads, size), axis=2)
    part = g_gain.shape[1] // lax.axis_size("seq")
    g_gain = lax.dynamic_slice_in_dim(g_gain, lax.axis_index("seq") * part, part, 1)
    return (hidden_out, grad_in, g_gain, g_w_zx, g_w_bc, g_w_dt, g_conv_x, g_conv_bc,
            g_vec[:, :heads], g_vec[:, LANE : LANE + heads], g_skip, g_gate, g_w_out)


def solution(mesh):
    placed = (
        P("seq", None), P("seq"), P("seq", None), P(), P(None, None, None, "head"), P(), P(None, None, "head"),
        P(None, None, "head"), P(), P(None, "head"), P(None, "head"), P(None, "head"), P(None, "head"), P(None, "head", None),
    )
    return jax.shard_map(
        local,
        mesh=mesh,
        in_specs=placed,
        out_specs=(
            P("seq", None), P("seq", None), P(None, "seq"), P(None, "seq", None, "head"), P(None, "seq", "head"),
            P(None, "seq", "head"), P(None, None, "head"), P(), P(None, "head"), P(None, "head"), P(None, "head"),
            P(None, "head"), P(None, "head", "seq"),
        ),
        check_vma=False,
    )
```

time: 1770 us -> 825 us (0.47)
  waiting for transfers between devices: 1090 us -> 144 us
  Pallas kernels: 0 us -> 495 us
  matrix products: 187 us -> 20.4 us
  other arithmetic: 171 us -> 40.1 us
  blocking collectives: 106 us -> 0 us
  local copies, waits for them, and re-layouts: 170 us -> 96 us
    pallas_call x0 -> x21, Pallas kernels: none -> 495 us  [the longest x1 119 us: sums_kernel(): pl.pallas_call(partial(sums_body, parts), name='sums_small', in_specs=[vm...]
    unnamed x18 -> x0, waiting for transfers between devices: 401 us -> none
    reduce_scatter x1 -> x0, waiting for transfers between devices: 314 us -> none  [local(): lax.psum_scatter(stack_layers(large_list, 1), 'seq', scatter_dimension=1,...]
    psum x5 -> x0, waiting for transfers between devices: 285 us -> none  [the longest x2 168 us: forward_layer(): branch = lax.psum(head_out, 'head')]
    dot_general x54 -> x6, matrix products: 187 us -> 20.4 us  [dot(): lax.dot_general(a.astype(BF16), b.astype(BF16), (dims, ((), ())), preferr...]
    ppermute x4 -> x19, waiting for transfers between devices: 6.38 us -> 144 us  [the longest x18 144 us: swap(): return lax.ppermute(x, axis, [(i, i ^ bit) for i in range(n)])]
    all_gather x4 -> x0, waiting for transfers between devices: 85.7 us -> none  [entering_2(): gathered = jax.tree.map(lambda a: lax.all_gather(a, axis), part)]
    psum x5 -> x0, blocking collectives: 64.2 us -> none  [the longest x1 38.8 us: local(): lax.psum((stack_layers(small_list, 0), stack_layers(small_list, 1), stack...]
  transfers between devices with their start and end apart: 18 -> 19, of which waited for: 15 -> 12; matrix products, arithmetic and copies ran while one was open for 13% -> 14% of each run, Pallas kernels for 0% -> 15%
where the time goes in v1:
time: 825 us; the launch traced here: 814 us
  Pallas kernels  495 us (60%)
  waiting for transfers between devices  144 us (17%)
  local copies, waits for them, and re-layouts  96 us (12%)
  other arithmetic  40.1 us (5%)
  matrix products  20.4 us (2%)
  starting transfers between devices  16.9 us (2%)
    ppermute x18, waiting for transfers between devices, swap(): return lax.ppermute(x, axis, [(i, i ^ bit) for i in range(n)])  144 us
    pallas_call x1, Pallas kernels, sums_kernel(): pl.pallas_call(partial(sums_body, parts), name='sums_small', in_specs=[vm...  119 us
    pallas_call x4, Pallas kernels, carry_kernel(): pl.pallas_call(partial(carry_body, bits, reverse, heads, size), name='car...  101 us
    pallas_call x2, Pallas kernels, head_fwd(): pl.pallas_call(partial(head_fwd_body, tokens, last, width), name='head_fw...  63.4 us
    pallas_call x2, Pallas kernels, head_bwd(): pl.pallas_call(partial(head_bwd_body, tokens), name='head_bwd', in_specs=...  58.8 us
    pallas_call x2, Pallas kernels, fwd_mix(): pl.pallas_call(partial(fwd_mix_body, heads, size), name='fwd_mix', grid=(...  35.1 us
    pallas_call x2, Pallas kernels, bwd_carry(): pl.pallas_call(partial(bwd_carry_body, size), name='bwd_carry', grid=(inn...  34.8 us
    pallas_call x2, Pallas kernels, maps_bwd(): pl.pallas_call(partial(maps_bwd_body, tokens), name='maps_bwd', in_specs=...  28.8 us
  transfers between devices with their start and end apart: 19, of which 12 were waited for; matrix products, arithmetic and copies ran while one was open for 14% of the time, Pallas kernels for 15%

profile of v1, /device:TPU:0, one launch (start us, length us, event | category | flops | bytes accessed | tf_op | source)
XLA Modules:
  0.0 814.5 jit_solution(14904413783974549750)
XLA Ops:
  2.1 1.8 multiply_reduce_fusion
  5.0 5.4 collective-permute-start
  10.4 8.6 %copy.89 = bf16[2,1536,2,768]{3,1,2,0:T(8,128)(2,1)} copy(bf16[2,1536,2,768]{3,2,1,0:T(2,128)(2,1)} %param.18) | data formatting | bytes 18874368 | tf_op args[4]
  19.0 8.0 slice_bitcast_fusion
  27.0 1.8 fusion.48
  30.7 1.9 copy.63
  41.7 4.8 slice_bitcast_fusion.2
  46.5 2.1 convert.5
  48.6 2.8 constant_dynamic-slice_fusion.8
  52.3 2.2 dynamic-slice_bitcast_fusion.h_own
  56.5 2.7 fusion.41
  59.3 2.9 bitcast_select_fusion
  73.6 2.1 pad_maximum_fusion.1.nx
  77.2 17.6 %fwd_mix.2 = (bf16[512,768]{1,0:T(8,128)(2,1)}, bf16[528,768]{1,0:T(8,128)(2,1)}, bf16[528,256]{1,0:T(8,128)(2,1)}, bf16[512,256]{1,0:T(8,128)(2,1)}, bf16[512,1...) custom-call(bf16[528,1536]{1,0:T(8,128)(2,1)} %pad_maximum_fusion.1., ...), custom_call_target="tpu_custom_call" | custom-call | flops 4114612224 | bytes 11010048 | tf_op jit(solution)/shard_map/fwd_mix/pallas_call | solution.py:265
  94.8 23.7 %carry_on.2.enter = f32[768,128]{1,0:T(8,128)} custom-call(f32[768,128]{1,0:T(8,128)} %get-tuple-element.114.st, f32[16,128]{1,0:T(8,128)} %get-tuple-element.115.dec), custom_call_target="tpu_custom_call" | custom-call | tf_op jit(solution)/shard_map/carry_on/pallas_call | solution.py:613
  118.5 6.8 fwd_gate.2
  125.4 32.7 %head_fwd.1 = (bf16[528,1536]{1,0:T(8,128)(2,1)}, f32[128,1536]{1,0:T(8,128)}, f32[128,1536]{1,0:T(8,128)}, f32[512,128]{1,0:T(8,128)}, f32[32,128]{1,0:T(8,128)}) custom-call(f32[512,768]{1,0:T(8,128)} %get-tuple-element.116.gated, f32[8,512]{1,0:T(8,128)} %get-tuple-element.117.sq, f32[1,768]{1,0:T(1,128)} %get-tuple-element.257.ggain.gain, ...), custom_call_target="tpu_custom_call" | custom-call | tf_op jit(solution)/shard_map/head_fwd/pallas_call | solution.py:774
  158.1 17.6 %fwd_mix.3 = (bf16[512,768]{1,0:T(8,128)(2,1)}, bf16[528,768]{1,0:T(8,128)(2,1)}, bf16[528,256]{1,0:T(8,128)(2,1)}, bf16[512,256]{1,0:T(8,128)(2,1)}, bf16[512,1...) custom-call(bf16[528,1536]{1,0:T(8,128)(2,1)} %get-tuple-element.118, ...), custom_call_target="tpu_custom_call" | custom-call | flops 4114612224 | bytes 11010048 | tf_op jit(solution)/shard_map/fwd_mix/pallas_call | solution.py:265
  175.6 25.7 %carry_on.3.enter = f32[768,128]{1,0:T(8,128)} custom-call(f32[768,128]{1,0:T(8,128)} %get-tuple-element.123.st, f32[16,128]{1,0:T(8,128)} %get-tuple-element.124.dec), custom_call_target="tpu_custom_call" | custom-call | tf_op jit(solution)/shard_map/carry_on/pallas_call | solution.py:613
  201.3 7.0 fwd_gate.3
  208.3 30.7 %head_fwd_last.1 = (bf16[512,1536]{1,0:T(8,128)(2,1)}, f32[128,1536]{1,0:T(8,128)}, f32[128,1536]{1,0:T(8,128)}, f32[512,128]{1,0:T(8,128)}, f32[32,128]{1,0:T(8,128)}) custom-call(f32[512,768]{1,0:T(8,128)} %get-tuple-element.125.gated, f32[8,512]{1,0:T(8,128)} %get-tuple-element.126.sq, f32[1,768]{1,0:T(1,128)} %get-tuple-element.256.ggain.gain, ...), custom_call_target="tpu_custom_call" | custom-call | tf_op jit(solution)/shard_map/head_fwd_last/pallas_call | solution.py:774
  239.7 1.8 multiply_multiply_fusion.1.krb
  241.5 9.3 %bwd_gate.2 = (f32[512,768]{1,0:T(8,128)}, bf16[512,768]{1,0:T(8,128)(2,1)}, bf16[512,768]{1,0:T(8,128)(2,1)}, f32[768,128]{1,0:T(8,128)}, f32[1,768]{1,0:T(1,128)}, /*index=5*/f32[1,768]{1,0:T(1,128)}) custom-call(bf16[512,1536]{1,0:T(8,128)(2,1)} %gb.1, bf16[768,1536]{1,0:T(8,128)(2,1)} %get-tuple-element.237.wout, ...), custom_call_target="tpu_custom_call" | custom-call | flops 1207959552 | bytes 12582912 | tf_op jit(solution)/shard_map/bwd_gate/pallas_call | solution.py:352
  250.8 24.9 %carry_back.2.later = f32[768,128]{1,0:T(8,128)} custom-call(f32[768,128]{1,0:T(8,128)} %get-tuple-element.143.st, f32[16,128]{1,0:T(8,128)} %get-tuple-element.124.dec), custom_call_target="tpu_custom_call" | custom-call | tf_op jit(solution)/shard_map/carry_back/pallas_call | solution.py:613
  277.6 10.9 %bwd_local.2 = (f32[512,768]{1,0:T(8,128)}, f32[512,128]{1,0:T(8,128)}, f32[128,512]{1,0:T(8,128)}, f32[512,256]{1,0:T(8,128)}) custom-call(f32[512,768]{1,0:T(8,128)} %get-tuple-element.134.gy_r, f32[512,768]{1,0:T(8,128)} %get-tuple-element.130.mixed, bf16[512,256]{1,0:T(8,128)(2,1)} %get-tuple-element.122.krs, f32[512,128]{1,0:T(8,128)} %get-tuple-element.135.cum, ...), custom_call_target="tpu_custom_call" | custom-call | flops 2415919104 | bytes 7864320 | tf_op jit(solution)/shard_map/bwd_local/pallas_call | solution.py:441
  288.5 22.7 %bwd_carry.2 = (f32[8,768]{1,0:T(8,128)}, bf16[512,768]{1,0:T(8,128)(2,1)}, f32[16,768]{1,0:T(8,128)}, f32[8,768]{1,0:T(8,128)}, bf16[512,128]{1,0:T(8,128)(2,1)}, /*index=5*/f32[8,128]{1,0:T(8,128)}, f32[512,256]{1,0:T(8,128)}) custom-call(f32[512,768]{1,0:T(8,128)} %get-tuple-element.134.gy_r, f32[512,768]{1,0:T(8,128)} %get-tuple-element.139.dvd_r, ...), custom_call_target="tpu_custom_call" | custom-call | flops 201326592 | bytes 9437184 | tf_op jit(solution)/shard_map/bwd_carry/pallas_call | solution.py:535
  311.3 14.3 %maps_bwd.2 = (bf16[512,128]{1,0:T(8,128)(2,1)}, f32[8,128]{1,0:T(8,128)}, bf16[16,768]{1,0:T(8,128)(2,1)}) custom-call(f32[512,256]{1,0:T(8,128)} %get-tuple-element.149.dkr, bf16[528,256]{1,0:T(8,128)(2,1)} %get-tuple-element.150.ubc, f32[8,256]{1,0:T(8,128)} %pad.44.tapbc.taps, f32[6,512,128]{2,1,0:T(8,128)} %broadcast_in_dim.31.aux, ...), custom_call_target="tpu_custom_call" | custom-call | tf_op jit(solution)/shard_map/maps_bwd/pallas_call | solution.py:927
  327.3 5.4 fusion.6
  332.7 29.4 %head_bwd.2 = (bf16[512,1536]{1,0:T(8,128)(2,1)}, f32[128,1536]{1,0:T(8,128)}, f32[1,1536]{1,0:T(1,128)}, f32[32,128]{1,0:T(8,128)}) custom-call(bf16[512,768]{1,0:T(8,128)(2,1)} %get-tuple-element.133.gz, bf16[512,768]{1,0:T(8,128)(2,1)} %copy-done.20, bf16[512,128]{1,0:T(8,128)(2,1)} %get-tuple-element.155.small, ...), custom_call_target="tpu_custom_call" | custom-call | tf_op jit(solution)/shard_map/head_bwd/pallas_call | solution.py:826
  363.7 9.3 %bwd_gate.3 = (f32[512,768]{1,0:T(8,128)}, bf16[512,768]{1,0:T(8,128)(2,1)}, bf16[512,768]{1,0:T(8,128)(2,1)}, f32[768,128]{1,0:T(8,128)}, f32[1,768]{1,0:T(1,128)}, /*index=5*/f32[1,768]{1,0:T(1,128)}) custom-call(bf16[512,1536]{1,0:T(8,128)(2,1)} %get-tuple-element.157.gb, bf16[768,1536]{1,0:T(8,128)(2,1)} %get-tuple-element.238.wout, ...), custom_call_target="tpu_custom_call" | custom-call | flops 1207959552 | bytes 12582912 | tf_op jit(solution)/shard_map/bwd_gate/pallas_call | solution.py:352
  373.0 26.6 %carry_back.3.later = f32[768,128]{1,0:T(8,128)} custom-call(f32[768,128]{1,0:T(8,128)} %get-tuple-element.172.st, f32[16,128]{1,0:T(8,128)} %get-tuple-element.115.dec), custom_call_target="tpu_custom_call" | custom-call | tf_op jit(solution)/shard_map/carry_back/pallas_call | solution.py:613
  400.8 10.9 %bwd_local.3 = (f32[512,768]{1,0:T(8,128)}, f32[512,128]{1,0:T(8,128)}, f32[128,512]{1,0:T(8,128)}, f32[512,256]{1,0:T(8,128)}) custom-call(f32[512,768]{1,0:T(8,128)} %get-tuple-element.163.gy_r, f32[512,768]{1,0:T(8,128)} %get-tuple-element.159.mixed, bf16[512,256]{1,0:T(8,128)(2,1)} %get-tuple-element.113.krs, f32[512,128]{1,0:T(8,128)} %get-tuple-element.164.cum, ...), custom_call_target="tpu_custom_call" | custom-call | flops 2415919104 | bytes 7864320 | tf_op jit(solution)/shard_map/bwd_local/pallas_call | solution.py:441
  411.7 12.1 %bwd_carry.3 = (f32[8,768]{1,0:T(8,128)}, bf16[512,768]{1,0:T(8,128)(2,1)}, f32[16,768]{1,0:T(8,128)}, f32[8,768]{1,0:T(8,128)}, bf16[512,128]{1,0:T(8,128)(2,1)}, /*index=5*/f32[8,128]{1,0:T(8,128)}, f32[512,256]{1,0:T(8,128)}) custom-call(f32[512,768]{1,0:T(8,128)} %get-tuple-element.163.gy_r, f32[512,768]{1,0:T(8,128)} %get-tuple-element.168.dvd_r, ...), custom_call_target="tpu_custom_call" | custom-call | flops 201326592 | bytes 9437184 | tf_op jit(solution)/shard_map/bwd_carry/pallas_call | solution.py:535
  423.8 14.5 %maps_bwd.3 = (bf16[512,128]{1,0:T(8,128)(2,1)}, f32[8,128]{1,0:T(8,128)}, bf16[16,768]{1,0:T(8,128)(2,1)}) custom-call(f32[512,256]{1,0:T(8,128)} %get-tuple-element.178.dkr, bf16[528,256]{1,0:T(8,128)(2,1)} %get-tuple-element.179.ubc, f32[8,256]{1,0:T(8,128)} %pad.39.tapbc.taps, f32[6,512,128]{2,1,0:T(8,128)} %broadcast_in_dim.31.aux, ...), custom_call_target="tpu_custom_call" | custom-call | tf_op jit(solution)/shard_map/maps_bwd/pallas_call | solution.py:927
  438.3 1.6 fusion.58
  440.0 5.6 fusion.2
  445.6 29.3 %head_bwd.3 = (bf16[512,1536]{1,0:T(8,128)(2,1)}, f32[128,1536]{1,0:T(8,128)}, f32[1,1536]{1,0:T(1,128)}, f32[32,128]{1,0:T(8,128)}) custom-call(bf16[512,768]{1,0:T(8,128)(2,1)} %get-tuple-element.162.gz, bf16[512,768]{1,0:T(8,128)(2,1)} %copy-done.18, bf16[512,128]{1,0:T(8,128)(2,1)} %get-tuple-element.184.small, ...), custom_call_target="tpu_custom_call" | custom-call | tf_op jit(solution)/shard_map/head_bwd/pallas_call | solution.py:826
  475.0 3.5 convert_element_type.200
  478.5 4.0 fusion.1
  483.6 4.1 fusion
  492.1 119.2 %sums_small.1 = (f32[2,5,768]{2,1,0:T(8,128)}, f32[2,5,256]{2,1,0:T(8,128)}, f32[2,768]{1,0:T(2,128)}, f32[2,768]{1,0:T(2,128)}, f32[2,256]{1,0:T(2,128)}, /*index=5*/f32[2,1536]{1,0:T(2,128)}) custom-call(f32[8,768]{1,0:T(8,128)} %get-tuple-element.187.refs_0_, f32[1,768]{1,0:T(1,128)} %get-tuple-element.188.refs_1_, f32[1,768]{1,0:T(1,128)} %get-tuple-element.189.refs_2_, ...), custom_call_target="tpu_custom_call" | custom-call | tf_op jit(solution)/shard_map/sums_small/pallas_call | solution.py:990
  615.4 4.7 convolution_bitcast_fusion
  620.1 6.3 copy.58
  626.4 1.9 fusion.15
  634.2 4.5 collective-permute-done.8
  638.8 4.6 collective-permute-done.11
  643.5 5.7 collective-permute-done.9
  649.2 5.0 collective-permute-done.12
  654.2 3.1 collective-permute-done.16
  658.4 22.9 %collective-permute-done.13 = bf16[2,2,192,768]{3,2,0,1:T(8,128)(2,1)S(1)} collective-permute-done((bf16[2,2,192,768]{3,2,0,1:T(8,128)(2,1)S(1)}, bf16[2,2,192,768]{3,2,0,1:T(8,128)(2,1)S(1)}, u32[]{:S(2)}, u32[]{:S(2)}) %collective-permute-start.13) | collective-permute-done | bytes 1179680 | tf_op jit(solution)/shard_map/ppermute | solution.py:35
  684.8 1.7 copy.59
  686.4 1.8 fusion.26
  688.2 1.6 copy.60
  691.2 2.2 collective-permute-start.18
  693.4 9.4 %collective-permute-done.14 = bf16[2,192,768]{2,1,0:T(8,128)(2,1)} collective-permute-done((bf16[2,192,768]{2,1,0:T(8,128)(2,1)}, bf16[2,192,768]{2,1,0:T(8,128)(2,1)}, u32[]{:S(2)}, u32[]{:S(2)}) %collective-permute-start.14) | collective-permute-done | bytes 589856 | tf_op jit(solution)/shard_map/ppermute | solution.py:35
  704.5 4.0 bitcast_add_fusion
  708.6 2.3 collective-permute-start.5
  710.9 2.4 bitcast_add_fusion.1
  713.9 5.3 collective-permute-done.15
  719.2 31.6 %collective-permute-done.5 = bf16[2,192,1536]{2,1,0:T(8,128)(2,1)S(1)} collective-permute-done((bf16[2,192,1536]{2,1,0:T(8,128)(2,1)S(1)}, bf16[2,192,1536]{2,1,0:T(8,128)(2,1)S(1)}, u32[]{:S(2)}, u32[]{:S(2)}) %collective-permute-start.5) | collective-permute-done | bytes 1179680 | tf_op jit(solution)/shard_map/ppermute | solution.py:35
  751.2 28.8 %collective-permute-done.2 = bf16[2,192,1536]{2,1,0:T(8,128)(2,1)S(1)} collective-permute-done((bf16[2,192,1536]{2,1,0:T(8,128)(2,1)S(1)}, bf16[2,192,1536]{2,1,0:T(8,128)(2,1)S(1)}, u32[]{:S(2)}, u32[]{:S(2)}) %collective-permute-start.2) | collective-permute-done | bytes 1179680 | tf_op jit(solution)/shard_map/ppermute | solution.py:35
  782.5 1.8 stack.76
  784.3 23.1 %collective-permute-done.3 = bf16[192,1536]{1,0:T(8,128)(2,1)} collective-permute-done((bf16[192,1536]{1,0:T(8,128)(2,1)}, bf16[192,1536]{1,0:T(8,128)(2,1)}, u32[]{:S(2)}, u32[]{:S(2)}) %collective-permute-start.3) | collective-permute-done | bytes 589856 | tf_op jit(solution)/shard_map/ppermute | solution.py:35
  809.8 2.5 pad_maximum_fusion
  (184 shorter events, 67.6 us)
Async XLA Ops:
  0.6 3.3 copy-start
  5.0 68.6 %collective-permute-start = (bf16[16,1536]{1,0:T(8,128)(2,1)}, bf16[16,1536]{1,0:T(8,128)(2,1)}, u32[]{:S(2)}, u32[]{:S(2)}) collective-permute-start(bf16[16,1536]{1,0:T(8,128)(2,1)} %slice.176), channel_id=1, source_target_pairs={{0,4},{4,8},{8,12},{12,16},{16,20},{20,24},{24,28},{1,5},{5,9},{9,... | collective-permute-start | bytes 147464 | tf_op jit(solution)/shard_map/ppermute | solution.py:40
  19.0 8.0 copy-start.11
  27.0 1.8 copy-start.22
  39.1 0.6 copy-start.23
  48.5 2.8 copy-start.1
  52.3 3.3 copy-start.7
  52.3 2.2 copy-start.9
  54.4 4.8 copy-start.8
  59.3 2.9 copy-start.29
  241.5 35.4 %copy-start.24 = (f32[512]{0:T(512)S(1)}, f32[512]{0:T(512)}, u32[]{:S(2)}) copy-start(f32[512]{0:T(512)} %copy-done.23) | copy-start | bytes 6148
  311.3 14.4 %copy-start.12 = (bf16[528,1536]{1,0:T(8,128)(2,1)S(1)}, bf16[528,1536]{1,0:T(8,128)(2,1)}, u32[]{:S(2)}) copy-start(bf16[528,1536]{1,0:T(8,128)(2,1)} %get-tuple-element.118.nx) | copy-start | bytes 4866052
  325.6 1.7 copy-start.19
  325.6 1.7 copy-start.26
  325.6 1.7 copy-start.16
  327.3 5.4 copy-start.20
  332.7 30.2 %copy-start.13 = (f32[512,128]{1,0:T(8,128)S(1)}, f32[512,128]{1,0:T(8,128)}, u32[]{:S(2)}) copy-start(f32[512,128]{1,0:T(8,128)} %get-tuple-element.160.r2b) | copy-start | bytes 786436
  438.3 1.7 copy-start.17
  438.3 1.7 copy-start.25
  438.3 1.7 copy-start.15
  440.0 5.7 copy-start.18
  482.5 222.0 %collective-permute-start.4 = (bf16[2,2,192,1536]{3,2,1,0:T(8,128)(2,1)}, bf16[2,2,192,1536]{3,2,1,0:T(8,128)(2,1)}, u32[]{:S(2)}, u32[]{:S(2)}) collective-permute-start(bf16[2,2,192,1536]{3,2,1,0:T(8,128)(2,1)} %fusion.1), channel_id=1, source_target_pairs={{0,4},{4,0},{8,12},{12,8},{16,20},{20,16},{24,28},{28,24},{1,5},{5... | collective-permute-start | bytes 7077896 | tf_op jit(solution)/shard_map/ppermute | solution.py:35
  483.6 131.8 %copy-start.2 = (bf16[512,1536]{1,0:T(8,128)(2,1)S(1)}, bf16[512,1536]{1,0:T(8,128)(2,1)}, u32[]{:S(2)}) copy-start(bf16[512,1536]{1,0:T(8,128)(2,1)} %gb.1) | copy-start | bytes 4718596
  487.7 223.2 %collective-permute-start.1 = (bf16[2,2,192,1536]{3,2,1,0:T(8,128)(2,1)}, bf16[2,2,192,1536]{3,2,1,0:T(8,128)(2,1)}, u32[]{:S(2)}, u32[]{:S(2)}) collective-permute-start(bf16[2,2,192,1536]{3,2,1,0:T(8,128)(2,1)} %fusion), channel_id=1, source_target_pairs={{0,4},{4,0},{8,12},{12,8},{16,20},{20,16},{24,28},{28,24},{1,5},{5... | collective-permute-start | bytes 7077896 | tf_op jit(solution)/shard_map/ppermute | solution.py:35
  489.4 143.6 %collective-permute-start.7 = (bf16[2,2,192,128]{3,2,0,1:T(8,128)(2,1)}, bf16[2,2,192,128]{3,2,0,1:T(8,128)(2,1)S(1)}, u32[]{:S(2)}, u32[]{:S(2)}) collective-permute-start(bf16[2,2,192,128]{3,2,0,1:T(8,128)(2,1)} %fusion.30), channel_id=1, source_target_pairs={{0,4},{4,0},{8,12},{12,8},{16,20},{20,16},{24,28},{28,24},{1,5},{5... | collective-permute-start | bytes 589832 | tf_op jit(solution)/shard_map/ppermute | solution.py:35
  491.2 142.9 %collective-permute-start.10 = (bf16[2,2,192,128]{3,2,0,1:T(8,128)(2,1)}, bf16[2,2,192,128]{3,2,0,1:T(8,128)(2,1)S(1)}, u32[]{:S(2)}, u32[]{:S(2)}) collective-permute-start(bf16[2,2,192,128]{3,2,0,1:T(8,128)(2,1)} %fusion.31), channel_id=1, source_target_pairs={{0,4},{4,0},{8,12},{12,8},{16,20},{20,16},{24,28},{28,24},{1,5},{5... | collective-permute-start | bytes 589832 | tf_op jit(solution)/shard_map/ppermute | solution.py:35
  626.4 3.0 copy-start.3
  626.4 3.0 copy-start.21
  628.4 28.9 %collective-permute-start.16 = (bf16[2,2,192,768]{3,2,1,0:T(8,128)(2,1)S(1)}, bf16[2,2,192,768]{3,2,1,0:T(8,128)(2,1)S(1)}, u32[]{:S(2)}, u32[]{:S(2)}) collective-permute-start(bf16[2,2,192,768]{3,2,1,0:T(8,128)(2,1)S(1)} %fusion.15), channel_id=1, source_target_pairs={{0,4},{4,0},{8,12},{12,8},{16,20},{20,16},{24,28},{28,24},{1,5},{5... | collective-permute-start | bytes 3538952 | tf_op jit(solution)/shard_map/ppermute | solution.py:35
  629.4 27.9 %slice-start = ((s8[4718592]{0:T(1024)(128)(4,1)}), s8[4194304]{0:T(1024)(128)(4,1)S(1)}, s32[]{:S(2)}) async-start(s8[4718592]{0:T(1024)(128)(4,1)} %bitcast.169), calls=%async_computation | async-start | bytes 8388608
  629.4 27.9 %slice-start.1 = ((s8[4718592]{0:T(1024)(128)(4,1)}), s8[524288]{0:T(1024)(128)(4,1)S(1)}, s32[]{:S(2)}) async-start(s8[4718592]{0:T(1024)(128)(4,1)} %bitcast.169), calls=%async_computation.1 | async-start | bytes 1048576
  630.9 1.5 copy-start.28
  632.9 48.4 %collective-permute-start.13 = (bf16[2,2,192,768]{3,2,0,1:T(8,128)(2,1)S(1)}, bf16[2,2,192,768]{3,2,0,1:T(8,128)(2,1)S(1)}, u32[]{:S(2)}, u32[]{:S(2)}) collective-permute-start(bf16[2,2,192,768]{3,2,0,1:T(8,128)(2,1)S(1)} %fusion.16), channel_id=1, source_target_pairs={{0,4},{4,0},{8,12},{12,8},{16,20},{20,16},{24,28},{28,24},{1,5},{5... | collective-permute-start | bytes 3538952 | tf_op jit(solution)/shard_map/ppermute | solution.py:35
  634.1 4.7 collective-permute-start.8
  638.7 4.6 collective-permute-start.11
  643.4 5.8 collective-permute-start.9
  649.2 5.0 collective-permute-start.12
  654.2 29.8 %copy-start.14 = (f32[1,192,128]{2,1,0:T(8,128)}, f32[1,192,128]{2,1,0:T(8,128)S(1)}, u32[]{:S(2)}) copy-start(f32[1,192,128]{2,1,0:T(8,128)S(1)} %fusion.34) | copy-start | bytes 294916
  658.4 31.4 %collective-permute-start.17 = (bf16[2,192,768]{2,1,0:T(8,128)(2,1)}, bf16[2,192,768]{2,1,0:T(8,128)(2,1)}, u32[]{:S(2)}, u32[]{:S(2)}) collective-permute-start(bf16[2,192,768]{2,1,0:T(8,128)(2,1)} %fusion.20), channel_id=1, source_target_pairs={{0,8},{4,12},{8,0},{12,4},{16,24},{20,28},{24,16},{28,20},{1,9},{5... | collective-permute-start | bytes 1769480 | tf_op jit(solution)/shard_map/ppermute | solution.py:35
  681.6 1.5 copy-start.4
  683.9 18.9 %collective-permute-start.14 = (bf16[2,192,768]{2,1,0:T(8,128)(2,1)}, bf16[2,192,768]{2,1,0:T(8,128)(2,1)}, u32[]{:S(2)}, u32[]{:S(2)}) collective-permute-start(bf16[2,192,768]{2,1,0:T(8,128)(2,1)} %fusion.19), channel_id=1, source_target_pairs={{0,8},{4,12},{8,0},{12,4},{16,24},{20,28},{24,16},{28,20},{1,9},{5... | collective-permute-start | bytes 1769480 | tf_op jit(solution)/shard_map/ppermute | solution.py:35
  683.9 27.0 %slice-start.2 = ((s8[9437184]{0:T(1024)(128)(4,1)}), s8[1048576]{0:T(1024)(128)(4,1)S(1)}, s32[]{:S(2)}) async-start(s8[9437184]{0:T(1024)(128)(4,1)} %bitcast.177), calls=%async_computation.2 | async-start | bytes 2097152
  689.9 12.9 %copy-start.5 = (f32[2,2,192,768]{3,2,0,1:T(8,128)S(1)}, f32[2,2,192,768]{3,2,0,1:T(8,128)}, u32[]{:S(2)}) copy-start(f32[2,2,192,768]{3,2,0,1:T(8,128)} %copy-done.4) | copy-start | bytes 7077892
  691.2 19.7 %slice-start.3 = ((s8[9437184]{0:T(1024)(128)(4,1)}), s8[4194304]{0:T(1024)(128)(4,1)S(1)}, s32[]{:S(2)}) async-start(s8[9437184]{0:T(1024)(128)(4,1)} %bitcast.177), calls=%async_computation.3 | async-start | bytes 8388608
  691.2 22.6 %collective-permute-start.18 = (bf16[192,768]{1,0:T(8,128)(2,1)S(1)}, bf16[192,768]{1,0:T(8,128)(2,1)S(1)}, u32[]{:S(2)}, u32[]{:S(2)}) collective-permute-start(bf16[192,768]{1,0:T(8,128)(2,1)S(1)} %fusion.24), channel_id=1, source_target_pairs={{0,16},{4,20},{8,24},{12,28},{16,0},{20,4},{24,8},{28,12},{1,17},{... | collective-permute-start | bytes 884744 | tf_op jit(solution)/shard_map/ppermute | solution.py:35
  704.0 6.9 slice-start.4
  704.0 15.1 %collective-permute-start.15 = (bf16[192,768]{1,0:T(8,128)(2,1)S(1)}, bf16[192,768]{1,0:T(8,128)(2,1)S(1)}, u32[]{:S(2)}, u32[]{:S(2)}) collective-permute-start(bf16[192,768]{1,0:T(8,128)(2,1)S(1)} %fusion.23), channel_id=1, source_target_pairs={{0,16},{4,20},{8,24},{12,28},{16,0},{20,4},{24,8},{28,12},{1,17},{... | collective-permute-start | bytes 884744 | tf_op jit(solution)/shard_map/ppermute | solution.py:35
  708.6 42.2 %collective-permute-start.5 = (bf16[2,192,1536]{2,1,0:T(8,128)(2,1)S(1)}, bf16[2,192,1536]{2,1,0:T(8,128)(2,1)S(1)}, u32[]{:S(2)}, u32[]{:S(2)}) collective-permute-start(bf16[2,192,1536]{2,1,0:T(8,128)(2,1)S(1)} %fusion.14), channel_id=1, source_target_pairs={{0,8},{4,12},{8,0},{12,4},{16,24},{20,28},{24,16},{28,20},{1,9},{5... | collective-permute-start | bytes 3538952 | tf_op jit(solution)/shard_map/ppermute | solution.py:35
  713.5 66.6 %collective-permute-start.2 = (bf16[2,192,1536]{2,1,0:T(8,128)(2,1)S(1)}, bf16[2,192,1536]{2,1,0:T(8,128)(2,1)S(1)}, u32[]{:S(2)}, u32[]{:S(2)}) collective-permute-start(bf16[2,192,1536]{2,1,0:T(8,128)(2,1)S(1)} %fusion.13), channel_id=1, source_target_pairs={{0,8},{4,12},{8,0},{12,4},{16,24},{20,28},{24,16},{28,20},{1,9},{5... | collective-permute-start | bytes 3538952 | tf_op jit(solution)/shard_map/ppermute | solution.py:35
  751.2 31.2 %collective-permute-start.6 = (bf16[192,1536]{1,0:T(8,128)(2,1)S(1)}, bf16[192,1536]{1,0:T(8,128)(2,1)S(1)}, u32[]{:S(2)}, u32[]{:S(2)}) collective-permute-start(bf16[192,1536]{1,0:T(8,128)(2,1)S(1)} %fusion.18), channel_id=1, source_target_pairs={{0,16},{4,20},{8,24},{12,28},{16,0},{20,4},{24,8},{28,12},{1,17},{... | collective-permute-start | bytes 1769480 | tf_op jit(solution)/shard_map/ppermute | solution.py:35
  781.2 26.1 %collective-permute-start.3 = (bf16[192,1536]{1,0:T(8,128)(2,1)}, bf16[192,1536]{1,0:T(8,128)(2,1)}, u32[]{:S(2)}, u32[]{:S(2)}) collective-permute-start(bf16[192,1536]{1,0:T(8,128)(2,1)} %fusion.17), channel_id=1, source_target_pairs={{0,16},{4,20},{8,24},{12,28},{16,0},{20,4},{24,8},{28,12},{1,17},{... | collective-permute-start | bytes 1769480 | tf_op jit(solution)/shard_map/ppermute | solution.py:35
  808.5 1.3 copy-start.6
  809.8 2.5 copy-start.10
  812.3 1.1 copy-start.27

commit v2 on v1

--- a/solution.py
+++ b/solution.py
@@ -136,6 +136,17 @@
     return lax.dot_general(a.astype(BF16), b.astype(BF16), (dims, ((), ())), preferred_element_type=F32)
 
 
+def halves(x):
+    high = x.astype(BF16)
+    return high, (x - high.astype(F32)).astype(BF16)
+
+
+def dot3(a, b, dims):
+    ah, al = halves(a)
+    bh, bl = halves(b)
+    return bdot(ah, bh, dims) + (bdot(ah, bl, dims) + bdot(al, bh, dims))
+
+
 def hdot(a, b, dims):
     return lax.dot_general(a, b, (dims, ((), ())), precision=lax.Precision.HIGHEST, preferred_element_type=F32)
 
@@ -182,9 +193,9 @@
         ubc[...] = bc
         usbc[...] = bc.astype(F32)
         m = mix_taps(usbc, tapbc, aux, 2 * states)
-        act = (m * sig(m)).astype(BF16)
+        act = m * sig(m)
         krs[...] = act
-        g = bdot(act[:, states:], act[:, :states], NT)
+        g = dot3(act[:, states:], act[:, :states], NT)
         ii = lax.broadcasted_iota(jnp.int32, (tokens, tokens), 0)
         jj = lax.broadcasted_iota(jnp.int32, (tokens, tokens), 1)
         segc = jnp.concatenate([aux[5]] * (tokens // LANE), axis=1)
@@ -214,7 +225,8 @@
     h0 = p * (LANE // size)
     dd = jnp.where(half, pick_lane(st, h0, lanes), pick_lane(st, h0 + 1, lanes))
     vd = v * dd
-    vdb = vd.astype(BF16)
+    vh, vl = halves(vd)
+    vhl = jnp.concatenate([vh, vl], axis=1)
     ys = []
     for k in range(LANE // size):
         h = h0 + k
@@ -222,22 +234,25 @@
         row = cT[pl.ds(h, 1), :]
         parts = []
         for ib in range(tokens // LANE):
-            tiles = []
+            tiles, lows = [], []
             ci = cb[k, pl.ds(ib * LANE, LANE), :]
             for jb in range(ib + 1):
                 spread = ci - row[:, jb * LANE : (jb + 1) * LANE]
                 if jb == ib:
                     spread = jnp.minimum(spread, 0.0)
-                tiles.append((jnp.exp(spread) * gram[pl.ds(ib * LANE, LANE), pl.ds(jb * LANE, LANE)]).astype(BF16))
-            w = tiles[0] if ib == 0 else jnp.concatenate(tiles, axis=1)
-            parts.append(bdot(w, vdb[: (ib + 1) * LANE], NN))
+                wh, wl = halves(jnp.exp(spread) * gram[pl.ds(ib * LANE, LANE), pl.ds(jb * LANE, LANE)])
+                tiles.append(wh)
+                lows.append(wl)
+            joined = lambda t: t[0] if ib == 0 else jnp.concatenate(t, axis=1)
+            both = bdot(joined(tiles), vhl[: (ib + 1) * LANE], NN)
+            parts.append(both[:, :LANE] + (both[:, LANE:] + bdot(joined(lows), vh[: (ib + 1) * LANE], NN)))
         ys.append(jnp.concatenate(parts, axis=0))
     y = jnp.where(half, ys[0], ys[1])
     ypart[...] = y + skip[...] * v
     ct = jnp.where(half, cb[0], cb[1])
     entry_o[...] = jnp.exp(ct) * aux[3]
     tail = jnp.exp(ct[tokens - 1 : tokens, :] - ct) * aux[4]
-    state[...] = bdot(vd * tail, krs[:, :states], TN)
+    state[...] = dot3(vd * tail, krs[:, :states], TN)
 
 
 def full(shape):
@@ -253,40 +268,10 @@
     return pl.BlockSpec((LANE, width), lambda p: (p, 0))
 
 
-VMEM_LIMIT = 56 * 1024 * 1024
-
-
-def fwd_mix(heads, size, nx, wzx, wbc, wdt, tapx, tapbc, dtb, lograte, skip, aux, segrow):
-    tokens = aux.shape[1]
-    ext, d = nx.shape
-    inner = wzx.shape[2]
-    two = wbc.shape[1]
-    S = jax.ShapeDtypeStruct
-    return pl.pallas_call(
-        partial(fwd_mix_body, heads, size),
-        name="fwd_mix",
-        grid=(inner // LANE,),
-        in_specs=[full(nx.shape), pl.BlockSpec((2, d, LANE), lambda p: (0, 0, p)), full(wbc.shape), full(wdt.shape),
-                  cols(tapx.shape[0]), full(tapbc.shape), full(dtb.shape), full(lograte.shape), cols(1),
-                  full(aux.shape), full(segrow.shape)],
-        out_specs=[cols(tokens), cols(ext), full((ext, two)), full((tokens, two)), full((tokens, LANE)), full((tokens, LANE)),
-                   full((tokens, LANE)), full((LANE, tokens)), full((tokens, tokens)), cols(tokens), cols(tokens),
-                   cols(tokens), rowsb(two // 2), full((16, LANE)), full((8, LANE))],
-        out_shape=[S((tokens, inner), BF16), S((ext, inner), BF16), S((ext, two), BF16), S((tokens, two), BF16),
-                   S((tokens, LANE), BF16), S((tokens, LANE), F32), S((tokens, LANE), F32), S((LANE, tokens), F32),
-                   S((tokens, tokens), F32), S((tokens, inner), F32), S((tokens, inner), F32), S((tokens, inner), F32),
-                   S((inner, two // 2), F32), S((16, LANE), F32), S((8, LANE), F32)],
-        scratch_shapes=[pltpu.VMEM((ext, LANE), F32), pltpu.VMEM((ext, two), F32), pltpu.VMEM((2, tokens, LANE), F32)],
-        compiler_params=pltpu.CompilerParams(vmem_limit_bytes=VMEM_LIMIT),
-        cost_estimate=pl.CostEstimate(flops=2 * ext * d * (2 * inner + two) + 6 * tokens * tokens * inner,
-                                      bytes_accessed=4 * d * inner + 16 * tokens * inner, transcendentals=tokens * tokens * heads),
-    )(nx, wzx, wbc, wdt, tapx, tapbc, dtb, lograte, skip, aux, segrow)
-
-
 def fwd_gate_body(ypart, entry, gate, krs, enter, y, carr, gated, sq, sqacc):
     p = pl.program_id(0)
     states = krs.shape[1] // 2
-    c = bdot(krs[:, states:], enter[...], NT) * entry[...]
+    c = dot3(krs[:, states:], enter[...], NT) * entry[...]
     carr[...] = c
     yy = ypart[...] + c
     y[...] = yy
@@ -305,22 +290,6 @@
     @pl.when(p == pl.num_programs(0) - 1)
     def _():
         sq[...] = jnp.broadcast_to(jnp.sum(jnp.transpose(sqacc[...]), axis=0, keepdims=True), sq.shape)
-
-
-def fwd_gate(ypart, entry, gate, krs, enter):
-    tokens, inner = ypart.shape
-    S = jax.ShapeDtypeStruct
-    return pl.pallas_call(
-        fwd_gate_body,
-        name="fwd_gate",
-        grid=(inner // LANE,),
-        in_specs=[cols(tokens), cols(tokens), cols(tokens), full(krs.shape), rowsb(enter.shape[1])],
-        out_specs=[cols(tokens), cols(tokens), cols(tokens), full((8, tokens))],
-        scratch_shapes=[pltpu.VMEM((tokens, LANE), F32)],
-        out_shape=[S((tokens, inner), F32)] * 3 + [S((8, tokens), F32)],
-        compiler_params=pltpu.CompilerParams(vmem_limit_bytes=VMEM_LIMIT),
-        cost_estimate=pl.CostEstimate(flops=2 * tokens * inner * LANE, bytes_accessed=26 * tokens * inner, transcendentals=tokens * inner),
-    )(ypart, entry, gate, krs, enter)
 
 
 def bwd_gate_body(gb, wout, gate, y, mixed, entry, krs, r2b, krb, gain, gy_o, gz_o, scaled_o, qloc, ggate, gskip):
@@ -342,25 +311,6 @@
     m = mixed[...]
     gskip[...] = jnp.sum(gy * (m * sig(m)), axis=0, keepdims=True)
     qloc[...] = bdot(gy * entry[...], krs[:, states:], TN)
-
-
-def bwd_gate(gb, wout, gate, y, mixed, entry, krs, r2b, krb, gain):
-    tokens, inner = y.shape
-    d = gb.shape[1]
-    states = krs.shape[1] // 2
-    S = jax.ShapeDtypeStruct
-    return pl.pallas_call(
-        bwd_gate_body,
-        name="bwd_gate",
-        grid=(inner // LANE,),
-        in_specs=[full(gb.shape), rowsb(d), cols(tokens), cols(tokens), cols(tokens), cols(tokens), full(krs.shape),
-                  full(r2b.shape), full(krb.shape), cols(1)],
-        out_specs=[cols(tokens), cols(tokens), cols(tokens), rowsb(states), cols(1), cols(1)],
-        out_shape=[S((tokens, inner), F32), S((tokens, inner), BF16), S((tokens, inner), BF16), S((inner, states), F32),
-                   S((1, inner), F32), S((1, inner), F32)],
-        compiler_params=pltpu.CompilerParams(vmem_limit_bytes=VMEM_LIMIT),
-        cost_estimate=pl.CostEstimate(flops=2 * tokens * inner * d, bytes_accessed=26 * tokens * inner + 2 * d * inner, transcendentals=2 * tokens * inner),
-    )(gb, wout, gate, y, mixed, entry, krs, r2b, krb, gain)
 
 
 def bwd_local_body(size, gy_r, mixed, krs, cum, steps, cT, gram, entry, enter, segc, segrow,
@@ -434,25 +384,6 @@
         dkr[:, states:] += bdot(g, krs[:, :states], TN)
 
 
-def bwd_local(size, gy, mixed, krs, cum, steps, cT, gram, entry, enter, segc, segrow):
-    tokens, inner = gy.shape
-    two = krs.shape[1]
-    S = jax.ShapeDtypeStruct
-    return pl.pallas_call(
-        partial(bwd_local_body, size),
-        name="bwd_local",
-        grid=(inner // LANE,),
-        in_specs=[cols(tokens), cols(tokens), full(krs.shape), full(cum.shape), full(steps.shape), full(cT.shape), full(gram.shape),
-                  cols(tokens), rowsb(two // 2), full(segc.shape), full(segrow.shape)],
-        out_specs=[cols(tokens), full((tokens, LANE)), full((LANE, tokens)), full((tokens, two))],
-        out_shape=[S((tokens, inner), F32), S((tokens, LANE), F32), S((LANE, tokens), F32), S((tokens, two), F32)],
-        scratch_shapes=[pltpu.VMEM((tokens, LANE), F32), pltpu.VMEM((tokens, LANE), F32), pltpu.VMEM((tokens, tokens), F32),
-                        pltpu.VMEM((tokens, tokens), F32), pltpu.VMEM((tokens, LANE), BF16), pltpu.VMEM((tokens, LANE), BF16)],
-        compiler_params=pltpu.CompilerParams(vmem_limit_bytes=VMEM_LIMIT),
-        cost_estimate=pl.CostEstimate(flops=12 * tokens * tokens * inner, bytes_accessed=20 * tokens * inner, transcendentals=tokens * tokens * inner // size),
-    )(gy, mixed, krs, cum, steps, cT, gram, entry, enter, segc, segrow)
-
-
 def bwd_carry_body(size, gy_r, dvd_r, mixed, carr, entry, krs, cum, steps, pdt, dtb, lograte, skip, ux, tapx, aux, later, enter,
                    dd_r, rowT, dkr_r, decay,
                    gm_o, gu_o, gtail_o, gtaps, gdt_o, gvec, dkr, us, ms, ddacc, dcum, last):
@@ -497,7 +428,7 @@
         ddacc[...] += jnp.where(lanes == h, td, 0.0)
         dcum[...] += jnp.where(lanes == h, ec - tdd, 0.0)
         dot_qs = jnp.sum(jnp.sum(qs[k * size : (k + 1) * size, :], axis=0, keepdims=True), axis=1, keepdims=True)
-        last[...] += jnp.where(lane1 == h, jnp.sum(tdd, axis=0, keepdims=True) + dot_qs * decay[...], 0.0)
+        last[...] += jnp.where(lane1 == h, jnp.sum(tdd, axis=0, keepdims=True) + dot_qs * decay[0:1, :], 0.0)
     dv = dvd * dpair + skip[...] * gy
     gm = dv * (s * (1.0 + m * (1.0 - s)))
     gm_o[...] = gm[:8]
@@ -527,29 +458,8 @@
         gvec[1:2, :] = jnp.sum(st * dlog, axis=0, keepdims=True) * rates
 
 
-def bwd_carry(size, gy, dvd, mixed, carr, entry, krs, cum, steps, pdt, dtb, lograte, skip, ux, tapx, aux, later, enter, dd, rowT, dkr, decay):
-    tokens, inner = gy.shape
-    ext = ux.shape[0]
-    two = krs.shape[1]
-    S = jax.ShapeDtypeStruct
-    return pl.pallas_call(
-        partial(bwd_carry_body, size),
-        name="bwd_carry",
-        grid=(inner // LANE,),
-        in_specs=[cols(tokens), cols(tokens), cols(tokens), cols(tokens), cols(tokens), full(krs.shape), full(cum.shape), full(steps.shape),
-                  full(pdt.shape), full(dtb.shape), full(lograte.shape), cols(1), cols(ext), cols(tapx.shape[0]), full(aux.shape),
-                  rowsb(two // 2), rowsb(two // 2), full(dd.shape), full(rowT.shape), full(dkr.shape), full(decay.shape)],
-        out_specs=[cols(8), cols(tokens), cols(16), cols(8), full((tokens, LANE)), full((8, LANE)), full((tokens, two))],
-        out_shape=[S((8, inner), F32), S((tokens, inner), BF16), S((16, inner), F32), S((8, inner), F32), S((tokens, LANE), BF16),
-                   S((8, LANE), F32), S((tokens, two), F32)],
-        scratch_shapes=[pltpu.VMEM((ext, LANE), F32), pltpu.VMEM((tokens + 8, LANE), F32), pltpu.VMEM((tokens, LANE), F32),
-                        pltpu.VMEM((tokens, LANE), F32), pltpu.VMEM((1, LANE), F32)],
-        compiler_params=pltpu.CompilerParams(vmem_limit_bytes=VMEM_LIMIT),
-        cost_estimate=pl.CostEstimate(flops=4 * tokens * inner * LANE, bytes_accessed=24 * tokens * inner, transcendentals=2 * tokens * inner),
-    )(gy, dvd, mixed, carr, entry, krs, cum, steps, pdt, dtb, lograte, skip, ux, tapx, aux, later, enter, dd, rowT, dkr, decay)
-
-
 MESH = pl.DeviceIdType.MESH
+VMEM_LIMIT = 56 * 1024 * 1024
 SUBS = 2
 
 
@@ -579,9 +489,10 @@
     total_d = dec[...]
     for i, b in enumerate(bits):
         src = st if i == 0 else tot
-        tx[...] = src[...].astype(BF16)
+        if reverse:
+            tx[...] = src[...].astype(BF16)
         dtx[...] = total_d
-        one = send(tx, rx.at[i], (ssem.at[2 * i], rsem.at[2 * i]), wheres[i])
+        one = send(tx if reverse else src, rx.at[i], (ssem.at[2 * i], rsem.at[2 * i]), wheres[i])
         two = send(dtx, drx.at[i], (ssem.at[2 * i + 1], rsem.at[2 * i + 1]), wheres[i])
         bit = (me // b) % 2
         second = (1 - bit) if reverse else bit
@@ -606,23 +517,6 @@
         total_d = total_d * other_d
 
 
-def carry_kernel(state, dec, heads, size, reverse, cid):
-    bits = bits_of("seq")
-    rows, states = state.shape
-    n = len(bits)
-    return pl.pallas_call(
-        partial(carry_body, bits, reverse, heads, size),
-        name="carry_back" if reverse else "carry_on",
-        in_specs=[pl.BlockSpec(memory_space=pltpu.VMEM)] * 2,
-        out_specs=pl.BlockSpec(memory_space=pltpu.VMEM),
-        out_shape=jax.ShapeDtypeStruct((rows, states), F32),
-        scratch_shapes=[pltpu.VMEM((rows, states), BF16), pltpu.VMEM((n, rows, states), BF16), pltpu.VMEM(dec.shape, F32),
-                        pltpu.VMEM((n,) + dec.shape, F32), pltpu.VMEM((rows, states), F32),
-                        pltpu.SemaphoreType.DMA((2 * n,)), pltpu.SemaphoreType.DMA((2 * n,))],
-        compiler_params=pltpu.CompilerParams(collective_id=cid, has_side_effects=True, vmem_limit_bytes=VMEM_LIMIT),
-    )(state, dec)
-
-
 def head_core(tokens, part, middle, nx, off, side, tx0, rx0, tx1, rx1, acc, ssem, rsem, me, core_at, y_at):
     quarter = tokens // 4
     sub = quarter // SUBS
@@ -645,13 +539,13 @@
     first = []
     for i, base in enumerate((other_y, own_y)):
         for s in range(SUBS):
-            tx0[i, s] = acc[pl.ds(pl.multiple_of(base + s * sub, sub), sub), :].astype(BF16)
+            tx0[i, s] = acc[pl.ds(pl.multiple_of(base + s * sub, sub), sub), :].astype(tx0.dtype)
             first.append(go(tx0.at[i, s], rx0.at[i, s], core_at))
     acc[...] = part(pl.multiple_of(c * half, half), half)
     second = []
     for s in range(SUBS):
         first[s].wait_recv()
-        tx1[s] = (acc[pl.ds(pl.multiple_of(other_y + s * sub, sub), sub), :] + rx0[0, s].astype(F32)).astype(BF16)
+        tx1[s] = (acc[pl.ds(pl.multiple_of(other_y + s * sub, sub), sub), :] + rx0[0, s].astype(F32)).astype(tx1.dtype)
         second.append(go(tx1.at[s], rx1.at[s], y_at))
     own = (c * 2 + y) * quarter
     theirs = (c * 2 + 1 - y) * quarter
@@ -685,8 +579,12 @@
 HEAD_COPIES = 3 * SUBS + 3 * SUBS + 3
 
 
-def head_fwd_body(tokens, last, width, gated, sq, ggain, wout, h_own, extra,
-                  nx, h_new, branch, r2b, side, sqrx, tx0, rx0, tx1, rx1, acc, krc, ssem, rsem, qs, qr, hs, hr):
+def head_fwd_body(l, tokens, last, width, gated, sq, ggain_all, wout_all, h_own, extra,
+                  nx, h_new, branch, r2b, side, sqrx, tx0, rx0, tx1, rx1, acc, krc, ssem, rsem, qs, qr, hs, hr, wout, wsem):
+    load = pltpu.make_async_copy(wout_all.at[l], wout, wsem.at[0])
+    load.start()
+    ggain = ggain_all.at[l]
+    extra = extra if last else extra.at[l + 1]
     me = lax.axis_index("head")
     at = lax.axis_index("seq")
     count = lax.axis_size("seq")
@@ -735,6 +633,7 @@
         return (h * r1 * extra[...]).astype(BF16)
 
     off = 0 if last else HALO
+    load.wait()
     if not last:
         side[...] = jnp.zeros_like(side)
     head_core(tokens, part, middle, nx, off, side if last else None, tx0, rx0, tx1, rx1, acc, ssem, rsem, me,
@@ -759,33 +658,19 @@
             nx[pl.ds(0, HALO), :] = jnp.zeros((HALO, d), BF16)
 
 
-def head_scratch(tokens, d):
+def head_scratch(tokens, d, kind=BF16):
     sub = tokens // 4 // SUBS
-    return [pltpu.VMEM((2, SUBS, sub, d), BF16), pltpu.VMEM((2, SUBS, sub, d), BF16), pltpu.VMEM((SUBS, sub, d), BF16),
-            pltpu.VMEM((SUBS, sub, d), BF16), pltpu.VMEM((tokens // 2, d), F32), pltpu.VMEM((tokens // 4, LANE), F32),
+    return [pltpu.VMEM((2, SUBS, sub, d), kind), pltpu.VMEM((2, SUBS, sub, d), kind), pltpu.VMEM((SUBS, sub, d), kind),
+            pltpu.VMEM((SUBS, sub, d), kind), pltpu.VMEM((tokens // 2, d), F32), pltpu.VMEM((tokens // 4, LANE), F32),
             pltpu.SemaphoreType.DMA((HEAD_COPIES,)), pltpu.SemaphoreType.DMA((HEAD_COPIES,))]
 
 
-def head_fwd(gated, sq, ggain, wout, h_own, extra, last, width, cid):
-    tokens, inner = gated.shape
-    d = wout.shape[1]
-    S = jax.ShapeDtypeStruct
-    vm = pl.BlockSpec(memory_space=pltpu.VMEM)
-    return pl.pallas_call(
-        partial(head_fwd_body, tokens, last, width),
-        name="head_fwd_last" if last else "head_fwd",
-        in_specs=[vm] * 6,
-        out_specs=[vm] * 5,
-        out_shape=[S((tokens if last else tokens + HALO, d), BF16), S((tokens // 4, d), F32), S((tokens // 4, d), F32),
-                   S((tokens, LANE), F32), S((32, LANE), F32)],
-        scratch_shapes=[pltpu.VMEM((3, 8, tokens), F32)] + head_scratch(tokens, d)
-        + [pltpu.SemaphoreType.DMA((3,)), pltpu.SemaphoreType.DMA((3,)), pltpu.SemaphoreType.DMA((1,)), pltpu.SemaphoreType.DMA((1,))],
-        compiler_params=pltpu.CompilerParams(collective_id=cid, has_side_effects=True, vmem_limit_bytes=VMEM_LIMIT),
-    )(gated, sq, ggain, wout, h_own, extra)
-
-
-def head_bwd_body(tokens, gz, gu, small, wzx, wsmall, h_own, gain, g_own, branch,
-                  gb, g_new, ggain, side, tx0, rx0, tx1, rx1, acc, krc, ssem, rsem):
+def head_bwd_body(l, tokens, gz, gu, small, wzx_all, wsmall_all, h_own, gain_all, g_own, branch,
+                  gb, g_new, ggain, side, tx0, rx0, tx1, rx1, acc, krc, ssem, rsem, wzx, wsem):
+    load = pltpu.make_async_copy(wzx_all.at[l], wzx, wsem.at[0])
+    load.start()
+    wsmall = wsmall_all.at[l]
+    gain = gain_all.at[l]
     me = lax.axis_index("head")
     core_at, y_at = {"head": flip(me, 1)}, {"head": flip(me, 2)}
     greet([core_at, y_at])
@@ -815,27 +700,13 @@
             side[mine, :] = jnp.transpose(krc[...])[0:8, :]
         return low
 
+    load.wait()
     head_core(tokens, part, middle, gb, 0, side, tx0, rx0, tx1, rx1, acc, ssem, rsem, me, core_at, y_at)
 
 
-def head_bwd(gz, gu, small, wzx, wsmall, h_own, gain, g_own, branch, cid):
-    tokens = gz.shape[0]
-    d = gain.shape[1]
-    S = jax.ShapeDtypeStruct
-    vm = pl.BlockSpec(memory_space=pltpu.VMEM)
-    return pl.pallas_call(
-        partial(head_bwd_body, tokens),
-        name="head_bwd",
-        in_specs=[vm] * 9,
-        out_specs=[vm] * 4,
-        out_shape=[S((tokens, d), BF16), S((tokens // 4, d), F32), S((1, d), F32), S((32, LANE), F32)],
-        scratch_shapes=head_scratch(tokens, d),
-        compiler_params=pltpu.CompilerParams(collective_id=cid, has_side_effects=True, vmem_limit_bytes=VMEM_LIMIT),
-    )(gz, gu, small, wzx, wsmall, h_own, gain, g_own, branch)
-
-
-def maps_bwd_body(tokens, dkr, ubc, taps, aux, gdt, gtail, gm8, tapx,
+def maps_bwd_body(l, tokens, dkr, ubc, taps_all, aux, gdt, gtail, gm8, tapx_all,
                   small, gtaps, gtail_o, ytx, yrx, yacc, ctx, crx, us, ms, nextx, nextb, gmb, sems, semr):
+    taps, tapx = taps_all.at[l], tapx_all.at[l]
     me = lax.axis_index("head")
     at = lax.axis_index("seq")
     count = lax.axis_size("seq")
@@ -918,34 +789,13 @@
         ahead_b.wait_send()
 
 
-def maps_bwd(dkr, ubc, taps, aux, gdt, gtail, gm8, tapx, cid):
-    tokens = dkr.shape[0]
-    inner = tapx.shape[1]
-    S = jax.ShapeDtypeStruct
-    vm = pl.BlockSpec(memory_space=pltpu.VMEM)
-    tile = pltpu.VMEM((tokens, LANE), F32)
-    return pl.pallas_call(
-        partial(maps_bwd_body, tokens),
-        name="maps_bwd",
-        in_specs=[vm] * 8,
-        out_specs=[vm] * 3,
-        out_shape=[S((tokens, LANE), BF16), S((8, LANE), F32), S((16, inner), BF16)],
-        scratch_shapes=[tile, tile, tile, tile, tile, pltpu.VMEM((tokens + HALO, LANE), F32), pltpu.VMEM((tokens + 8, LANE), F32),
-                        pltpu.VMEM((8, inner), F32), pltpu.VMEM((8, LANE), F32), pltpu.VMEM((8, LANE), F32),
-                        pltpu.SemaphoreType.DMA((4,)), pltpu.SemaphoreType.DMA((4,))],
-        compiler_params=pltpu.CompilerParams(collective_id=cid, has_side_effects=True, vmem_limit_bytes=VMEM_LIMIT),
-    )(dkr, ubc, taps, aux, gdt, gtail, gm8, tapx)
-
-
-def sums_body(parts, *refs):
+def pack_body(parts, *refs):
     ins = refs[: 6 * parts]
-    conv_x, conv_bc, ggate, gskip, gvec, ggain = refs[6 * parts : 6 * parts + 6]
-    stage, rx, ssem, rsem = refs[6 * parts + 6 :]
+    stage, rx, ssem, rsem = refs[6 * parts :]
     inner = stage.shape[2]
     me = lax.axis_index("head")
-    tile = pl.multiple_of((me // 2) * LANE, LANE)
-    steps = [("seq", b) for b in bits_of("seq")] + [("head", b) for b in bits_of("head")]
-    wheres = [{axis: flip(lax.axis_index(axis), b)} for axis, b in steps]
+    bits = bits_of("head")
+    wheres = [{"head": flip(me, b)} for b in bits]
     greet(wheres)
     stage[...] = jnp.zeros_like(stage)
     for l in range(parts):
@@ -961,16 +811,15 @@
             row = maps[r : r + 1, :] * 0.5
             here = [jnp.where(me // 2 == k, row, 0.0) for k in range(2)]
             stage[l, 10 + r // 3 : 11 + r // 3, (r % 3) * 2 * LANE : ((r % 3) * 2 + 2) * LANE] = jnp.concatenate(here, axis=1)
-    for i, (axis, b) in enumerate(steps):
-        if axis == "seq":
-            copy = send(stage, rx.at[i], (ssem.at[i], rsem.at[i]), wheres[i])
-            copy.wait()
-            stage[...] += rx[i]
-        else:
-            where = pl.ds(8, 8)
-            copy = send(stage.at[:, where, :], rx.at[i, :, where, :], (ssem.at[i], rsem.at[i]), wheres[i])
-            copy.wait()
-            stage[:, 8:16, :] += rx[i, :, 8:16, :]
+    where = pl.ds(8, 8)
+    for i in range(len(bits)):
+        copy = send(stage.at[:, where, :], rx.at[i], (ssem.at[i], rsem.at[i]), wheres[i])
+        copy.wait()
+        stage[:, 8:16, :] += rx[i]
+
+
+def unpack_body(parts, stage, conv_x, conv_bc, ggate, gskip, gvec, ggain):
+    inner = stage.shape[2]
     for l in range(parts):
         conv_x[l] = stage[l, 0 : CONV + 1, :]
         ggate[l : l + 1, :] = stage[l, 5:6, :]
@@ -982,22 +831,278 @@
             conv_bc[l, r : r + 1, :] = stage[l, 10 + r // 3 : 11 + r // 3, (r % 3) * 2 * LANE : ((r % 3) * 2 + 2) * LANE]
 
 
-def sums_kernel(smalls, inner, d, cid):
+VM = pl.BlockSpec(memory_space=pltpu.VMEM)
+S = jax.ShapeDtypeStruct
+
+
+def of_layer(l, shape, steps=False):
+    n = len(shape) - 1
+    if steps:
+        return pl.BlockSpec((None,) + shape[1:-1] + (LANE,), lambda p: (l,) + (0,) * (n - 1) + (p,))
+    return pl.BlockSpec((None,) + shape[1:], lambda *p: (l,) + (0,) * n)
+
+
+def rows_of_layer(l, shape):
+    return pl.BlockSpec((None, LANE, shape[2]), lambda p: (l, p, 0))
+
+
+def kcall(body, args, specs, us, after=(), cid=None, **kw):
+    n, k = len(args), len(after)
+
+    def wrapped(*refs):
+        body(*refs[:n], *refs[n + k :])
+
+    extra = {} if cid is None else dict(collective_id=cid, has_side_effects=True)
+    return pl.pallas_call(
+        wrapped,
+        in_specs=list(specs) + [pl.BlockSpec(memory_space=pl.ANY)] * k,
+        compiler_params=pltpu.CompilerParams(vmem_limit_bytes=VMEM_LIMIT, **extra),
+        cost_estimate=pl.CostEstimate(flops=int(us * 1e9), bytes_accessed=int(us * 3e6), transcendentals=0),
+        **kw,
+    )(*args, *after)
+
+
+def fwd_mix(l, heads, size, nx, q, aux, segrow):
+    tokens = aux.shape[1]
+    ext, d = nx.shape
+    inner = q["conv_x"].shape[2]
+    two = q["w_bc"].shape[2]
+    args = [nx, q["w_zx"], q["w_bc"], q["w_dt"], q["conv_x"], q["conv_bc"], q["dt_bias"], q["a_log"], q["skip"], aux, segrow]
+    specs = [full(nx.shape), of_layer(l, q["w_zx"].shape, True), of_layer(l, q["w_bc"].shape), of_layer(l, q["w_dt"].shape),
+             of_layer(l, q["conv_x"].shape, True), of_layer(l, q["conv_bc"].shape), of_layer(l, q["dt_bias"].shape),
+             of_layer(l, q["a_log"].shape), of_layer(l, q["skip"].shape, True), full(aux.shape), full(segrow.shape)]
+    return kcall(
+        partial(fwd_mix_body, heads, size), args, specs, 16,
+        name="fwd_mix",
+        grid=(inner // LANE,),
+        out_specs=[cols(tokens), cols(ext), full((ext, two)), full((tokens, two)), full((tokens, LANE)), full((tokens, LANE)),
+                   full((tokens, LANE)), full((LANE, tokens)), full((tokens, tokens)), cols(tokens), cols(tokens),
+                   cols(tokens), rowsb(two // 2), full((16, LANE)), full((8, LANE))],
+        out_shape=[S((tokens, inner), BF16), S((ext, inner), BF16), S((ext, two), BF16), S((tokens, two), F32),
+                   S((tokens, LANE), BF16), S((tokens, LANE), F32), S((tokens, LANE), F32), S((LANE, tokens), F32),
+                   S((tokens, tokens), F32), S((tokens, inner), F32), S((tokens, inner), F32), S((tokens, inner), F32),
+                   S((inner, two // 2), F32), S((16, LANE), F32), S((8, LANE), F32)],
+        scratch_shapes=[pltpu.VMEM((ext, LANE), F32), pltpu.VMEM((ext, two), F32), pltpu.VMEM((2, tokens, LANE), F32)],
+    )
+
+
+def fwd_gate(ypart, entry, gate, krs, enter):
+    tokens, inner = ypart.shape
+    return kcall(
+        fwd_gate_body, [ypart, entry, gate, krs, enter],
+        [cols(tokens), cols(tokens), cols(tokens), full(krs.shape), rowsb(enter.shape[1])], 7,
+        name="fwd_gate",
+        grid=(inner // LANE,),
+        out_specs=[cols(tokens), cols(tokens), cols(tokens), full((8, tokens))],
+        out_shape=[S((tokens, inner), F32)] * 3 + [S((8, tokens), F32)],
+        scratch_shapes=[pltpu.VMEM((tokens, LANE), F32)],
+    )
+
+
+def bwd_gate(l, gb, q, gate, y, mixed, entry, krs, r2b, krb):
+    tokens, inner = y.shape
+    states = krs.shape[1] // 2
+    return kcall(
+        bwd_gate_body, [gb, q["w_out"], gate, y, mixed, entry, krs, r2b, krb, q["gate_gain"]],
+        [full(gb.shape), rows_of_layer(l, q["w_out"].shape), cols(tokens), cols(tokens), cols(tokens), cols(tokens), full(krs.shape),
+         full(r2b.shape), full(krb.shape), of_layer(l, q["gate_gain"].shape, True)], 9,
+        name="bwd_gate",
+        grid=(inner // LANE,),
+        out_specs=[cols(tokens), cols(tokens), cols(tokens), rowsb(states), cols(1), cols(1)],
+        out_shape=[S((tokens, inner), F32), S((tokens, inner), BF16), S((tokens, inner), BF16), S((inner, states), F32),
+                   S((1, inner), F32), S((1, inner), F32)],
+    )
+
+
+def bwd_local(size, gy, mixed, krs, cum, steps, cT, gram, entry, enter, aux, segrow, after):
+    tokens, inner = gy.shape
+    two = krs.shape[1]
+    return kcall(
+        partial(bwd_local_body, size), [gy, mixed, krs, cum, steps, cT, gram, entry, enter, aux, segrow],
+        [cols(tokens), cols(tokens), full(krs.shape), full(cum.shape), full(steps.shape), full(cT.shape), full(gram.shape),
+         cols(tokens), rowsb(two // 2), pl.BlockSpec((None, tokens, LANE), lambda p: (5, 0, 0)), full(segrow.shape)], 10, after,
+        name="bwd_local",
+        grid=(inner // LANE,),
+        out_specs=[cols(tokens), full((tokens, LANE)), full((LANE, tokens)), full((tokens, two))],
+        out_shape=[S((tokens, inner), F32), S((tokens, LANE), F32), S((LANE, tokens), F32), S((tokens, two), F32)],
+        scratch_shapes=[pltpu.VMEM((tokens, LANE), F32), pltpu.VMEM((tokens, LANE), F32), pltpu.VMEM((tokens, tokens), F32),
+                        pltpu.VMEM((tokens, tokens), F32), pltpu.VMEM((tokens, LANE), BF16), pltpu.VMEM((tokens, LANE), BF16)],
+    )
+
+
+def bwd_carry(l, size, gy, dvd, mixed, carr, entry, krs, cum, steps, pdt, q, ux, aux, later, enter, dd, rowT, dkr, decl):
+    tokens, inner = gy.shape
+    ext = ux.shape[0]
+    two = krs.shape[1]
+    return kcall(
+        partial(bwd_carry_body, size),
+        [gy, dvd, mixed, carr, entry, krs, cum, steps, pdt, q["dt_bias"], q["a_log"], q["skip"], ux, q["conv_x"], aux, later, enter,
+         dd, rowT, dkr, decl],
+        [cols(tokens), cols(tokens), cols(tokens), cols(tokens), cols(tokens), full(krs.shape), full(cum.shape), full(steps.shape),
+         full(pdt.shape), of_layer(l, q["dt_bias"].shape), of_layer(l, q["a_log"].shape), of_layer(l, q["skip"].shape, True), cols(ext),
+         of_layer(l, q["conv_x"].shape, True), full(aux.shape), rowsb(two // 2), rowsb(two // 2), full(dd.shape), full(rowT.shape),
+         full(dkr.shape), full(decl.shape)], 11,
+        name="bwd_carry",
+        grid=(inner // LANE,),
+        out_specs=[cols(8), cols(tokens), cols(16), cols(8), full((tokens, LANE)), full((8, LANE)), full((tokens, two))],
+        out_shape=[S((8, inner), F32), S((tokens, inner), BF16), S((16, inner), F32), S((8, inner), F32), S((tokens, LANE), BF16),
+                   S((8, LANE), F32), S((tokens, two), F32)],
+        scratch_shapes=[pltpu.VMEM((ext, LANE), F32), pltpu.VMEM((tokens + 8, LANE), F32), pltpu.VMEM((tokens, LANE), F32),
+                        pltpu.VMEM((tokens, LANE), F32), pltpu.VMEM((1, LANE), F32)],
+    )
+
+
+def carry_kernel(state, dec, heads, size, reverse, cid, after=()):
+    bits = bits_of("seq")
+    rows, states = state.shape
+    n = len(bits)
+    return kcall(
+        partial(carry_body, bits, reverse, heads, size), [state, dec], [VM] * 2, 25, after, cid,
+        name="carry_back" if reverse else "carry_on",
+        out_specs=VM,
+        out_shape=S((rows, states), F32),
+        scratch_shapes=[pltpu.VMEM((rows, states), BF16), pltpu.VMEM((n, rows, states), BF16 if reverse else F32), pltpu.VMEM(dec.shape, F32),
+                        pltpu.VMEM((n,) + dec.shape, F32), pltpu.VMEM((rows, states), F32),
+                        pltpu.SemaphoreType.DMA((2 * n,)), pltpu.SemaphoreType.DMA((2 * n,))],
+    )
+
+
+def head_fwd(l, gated, sq, q, h_own, extra, last, width, cid):
+    tokens, inner = gated.shape
+    d = q["w_out"].shape[2]
+    return kcall(
+        partial(head_fwd_body, l, tokens, last, width), [gated, sq, q["gate_gain"], q["w_out"], h_own, extra],
+        [VM, VM, VM, pl.BlockSpec(memory_space=pl.ANY), VM, VM], 30, (), cid,
+        name="head_fwd_last" if last else "head_fwd",
+        out_specs=[VM] * 5,
+        out_shape=[S((tokens if last else tokens + HALO, d), BF16), S((tokens // 4, d), F32), S((tokens // 4, d), F32),
+                   S((tokens, LANE), F32), S((32, LANE), F32)],
+        scratch_shapes=[pltpu.VMEM((3, 8, tokens), F32)] + head_scratch(tokens, d, BF16 if last else F32)
+        + [pltpu.SemaphoreType.DMA((3,)), pltpu.SemaphoreType.DMA((3,)), pltpu.SemaphoreType.DMA((1,)), pltpu.SemaphoreType.DMA((1,)), pltpu.VMEM((inner, d), BF16), pltpu.SemaphoreType.DMA((1,))],
+    )
+
+
+def head_bwd(l, gz, gu, small, q, h_own, g_own, branch, cid, after=()):
+    tokens = gz.shape[0]
+    d = h_own.shape[1]
+    return kcall(
+        partial(head_bwd_body, l, tokens), [gz, gu, small, q["w_zx"], q["w_small"], h_own, q["gain"], g_own, branch],
+        [VM, VM, VM, pl.BlockSpec(memory_space=pl.ANY), VM, VM, VM, VM, VM], 29, after, cid,
+        name="head_bwd",
+        out_specs=[VM] * 4,
+        out_shape=[S((tokens, d), BF16), S((tokens // 4, d), F32), S((1, d), F32), S((32, LANE), F32)],
+        scratch_shapes=head_scratch(tokens, d) + [pltpu.VMEM(q["w_zx"].shape[1:], BF16), pltpu.SemaphoreType.DMA((1,))],
+    )
+
+
+def maps_bwd(l, dkr, ubc, q, aux, gdt, gtail, gm8, cid, after=()):
+    tokens = dkr.shape[0]
+    inner = gtail.shape[1]
+    tile = pltpu.VMEM((tokens, LANE), F32)
+    return kcall(
+        partial(maps_bwd_body, l, tokens), [dkr, ubc, q["conv_bc"], aux, gdt, gtail, gm8, q["conv_x"]],
+        [VM] * 8, 14, after, cid,
+        name="maps_bwd",
+        out_specs=[VM] * 3,
+        out_shape=[S((tokens, LANE), BF16), S((8, LANE), F32), S((16, inner), BF16)],
+        scratch_shapes=[tile, tile, tile, tile, tile, pltpu.VMEM((tokens + HALO, LANE), F32), pltpu.VMEM((tokens + 8, LANE), F32),
+                        pltpu.VMEM((8, inner), F32), pltpu.VMEM((8, LANE), F32), pltpu.VMEM((8, LANE), F32),
+                        pltpu.SemaphoreType.DMA((4,)), pltpu.SemaphoreType.DMA((4,))],
+    )
+
+
+def pack_small(smalls, inner, cid):
     parts = len(smalls)
-    n = len(bits_of("seq")) + len(bits_of("head"))
-    vm = pl.BlockSpec(memory_space=pltpu.VMEM)
-    S = jax.ShapeDtypeStruct
-    return pl.pallas_call(
-        partial(sums_body, parts),
-        name="sums_small",
-        in_specs=[vm] * (6 * parts),
-        out_specs=[vm] * 6,
+    n = len(bits_of("head"))
+    return kcall(
+        partial(pack_body, parts), [x for part in smalls for x in part], [VM] * (6 * parts), 8, (), cid,
+        name="pack_small",
+        out_specs=VM,
+        out_shape=S((parts, 16, inner), F32),
+        scratch_shapes=[pltpu.VMEM((n, parts, 8, inner), F32), pltpu.SemaphoreType.DMA((n,)), pltpu.SemaphoreType.DMA((n,))],
+    )
+
+
+def unpack_small(stage, d):
+    parts, _, inner = stage.shape
+    return kcall(
+        partial(unpack_body, parts), [stage], [VM], 2,
+        name="unpack_small",
+        out_specs=[VM] * 6,
         out_shape=[S((parts, CONV + 1, inner), F32), S((parts, CONV + 1, 2 * LANE), F32), S((parts, inner), F32), S((parts, inner), F32),
                    S((parts, 2 * LANE), F32), S((parts, d), F32)],
-        scratch_shapes=[pltpu.VMEM((parts, 16, inner), F32), pltpu.VMEM((n, parts, 16, inner), F32),
-                        pltpu.SemaphoreType.DMA((n,)), pltpu.SemaphoreType.DMA((n,))],
-        compiler_params=pltpu.CompilerParams(collective_id=cid, has_side_effects=True, vmem_limit_bytes=VMEM_LIMIT),
-    )(*[x for part in smalls for x in part])
+    )
+
+
+def wgrad_body(blocks, bit, off, n_rhs, lhs, *refs):
+    rhs, (away, keep, lt) = refs[:n_rhs], refs[n_rhs:]
+    tokens = rhs[0].shape[0]
+    lt[...] = jnp.transpose(lhs[pl.ds(off, tokens), :])
+    mine = (lax.axis_index("seq") // bit) % 2
+    block = lt.shape[0] // blocks
+
+    def one(k, carry):
+        for dst, want in ((away, 1 - mine), (keep, mine)):
+            at = (k // bit) * (2 * bit) + want * bit + lax.rem(k, bit)
+            rows = lt[pl.ds(pl.multiple_of(at * block, 16), block), :]
+            c = 0
+            for r in rhs:
+                w = r.shape[1]
+                dst[k, :, c : c + w] = bdot(rows, r[...], NN).astype(BF16)
+                c += w
+        return carry
+
+    lax.fori_loop(0, blocks // 2, one, 0)
+
+
+def wgrad(lhs, rhs, bit, after=()):
+    blocks = lax.axis_size("seq")
+    tokens = rhs[0].shape[0]
+    d = lhs.shape[1]
+    width = sum(r.shape[1] for r in rhs)
+    shape = (blocks // 2, d // blocks, width)
+    return kcall(
+        partial(wgrad_body, blocks, bit, lhs.shape[0] - tokens, len(rhs)), [lhs] + list(rhs), [VM] * (1 + len(rhs)), 3, after,
+        name="wgrad",
+        out_specs=[VM] * 2,
+        out_shape=[S(shape, BF16)] * 2,
+        scratch_shapes=[pltpu.VMEM((d, tokens), BF16)],
+    )
+
+
+class Halving:
+    def __init__(self, lhs, rhs, order, after=()):
+        bits = bits_of("seq")
+        self.order = [bits[i % len(bits)] for i in order] + [b for i, b in enumerate(bits) if i not in order]
+        self.left = [b for b in reversed(bits)]
+        self.away, self.keep = wgrad(lhs, rhs, self.order[0], after)
+        self.left.remove(self.order[0])
+        self.step = 0
+        self.got = None
+
+    def go(self):
+        self.got = swap(self.away, "seq", self.order[self.step])
+        self.step += 1
+        return self.got
+
+    def fold(self):
+        total = self.keep.astype(F32) + self.got.astype(F32)
+        if self.step == len(self.order):
+            self.total = total[0] if total.ndim == 3 else total
+            return self.total
+        bit = self.order[self.step]
+        axis = self.left.index(bit)
+        view = total.reshape((2,) * len(self.left) + total.shape[-2:])
+        me = my_bit("seq", bit)
+        pick = lambda i: take(view, axis, i).astype(BF16).reshape((-1,) + total.shape[-2:])
+        self.away, self.keep = pick(1 - me), pick(me)
+        self.left.remove(bit)
+
+    def finish(self):
+        while self.step < len(self.order):
+            self.go()
+            self.fold()
+        return self.total
 
 
 def pad_lanes(x, to=LANE):
@@ -1006,38 +1111,30 @@
 
 def forward_layer(nx, h_own, extra, q, aux, segrow, layer):
     heads, size, inner = q["heads"], q["size"], q["inner"]
-    (gate, ux, ubc, krs, pdt, steps, cum, cT, gram, mixed, ypart, entry, state, dec, decl) = fwd_mix(
-        heads, size, nx, q["w_zx"], q["w_bc"], q["w_dt"], q["taps_x"], q["taps_bc"], q["dt_bias"], q["a_log"], q["skip"], aux, segrow)
+    (gate, ux, ubc, krs, pdt, steps, cum, cT, gram, mixed, ypart, entry, state, dec, decl) = fwd_mix(layer, heads, size, nx, q, aux, segrow)
     enter = carry_kernel(state, dec, heads, size, False, layer)
     y, carr, gated, sq = fwd_gate(ypart, entry, gate, krs, enter)
     width = inner * lax.axis_size("head")
-    nx_next, h_new, branch, r2b, side = head_fwd(gated, sq, q["gate_gain"], q["w_out"], h_own, extra, layer == LAYERS - 1, width, LAYERS + layer)
+    nx_next, h_new, branch, r2b, side = head_fwd(layer, gated, sq, q, h_own, extra, layer == LAYERS - 1, width, LAYERS + layer)
     stored = dict(nx=nx, gate=gate, ux=ux, ubc=ubc, krs=krs, pdt=pdt, steps=steps, cum=cum, cT=cT, gram=gram, mixed=mixed,
                   entry=entry, dec=dec, decl=decl, enter=enter, y=y, carr=carr, r2b=r2b, branch=branch, h_own=h_own)
     return nx_next, h_new, side, stored
 
 
-def backward_layer(g_own, gb, side, s, q, aux, segrow, layer, branch_before):
+def backward_gate(gb, side, s, q, layer):
     tokens = gb.shape[0]
-    heads, size, inner = q["heads"], q["size"], q["inner"]
-    width = inner * lax.axis_size("head")
+    width = q["inner"] * lax.axis_size("head")
     kr = side.reshape(4, 8, LANE)[:, 0, :].reshape(tokens)
     r2b = s["r2b"]
     krb = r2b * r2b * (kr[:, None] / width)
-    gy, gz, scaled, qloc, ggate, gskip = bwd_gate(gb, q["w_out"], s["gate"], s["y"], s["mixed"], s["entry"], s["krs"], r2b, krb, q["gate_gain"])
-    g_w_out = scatter_rows(mm_tn(gb, scaled))
-    later = carry_kernel(qloc, s["dec"], heads, size, True, 2 * LAYERS + layer)
-    dvd, dd, rowT, dkr = bwd_local(size, gy, s["mixed"], s["krs"], s["cum"], s["steps"], s["cT"], s["gram"], s["entry"], s["enter"], aux[5], segrow)
-    gm8, gu, gtail, gtaps_x, gdt, gvec, dkr = bwd_carry(
-        size, gy, dvd, s["mixed"], s["carr"], s["entry"], s["krs"], s["cum"], s["steps"], s["pdt"], q["dt_bias"], q["a_log"], q["skip"],
-        s["ux"], q["taps_x"], aux, later, s["enter"], dd, rowT, dkr, s["decl"][:1])
-    small, gtaps_bc, gtail = maps_bwd(dkr, s["ubc"], q["taps_bc"], aux, gdt, gtail, gm8, q["taps_x"], 3 * LAYERS + layer)
-    gu = lax.dynamic_update_slice(gu, gtail, (tokens - 16, 0))
-    normed = s["nx"][HALO:]
-    g_w_zx = scatter_rows(mm_tn(normed, jnp.concatenate([gz, gu], 1)))
-    g_w_small = scatter_rows(mm_tn(normed, small))
-    gb, g_own, g_gain, side = head_bwd(gz, gu, small, q["w_zx"], q["w_small"], s["h_own"], q["gain"][None], g_own, branch_before, 4 * LAYERS + layer)
-    return gb, g_own, side, (g_w_zx, g_w_small, g_w_out), (gtaps_x, ggate, gskip, gvec, gtaps_bc, g_gain)
+    return bwd_gate(layer, gb, q, s["gate"], s["y"], s["mixed"], s["entry"], s["krs"], r2b, krb)
+
+
+def backward_mix(gy, later, s, q, aux, segrow, layer, after_local):
+    size = q["size"]
+    dvd, dd, rowT, dkr = bwd_local(size, gy, s["mixed"], s["krs"], s["cum"], s["steps"], s["cT"], s["gram"], s["entry"], s["enter"], aux, segrow, after_local)
+    return bwd_carry(layer, size, gy, dvd, s["mixed"], s["carr"], s["entry"], s["krs"], s["cum"], s["steps"], s["pdt"], q,
+                     s["ux"], aux, later, s["enter"], dd, rowT, dkr, s["decl"])
 
 
 def local(hidden_in, seg, cot, norm_gain, w_zx, w_bc, w_dt, conv_x, conv_bc, dt_bias, a_log, skip_d, gate_gain, w_out):
@@ -1052,18 +1149,15 @@
     vecs += [(segf == segf[0]).astype(F32), (segf == segf[-1]).astype(F32), segf]
     aux = jnp.broadcast_to(jnp.stack(vecs, 0)[:, :, None], (len(vecs), tokens, LANE))
     segrow = segf[None]
-    wt = jnp.transpose(w_zx, (0, 2, 1, 3))
     lanes = jnp.arange(LANE)
-    own = jnp.where(rank % 2 == 0, lanes, LANE - 1 - lanes) < LANE // 2
-    qs = []
-    for l in range(LAYERS):
-        dt_pad = pad_lanes(w_dt[l])
-        tile = lax.dynamic_slice_in_dim(w_bc[l], (rank // 2) * LANE, LANE, 1)
-        w_small = jnp.where(own[None], tile, jnp.where(rank % 2 == 0, jnp.roll(dt_pad, LANE // 2, axis=1), dt_pad))
-        qs.append(dict(heads=heads, size=size, inner=inner, gain=norm_gain[l], w_zx=wt[l], w_bc=w_bc[l], w_dt=dt_pad, w_small=w_small,
-                       taps_x=jnp.pad(conv_x[l], ((0, 3), (0, 0))), taps_bc=jnp.pad(conv_bc[l], ((0, 3), (0, 0))),
-                       dt_bias=pad_lanes(dt_bias[l][None]), a_log=pad_lanes(a_log[l][None]), skip=jnp.repeat(skip_d[l], size)[None],
-                       gate_gain=gate_gain[l][None], w_out=w_out[l]))
+    even = rank % 2 == 0
+    own = jnp.where(even, lanes, LANE - 1 - lanes) < LANE // 2
+    dt_pad = pad_lanes(w_dt)
+    tile = lax.dynamic_slice_in_dim(w_bc, (rank // 2) * LANE, LANE, 2)
+    w_small = jnp.where(own[None, None], tile, jnp.where(even, jnp.roll(dt_pad, LANE // 2, axis=2), dt_pad))
+    q = dict(heads=heads, size=size, inner=inner, gain=norm_gain[:, None, :], w_zx=jnp.transpose(w_zx, (0, 2, 1, 3)), w_bc=w_bc, w_dt=dt_pad,
+             w_small=w_small, conv_x=conv_x, conv_bc=conv_bc, dt_bias=pad_lanes(dt_bias[:, None, :]), a_log=pad_lanes(a_log[:, None, :]),
+             skip=jnp.repeat(skip_d, size, axis=1)[:, None, :], gate_gain=gate_gain[:, None, :], w_out=w_out)
     h = hidden_in.astype(F32)
     h_own = own_rows(h)
     cot_own = own_rows(cot)
@@ -1071,28 +1165,54 @@
     nx = jnp.concatenate([shift(normed[tokens - HALO :], "seq", 1), normed], 0)
     stored = []
     for l in range(LAYERS):
-        extra = cot_own if l == LAYERS - 1 else norm_gain[l + 1][None]
-        nx, h_own, side, s = forward_layer(nx, h_own, extra, qs[l], aux, segrow, l)
+        extra = cot_own if l == LAYERS - 1 else q["gain"]
+        nx, h_own, side, s = forward_layer(nx, h_own, extra, q, aux, segrow, l)
         stored.append(s)
     hidden_out = nx
     gb = cot
     g_own = cot_own.astype(F32)
-    larges, smalls = [], []
+    smalls = [None] * LAYERS
+    sums = [None] * LAYERS
+    pending = []
     for l in reversed(range(LAYERS)):
+        s = stored[l]
+        gy, gz, scaled, qloc, ggate, gskip = backward_gate(gb, side, s, q, l)
+        later = carry_kernel(qloc, s["dec"], heads, size, True, 2 * LAYERS + l, after=[p.got for p in pending])
+        if pending:
+            for p in pending:
+                p.fold()
+            out_up, z_up, x_up = pending
+        out = Halving(gb, [scaled], (0, 1, 2), after=[later])
+        z = Halving(s["nx"], [gz], (0, 1, 2), after=[later])
+        first = [out.go()]
+        gm8, gu, gtail, gtaps_x, gdt, gvec, dkr = backward_mix(gy, later, s, q, aux, segrow, l, ())
+        small, gtaps_bc, gtail = maps_bwd(l, dkr, s["ubc"], q, aux, gdt, gtail, gm8, 3 * LAYERS + l, after=first)
+        gu = lax.dynamic_update_slice(gu, gtail, (tokens - 16, 0))
+        out.fold()
+        z.go()
+        out.go()
+        x = Halving(s["nx"], [gu, small], (0, 1, 2))
         before = stored[max(l - 1, 0)]["branch"]
-        gb, g_own, side, large, small = backward_layer(g_own, gb, side, stored[l], qs[l], aux, segrow, l, before)
-        larges.insert(0, large)
-        smalls.insert(0, small)
+        gb, g_own, g_gain, side = head_bwd(l, gz, gu, small, q, s["h_own"], g_own, before, 4 * LAYERS + l, after=[x.away])
+        x.go()
+        smalls[l] = (gtaps_x, ggate, gskip, gvec, gtaps_bc, g_gain)
+        pending = [out, z, x]
+        sums[l] = pending
     grad_in = gb.astype(F32)
-    stack = lambda which, i: jnp.stack([m[i] for m in which], 0)
-    g_w_zx = stack(larges, 0)
-    g_w_zx = g_w_zx.reshape(g_w_zx.shape[0], g_w_zx.shape[1], 2, inner)
-    g_small = stack(larges, 1)
-    even = rank % 2 == 0
+    for l in range(LAYERS):
+        for p in sums[l]:
+            if l == 0:
+                p.fold()
+            p.finish()
+    g_w_zx = jnp.stack([jnp.stack([z.total, x.total[:, :inner]], 1) for _, z, x in sums], 0)
+    g_small = jnp.stack([x.total[:, inner:] for _, _, x in sums], 0)
     g_w_bc = jnp.where(even, g_small[:, :, : LANE // 2], g_small[:, :, LANE // 2 :])
     g_w_dt = jnp.where(even, g_small[:, :, LANE // 2 : LANE // 2 + heads], g_small[:, :, :heads])
-    g_w_out = jnp.transpose(stack(larges, 2), (0, 2, 1))
-    g_conv_x, g_conv_bc, g_gate, g_skip, g_vec, g_gain = sums_kernel(smalls, inner, norm_gain.shape[1], 5 * LAYERS)
+    g_w_out = jnp.stack([jnp.transpose(out.total) for out, _, _ in sums], 0)
+    stage = pack_small(smalls, inner, 5 * LAYERS)
+    for bit in bits_of("seq"):
+        stage = stage + swap(stage, "seq", bit)
+    g_conv_x, g_conv_bc, g_gate, g_skip, g_vec, g_gain = unpack_small(stage, norm_gain.shape[1])
     g_skip = jnp.sum(g_skip.reshape(LAYERS, heads, size), axis=2)
     part = g_gain.shape[1] // lax.axis_size("seq")
     g_gain = lax.dynamic_slice_in_dim(g_gain, lax.axis_index("seq") * part, part, 1)

time: 825 us -> 671 us (0.81)
  waiting for transfers between devices: 144 us -> 81.7 us
  local copies, waits for them, and re-layouts: 96 us -> 43.9 us
  matrix products: 20.4 us -> 0 us
  Pallas kernels: 495 us -> 480 us
  other arithmetic: 40.1 us -> 29 us
    ppermute x18 -> x21, waiting for transfers between devices: 144 us -> 81.7 us  [swap(): return lax.ppermute(x, axis, [(i, i ^ bit) for i in range(n)])]
    dot_general x6 -> x0, matrix products: 20.4 us -> none  [dot(): lax.dot_general(a.astype(BF16), b.astype(BF16), (dims, ((), ())), preferr...]
    pallas_call x21 -> x28, Pallas kernels: 495 us -> 480 us  [kcall(): pl.pallas_call(wrapped, in_specs=list(specs) + [pl.BlockSpec(memory_space...]
    squeeze x3 -> x0, local copies, waits for them, and re-layouts: 12.8 us -> none  [the longest x1 8.02 us: local(): wt[l]]
    convert_element_type x18 -> x12, local copies, waits for them, and re-layouts: 14.8 us -> 2.09 us  [fold(): take(view, axis, i).astype(BF16).reshape((-1,) + total.shape[-2:])]
    slice x10 -> x1, local copies, waits for them, and re-layouts: 12.5 us -> 0.15 us  [local(): jnp.roll(dt_pad, LANE // 2, axis=2)]
    ppermute x18 -> x21, starting transfers between devices: 11.4 us -> 19.2 us  [swap(): return lax.ppermute(x, axis, [(i, i ^ bit) for i in range(n)])]
    unnamed x83 -> x78, local copies, waits for them, and re-layouts: 24.2 us -> 25.1 us
  transfers between devices with their start and end apart: 19 -> 22, of which waited for: 12 -> 11; matrix products, arithmetic and copies ran while one was open for 14% -> 8% of each run, Pallas kernels for 15% -> 35%
where the time goes in v2:
time: 671 us; the launch traced here: 660 us
  Pallas kernels  480 us (72%)
  waiting for transfers between devices  81.7 us (12%)
  local copies, waits for them, and re-layouts  43.9 us (7%)
  other arithmetic  29 us (4%)
  starting transfers between devices  24.2 us (4%)
    pallas_call x28, Pallas kernels, kcall(): pl.pallas_call(wrapped, in_specs=list(specs) + [pl.BlockSpec(memory_space...  480 us
    ppermute x21, waiting for transfers between devices, swap(): return lax.ppermute(x, axis, [(i, i ^ bit) for i in range(n)])  81.7 us
    unnamed x78, local copies, waits for them, and re-layouts  25.1 us
    ppermute x21, starting transfers between devices, swap(): return lax.ppermute(x, axis, [(i, i ^ bit) for i in range(n)])  19.2 us
  transfers between devices with their start and end apart: 22, of which 11 were waited for; matrix products, arithmetic and copies ran while one was open for 8% of the time, Pallas kernels for 35%

profile of v2, /device:TPU:0, one launch (start us, length us, event | category | flops | bytes accessed | tf_op | source)
XLA Modules:
  0.0 660.3 jit_solution(3936102534682012193)
XLA Ops:
  1.5 1.8 multiply_reduce_fusion
  4.9 5.0 collective-permute-start
  11.2 2.1 convert.23
  13.2 1.6 constant_dynamic-slice_fusion.2
  18.6 1.7 select_select_fusion
  20.4 1.4 fusion.20
  22.4 8.7 %copy.104 = bf16[2,1536,2,768]{3,1,2,0:T(8,128)(2,1)} copy(bf16[2,1536,2,768]{3,2,1,0:T(2,128)(2,1)} %param.18) | data formatting | bytes 18874368 | tf_op args[4]
  34.9 1.3 pad_maximum_fusion.1.refs_0_
  36.1 1.6 broadcast_in_dim.36.refs_9_.refs_14_.refs_3_
  37.7 19.8 %fwd_mix.2 = (bf16[512,768]{1,0:T(8,128)(2,1)}, bf16[528,768]{1,0:T(8,128)(2,1)}, bf16[528,256]{1,0:T(8,128)(2,1)}, f32[512,256]{1,0:T(8,128)}, bf16[512,128]{1,...) custom-call(bf16[528,1536]{1,0:T(8,128)(2,1)} %pad_maximum_fusion.1., ...), custom_call_target="tpu_custom_call" | custom-call | flops 16000000000 | bytes 48000000 | tf_op jit(solution)/shard_map/fwd_mix/pallas_call | solution.py:856
  57.5 41.1 %carry_on.2.refs_4_.refs_8_.refs_16_ = f32[768,128]{1,0:T(8,128)} custom-call(f32[768,128]{1,0:T(8,128)} %get-tuple-element.126.refs_0_, f32[16,128]{1,0:T(8,128)} %get-tuple-element.127.refs_1_), custom_call_target="tpu_custom_call" | custom-call | flops 24999999488 | bytes 75000000 | tf_op jit(solution)/shard_map/carry_on/pallas_call | solution.py:856
  98.7 7.1 %fwd_gate.2 = (f32[512,768]{1,0:T(8,128)}, f32[512,768]{1,0:T(8,128)}, f32[512,768]{1,0:T(8,128)}, f32[8,512]{1,0:T(8,128)}) custom-call(f32[512,768]{1,0:T(8,128)} %get-tuple-element.122.refs_0_, f32[512,768]{1,0:T(8,128)} %get-tuple-element.123.refs_1_.refs_5_.refs_7_.refs_4_, bf16[512,768]{1,0:T(8,128)(2,1)} %get-tuple-element.124.refs_2_, ...), custom_call_target="tpu_custom_call" | custom-call | flops 7000000000 | bytes 21000000 | tf_op jit(solution)/shard_map/fwd_gate/pallas_call | solution.py:856
  105.8 41.0 %head_fwd.1 = (bf16[528,1536]{1,0:T(8,128)(2,1)}, f32[128,1536]{1,0:T(8,128)}, f32[128,1536]{1,0:T(8,128)}, f32[512,128]{1,0:T(8,128)}, f32[32,128]{1,0:T(8,128)}) custom-call(f32[512,768]{1,0:T(8,128)} %get-tuple-element.128.refs_0_, f32[8,512]{1,0:T(8,128)} %get-tuple-element.129.refs_1_, f32[2,1,768]{2,1,0:T(1,128)} %broadcast_in_dim.37.refs_2_.refs_9_, ...), custom_call_target="tpu_custom_call" | custom-call | flops 30000001024 | bytes 90000000 | tf_op jit(solution)/shard_map/head_fwd/pallas_call | solution.py:856
  146.8 19.8 %fwd_mix.3 = (bf16[512,768]{1,0:T(8,128)(2,1)}, bf16[528,768]{1,0:T(8,128)(2,1)}, bf16[528,256]{1,0:T(8,128)(2,1)}, f32[512,256]{1,0:T(8,128)}, bf16[512,128]{1,...) custom-call(bf16[528,1536]{1,0:T(8,128)(2,1)} %get-tuple-element.130, ...), custom_call_target="tpu_custom_call" | custom-call | flops 16000000000 | bytes 48000000 | tf_op jit(solution)/shard_map/fwd_mix/pallas_call | solution.py:856
  166.7 42.4 %carry_on.3.refs_4_.refs_8_.refs_16_ = f32[768,128]{1,0:T(8,128)} custom-call(f32[768,128]{1,0:T(8,128)} %get-tuple-element.135.refs_0_, f32[16,128]{1,0:T(8,128)} %get-tuple-element.136.refs_1_), custom_call_target="tpu_custom_call" | custom-call | flops 24999999488 | bytes 75000000 | tf_op jit(solution)/shard_map/carry_on/pallas_call | solution.py:856
  209.1 7.2 %fwd_gate.3 = (f32[512,768]{1,0:T(8,128)}, f32[512,768]{1,0:T(8,128)}, f32[512,768]{1,0:T(8,128)}, f32[8,512]{1,0:T(8,128)}) custom-call(f32[512,768]{1,0:T(8,128)} %get-tuple-element.131.refs_0_, f32[512,768]{1,0:T(8,128)} %get-tuple-element.132.refs_1_.refs_5_.refs_7_.refs_4_, bf16[512,768]{1,0:T(8,128)(2,1)} %get-tuple-element.133.refs_2_, ...), custom_call_target="tpu_custom_call" | custom-call | flops 7000000000 | bytes 21000000 | tf_op jit(solution)/shard_map/fwd_gate/pallas_call | solution.py:856
  216.4 30.1 %head_fwd_last.1 = (bf16[512,1536]{1,0:T(8,128)(2,1)}, f32[128,1536]{1,0:T(8,128)}, f32[128,1536]{1,0:T(8,128)}, f32[512,128]{1,0:T(8,128)}, f32[32,128]{1,0:T(8,128)}) custom-call(f32[512,768]{1,0:T(8,128)} %get-tuple-element.137.refs_0_, f32[8,512]{1,0:T(8,128)} %get-tuple-element.138.refs_1_, f32[2,1,768]{2,1,0:T(1,128)} %broadcast_in_dim.37.refs_2_.refs_9_, ...), custom_call_target="tpu_custom_call" | custom-call | flops 30000001024 | bytes 90000000 | tf_op jit(solution)/shard_map/head_fwd_last/pallas_call | solution.py:856
  247.2 1.8 multiply_multiply_fusion.1.refs_8_
  249.0 9.4 %bwd_gate.2 = (f32[512,768]{1,0:T(8,128)}, bf16[512,768]{1,0:T(8,128)(2,1)}, bf16[512,768]{1,0:T(8,128)(2,1)}, f32[768,128]{1,0:T(8,128)}, f32[1,768]{1,0:T(1,128)}, /*index=5*/f32[1,768]{1,0:T(1,128)}) custom-call(bf16[512,1536]{1,0:T(8,128)(2,1)} %refs_0_.3, bf16[2,768,1536]{2,1,0:T(8,128)(2,1)} %refs_1_.3, bf16[512,768]{1,0:T(8,128)(2,1)} %get-tuple-element.133.refs_2_, ...), custom_call_target="tpu_custom_call" | custom-call | flops 8999999488 | bytes 27000000 | tf_op jit(solution)/shard_map/bwd_gate/pallas_call | solution.py:856
  258.4 24.9 %carry_back.2.refs_15_.refs_2_ = f32[768,128]{1,0:T(8,128)} custom-call(f32[768,128]{1,0:T(8,128)} %get-tuple-element.155.refs_0_, f32[16,128]{1,0:T(8,128)} %get-tuple-element.136.refs_1_), custom_call_target="tpu_custom_call" | custom-call | flops 24999999488 | bytes 75000000 | tf_op jit(solution)/shard_map/carry_back/pallas_call | solution.py:856
  283.2 5.3 wgrad.6
  289.5 5.4 wgrad.8
  296.0 22.3 %bwd_local.2 = (f32[512,768]{1,0:T(8,128)}, f32[512,128]{1,0:T(8,128)}, f32[128,512]{1,0:T(8,128)}, f32[512,256]{1,0:T(8,128)}) custom-call(f32[512,768]{1,0:T(8,128)} %get-tuple-element.146.refs_0_, f32[512,768]{1,0:T(8,128)} %get-tuple-element.142.refs_4_.refs_1_.refs_2_, f32[512,256]{1,0:T(8,128)} %get-tuple-element.134.refs_3_.refs_6_.refs_2_.refs_5_, ...), custom_call_target="tpu_custom_call" | custom-call | flops 10000000000 | bytes 30000000 | tf_op jit(solution)/shard_map/bwd_local/pallas_call | solution.py:856
  318.3 12.1 %bwd_carry.2 = (f32[8,768]{1,0:T(8,128)}, bf16[512,768]{1,0:T(8,128)(2,1)}, f32[16,768]{1,0:T(8,128)}, f32[8,768]{1,0:T(8,128)}, bf16[512,128]{1,0:T(8,128)(2,1)}, /*index=5*/f32[8,128]{1,0:T(8,128)}, f32[512,256]{1,0:T(8,128)}) custom-call(f32[512,768]{1,0:T(8,128)} %get-tuple-element.146.refs_0_, f32[512,768]{1,0:T(8,128)} %get-tuple-element.151.refs_1_, ...), custom_call_target="tpu_custom_call" | custom-call | flops 11000000512 | bytes 33000000 | tf_op jit(solution)/shard_map/bwd_carry/pallas_call | solution.py:856
  331.6 14.2 %maps_bwd.2 = (bf16[512,128]{1,0:T(8,128)(2,1)}, f32[8,128]{1,0:T(8,128)}, bf16[16,768]{1,0:T(8,128)(2,1)}) custom-call(f32[512,256]{1,0:T(8,128)} %get-tuple-element.161.refs_0_, bf16[528,256]{1,0:T(8,128)(2,1)} %get-tuple-element.162.refs_1_, f32[2,5,256]{2,1,0:T(8,128)} %copy.61.refs_5_.refs_2_, f32[6,512,128]{2,1,0:T(8,128)} %broadcast_in_dim.36.refs_9_.refs_14_.refs_3_, ...), custom_call_target="tpu_custom_call" | custom-call | flops 14000000000 | bytes 42000000 | tf_op jit(solution)/shard_map/maps_bwd/pallas_call | solution.py:856
  345.7 1.3 constant_dynamic-update-slice_fusion.1.refs_1_
  347.1 5.8 wgrad.7
  352.9 2.0 collective-permute-start.4
  354.9 30.2 %head_bwd.2 = (bf16[512,1536]{1,0:T(8,128)(2,1)}, f32[128,1536]{1,0:T(8,128)}, f32[1,1536]{1,0:T(1,128)}, f32[32,128]{1,0:T(8,128)}) custom-call(bf16[512,768]{1,0:T(8,128)(2,1)} %get-tuple-element.145.refs_0_.refs_1_, bf16[512,768]{1,0:T(8,128)(2,1)} %constant_dynamic-update-slice_fusion.1.refs_1_, bf16[512,128]{1,0:T(8,128)(2,1)} %get-tuple-element.169.refs_2_, ...), custom_call_target="tpu_custom_call" | custom-call | flops 28999999488 | bytes 87000000 | tf_op jit(solution)/shard_map/head_bwd/pallas_call | solution.py:856
  386.9 1.7 collective-permute-start.15
  389.4 9.4 %bwd_gate.3 = (f32[512,768]{1,0:T(8,128)}, bf16[512,768]{1,0:T(8,128)(2,1)}, bf16[512,768]{1,0:T(8,128)(2,1)}, f32[768,128]{1,0:T(8,128)}, f32[1,768]{1,0:T(1,128)}, /*index=5*/f32[1,768]{1,0:T(1,128)}) custom-call(bf16[512,1536]{1,0:T(8,128)(2,1)} %get-tuple-element.172.refs_0_, bf16[2,768,1536]{2,1,0:T(8,128)(2,1)} %refs_1_.3, ...), custom_call_target="tpu_custom_call" | custom-call | flops 8999999488 | bytes 27000000 | tf_op jit(solution)/shard_map/bwd_gate/pallas_call | solution.py:856
  398.9 3.7 collective-permute-done.15
  402.8 2.4 collective-permute-start.16
  406.0 11.0 %bwd_local.3 = (f32[512,768]{1,0:T(8,128)}, f32[512,128]{1,0:T(8,128)}, f32[128,512]{1,0:T(8,128)}, f32[512,256]{1,0:T(8,128)}) custom-call(f32[512,768]{1,0:T(8,128)} %get-tuple-element.178.refs_0_, f32[512,768]{1,0:T(8,128)} %get-tuple-element.174.refs_4_.refs_1_.refs_2_, f32[512,256]{1,0:T(8,128)} %get-tuple-element.125.refs_3_.refs_6_.refs_2_.refs_5_, ...), custom_call_target="tpu_custom_call" | custom-call | flops 10000000000 | bytes 30000000 | tf_op jit(solution)/shard_map/bwd_local/pallas_call | solution.py:856
  417.0 9.0 %collective-permute-done.16 = bf16[1,192,768]{2,1,0:T(8,128)(2,1)S(1)} collective-permute-done((bf16[1,192,768]{2,1,0:T(8,128)(2,1)S(1)}, bf16[1,192,768]{2,1,0:T(8,128)(2,1)S(1)}, u32[]{:S(2)}, u32[]{:S(2)}) %collective-permute-start.16) | collective-permute-done | bytes 294944 | tf_op jit(solution)/shard_map/ppermute | solution.py:35
  426.1 5.0 collective-permute-done.21
  433.3 30.9 %carry_back.3.refs_15_.refs_2_ = f32[768,128]{1,0:T(8,128)} custom-call(f32[768,128]{1,0:T(8,128)} %get-tuple-element.187.refs_0_, f32[16,128]{1,0:T(8,128)} %get-tuple-element.127.refs_1_, bf16[2,192,768]{2,1,0:T(8,128)(2,1)} %copy-done.19, bf16[4,192,768]{2,1,0:T(8,128)(2,1)} %copy-done.9, bf16[4,192,896]{2,1,0:T(8,128)(2,1)} %copy-done.7), custom_call_target="tpu_custom_call" | custom-call | flops 24999999488 | bytes 75000000 | tf_op jit(solution)/shard_map/carry_back/pallas_call | solution.py:856
  464.2 5.3 wgrad.9
  470.4 5.3 wgrad.11
  477.2 12.3 %bwd_carry.3 = (f32[8,768]{1,0:T(8,128)}, bf16[512,768]{1,0:T(8,128)(2,1)}, f32[16,768]{1,0:T(8,128)}, f32[8,768]{1,0:T(8,128)}, bf16[512,128]{1,0:T(8,128)(2,1)}, /*index=5*/f32[8,128]{1,0:T(8,128)}, f32[512,256]{1,0:T(8,128)}) custom-call(f32[512,768]{1,0:T(8,128)} %get-tuple-element.178.refs_0_, f32[512,768]{1,0:T(8,128)} %get-tuple-element.183.refs_1_, ...), custom_call_target="tpu_custom_call" | custom-call | flops 11000000512 | bytes 33000000 | tf_op jit(solution)/shard_map/bwd_carry/pallas_call | solution.py:856
  489.5 3.0 collective-permute-done.18
  493.4 5.3 collective-permute-done.5.refs_8_
  499.7 23.9 %maps_bwd.3 = (bf16[512,128]{1,0:T(8,128)(2,1)}, f32[8,128]{1,0:T(8,128)}, bf16[16,768]{1,0:T(8,128)(2,1)}) custom-call(f32[512,256]{1,0:T(8,128)} %get-tuple-element.195.refs_0_, bf16[528,256]{1,0:T(8,128)(2,1)} %get-tuple-element.196.refs_1_, f32[2,5,256]{2,1,0:T(8,128)} %copy.61.refs_5_.refs_2_, f32[6,512,128]{2,1,0:T(8,128)} %broadcast_in_dim.36.refs_9_.refs_14_.refs_3_, ...), custom_call_target="tpu_custom_call" | custom-call | flops 14000000000 | bytes 42000000 | tf_op jit(solution)/shard_map/maps_bwd/pallas_call | solution.py:856
  523.5 1.4 constant_dynamic-update-slice_fusion.refs_1_
  524.9 5.8 wgrad.10
  530.7 29.1 %head_bwd.3 = (bf16[512,1536]{1,0:T(8,128)(2,1)}, f32[128,1536]{1,0:T(8,128)}, f32[1,1536]{1,0:T(1,128)}, f32[32,128]{1,0:T(8,128)}) custom-call(bf16[512,768]{1,0:T(8,128)(2,1)} %get-tuple-element.177.refs_0_.refs_1_, bf16[512,768]{1,0:T(8,128)(2,1)} %constant_dynamic-update-slice_fusion.refs_1_, bf16[512,128]{1,0:T(8,128)(2,1)} %get-tuple-element.203.refs_2_, ...), custom_call_target="tpu_custom_call" | custom-call | flops 28999999488 | bytes 87000000 | tf_op jit(solution)/shard_map/head_bwd/pallas_call | solution.py:856
  559.8 3.5 convert_element_type.279
  563.3 6.9 %pack_small.1 = f32[2,16,768]{2,1,0:T(8,128)} custom-call(f32[8,768]{1,0:T(8,128)} %get-tuple-element.207.refs_0_, f32[1,768]{1,0:T(1,128)} %get-tuple-element.208.refs_1_, f32[1,768]{1,0:T(1,128)} %get-tuple-element.209.refs_2_, f32[8,128]{1,0:T(8,128)} %get-tuple-element.210.refs_3_, f32[8,128]{1,0:T(8,128)} %get-tuple-element.211.refs_4_, ...), custom_call_target="tpu_custom_call" | custom-call | flops 8000000000 | bytes 24000000 | tf_op jit(solution)/shard_map/pack_small/pallas_call | solution.py:856
  570.2 2.1 collective-permute-start.6
  573.4 1.8 collective-permute-done.6
  576.6 1.5 convert_add_fusion.4
  578.1 12.4 %collective-permute-done.7 = f32[2,16,768]{2,1,0:T(8,128)S(1)} collective-permute-done((f32[2,16,768]{2,1,0:T(8,128)S(1)}, f32[2,16,768]{2,1,0:T(8,128)S(1)}, u32[]{:S(2)}, u32[]{:S(2)}) %collective-permute-start.7) | collective-permute-done | bytes 98336 | tf_op jit(solution)/shard_map/ppermute | solution.py:35
  592.0 1.7 collective-permute-start.10
  593.7 3.2 collective-permute-done.8
  597.6 1.5 unpack_small.1
  599.1 1.4 copy.89
  600.6 1.3 copy.90
  603.3 1.4 constant_dynamic-slice_fusion
  607.2 1.7 convert_add_fusion.1
  609.3 2.2 collective-permute-start.20
  613.6 17.9 %collective-permute-done.20 = bf16[1,192,768]{2,1,0:T(8,128)(2,1)S(1)} collective-permute-done((bf16[1,192,768]{2,1,0:T(8,128)(2,1)S(1)}, bf16[1,192,768]{2,1,0:T(8,128)(2,1)S(1)}, u32[]{:S(2)}, u32[]{:S(2)}) %collective-permute-start.20) | collective-permute-done | bytes 294944 | tf_op jit(solution)/shard_map/ppermute | solution.py:35
  631.5 5.3 collective-permute-done.13
  638.3 15.1 %collective-permute-done.14 = bf16[1,192,896]{2,1,0:T(8,128)(2,1)S(1)} collective-permute-done((bf16[1,192,896]{2,1,0:T(8,128)(2,1)S(1)}, bf16[1,192,896]{2,1,0:T(8,128)(2,1)S(1)}, u32[]{:S(2)}, u32[]{:S(2)}) %collective-permute-start.14) | collective-permute-done | bytes 344096 | tf_op jit(solution)/shard_map/ppermute | solution.py:35
  654.0 3.2 copy.86
  (165 shorter events, 41.3 us)
Async XLA Ops:
  0.6 2.7 copy-start
  3.3 6.6 %copy-start.24 = (bf16[2,1536,12]{1,0,2:T(2,128)(2,1)S(1)}, bf16[2,1536,12]{1,0,2:T(2,128)(2,1)}, u32[]{:S(2)}) copy-start(bf16[2,1536,12]{1,0,2:T(2,128)(2,1)} %param.20) | copy-start | bytes 221188
  3.8 1.1 copy-start.1
  4.9 5.6 copy-start.29
  4.9 29.9 %collective-permute-start = (bf16[16,1536]{1,0:T(8,128)(2,1)S(1)}, bf16[16,1536]{1,0:T(8,128)(2,1)S(1)}, u32[]{:S(2)}, u32[]{:S(2)}) collective-permute-start(bf16[16,1536]{1,0:T(8,128)(2,1)S(1)} %slice.84), channel_id=1, source_target_pairs={{0,4},{4,8},{8,12},{12,16},{16,20},{20,24},{24,28},{1,5},{5,9},{9,... | collective-permute-start | bytes 147464 | tf_op jit(solution)/shard_map/ppermute | solution.py:40
  10.6 24.3 %copy-start.27 = (f32[512]{0:T(512)}, f32[512]{0:T(512)S(1)}, u32[]{:S(2)}) copy-start(f32[512]{0:T(512)S(1)} %convert_element_type.273) | copy-start | bytes 6148
  13.2 1.9 copy-start.20
  16.0 1.4 copy-start.4
  17.0 1.6 copy-start.21
  18.6 3.1 copy-start.26
  22.3 8.8 %copy-start.25 = (f32[2,5,768]{2,0,1:T(2,128)S(1)}, f32[2,5,768]{2,0,1:T(2,128)}, u32[]{:S(2)}) copy-start(f32[2,5,768]{2,0,1:T(2,128)} %param.21) | copy-start | bytes 92164
  22.3 9.4 %copy-start.28 = (f32[2,5,256]{2,0,1:T(2,128)S(1)}, f32[2,5,256]{2,0,1:T(2,128)}, u32[]{:S(2)}) copy-start(f32[2,5,256]{2,0,1:T(2,128)} %param.22) | copy-start | bytes 30724
  22.3 10.0 %copy-start.32 = (f32[2,12]{1,0:T(2,128)S(1)}, f32[2,12]{1,0:T(2,128)}, u32[]{:S(2)}) copy-start(f32[2,12]{1,0:T(2,128)} %param.23) | copy-start | bytes 292
  22.3 10.6 %copy-start.33 = (f32[2,12]{1,0:T(2,128)S(1)}, f32[2,12]{1,0:T(2,128)}, u32[]{:S(2)}) copy-start(f32[2,12]{1,0:T(2,128)} %param.24) | copy-start | bytes 292
  22.3 11.1 %copy-start.31 = (f32[2,12]{1,0:T(2,128)S(1)}, f32[2,12]{1,0:T(2,128)}, u32[]{:S(2)}) copy-start(f32[2,12]{1,0:T(2,128)} %param.25) | copy-start | bytes 292
  22.4 11.9 %copy-start.30 = (f32[2,768]{1,0:T(2,128)S(1)}, f32[2,768]{1,0:T(2,128)}, u32[]{:S(2)}) copy-start(f32[2,768]{1,0:T(2,128)} %param.26) | copy-start | bytes 18436
  22.4 12.5 %copy-start.2 = (bf16[512,1536]{1,0:T(8,128)(2,1)S(1)}, bf16[512,1536]{1,0:T(8,128)(2,1)}, u32[]{:S(2)}) copy-start(bf16[512,1536]{1,0:T(8,128)(2,1)} %copy-done.1) | copy-start | bytes 4718596
  288.6 41.9 %collective-permute-start.1 = (bf16[4,192,768]{2,1,0:T(8,128)(2,1)}, bf16[4,192,768]{2,1,0:T(8,128)(2,1)S(1)}, u32[]{:S(2)}, u32[]{:S(2)}) collective-permute-start(bf16[4,192,768]{2,1,0:T(8,128)(2,1)} %get-tuple-element.167), channel_id=1, source_target_pairs={{0,4},{4,0},{8,12},{12,8},{16,20},{20,16},{24,28},{28,24},{1,5},{5... | collective-permute-start | bytes 3538952 | tf_op jit(solution)/shard_map/ppermute | solution.py:35
  294.9 90.9 %collective-permute-start.3 = (bf16[4,192,768]{2,1,0:T(8,128)(2,1)}, bf16[4,192,768]{2,1,0:T(8,128)(2,1)S(1)}, u32[]{:S(2)}, u32[]{:S(2)}) collective-permute-start(bf16[4,192,768]{2,1,0:T(8,128)(2,1)} %get-tuple-element.189), channel_id=1, source_target_pairs={{0,4},{4,0},{8,12},{12,8},{16,20},{20,16},{24,28},{28,24},{1,5},{5... | collective-permute-start | bytes 3538952 | tf_op jit(solution)/shard_map/ppermute | solution.py:35
  318.3 12.1 %copy-start.17 = (bf16[4,192,768]{2,1,0:T(8,128)(2,1)S(1)}, bf16[4,192,768]{2,1,0:T(8,128)(2,1)}, u32[]{:S(2)}) copy-start(bf16[4,192,768]{2,1,0:T(8,128)(2,1)} %get-tuple-element.188) | copy-start | bytes 3538948
  330.4 1.0 copy-start.16
  331.5 73.6 %collective-permute-start.2 = (bf16[2,192,768]{2,1,0:T(8,128)(2,1)S(1)}, bf16[2,192,768]{2,1,0:T(8,128)(2,1)S(1)}, u32[]{:S(2)}, u32[]{:S(2)}) collective-permute-start(bf16[2,192,768]{2,1,0:T(8,128)(2,1)S(1)} %fusion.4), channel_id=1, source_target_pairs={{0,8},{4,12},{8,0},{12,4},{16,24},{20,28},{24,16},{28,20},{1,9},{5... | collective-permute-start | bytes 1769480 | tf_op jit(solution)/shard_map/ppermute | solution.py:35
  352.9 79.2 %collective-permute-start.4 = (bf16[4,192,896]{2,1,0:T(8,128)(2,1)}, bf16[4,192,896]{2,1,0:T(8,128)(2,1)S(1)}, u32[]{:S(2)}, u32[]{:S(2)}) collective-permute-start(bf16[4,192,896]{2,1,0:T(8,128)(2,1)} %get-tuple-element.171.refs_9_), channel_id=1, source_target_pairs={{0,4},{4,0},{8,12},{12,8},{16,20},{20,16},{24,28},{28,24},{1,5},{5... | collective-permute-start | bytes 4128776 | tf_op jit(solution)/shard_map/ppermute | solution.py:35
  354.9 30.9 %copy-start.15 = (bf16[4,192,768]{2,1,0:T(8,128)(2,1)S(1)}, bf16[4,192,768]{2,1,0:T(8,128)(2,1)}, u32[]{:S(2)}) copy-start(bf16[4,192,768]{2,1,0:T(8,128)(2,1)} %get-tuple-element.223) | copy-start | bytes 3538948
  385.8 1.0 copy-start.9
  385.8 2.8 copy-start.22
  386.9 15.7 %collective-permute-start.15 = (bf16[2,192,768]{2,1,0:T(8,128)(2,1)S(1)}, bf16[2,192,768]{2,1,0:T(8,128)(2,1)S(1)}, u32[]{:S(2)}, u32[]{:S(2)}) collective-permute-start(bf16[2,192,768]{2,1,0:T(8,128)(2,1)S(1)} %fusion.8), channel_id=1, source_target_pairs={{0,8},{4,12},{8,0},{12,4},{16,24},{20,28},{24,16},{28,20},{1,9},{5... | collective-permute-start | bytes 1769480 | tf_op jit(solution)/shard_map/ppermute | solution.py:35
  402.8 23.3 %collective-permute-start.16 = (bf16[1,192,768]{2,1,0:T(8,128)(2,1)S(1)}, bf16[1,192,768]{2,1,0:T(8,128)(2,1)S(1)}, u32[]{:S(2)}, u32[]{:S(2)}) collective-permute-start(bf16[1,192,768]{2,1,0:T(8,128)(2,1)S(1)} %dynamic-slice_convert_fusion.8), channel_id=1, source_target_pairs={{0,16},{4,20},{8,24},{12,28},{16,0},{20,4},{24,8},{28,12},{1,17},{... | collective-permute-start | bytes 884744 | tf_op jit(solution)/shard_map/ppermute | solution.py:35
  405.1 11.9 %copy-start.19 = (bf16[2,192,768]{2,1,0:T(8,128)(2,1)}, bf16[2,192,768]{2,1,0:T(8,128)(2,1)S(1)}, u32[]{:S(2)}) copy-start(bf16[2,192,768]{2,1,0:T(8,128)(2,1)S(1)} %collective-permute-done.2.refs_2_) | copy-start | bytes 1769476
  405.3 25.8 %collective-permute-start.21 = (bf16[1,192,768]{2,1,0:T(8,128)(2,1)S(1)}, bf16[1,192,768]{2,1,0:T(8,128)(2,1)S(1)}, u32[]{:S(2)}, u32[]{:S(2)}) collective-permute-start(bf16[1,192,768]{2,1,0:T(8,128)(2,1)S(1)} %dynamic-slice_convert_fusion.4), channel_id=1, source_target_pairs={{0,16},{4,20},{8,24},{12,28},{16,0},{20,4},{24,8},{28,12},{1,17},{... | collective-permute-start | bytes 884744 | tf_op jit(solution)/shard_map/ppermute | solution.py:35
  417.0 15.1 %copy-start.8 = (bf16[4,192,896]{2,1,0:T(8,128)(2,1)S(1)}, bf16[4,192,896]{2,1,0:T(8,128)(2,1)}, u32[]{:S(2)}) copy-start(bf16[4,192,896]{2,1,0:T(8,128)(2,1)} %get-tuple-element.224) | copy-start | bytes 4128772
  432.1 1.1 copy-start.7
  433.2 43.7 %collective-permute-start.17 = (bf16[2,192,896]{2,1,0:T(8,128)(2,1)S(1)}, bf16[2,192,896]{2,1,0:T(8,128)(2,1)S(1)}, u32[]{:S(2)}, u32[]{:S(2)}) collective-permute-start(bf16[2,192,896]{2,1,0:T(8,128)(2,1)S(1)} %fusion.3), channel_id=1, source_target_pairs={{0,8},{4,12},{8,0},{12,4},{16,24},{20,28},{24,16},{28,20},{1,9},{5... | collective-permute-start | bytes 2064392 | tf_op jit(solution)/shard_map/ppermute | solution.py:35
  469.5 29.1 %collective-permute-start.5 = (bf16[4,192,768]{2,1,0:T(8,128)(2,1)}, bf16[4,192,768]{2,1,0:T(8,128)(2,1)S(1)}, u32[]{:S(2)}, u32[]{:S(2)}) collective-permute-start(bf16[4,192,768]{2,1,0:T(8,128)(2,1)} %get-tuple-element.201), channel_id=1, source_target_pairs={{0,4},{4,0},{8,12},{12,8},{16,20},{20,16},{24,28},{28,24},{1,5},{5... | collective-permute-start | bytes 3538952 | tf_op jit(solution)/shard_map/ppermute | solution.py:35
  475.7 99.8 %collective-permute-start.9 = (bf16[4,192,768]{2,1,0:T(8,128)(2,1)}, bf16[4,192,768]{2,1,0:T(8,128)(2,1)S(1)}, u32[]{:S(2)}, u32[]{:S(2)}) collective-permute-start(bf16[4,192,768]{2,1,0:T(8,128)(2,1)} %get-tuple-element.221), channel_id=1, source_target_pairs={{0,4},{4,0},{8,12},{12,8},{16,20},{20,16},{24,28},{28,24},{1,5},{5... | collective-permute-start | bytes 3538952 | tf_op jit(solution)/shard_map/ppermute | solution.py:35
  477.1 15.4 %collective-permute-start.18 = (bf16[1,192,896]{2,1,0:T(8,128)(2,1)S(1)}, bf16[1,192,896]{2,1,0:T(8,128)(2,1)S(1)}, u32[]{:S(2)}, u32[]{:S(2)}) collective-permute-start(bf16[1,192,896]{2,1,0:T(8,128)(2,1)S(1)} %dynamic-slice_convert_fusion), channel_id=1, source_target_pairs={{0,16},{4,20},{8,24},{12,28},{16,0},{20,4},{24,8},{28,12},{1,17},{... | collective-permute-start | bytes 1032200 | tf_op jit(solution)/shard_map/ppermute | solution.py:35
  498.7 1.0 copy-start.13
  530.7 76.5 %collective-permute-start.12 = (bf16[4,192,896]{2,1,0:T(8,128)(2,1)}, bf16[4,192,896]{2,1,0:T(8,128)(2,1)}, u32[]{:S(2)}, u32[]{:S(2)}) collective-permute-start(bf16[4,192,896]{2,1,0:T(8,128)(2,1)} %get-tuple-element.205.refs_9_), channel_id=1, source_target_pairs={{0,4},{4,0},{8,12},{12,8},{16,20},{20,16},{24,28},{28,24},{1,5},{5... | collective-permute-start | bytes 4128776 | tf_op jit(solution)/shard_map/ppermute | solution.py:35
  563.3 9.0 %copy-start.12 = (bf16[4,192,768]{2,1,0:T(8,128)(2,1)S(1)}, bf16[4,192,768]{2,1,0:T(8,128)(2,1)}, u32[]{:S(2)}) copy-start(bf16[4,192,768]{2,1,0:T(8,128)(2,1)} %get-tuple-element.230) | copy-start | bytes 3538948
  563.3 9.0 %copy-start.14 = (bf16[4,192,768]{2,1,0:T(8,128)(2,1)S(1)}, bf16[4,192,768]{2,1,0:T(8,128)(2,1)}, u32[]{:S(2)}) copy-start(bf16[4,192,768]{2,1,0:T(8,128)(2,1)} %copy-done.13) | copy-start | bytes 3538948
  570.2 5.0 collective-permute-start.6
  572.3 2.9 copy-start.23
  572.6 4.0 copy-start.10
  573.4 32.6 %collective-permute-start.19 = (bf16[2,192,768]{2,1,0:T(8,128)(2,1)}, bf16[2,192,768]{2,1,0:T(8,128)(2,1)}, u32[]{:S(2)}, u32[]{:S(2)}) collective-permute-start(bf16[2,192,768]{2,1,0:T(8,128)(2,1)} %fusion.10), channel_id=1, source_target_pairs={{0,8},{4,12},{8,0},{12,4},{16,24},{20,28},{24,16},{28,20},{1,9},{5... | collective-permute-start | bytes 1769480 | tf_op jit(solution)/shard_map/ppermute | solution.py:35
  575.2 15.2 %collective-permute-start.7 = (f32[2,16,768]{2,1,0:T(8,128)S(1)}, f32[2,16,768]{2,1,0:T(8,128)S(1)}, u32[]{:S(2)}, u32[]{:S(2)}) collective-permute-start(f32[2,16,768]{2,1,0:T(8,128)S(1)} %add.180), channel_id=1, source_target_pairs={{0,8},{4,12},{8,0},{12,4},{16,24},{20,28},{24,16},{28,20},{1,9},{5... | collective-permute-start | bytes 294920 | tf_op jit(solution)/shard_map/ppermute | solution.py:35
  575.5 1.0 copy-start.11
  590.5 6.5 collective-permute-start.8
  592.0 19.5 %collective-permute-start.10 = (bf16[2,192,768]{2,1,0:T(8,128)(2,1)}, bf16[2,192,768]{2,1,0:T(8,128)(2,1)}, u32[]{:S(2)}, u32[]{:S(2)}) collective-permute-start(bf16[2,192,768]{2,1,0:T(8,128)(2,1)} %fusion.6), channel_id=1, source_target_pairs={{0,8},{4,12},{8,0},{12,4},{16,24},{20,28},{24,16},{28,20},{1,9},{5... | collective-permute-start | bytes 1769480 | tf_op jit(solution)/shard_map/ppermute | solution.py:35
  603.3 3.9 copy-start.6
  609.0 27.8 %collective-permute-start.13 = (bf16[2,192,896]{2,1,0:T(8,128)(2,1)S(1)}, bf16[2,192,896]{2,1,0:T(8,128)(2,1)S(1)}, u32[]{:S(2)}, u32[]{:S(2)}) collective-permute-start(bf16[2,192,896]{2,1,0:T(8,128)(2,1)S(1)} %fusion.1), channel_id=1, source_target_pairs={{0,8},{4,12},{8,0},{12,4},{16,24},{20,28},{24,16},{28,20},{1,9},{5... | collective-permute-start | bytes 2064392 | tf_op jit(solution)/shard_map/ppermute | solution.py:35
  609.3 22.2 %collective-permute-start.20 = (bf16[1,192,768]{2,1,0:T(8,128)(2,1)S(1)}, bf16[1,192,768]{2,1,0:T(8,128)(2,1)S(1)}, u32[]{:S(2)}, u32[]{:S(2)}) collective-permute-start(bf16[1,192,768]{2,1,0:T(8,128)(2,1)S(1)} %dynamic-slice_convert_fusion.6), channel_id=1, source_target_pairs={{0,16},{4,20},{8,24},{12,28},{16,0},{20,4},{24,8},{28,12},{1,17},{... | collective-permute-start | bytes 884744 | tf_op jit(solution)/shard_map/ppermute | solution.py:35
  612.7 25.5 %collective-permute-start.11 = (bf16[1,192,768]{2,1,0:T(8,128)(2,1)S(1)}, bf16[1,192,768]{2,1,0:T(8,128)(2,1)S(1)}, u32[]{:S(2)}, u32[]{:S(2)}) collective-permute-start(bf16[1,192,768]{2,1,0:T(8,128)(2,1)S(1)} %dynamic-slice_convert_fusion.10), channel_id=1, source_target_pairs={{0,16},{4,20},{8,24},{12,28},{16,0},{20,4},{24,8},{28,12},{1,17},{... | collective-permute-start | bytes 884744 | tf_op jit(solution)/shard_map/ppermute | solution.py:35
  631.5 5.6 copy-start.3
  637.0 16.3 %collective-permute-start.14 = (bf16[1,192,896]{2,1,0:T(8,128)(2,1)S(1)}, bf16[1,192,896]{2,1,0:T(8,128)(2,1)S(1)}, u32[]{:S(2)}, u32[]{:S(2)}) collective-permute-start(bf16[1,192,896]{2,1,0:T(8,128)(2,1)S(1)} %dynamic-slice_convert_fusion.2), channel_id=1, source_target_pairs={{0,16},{4,20},{8,24},{12,28},{16,0},{20,4},{24,8},{28,12},{1,17},{... | collective-permute-start | bytes 1032200 | tf_op jit(solution)/shard_map/ppermute | solution.py:35
  638.3 15.2 %copy-start.18 = (f32[1,192,128]{2,1,0:T(8,128)S(1)}, f32[1,192,128]{2,1,0:T(8,128)}, u32[]{:S(2)}) copy-start(f32[1,192,128]{2,1,0:T(8,128)} %slice_bitcast_fusion.2) | copy-start | bytes 294916
  654.0 4.7 copy-start.5

commit v3 on v2

--- a/solution.py
+++ b/solution.py
@@ -9,6 +9,7 @@
 
 CONV = 4
 LAYERS = 2
+Z_ORDER = (1, 2, 0)
 EPS = 1e-05
 F32 = jnp.float32
 BF16 = jnp.bfloat16
@@ -178,9 +179,9 @@
     return jnp.sum(jnp.where(lanes == h, values, 0.0), axis=1, keepdims=True)
 
 
-def fwd_mix_body(heads, size, nx, wzx, wbc, wdt, tapx, tapbc, dtb, lograte, skip, aux, segrow,
-                 gate, ux, ubc, krs, pdt, steps_o, cum_o, cT, gram, mixed_o, ypart, entry_o, state, dec, decl,
-                 us, usbc, cb):
+def fwd_mix_body(size, nx, wzx, wbc, wdt, tapx, tapbc, dtb, lograte, aux, segrow,
+                 gate, ux, ubc, krs, pdt, steps_o, cum_o, cT, gram, mixed_o, entry_o, state, dec, decl,
+                 us, usbc):
     p = pl.program_id(0)
     tokens = aux.shape[1]
     states = wbc.shape[1] // 2
@@ -225,12 +226,30 @@
     h0 = p * (LANE // size)
     dd = jnp.where(half, pick_lane(st, h0, lanes), pick_lane(st, h0 + 1, lanes))
     vd = v * dd
-    vh, vl = halves(vd)
+    ct = jnp.where(half, pick_lane(cum, h0, lanes), pick_lane(cum, h0 + 1, lanes))
+    entry_o[...] = jnp.exp(ct) * aux[3]
+    tail = jnp.exp(ct[tokens - 1 : tokens, :] - ct) * aux[4]
+    state[...] = dot3(vd * tail, krs[:, :states], TN)
+
+
+def fwd_inside_body(stages_of, size, mixed, steps, cum, cT, gram, skip, state, dec, ypart, enter, cb, *rest):
+    p = pl.program_id(0)
+    tokens = mixed.shape[0]
+    stages = stages_of(state, dec, enter, *rest)
+    for k, stage in enumerate(stages[:-1]):
+        pl.when(p == k)(stage)
+    lanes = lax.broadcasted_iota(jnp.int32, (tokens, LANE), 1)
+    half = lanes < size
+    h0 = p * (LANE // size)
+    m = mixed[...]
+    v = m * sig(m)
+    st = steps[...]
+    vh, vl = halves(v * jnp.where(half, pick_lane(st, h0, lanes), pick_lane(st, h0 + 1, lanes)))
     vhl = jnp.concatenate([vh, vl], axis=1)
     ys = []
     for k in range(LANE // size):
         h = h0 + k
-        cb[k] = jnp.broadcast_to(pick_lane(cum, h, lanes), (tokens, LANE))
+        cb[k] = jnp.broadcast_to(pick_lane(cum[...], h, lanes), (tokens, LANE))
         row = cT[pl.ds(h, 1), :]
         parts = []
         for ib in range(tokens // LANE):
@@ -247,12 +266,8 @@
             both = bdot(joined(tiles), vhl[: (ib + 1) * LANE], NN)
             parts.append(both[:, :LANE] + (both[:, LANE:] + bdot(joined(lows), vh[: (ib + 1) * LANE], NN)))
         ys.append(jnp.concatenate(parts, axis=0))
-    y = jnp.where(half, ys[0], ys[1])
-    ypart[...] = y + skip[...] * v
-    ct = jnp.where(half, cb[0], cb[1])
-    entry_o[...] = jnp.exp(ct) * aux[3]
-    tail = jnp.exp(ct[tokens - 1 : tokens, :] - ct) * aux[4]
-    state[...] = dot3(vd * tail, krs[:, :states], TN)
+    ypart[...] = jnp.where(half, ys[0], ys[1]) + skip[...] * v
+    pl.when(p == pl.num_programs(0) - 1)(stages[-1])
 
 
 def full(shape):
@@ -313,9 +328,12 @@
     qloc[...] = bdot(gy * entry[...], krs[:, states:], TN)
 
 
-def bwd_local_body(size, gy_r, mixed, krs, cum, steps, cT, gram, entry, enter, segc, segrow,
-                   dvd, dd_o, rowT, dkr, cb, db, gramT, dgT, vb, gk):
+def bwd_local_body(stages_of, size, gy_r, mixed, krs, cum, steps, cT, gram, entry, enter, segc, segrow, qloc, dec,
+                   dvd, dd_o, rowT, dkr, later, cb, db, gramT, dgT, vb, gk, *rest):
     p = pl.program_id(0)
+    stages = stages_of(qloc, dec, later, *rest)
+    for k, stage in enumerate(stages[:-1]):
+        pl.when(p == k)(stage)
     tokens = gy_r.shape[0]
     states = krs.shape[1] // 2
     lanes = lax.broadcasted_iota(jnp.int32, (tokens, LANE), 1)
@@ -382,6 +400,7 @@
         g = jnp.where((ii >= jj) & (segs == segrow[...]), dgT[...], 0.0)
         dkr[:, :states] += bdot(g, krs[:, states:], NN)
         dkr[:, states:] += bdot(g, krs[:, :states], TN)
+        stages[-1]()
 
 
 def bwd_carry_body(size, gy_r, dvd_r, mixed, carr, entry, krs, cum, steps, pdt, dtb, lograte, skip, ux, tapx, aux, later, enter,
@@ -481,40 +500,110 @@
     return me + bit * (1 - 2 * ((me // bit) % 2))
 
 
-def carry_body(bits, reverse, heads, size, st, dec, out, tx, rx, dtx, drx, tot, ssem, rsem):
+def carry_stages(bits, reverse, heads, size, st, dec, out, tx, rx, rxd, tot, zp, btx, brx, bdtx, bdrx, pd, ed, ptx, prx, ssem, rsem):
     me = lax.axis_index("seq")
-    wheres = [{"seq": flip(me, b)} for b in bits]
-    greet(wheres)
-    enter_d = jnp.ones_like(dec[...])
-    total_d = dec[...]
-    for i, b in enumerate(bits):
-        src = st if i == 0 else tot
-        if reverse:
-            tx[...] = src[...].astype(BF16)
-        dtx[...] = total_d
-        one = send(tx if reverse else src, rx.at[i], (ssem.at[2 * i], rsem.at[2 * i]), wheres[i])
-        two = send(dtx, drx.at[i], (ssem.at[2 * i + 1], rsem.at[2 * i + 1]), wheres[i])
-        bit = (me // b) % 2
+    n = len(bits)
+    hh = heads // 2
+    rows = hh * size
+    x = me % 2
+    r = (1 - x) if reverse else x
+    pair_at = {"seq": flip(me, bits[0])}
+    wheres = [{"seq": flip(me, b)} for b in bits[1:]]
+    kind = tx.dtype
+    mine = pl.ds(pl.multiple_of(r * rows, rows), rows)
+    theirs = pl.ds(pl.multiple_of((1 - r) * rows, rows), rows)
+
+    def copy(k, src, dst, where):
+        return pltpu.make_async_remote_copy(src_ref=src, dst_ref=dst, send_sem=ssem.at[k], recv_sem=rsem.at[k],
+                                            device_id=where, device_id_type=MESH)
+
+    one = [copy(0, tx, rx, pair_at), copy(1, dec, rxd, pair_at)]
+    steps = [[copy(2 + 2 * i, btx, brx.at[i], w), copy(3 + 2 * i, bdtx, bdrx.at[i], w)] for i, w in enumerate(wheres)]
+    last = [copy(2 * n, ptx, prx, pair_at)]
+
+    def begin(copies):
+        for c in copies:
+            c.start()
+
+    def end(copies):
+        for c in copies:
+            c.wait()
+
+    def per_head(fn):
+        for k in range(hh):
+            fn(pl.ds(k * size, size), r * hh + k, pl.ds(pl.multiple_of(r * rows + k * size, size), size))
+
+    def open_():
+        greet([pair_at] + wheres)
+        tx[...] = st[theirs, :].astype(kind)
+        begin(one)
+
+    def pair():
+        end(one)
+        pd[...] = dec[...] * rxd[...]
+        ed[...] = jnp.ones_like(ed)
+        zp[...] = jnp.zeros_like(zp)
+
+        def add(rk, h, own):
+            a, b = st[own, :], rx[rk, :].astype(F32)
+            row = pl.ds(h, 1)
+            tot[rk, :] = jnp.where(r == 0, rxd[row, :] * a + b, dec[row, :] * b + a)
+
+        per_head(add)
+        go(0)
+
+    def go(i):
+        btx[...] = tot[...].astype(kind)
+        bdtx[...] = pd[...]
+        begin(steps[i])
+
+    def butterfly(i):
+        end(steps[i])
+        bit = (me // bits[1 + i]) % 2
         second = (1 - bit) if reverse else bit
-        two.wait()
-        other_d = drx[i]
-        one.wait()
         keep = second.astype(F32)
-        for h in range(heads):
-            rows = pl.ds(h * size, size)
-            other = rx[i, rows, :].astype(F32)
-            add = other * (enter_d[h : h + 1] * keep)
-            if i == 0:
-                out[rows, :] = add
-            else:
-                out[rows, :] += add
-            if i + 1 < len(bits):
-                mine = src[rows, :]
-                a = jnp.where(second == 1, total_d[h : h + 1], 1.0)
-                c = jnp.where(second == 1, 1.0, other_d[h : h + 1])
-                tot[rows, :] = a * other + c * mine
-        enter_d = jnp.where(second == 1, enter_d * other_d, enter_d)
-        total_d = total_d * other_d
+
+        def add(rk, h, own):
+            other = brx[i, rk, :].astype(F32)
+            row = pl.ds(h, 1)
+            zp[rk, :] += other * (ed[row, :] * keep)
+            if i + 1 < len(steps):
+                a = jnp.where(second == 1, pd[row, :], 1.0)
+                c = jnp.where(second == 1, 1.0, bdrx[i, row, :])
+                tot[rk, :] = a * other + c * tot[rk, :]
+
+        per_head(add)
+        ed[...] = jnp.where(second == 1, ed[...] * bdrx[i], ed[...])
+        pd[...] = pd[...] * bdrx[i]
+        if i + 1 < len(steps):
+            go(i + 1)
+        else:
+            hand()
+
+    def hand():
+        def add(rk, h, own):
+            row = pl.ds(h, 1)
+            z = zp[rk, :]
+            after = jnp.where(r == 0, dec[row, :], rxd[row, :]) * z + jnp.where(r == 0, st[own, :], rx[rk, :].astype(F32))
+            out[own, :] = jnp.where(r == 0, z, after)
+            ptx[rk, :] = jnp.where(r == 0, after, z).astype(kind)
+
+        per_head(add)
+        begin(last)
+
+    def close():
+        end(last)
+        out[theirs, :] = prx[...].astype(F32)
+
+    return [open_, pair] + [partial(butterfly, i) for i in range(len(steps))] + [close]
+
+
+def carry_scratch(n, rows, states, kind):
+    part = pltpu.VMEM((rows // 2, states), kind)
+    wide = pltpu.VMEM((rows // 2, states), F32)
+    dec = pltpu.VMEM((16, states), F32)
+    return [part, part, dec, wide, wide, part, pltpu.VMEM((n - 1, rows // 2, states), kind), dec, pltpu.VMEM((n - 1, 16, states), F32),
+            dec, dec, part, part, pltpu.SemaphoreType.DMA((2 * n + 1,)), pltpu.SemaphoreType.DMA((2 * n + 1,))]
 
 
 def head_core(tokens, part, middle, nx, off, side, tx0, rx0, tx1, rx1, acc, ssem, rsem, me, core_at, y_at):
@@ -789,14 +878,57 @@
         ahead_b.wait_send()
 
 
-def pack_body(parts, *refs):
-    ins = refs[: 6 * parts]
-    stage, rx, ssem, rsem = refs[6 * parts :]
+class Job:
+    def __init__(self, got, keep, left, steps, out, bufs, sems):
+        self.got, self.keep, self.left, self.steps, self.out = got, keep, list(left), list(steps), out
+        self.bufs, (self.ssem, self.rsem) = bufs, sems
+        self.copy = None
+
+    def advance(self):
+        got, keep = self.got, self.keep
+        if self.copy is not None:
+            self.copy.wait()
+        if not self.steps:
+            if self.out is not None:
+                self.out[...] = keep[0].astype(F32) + got[0].astype(F32)
+            return
+        bit = self.steps.pop(0)
+        away, kept, came = self.bufs.pop(0)
+        stride = 1 << (len(self.left) - 1 - self.left.index(bit))
+        self.left.remove(bit)
+        me = (lax.axis_index("seq") // bit) % 2
+        for dst, want in ((away, 1 - me), (kept, me)):
+            for k in range(dst.shape[0]):
+                at = (k // stride) * 2 * stride + want * stride + k % stride
+                dst[k] = (keep[at].astype(F32) + got[at].astype(F32)).astype(dst.dtype)
+        where = {"seq": flip(lax.axis_index("seq"), bit)}
+        k = len(self.steps)
+        self.copy = send(away, came, (self.ssem.at[k], self.rsem.at[k]), where)
+        self.got, self.keep = came, kept
+
+
+def tail_body(parts, plan, *refs):
+    jobs_n = len(plan)
+    pairs = refs[: 2 * jobs_n]
+    ins = refs[2 * jobs_n : 2 * jobs_n + 6 * parts]
+    rest = refs[2 * jobs_n + 6 * parts :]
+    outs, rest = rest[:jobs_n], rest[jobs_n:]
+    conv_x, conv_bc, ggate, gskip, gvec, ggain = rest[:6]
+    stage, rx, hx, ssem, rsem = rest[6:11]
+    rest = list(rest[11:])
+    jobs = []
+    for i, (left, steps) in enumerate(plan):
+        bufs = []
+        for _ in steps:
+            bufs.append((rest.pop(0), rest.pop(0), rest.pop(0)))
+        jobs.append(Job(pairs[2 * i], pairs[2 * i + 1], left, steps, outs[i], bufs, (rest.pop(0), rest.pop(0))))
     inner = stage.shape[2]
     me = lax.axis_index("head")
-    bits = bits_of("head")
-    wheres = [{"head": flip(me, b)} for b in bits]
+    steps = [("head", b) for b in bits_of("head")] + [("seq", b) for b in bits_of("seq")]
+    wheres = [{axis: flip(lax.axis_index(axis), b)} for axis, b in steps]
     greet(wheres)
+    for job in jobs:
+        job.advance()
     stage[...] = jnp.zeros_like(stage)
     for l in range(parts):
         taps, gate, skip, vec, maps, gain = ins[6 * l : 6 * l + 6]
@@ -812,14 +944,28 @@
             here = [jnp.where(me // 2 == k, row, 0.0) for k in range(2)]
             stage[l, 10 + r // 3 : 11 + r // 3, (r % 3) * 2 * LANE : ((r % 3) * 2 + 2) * LANE] = jnp.concatenate(here, axis=1)
     where = pl.ds(8, 8)
-    for i in range(len(bits)):
-        copy = send(stage.at[:, where, :], rx.at[i], (ssem.at[i], rsem.at[i]), wheres[i])
-        copy.wait()
-        stage[:, 8:16, :] += rx[i]
-
-
-def unpack_body(parts, stage, conv_x, conv_bc, ggate, gskip, gvec, ggain):
-    inner = stage.shape[2]
+    heads = len(bits_of("head"))
+    longest = max(len(job.steps) for job in jobs)
+    for i, (axis, b) in enumerate(steps):
+        if axis == "head":
+            copy = send(stage.at[:, where, :], hx.at[i], (ssem.at[i], rsem.at[i]), wheres[i])
+            copy.wait()
+            stage[:, 8:16, :] += hx[i]
+        else:
+            copy = send(stage, rx.at[i - heads], (ssem.at[i], rsem.at[i]), wheres[i])
+            if i == heads:
+                for job in jobs:
+                    if len(job.steps) == longest:
+                        job.advance()
+            copy.wait()
+            stage[...] += rx[i - heads]
+    for _ in range(longest + 1):
+        for job in jobs:
+            if job.copy is not None and (job.steps or job.out is not None):
+                done = not job.steps
+                job.advance()
+                if done:
+                    job.out = None
     for l in range(parts):
         conv_x[l] = stage[l, 0 : CONV + 1, :]
         ggate[l : l + 1, :] = stage[l, 5:6, :]
@@ -862,27 +1008,44 @@
     )(*args, *after)
 
 
-def fwd_mix(l, heads, size, nx, q, aux, segrow):
+def fwd_mix(l, size, nx, q, aux, segrow):
     tokens = aux.shape[1]
     ext, d = nx.shape
     inner = q["conv_x"].shape[2]
     two = q["w_bc"].shape[2]
-    args = [nx, q["w_zx"], q["w_bc"], q["w_dt"], q["conv_x"], q["conv_bc"], q["dt_bias"], q["a_log"], q["skip"], aux, segrow]
+    args = [nx, q["w_zx"], q["w_bc"], q["w_dt"], q["conv_x"], q["conv_bc"], q["dt_bias"], q["a_log"], aux, segrow]
     specs = [full(nx.shape), of_layer(l, q["w_zx"].shape, True), of_layer(l, q["w_bc"].shape), of_layer(l, q["w_dt"].shape),
              of_layer(l, q["conv_x"].shape, True), of_layer(l, q["conv_bc"].shape), of_layer(l, q["dt_bias"].shape),
-             of_layer(l, q["a_log"].shape), of_layer(l, q["skip"].shape, True), full(aux.shape), full(segrow.shape)]
+             of_layer(l, q["a_log"].shape), full(aux.shape), full(segrow.shape)]
     return kcall(
-        partial(fwd_mix_body, heads, size), args, specs, 16,
+        partial(fwd_mix_body, size), args, specs, 12,
         name="fwd_mix",
         grid=(inner // LANE,),
         out_specs=[cols(tokens), cols(ext), full((ext, two)), full((tokens, two)), full((tokens, LANE)), full((tokens, LANE)),
-                   full((tokens, LANE)), full((LANE, tokens)), full((tokens, tokens)), cols(tokens), cols(tokens),
+                   full((tokens, LANE)), full((LANE, tokens)), full((tokens, tokens)), cols(tokens),
                    cols(tokens), rowsb(two // 2), full((16, LANE)), full((8, LANE))],
         out_shape=[S((tokens, inner), BF16), S((ext, inner), BF16), S((ext, two), BF16), S((tokens, two), F32),
                    S((tokens, LANE), BF16), S((tokens, LANE), F32), S((tokens, LANE), F32), S((LANE, tokens), F32),
-                   S((tokens, tokens), F32), S((tokens, inner), F32), S((tokens, inner), F32), S((tokens, inner), F32),
+                   S((tokens, tokens), F32), S((tokens, inner), F32), S((tokens, inner), F32),
                    S((inner, two // 2), F32), S((16, LANE), F32), S((8, LANE), F32)],
-        scratch_shapes=[pltpu.VMEM((ext, LANE), F32), pltpu.VMEM((ext, two), F32), pltpu.VMEM((2, tokens, LANE), F32)],
+        scratch_shapes=[pltpu.VMEM((ext, LANE), F32), pltpu.VMEM((ext, two), F32)],
+    )
+
+
+def fwd_inside(l, heads, size, mixed, steps, cum, cT, gram, q, state, dec, cid):
+    tokens, inner = mixed.shape
+    rows, states = state.shape
+    bits = bits_of("seq")
+    return kcall(
+        partial(fwd_inside_body, partial(carry_stages, bits, False, heads, size), size),
+        [mixed, steps, cum, cT, gram, q["skip"], state, dec],
+        [cols(tokens), full(steps.shape), full(cum.shape), full(cT.shape), full(gram.shape), of_layer(l, q["skip"].shape, True),
+         full(state.shape), full(dec.shape)], 28, (), cid,
+        name="fwd_inside",
+        grid=(inner // LANE,),
+        out_specs=[cols(tokens), full((rows, states))],
+        out_shape=[S((tokens, inner), F32), S((rows, states), F32)],
+        scratch_shapes=[pltpu.VMEM((2, tokens, LANE), F32)] + carry_scratch(len(bits), rows, states, F32),
     )
 
 
@@ -914,23 +1077,28 @@
     )
 
 
-def bwd_local(size, gy, mixed, krs, cum, steps, cT, gram, entry, enter, aux, segrow, after):
+def bwd_local(heads, size, gy, mixed, krs, cum, steps, cT, gram, entry, enter, aux, segrow, qloc, dec, cid, after):
     tokens, inner = gy.shape
     two = krs.shape[1]
+    rows, states = qloc.shape
+    bits = bits_of("seq")
     return kcall(
-        partial(bwd_local_body, size), [gy, mixed, krs, cum, steps, cT, gram, entry, enter, aux, segrow],
+        partial(bwd_local_body, partial(carry_stages, bits, True, heads, size), size),
+        [gy, mixed, krs, cum, steps, cT, gram, entry, enter, aux, segrow, qloc, dec],
         [cols(tokens), cols(tokens), full(krs.shape), full(cum.shape), full(steps.shape), full(cT.shape), full(gram.shape),
-         cols(tokens), rowsb(two // 2), pl.BlockSpec((None, tokens, LANE), lambda p: (5, 0, 0)), full(segrow.shape)], 10, after,
+         cols(tokens), rowsb(two // 2), pl.BlockSpec((None, tokens, LANE), lambda p: (5, 0, 0)), full(segrow.shape),
+         full(qloc.shape), full(dec.shape)], 20, after, cid,
         name="bwd_local",
         grid=(inner // LANE,),
-        out_specs=[cols(tokens), full((tokens, LANE)), full((LANE, tokens)), full((tokens, two))],
-        out_shape=[S((tokens, inner), F32), S((tokens, LANE), F32), S((LANE, tokens), F32), S((tokens, two), F32)],
+        out_specs=[cols(tokens), full((tokens, LANE)), full((LANE, tokens)), full((tokens, two)), full((rows, states))],
+        out_shape=[S((tokens, inner), F32), S((tokens, LANE), F32), S((LANE, tokens), F32), S((tokens, two), F32), S((rows, states), F32)],
         scratch_shapes=[pltpu.VMEM((tokens, LANE), F32), pltpu.VMEM((tokens, LANE), F32), pltpu.VMEM((tokens, tokens), F32),
-                        pltpu.VMEM((tokens, tokens), F32), pltpu.VMEM((tokens, LANE), BF16), pltpu.VMEM((tokens, LANE), BF16)],
+                        pltpu.VMEM((tokens, tokens), F32), pltpu.VMEM((tokens, LANE), BF16), pltpu.VMEM((tokens, LANE), BF16)]
+        + carry_scratch(len(bits), rows, states, BF16),
     )
 
 
-def bwd_carry(l, size, gy, dvd, mixed, carr, entry, krs, cum, steps, pdt, q, ux, aux, later, enter, dd, rowT, dkr, decl):
+def bwd_carry(l, size, gy, dvd, mixed, carr, entry, krs, cum, steps, pdt, q, ux, aux, later, enter, dd, rowT, dkr, decl, after):
     tokens, inner = gy.shape
     ext = ux.shape[0]
     two = krs.shape[1]
@@ -941,7 +1109,7 @@
         [cols(tokens), cols(tokens), cols(tokens), cols(tokens), cols(tokens), full(krs.shape), full(cum.shape), full(steps.shape),
          full(pdt.shape), of_layer(l, q["dt_bias"].shape), of_layer(l, q["a_log"].shape), of_layer(l, q["skip"].shape, True), cols(ext),
          of_layer(l, q["conv_x"].shape, True), full(aux.shape), rowsb(two // 2), rowsb(two // 2), full(dd.shape), full(rowT.shape),
-         full(dkr.shape), full(decl.shape)], 11,
+         full(dkr.shape), full(decl.shape)], 11, after,
         name="bwd_carry",
         grid=(inner // LANE,),
         out_specs=[cols(8), cols(tokens), cols(16), cols(8), full((tokens, LANE)), full((8, LANE)), full((tokens, two))],
@@ -949,21 +1117,6 @@
                    S((8, LANE), F32), S((tokens, two), F32)],
         scratch_shapes=[pltpu.VMEM((ext, LANE), F32), pltpu.VMEM((tokens + 8, LANE), F32), pltpu.VMEM((tokens, LANE), F32),
                         pltpu.VMEM((tokens, LANE), F32), pltpu.VMEM((1, LANE), F32)],
-    )
-
-
-def carry_kernel(state, dec, heads, size, reverse, cid, after=()):
-    bits = bits_of("seq")
-    rows, states = state.shape
-    n = len(bits)
-    return kcall(
-        partial(carry_body, bits, reverse, heads, size), [state, dec], [VM] * 2, 25, after, cid,
-        name="carry_back" if reverse else "carry_on",
-        out_specs=VM,
-        out_shape=S((rows, states), F32),
-        scratch_shapes=[pltpu.VMEM((rows, states), BF16), pltpu.VMEM((n, rows, states), BF16 if reverse else F32), pltpu.VMEM(dec.shape, F32),
-                        pltpu.VMEM((n,) + dec.shape, F32), pltpu.VMEM((rows, states), F32),
-                        pltpu.SemaphoreType.DMA((2 * n,)), pltpu.SemaphoreType.DMA((2 * n,))],
     )
 
 
@@ -1011,26 +1164,28 @@
     )
 
 
-def pack_small(smalls, inner, cid):
+def tail(sums, smalls, inner, d, cid):
     parts = len(smalls)
-    n = len(bits_of("head"))
+    plan = [(left, steps) for _, _, left, steps in sums]
+    heads, n = len(bits_of("head")), len(bits_of("seq"))
+    arrays, scratch, outs = [], [], []
+    for got, keep, left, steps in sums:
+        arrays += [got, keep]
+        blocks, block, width = keep.shape
+        outs.append(S((block, width), F32))
+        for _ in steps:
+            blocks //= 2
+            buf = pltpu.VMEM((blocks, block, width), BF16)
+            scratch += [buf, pltpu.VMEM((blocks, block, width), F32), buf]
+        scratch += [pltpu.SemaphoreType.DMA((max(len(steps), 1),))] * 2
     return kcall(
-        partial(pack_body, parts), [x for part in smalls for x in part], [VM] * (6 * parts), 8, (), cid,
-        name="pack_small",
-        out_specs=VM,
-        out_shape=S((parts, 16, inner), F32),
-        scratch_shapes=[pltpu.VMEM((n, parts, 8, inner), F32), pltpu.SemaphoreType.DMA((n,)), pltpu.SemaphoreType.DMA((n,))],
-    )
-
-
-def unpack_small(stage, d):
-    parts, _, inner = stage.shape
-    return kcall(
-        partial(unpack_body, parts), [stage], [VM], 2,
-        name="unpack_small",
-        out_specs=[VM] * 6,
-        out_shape=[S((parts, CONV + 1, inner), F32), S((parts, CONV + 1, 2 * LANE), F32), S((parts, inner), F32), S((parts, inner), F32),
-                   S((parts, 2 * LANE), F32), S((parts, d), F32)],
+        partial(tail_body, parts, plan), arrays + [x for part in smalls for x in part], [VM] * (2 * len(sums) + 6 * parts), 45, (), cid,
+        name="tail",
+        out_specs=[VM] * (len(sums) + 6),
+        out_shape=outs + [S((parts, CONV + 1, inner), F32), S((parts, CONV + 1, 2 * LANE), F32), S((parts, inner), F32), S((parts, inner), F32),
+                          S((parts, 2 * LANE), F32), S((parts, d), F32)],
+        scratch_shapes=[pltpu.VMEM((parts, 16, inner), F32), pltpu.VMEM((n, parts, 16, inner), F32), pltpu.VMEM((heads, parts, 8, inner), F32),
+                        pltpu.SemaphoreType.DMA((heads + n,)), pltpu.SemaphoreType.DMA((heads + n,))] + scratch,
     )
 
 
@@ -1085,6 +1240,10 @@
         self.step += 1
         return self.got
 
+    def rest(self):
+        shape = (-1,) + self.keep.shape[-2:]
+        return self.got.reshape(shape), self.keep.reshape(shape), tuple(self.left), tuple(self.order[self.step :])
+
     def fold(self):
         total = self.keep.astype(F32) + self.got.astype(F32)
         if self.step == len(self.order):
@@ -1111,8 +1270,8 @@
 
 def forward_layer(nx, h_own, extra, q, aux, segrow, layer):
     heads, size, inner = q["heads"], q["size"], q["inner"]
-    (gate, ux, ubc, krs, pdt, steps, cum, cT, gram, mixed, ypart, entry, state, dec, decl) = fwd_mix(layer, heads, size, nx, q, aux, segrow)
-    enter = carry_kernel(state, dec, heads, size, False, layer)
+    (gate, ux, ubc, krs, pdt, steps, cum, cT, gram, mixed, entry, state, dec, decl) = fwd_mix(layer, size, nx, q, aux, segrow)
+    ypart, enter = fwd_inside(layer, heads, size, mixed, steps, cum, cT, gram, q, state, dec, layer)
     y, carr, gated, sq = fwd_gate(ypart, entry, gate, krs, enter)
     width = inner * lax.axis_size("head")
     nx_next, h_new, branch, r2b, side = head_fwd(layer, gated, sq, q, h_own, extra, layer == LAYERS - 1, width, LAYERS + layer)
@@ -1128,13 +1287,6 @@
     r2b = s["r2b"]
     krb = r2b * r2b * (kr[:, None] / width)
     return bwd_gate(layer, gb, q, s["gate"], s["y"], s["mixed"], s["entry"], s["krs"], r2b, krb)
-
-
-def backward_mix(gy, later, s, q, aux, segrow, layer, after_local):
-    size = q["size"]
-    dvd, dd, rowT, dkr = bwd_local(size, gy, s["mixed"], s["krs"], s["cum"], s["steps"], s["cT"], s["gram"], s["entry"], s["enter"], aux, segrow, after_local)
-    return bwd_carry(layer, size, gy, dvd, s["mixed"], s["carr"], s["entry"], s["krs"], s["cum"], s["steps"], s["pdt"], q,
-                     s["ux"], aux, later, s["enter"], dd, rowT, dkr, s["decl"])
 
 
 def local(hidden_in, seg, cot, norm_gain, w_zx, w_bc, w_dt, conv_x, conv_bc, dt_bias, a_log, skip_d, gate_gain, w_out):
@@ -1177,42 +1329,42 @@
     for l in reversed(range(LAYERS)):
         s = stored[l]
         gy, gz, scaled, qloc, ggate, gskip = backward_gate(gb, side, s, q, l)
-        later = carry_kernel(qloc, s["dec"], heads, size, True, 2 * LAYERS + l, after=[p.got for p in pending])
-        if pending:
-            for p in pending:
-                p.fold()
-            out_up, z_up, x_up = pending
+        dvd, dd, rowT, dkr, later = bwd_local(heads, size, gy, s["mixed"], s["krs"], s["cum"], s["steps"], s["cT"], s["gram"], s["entry"], s["enter"],
+                                              aux, segrow, qloc, s["dec"], 2 * LAYERS + l, [p.got for p in pending])
+        for p in pending:
+            p.fold()
+            p.go()
         out = Halving(gb, [scaled], (0, 1, 2), after=[later])
-        z = Halving(s["nx"], [gz], (0, 1, 2), after=[later])
-        first = [out.go()]
-        gm8, gu, gtail, gtaps_x, gdt, gvec, dkr = backward_mix(gy, later, s, q, aux, segrow, l, ())
-        small, gtaps_bc, gtail = maps_bwd(l, dkr, s["ubc"], q, aux, gdt, gtail, gm8, 3 * LAYERS + l, after=first)
+        z = Halving(s["nx"], [gz], Z_ORDER, after=[later])
+        out.go()
+        z.go()
+        gm8, gu, gtail, gtaps_x, gdt, gvec, dkr = bwd_carry(
+            l, size, gy, dvd, s["mixed"], s["carr"], s["entry"], s["krs"], s["cum"], s["steps"], s["pdt"], q, s["ux"], aux, later, s["enter"],
+            dd, rowT, dkr, s["decl"], [out.away, z.away])
+        small, gtaps_bc, gtail = maps_bwd(l, dkr, s["ubc"], q, aux, gdt, gtail, gm8, 3 * LAYERS + l)
         gu = lax.dynamic_update_slice(gu, gtail, (tokens - 16, 0))
+        x = Halving(s["nx"], [gu, small], (0, 1, 2))
+        x.go()
         out.fold()
+        z.fold()
         z.go()
         out.go()
-        x = Halving(s["nx"], [gu, small], (0, 1, 2))
         before = stored[max(l - 1, 0)]["branch"]
-        gb, g_own, g_gain, side = head_bwd(l, gz, gu, small, q, s["h_own"], g_own, before, 4 * LAYERS + l, after=[x.away])
-        x.go()
+        gb, g_own, g_gain, side = head_bwd(l, gz, gu, small, q, s["h_own"], g_own, before, 4 * LAYERS + l, after=[x.away, out.away, z.away])
         smalls[l] = (gtaps_x, ggate, gskip, gvec, gtaps_bc, g_gain)
         pending = [out, z, x]
         sums[l] = pending
     grad_in = gb.astype(F32)
-    for l in range(LAYERS):
-        for p in sums[l]:
-            if l == 0:
-                p.fold()
-            p.finish()
+    under_way = [p for l in range(LAYERS) for p in reversed(sums[l])]
+    done = tail([p.rest() for p in under_way], smalls, inner, norm_gain.shape[1], 5 * LAYERS)
+    for p, total in zip(under_way, done):
+        p.total = total
+    g_conv_x, g_conv_bc, g_gate, g_skip, g_vec, g_gain = done[len(under_way) :]
     g_w_zx = jnp.stack([jnp.stack([z.total, x.total[:, :inner]], 1) for _, z, x in sums], 0)
     g_small = jnp.stack([x.total[:, inner:] for _, _, x in sums], 0)
     g_w_bc = jnp.where(even, g_small[:, :, : LANE // 2], g_small[:, :, LANE // 2 :])
     g_w_dt = jnp.where(even, g_small[:, :, LANE // 2 : LANE // 2 + heads], g_small[:, :, :heads])
     g_w_out = jnp.stack([jnp.transpose(out.total) for out, _, _ in sums], 0)
-    stage = pack_small(smalls, inner, 5 * LAYERS)
-    for bit in bits_of("seq"):
-        stage = stage + swap(stage, "seq", bit)
-    g_conv_x, g_conv_bc, g_gate, g_skip, g_vec, g_gain = unpack_small(stage, norm_gain.shape[1])
     g_skip = jnp.sum(g_skip.reshape(LAYERS, heads, size), axis=2)
     part = g_gain.shape[1] // lax.axis_size("seq")
     g_gain = lax.dynamic_slice_in_dim(g_gain, lax.axis_index("seq") * part, part, 1)

time: 671 us -> 566 us (0.84)
  waiting for transfers between devices: 81.7 us -> 0.27 us
  Pallas kernels: 480 us -> 469 us
  other arithmetic: 29 us -> 21.4 us
    ppermute x21 -> x13, waiting for transfers between devices: 81.7 us -> 0.26 us  [swap(): return lax.ppermute(x, axis, [(i, i ^ bit) for i in range(n)])]
    pallas_call x28 -> x25, Pallas kernels: 480 us -> 469 us  [kcall(): pl.pallas_call(wrapped, in_specs=list(specs) + [pl.BlockSpec(memory_space...]
    ppermute x21 -> x13, starting transfers between devices: 19.2 us -> 13.8 us  [swap(): return lax.ppermute(x, axis, [(i, i ^ bit) for i in range(n)])]
    unnamed x78 -> x107, local copies, waits for them, and re-layouts: 25.1 us -> 24 us
  transfers between devices with their start and end apart: 22 -> 14, of which waited for: 11 -> 1; matrix products, arithmetic and copies ran while one was open for 8% -> 7% of each run, Pallas kernels for 35% -> 32%
where the time goes in v3:
time: 566 us; the launch traced here: 556 us
  Pallas kernels  469 us (83%)
  local copies, waits for them, and re-layouts  45.2 us (8%)
  other arithmetic  21.4 us (4%)
  starting transfers between devices  18.7 us (3%)
    pallas_call x25, Pallas kernels, kcall(): pl.pallas_call(wrapped, in_specs=list(specs) + [pl.BlockSpec(memory_space...  469 us
    unnamed x107, local copies, waits for them, and re-layouts  24 us
    ppermute x13, starting transfers between devices, swap(): return lax.ppermute(x, axis, [(i, i ^ bit) for i in range(n)])  13.8 us
  transfers between devices with their start and end apart: 14, of which 1 were waited for; matrix products, arithmetic and copies ran while one was open for 7% of the time, Pallas kernels for 32%

profile of v3, /device:TPU:0, one launch (start us, length us, event | category | flops | bytes accessed | tf_op | source)
XLA Modules:
  0.0 556.0 jit_solution(839598286114829000)
XLA Ops:
  0.7 0.8 slice_reduce_fusion
  1.5 1.8 multiply_reduce_fusion
  3.8 1.1 copy-done.1
  4.9 5.0 collective-permute-start
  11.2 2.1 convert.11
  13.2 1.6 constant_dynamic-slice_fusion.2
  15.1 0.9 constant_dynamic-slice_fusion.1
  16.0 0.9 dynamic-slice_bitcast_fusion.refs_4_.refs_5_
  17.5 1.1 fusion.22
  18.6 1.7 select_select_fusion
  20.3 1.4 fusion.18
  22.3 8.7 %copy.82 = bf16[2,1536,2,768]{3,1,2,0:T(8,128)(2,1)} copy(bf16[2,1536,2,768]{3,2,1,0:T(2,128)(2,1)} %param.18) | data formatting | bytes 18874368 | tf_op args[4]
  34.8 1.3 pad_maximum_fusion.1.refs_0_
  36.1 1.6 broadcast_in_dim.35.refs_8_.refs_9_.refs_14_.refs_3_
  37.7 17.2 %fwd_mix.2 = (bf16[512,768]{1,0:T(8,128)(2,1)}, bf16[528,768]{1,0:T(8,128)(2,1)}, bf16[528,256]{1,0:T(8,128)(2,1)}, f32[512,256]{1,0:T(8,128)}, bf16[512,128]{1,...) custom-call(bf16[528,1536]{1,0:T(8,128)(2,1)} %pad_maximum_fusion.1., ...), custom_call_target="tpu_custom_call" | custom-call | flops 12000000000 | bytes 36000000 | tf_op jit(solution)/shard_map/fwd_mix/pallas_call | solution.py:1002
  54.8 29.6 %fwd_inside.2 = (f32[512,768]{1,0:T(8,128)}, f32[768,128]{1,0:T(8,128)}) custom-call(f32[512,768]{1,0:T(8,128)} %get-tuple-element.132.refs_0_.refs_4_.refs_1_.refs_2_, f32[512,128]{1,0:T(8,128)} %get-tuple-element.133.refs_1_.refs_4_.refs_7_, f32[512,128]{1,0:T(8,128)} %get-tuple-element.134.refs_2_.refs_3_.refs_6_, ...), custom_call_target="tpu_custom_call" | custom-call | flops 28000000000 | bytes 84000000 | tf_op jit(solution)/shard_map/fwd_inside/pallas_call | solution.py:1002
  84.5 7.2 %fwd_gate.2 = (f32[512,768]{1,0:T(8,128)}, f32[512,768]{1,0:T(8,128)}, f32[512,768]{1,0:T(8,128)}, f32[8,512]{1,0:T(8,128)}) custom-call(f32[512,768]{1,0:T(8,128)} %get-tuple-element.139.refs_0_, f32[512,768]{1,0:T(8,128)} %get-tuple-element.140.refs_1_.refs_5_.refs_7_.refs_4_, bf16[512,768]{1,0:T(8,128)(2,1)} %get-tuple-element.141.refs_2_, ...), custom_call_target="tpu_custom_call" | custom-call | flops 7000000000 | bytes 21000000 | tf_op jit(solution)/shard_map/fwd_gate/pallas_call | solution.py:1002
  91.6 41.4 %head_fwd.1 = (bf16[528,1536]{1,0:T(8,128)(2,1)}, f32[128,1536]{1,0:T(8,128)}, f32[128,1536]{1,0:T(8,128)}, f32[512,128]{1,0:T(8,128)}, f32[32,128]{1,0:T(8,128)}) custom-call(f32[512,768]{1,0:T(8,128)} %get-tuple-element.144.refs_0_, f32[8,512]{1,0:T(8,128)} %get-tuple-element.145.refs_1_, f32[2,1,768]{2,1,0:T(1,128)} %broadcast_in_dim.37.refs_2_.refs_9_, ...), custom_call_target="tpu_custom_call" | custom-call | flops 30000001024 | bytes 90000000 | tf_op jit(solution)/shard_map/head_fwd/pallas_call | solution.py:1002
  133.0 17.3 %fwd_mix.3 = (bf16[512,768]{1,0:T(8,128)(2,1)}, bf16[528,768]{1,0:T(8,128)(2,1)}, bf16[528,256]{1,0:T(8,128)(2,1)}, f32[512,256]{1,0:T(8,128)}, bf16[512,128]{1,...) custom-call(bf16[528,1536]{1,0:T(8,128)(2,1)} %get-tuple-element.146, ...), custom_call_target="tpu_custom_call" | custom-call | flops 12000000000 | bytes 36000000 | tf_op jit(solution)/shard_map/fwd_mix/pallas_call | solution.py:1002
  150.3 32.4 %fwd_inside.3 = (f32[512,768]{1,0:T(8,128)}, f32[768,128]{1,0:T(8,128)}) custom-call(f32[512,768]{1,0:T(8,128)} %get-tuple-element.147.refs_0_.refs_4_.refs_1_.refs_2_, f32[512,128]{1,0:T(8,128)} %get-tuple-element.148.refs_1_.refs_4_.refs_7_, f32[512,128]{1,0:T(8,128)} %get-tuple-element.149.refs_2_.refs_3_.refs_6_, ...), custom_call_target="tpu_custom_call" | custom-call | flops 28000000000 | bytes 84000000 | tf_op jit(solution)/shard_map/fwd_inside/pallas_call | solution.py:1002
  182.7 7.3 %fwd_gate.3 = (f32[512,768]{1,0:T(8,128)}, f32[512,768]{1,0:T(8,128)}, f32[512,768]{1,0:T(8,128)}, f32[8,512]{1,0:T(8,128)}) custom-call(f32[512,768]{1,0:T(8,128)} %get-tuple-element.154.refs_0_, f32[512,768]{1,0:T(8,128)} %get-tuple-element.155.refs_1_.refs_5_.refs_7_.refs_4_, bf16[512,768]{1,0:T(8,128)(2,1)} %get-tuple-element.156.refs_2_, ...), custom_call_target="tpu_custom_call" | custom-call | flops 7000000000 | bytes 21000000 | tf_op jit(solution)/shard_map/fwd_gate/pallas_call | solution.py:1002
  190.0 29.7 %head_fwd_last.1 = (bf16[512,1536]{1,0:T(8,128)(2,1)}, f32[128,1536]{1,0:T(8,128)}, f32[128,1536]{1,0:T(8,128)}, f32[512,128]{1,0:T(8,128)}, f32[32,128]{1,0:T(8,128)}) custom-call(f32[512,768]{1,0:T(8,128)} %get-tuple-element.159.refs_0_, f32[8,512]{1,0:T(8,128)} %get-tuple-element.160.refs_1_, f32[2,1,768]{2,1,0:T(1,128)} %broadcast_in_dim.37.refs_2_.refs_9_, ...), custom_call_target="tpu_custom_call" | custom-call | flops 30000001024 | bytes 90000000 | tf_op jit(solution)/shard_map/head_fwd_last/pallas_call | solution.py:1002
  220.4 1.8 multiply_multiply_fusion.1.refs_8_
  222.2 9.4 %bwd_gate.2 = (f32[512,768]{1,0:T(8,128)}, bf16[512,768]{1,0:T(8,128)(2,1)}, bf16[512,768]{1,0:T(8,128)(2,1)}, f32[768,128]{1,0:T(8,128)}, f32[1,768]{1,0:T(1,128)}, /*index=5*/f32[1,768]{1,0:T(1,128)}) custom-call(bf16[512,1536]{1,0:T(8,128)(2,1)} %refs_0_.3, bf16[2,768,1536]{2,1,0:T(8,128)(2,1)} %refs_1_.3, bf16[512,768]{1,0:T(8,128)(2,1)} %get-tuple-element.156.refs_2_, ...), custom_call_target="tpu_custom_call" | custom-call | flops 8999999488 | bytes 27000000 | tf_op jit(solution)/shard_map/bwd_gate/pallas_call | solution.py:1002
  231.6 22.8 %bwd_local.2 = (f32[512,768]{1,0:T(8,128)}, f32[512,128]{1,0:T(8,128)}, f32[128,512]{1,0:T(8,128)}, f32[512,256]{1,0:T(8,128)}, f32[768,128]{1,0:T(8,128)}) custom-call(f32[512,768]{1,0:T(8,128)} %get-tuple-element.167.refs_0_, f32[512,768]{1,0:T(8,128)} %get-tuple-element.147.refs_0_.refs_4_.refs_1_.refs_2_, ...), custom_call_target="tpu_custom_call" | custom-call | flops 20000000000 | bytes 60000000 | tf_op jit(solution)/shard_map/bwd_local/pallas_call | solution.py:1002
  254.4 5.3 wgrad.6
  259.8 15.7 %wgrad.7 = (bf16[4,192,768]{2,1,0:T(8,128)(2,1)}, bf16[4,192,768]{2,1,0:T(8,128)(2,1)}) custom-call(bf16[528,1536]{1,0:T(8,128)(2,1)} %get-tuple-element.146.refs_0_, bf16[512,768]{1,0:T(8,128)(2,1)} %get-tuple-element.166.refs_1_.refs_0_, f32[768,128]{1,0:T(8,128)} %get-tuple-element.173.refs_2_.refs_15_), custom_call_target="tpu_custom_call" | custom-call | flops 3000000000 | bytes 9000000 | tf_op jit(solution)/shard_map/wgrad/pallas_call | solution.py:1002
  276.3 12.0 %bwd_carry.2 = (f32[8,768]{1,0:T(8,128)}, bf16[512,768]{1,0:T(8,128)(2,1)}, f32[16,768]{1,0:T(8,128)}, f32[8,768]{1,0:T(8,128)}, bf16[512,128]{1,0:T(8,128)(2,1)}, /*index=5*/f32[8,128]{1,0:T(8,128)}, f32[512,256]{1,0:T(8,128)}) custom-call(f32[512,768]{1,0:T(8,128)} %get-tuple-element.167.refs_0_, f32[512,768]{1,0:T(8,128)} %get-tuple-element.169.refs_1_, ...), custom_call_target="tpu_custom_call" | custom-call | flops 11000000512 | bytes 33000000 | tf_op jit(solution)/shard_map/bwd_carry/pallas_call | solution.py:1002
  288.3 14.7 %maps_bwd.2 = (bf16[512,128]{1,0:T(8,128)(2,1)}, f32[8,128]{1,0:T(8,128)}, bf16[16,768]{1,0:T(8,128)(2,1)}) custom-call(f32[512,256]{1,0:T(8,128)} %get-tuple-element.182.refs_0_, bf16[528,256]{1,0:T(8,128)(2,1)} %get-tuple-element.183.refs_1_, f32[2,5,256]{2,1,0:T(8,128)} %copy.51.refs_5_.refs_2_, ...), custom_call_target="tpu_custom_call" | custom-call | flops 14000000000 | bytes 42000000 | tf_op jit(solution)/shard_map/maps_bwd/pallas_call | solution.py:1002
  303.0 1.3 constant_dynamic-update-slice_fusion.1.refs_1_
  304.3 5.9 %wgrad.8 = (bf16[4,192,896]{2,1,0:T(8,128)(2,1)}, bf16[4,192,896]{2,1,0:T(8,128)(2,1)}) custom-call(bf16[528,1536]{1,0:T(8,128)(2,1)} %get-tuple-element.146.refs_0_, bf16[512,768]{1,0:T(8,128)(2,1)} %constant_dynamic-update-slice_fusion.1.refs_1_, bf16[512,128]{1,0:T(8,128)(2,1)} %get-tuple-element.188.refs_2_), custom_call_target="tpu_custom_call" | custom-call | flops 3000000000 | bytes 9000000 | tf_op jit(solution)/shard_map/wgrad/pallas_call | solution.py:1002
  310.2 2.6 collective-permute-start.5
  313.2 1.1 collective-permute-start.3
  314.7 1.8 collective-permute-start.4
  316.5 28.5 %head_bwd.2 = (bf16[512,1536]{1,0:T(8,128)(2,1)}, f32[128,1536]{1,0:T(8,128)}, f32[1,1536]{1,0:T(1,128)}, f32[32,128]{1,0:T(8,128)}) custom-call(bf16[512,768]{1,0:T(8,128)(2,1)} %get-tuple-element.166.refs_1_.refs_0_, bf16[512,768]{1,0:T(8,128)(2,1)} %constant_dynamic-update-slice_fusion.1.refs_1_, bf16[512,128]{1,0:T(8,128)(2,1)} %get-tuple-element.188.refs_2_, ...), custom_call_target="tpu_custom_call" | custom-call | flops 28999999488 | bytes 87000000 | tf_op jit(solution)/shard_map/head_bwd/pallas_call | solution.py:1002
  345.7 0.9 multiply_multiply_fusion.refs_8_
  346.6 9.5 %bwd_gate.3 = (f32[512,768]{1,0:T(8,128)}, bf16[512,768]{1,0:T(8,128)(2,1)}, bf16[512,768]{1,0:T(8,128)(2,1)}, f32[768,128]{1,0:T(8,128)}, f32[1,768]{1,0:T(1,128)}, /*index=5*/f32[1,768]{1,0:T(1,128)}) custom-call(bf16[512,1536]{1,0:T(8,128)(2,1)} %get-tuple-element.193.refs_0_, bf16[2,768,1536]{2,1,0:T(8,128)(2,1)} %refs_1_.3, ...), custom_call_target="tpu_custom_call" | custom-call | flops 8999999488 | bytes 27000000 | tf_op jit(solution)/shard_map/bwd_gate/pallas_call | solution.py:1002
  357.2 1.0 fusion.1
  358.2 1.2 collective-permute-start.11
  359.5 0.8 copy-done.14
  360.5 30.4 %bwd_local.3 = (f32[512,768]{1,0:T(8,128)}, f32[512,128]{1,0:T(8,128)}, f32[128,512]{1,0:T(8,128)}, f32[512,256]{1,0:T(8,128)}, f32[768,128]{1,0:T(8,128)}) custom-call(f32[512,768]{1,0:T(8,128)} %get-tuple-element.198.refs_0_, f32[512,768]{1,0:T(8,128)} %get-tuple-element.132.refs_0_.refs_4_.refs_1_.refs_2_, ...), custom_call_target="tpu_custom_call" | custom-call | flops 20000000000 | bytes 60000000 | tf_op jit(solution)/shard_map/bwd_local/pallas_call | solution.py:1002
  390.9 5.3 wgrad.9
  396.2 5.4 wgrad.10
  402.1 12.2 %bwd_carry.3 = (f32[8,768]{1,0:T(8,128)}, bf16[512,768]{1,0:T(8,128)(2,1)}, f32[16,768]{1,0:T(8,128)}, f32[8,768]{1,0:T(8,128)}, bf16[512,128]{1,0:T(8,128)(2,1)}, /*index=5*/f32[8,128]{1,0:T(8,128)}, f32[512,256]{1,0:T(8,128)}) custom-call(f32[512,768]{1,0:T(8,128)} %get-tuple-element.198.refs_0_, f32[512,768]{1,0:T(8,128)} %get-tuple-element.200.refs_1_, ...), custom_call_target="tpu_custom_call" | custom-call | flops 11000000512 | bytes 33000000 | tf_op jit(solution)/shard_map/bwd_carry/pallas_call | solution.py:1002
  414.3 16.4 %maps_bwd.3 = (bf16[512,128]{1,0:T(8,128)(2,1)}, f32[8,128]{1,0:T(8,128)}, bf16[16,768]{1,0:T(8,128)(2,1)}) custom-call(f32[512,256]{1,0:T(8,128)} %get-tuple-element.213.refs_0_, bf16[528,256]{1,0:T(8,128)(2,1)} %get-tuple-element.214.refs_1_, f32[2,5,256]{2,1,0:T(8,128)} %copy.51.refs_5_.refs_2_, ...), custom_call_target="tpu_custom_call" | custom-call | flops 14000000000 | bytes 42000000 | tf_op jit(solution)/shard_map/maps_bwd/pallas_call | solution.py:1002
  430.7 1.3 constant_dynamic-update-slice_fusion.refs_1_
  432.1 5.9 %wgrad.11 = (bf16[4,192,896]{2,1,0:T(8,128)(2,1)}, bf16[4,192,896]{2,1,0:T(8,128)(2,1)}) custom-call(bf16[528,1536]{1,0:T(8,128)(2,1)} %pad_maximum_fusion.1.refs_0_, bf16[512,768]{1,0:T(8,128)(2,1)} %constant_dynamic-update-slice_fusion.refs_1_, bf16[512,128]{1,0:T(8,128)(2,1)} %get-tuple-element.219.refs_2_), custom_call_target="tpu_custom_call" | custom-call | flops 3000000000 | bytes 9000000 | tf_op jit(solution)/shard_map/wgrad/pallas_call | solution.py:1002
  437.9 1.7 collective-permute-start.8
  439.8 0.8 dynamic-slice_convert_fusion.6
  441.0 0.8 dynamic-slice_convert_fusion.4
  441.8 1.6 collective-permute-start.13
  443.7 0.9 fusion.4
  444.6 1.3 collective-permute-start.9
  446.3 0.9 fusion.8
  448.0 29.5 %head_bwd.3 = (bf16[512,1536]{1,0:T(8,128)(2,1)}, f32[128,1536]{1,0:T(8,128)}, f32[1,1536]{1,0:T(1,128)}, f32[32,128]{1,0:T(8,128)}) custom-call(bf16[512,768]{1,0:T(8,128)(2,1)} %get-tuple-element.197.refs_1_.refs_0_, bf16[512,768]{1,0:T(8,128)(2,1)} %constant_dynamic-update-slice_fusion.refs_1_, bf16[512,128]{1,0:T(8,128)(2,1)} %get-tuple-element.219.refs_2_, ...), custom_call_target="tpu_custom_call" | custom-call | flops 28999999488 | bytes 87000000 | tf_op jit(solution)/shard_map/head_bwd/pallas_call | solution.py:1002
  477.5 3.5 convert_element_type.158
  482.6 57.9 %tail.1 = (f32[192,896]{1,0:T(8,128)}, f32[192,768]{1,0:T(8,128)}, f32[192,768]{1,0:T(8,128)}, f32[192,896]{1,0:T(8,128)}, f32[192,768]{1,0:T(8,128)}, /*index=5...) custom-call(bf16[4,192,896]{2,1,0:T(8,128)(2,1)} %copy-done.42, ...), custom_call_target="tpu_custom_call" | custom-call | flops 44999999488 | bytes 135000000 | tf_op jit(solution)/shard_map/tail/pallas_call | solution.py:1002
  540.6 1.2 slice_bitcast_fusion.1
  541.8 0.9 slice_bitcast_fusion.3
  544.2 3.2 copy.70
  547.4 0.8 copy.71
  551.4 1.3 constant_dynamic-slice_fusion
  552.8 1.1 pad_maximum_fusion.2
  553.9 1.1 copy.87
  (156 shorter events, 20.3 us)
Async XLA Ops:
  0.6 2.7 copy-start
  3.3 6.6 %copy-start.27 = (bf16[2,1536,12]{1,0,2:T(2,128)(2,1)S(1)}, bf16[2,1536,12]{1,0,2:T(2,128)(2,1)}, u32[]{:S(2)}) copy-start(bf16[2,1536,12]{1,0,2:T(2,128)(2,1)} %param.20) | copy-start | bytes 221188
  3.8 1.1 copy-start.1
  4.9 5.6 %copy-start.34 = (s32[512]{0:T(512)S(1)}, s32[512]{0:T(512)}, u32[]{:S(2)}) copy-start(s32[512]{0:T(512)} %param.15) | copy-start | bytes 6148
  4.9 29.9 %collective-permute-start = (bf16[16,1536]{1,0:T(8,128)(2,1)S(1)}, bf16[16,1536]{1,0:T(8,128)(2,1)S(1)}, u32[]{:S(2)}, u32[]{:S(2)}) collective-permute-start(bf16[16,1536]{1,0:T(8,128)(2,1)S(1)} %slice.84), channel_id=1, source_target_pairs={{0,4},{4,8},{8,12},{12,16},{16,20},{20,24},{24,28},{1,5},{5,9},{9,... | collective-permute-start | bytes 147464 | tf_op jit(solution)/shard_map/ppermute | solution.py:41
  10.6 24.2 %copy-start.31 = (f32[512]{0:T(512)}, f32[512]{0:T(512)S(1)}, u32[]{:S(2)}) copy-start(f32[512]{0:T(512)S(1)} %convert_element_type.140) | copy-start | bytes 6148
  13.2 1.9 copy-start.24
  16.0 1.4 copy-start.3
  17.0 1.6 copy-start.25
  18.6 3.1 copy-start.30
  22.3 8.8 %copy-start.29 = (f32[2,5,768]{2,0,1:T(2,128)S(1)}, f32[2,5,768]{2,0,1:T(2,128)}, u32[]{:S(2)}) copy-start(f32[2,5,768]{2,0,1:T(2,128)} %param.21) | copy-start | bytes 92164
  22.3 9.4 %copy-start.33 = (f32[2,5,256]{2,0,1:T(2,128)S(1)}, f32[2,5,256]{2,0,1:T(2,128)}, u32[]{:S(2)}) copy-start(f32[2,5,256]{2,0,1:T(2,128)} %param.22) | copy-start | bytes 30724
  22.3 10.0 %copy-start.40 = (f32[2,12]{1,0:T(2,128)S(1)}, f32[2,12]{1,0:T(2,128)}, u32[]{:S(2)}) copy-start(f32[2,12]{1,0:T(2,128)} %param.23) | copy-start | bytes 292
  22.3 10.5 %copy-start.41 = (f32[2,12]{1,0:T(2,128)S(1)}, f32[2,12]{1,0:T(2,128)}, u32[]{:S(2)}) copy-start(f32[2,12]{1,0:T(2,128)} %param.24) | copy-start | bytes 292
  22.3 11.1 %copy-start.39 = (f32[2,12]{1,0:T(2,128)S(1)}, f32[2,12]{1,0:T(2,128)}, u32[]{:S(2)}) copy-start(f32[2,12]{1,0:T(2,128)} %param.25) | copy-start | bytes 292
  22.3 11.8 %copy-start.35 = (f32[2,768]{1,0:T(2,128)S(1)}, f32[2,768]{1,0:T(2,128)}, u32[]{:S(2)}) copy-start(f32[2,768]{1,0:T(2,128)} %param.26) | copy-start | bytes 18436
  22.3 12.5 %copy-start.2 = (bf16[512,1536]{1,0:T(8,128)(2,1)S(1)}, bf16[512,1536]{1,0:T(8,128)(2,1)}, u32[]{:S(2)}) copy-start(bf16[512,1536]{1,0:T(8,128)(2,1)} %copy-done.1) | copy-start | bytes 4718596
  259.8 15.7 %copy-start.43 = (bf16[4,192,768]{2,1,0:T(8,128)(2,1)S(1)}, bf16[4,192,768]{2,1,0:T(8,128)(2,1)}, u32[]{:S(2)}) copy-start(bf16[4,192,768]{2,1,0:T(8,128)(2,1)} %get-tuple-element.179.refs_21_) | copy-start | bytes 3538948
  275.4 37.4 %collective-permute-start.1 = (bf16[4,192,768]{2,1,0:T(8,128)(2,1)S(1)}, bf16[4,192,768]{2,1,0:T(8,128)(2,1)S(1)}, u32[]{:S(2)}, u32[]{:S(2)}) collective-permute-start(bf16[4,192,768]{2,1,0:T(8,128)(2,1)S(1)} %copy-done.43), channel_id=1, source_target_pairs={{0,4},{4,0},{8,12},{12,8},{16,20},{20,16},{24,28},{28,24},{1,5},{5... | collective-permute-start | bytes 3538952 | tf_op jit(solution)/shard_map/ppermute | solution.py:36
  276.0 38.4 %collective-permute-start.2 = (bf16[4,192,768]{2,1,0:T(8,128)(2,1)}, bf16[4,192,768]{2,1,0:T(8,128)(2,1)S(1)}, u32[]{:S(2)}, u32[]{:S(2)}) collective-permute-start(bf16[4,192,768]{2,1,0:T(8,128)(2,1)} %get-tuple-element.180.refs_22_), channel_id=1, source_target_pairs={{0,8},{4,12},{8,0},{12,4},{16,24},{20,28},{24,16},{28,20},{1,9},{5... | collective-permute-start | bytes 3538952 | tf_op jit(solution)/shard_map/ppermute | solution.py:36
  304.3 8.6 %copy-start.10 = (bf16[4,192,768]{2,1,0:T(8,128)(2,1)S(1)}, bf16[4,192,768]{2,1,0:T(8,128)(2,1)}, u32[]{:S(2)}) copy-start(bf16[4,192,768]{2,1,0:T(8,128)(2,1)} %get-tuple-element.191) | copy-start | bytes 3538948
  310.2 45.9 %collective-permute-start.5 = (bf16[4,192,896]{2,1,0:T(8,128)(2,1)}, bf16[4,192,896]{2,1,0:T(8,128)(2,1)S(1)}, u32[]{:S(2)}, u32[]{:S(2)}) collective-permute-start(bf16[4,192,896]{2,1,0:T(8,128)(2,1)} %get-tuple-element.190.refs_9_), channel_id=1, source_target_pairs={{0,4},{4,0},{8,12},{12,8},{16,20},{20,16},{24,28},{28,24},{1,5},{5... | collective-permute-start | bytes 4128776 | tf_op jit(solution)/shard_map/ppermute | solution.py:36
  312.9 1.5 copy-start.9
  313.2 1.4 copy-start.12
  313.2 46.2 %collective-permute-start.3 = (bf16[2,192,768]{2,1,0:T(8,128)(2,1)S(1)}, bf16[2,192,768]{2,1,0:T(8,128)(2,1)S(1)}, u32[]{:S(2)}, u32[]{:S(2)}) collective-permute-start(bf16[2,192,768]{2,1,0:T(8,128)(2,1)S(1)} %fusion.6.refs_10_), channel_id=1, source_target_pairs={{0,8},{4,12},{8,0},{12,4},{16,24},{20,28},{24,16},{28,20},{1,9},{5... | collective-permute-start | bytes 1769480 | tf_op jit(solution)/shard_map/ppermute | solution.py:36
  314.7 1.8 copy-start.13
  314.7 44.7 %collective-permute-start.4 = (bf16[2,192,768]{2,1,0:T(8,128)(2,1)S(1)}, bf16[2,192,768]{2,1,0:T(8,128)(2,1)S(1)}, u32[]{:S(2)}, u32[]{:S(2)}) collective-permute-start(bf16[2,192,768]{2,1,0:T(8,128)(2,1)S(1)} %fusion.2.refs_11_), channel_id=1, source_target_pairs={{0,16},{4,20},{8,24},{12,28},{16,0},{20,4},{24,8},{28,12},{1,17},{... | collective-permute-start | bytes 1769480 | tf_op jit(solution)/shard_map/ppermute | solution.py:36
  316.5 29.2 %copy-start.26 = (f32[512,128]{1,0:T(8,128)S(1)}, f32[512,128]{1,0:T(8,128)}, u32[]{:S(2)}) copy-start(f32[512,128]{1,0:T(8,128)} %get-tuple-element.195.refs_7_) | copy-start | bytes 786436
  346.6 9.5 %copy-start.6 = (bf16[4,192,896]{2,1,0:T(8,128)(2,1)S(1)}, bf16[4,192,896]{2,1,0:T(8,128)(2,1)}, u32[]{:S(2)}) copy-start(bf16[4,192,896]{2,1,0:T(8,128)(2,1)} %get-tuple-element.226) | copy-start | bytes 4128772
  356.1 1.1 copy-start.5
  358.2 88.9 %collective-permute-start.11 = (bf16[2,192,896]{2,1,0:T(8,128)(2,1)S(1)}, bf16[2,192,896]{2,1,0:T(8,128)(2,1)}, u32[]{:S(2)}, u32[]{:S(2)}) collective-permute-start(bf16[2,192,896]{2,1,0:T(8,128)(2,1)S(1)} %get-tuple-element.280), channel_id=1, source_target_pairs={{0,8},{4,12},{8,0},{12,4},{16,24},{20,28},{24,16},{28,20},{1,9},{5... | collective-permute-start | bytes 2064392 | tf_op jit(solution)/shard_map/ppermute | solution.py:36
  359.4 0.9 copy-start.14
  359.5 1.0 copy-start.16
  401.6 43.0 %collective-permute-start.6 = (bf16[4,192,768]{2,1,0:T(8,128)(2,1)}, bf16[4,192,768]{2,1,0:T(8,128)(2,1)S(1)}, u32[]{:S(2)}, u32[]{:S(2)}) collective-permute-start(bf16[4,192,768]{2,1,0:T(8,128)(2,1)} %get-tuple-element.210.refs_21_), channel_id=1, source_target_pairs={{0,4},{4,0},{8,12},{12,8},{16,20},{20,16},{24,28},{28,24},{1,5},{5... | collective-permute-start | bytes 3538952 | tf_op jit(solution)/shard_map/ppermute | solution.py:36
  402.1 39.7 %collective-permute-start.7 = (bf16[4,192,768]{2,1,0:T(8,128)(2,1)}, bf16[4,192,768]{2,1,0:T(8,128)(2,1)S(1)}, u32[]{:S(2)}, u32[]{:S(2)}) collective-permute-start(bf16[4,192,768]{2,1,0:T(8,128)(2,1)} %get-tuple-element.211.refs_22_), channel_id=1, source_target_pairs={{0,8},{4,12},{8,0},{12,4},{16,24},{20,28},{24,16},{28,20},{1,9},{5... | collective-permute-start | bytes 3538952 | tf_op jit(solution)/shard_map/ppermute | solution.py:36
  432.1 7.6 %copy-start.17 = (bf16[2,192,768]{2,1,0:T(8,128)(2,1)S(1)}, bf16[2,192,768]{2,1,0:T(8,128)(2,1)}, u32[]{:S(2)}) copy-start(bf16[2,192,768]{2,1,0:T(8,128)(2,1)} %copy-done.16) | copy-start | bytes 1769476
  437.9 2.9 copy-start.15
  437.9 43.0 %collective-permute-start.8 = (bf16[4,192,896]{2,1,0:T(8,128)(2,1)}, bf16[4,192,896]{2,1,0:T(8,128)(2,1)S(1)}, u32[]{:S(2)}, u32[]{:S(2)}) collective-permute-start(bf16[4,192,896]{2,1,0:T(8,128)(2,1)} %get-tuple-element.221.refs_9_), channel_id=1, source_target_pairs={{0,4},{4,0},{8,12},{12,8},{16,20},{20,16},{24,28},{28,24},{1,5},{5... | collective-permute-start | bytes 4128776 | tf_op jit(solution)/shard_map/ppermute | solution.py:36
  440.6 2.8 copy-start.8
  440.6 40.4 %collective-permute-start.12 = (bf16[1,192,768]{2,1,0:T(8,128)(2,1)S(1)}, bf16[1,192,768]{2,1,0:T(8,128)(2,1)S(1)}, u32[]{:S(2)}, u32[]{:S(2)}) collective-permute-start(bf16[1,192,768]{2,1,0:T(8,128)(2,1)S(1)} %get-tuple-element.290), channel_id=1, source_target_pairs={{0,4},{4,0},{8,12},{12,8},{16,20},{20,16},{24,28},{28,24},{1,5},{5... | collective-permute-start | bytes 884744 | tf_op jit(solution)/shard_map/ppermute | solution.py:36
  441.8 39.2 %collective-permute-start.13 = (bf16[1,192,768]{2,1,0:T(8,128)(2,1)S(1)}, bf16[1,192,768]{2,1,0:T(8,128)(2,1)S(1)}, u32[]{:S(2)}, u32[]{:S(2)}) collective-permute-start(bf16[1,192,768]{2,1,0:T(8,128)(2,1)S(1)} %get-tuple-element.288), channel_id=1, source_target_pairs={{0,16},{4,20},{8,24},{12,28},{16,0},{20,4},{24,8},{28,12},{1,17},{... | collective-permute-start | bytes 884744 | tf_op jit(solution)/shard_map/ppermute | solution.py:36
  443.7 2.3 copy-start.7
  444.6 1.7 copy-start.20
  444.6 36.6 %collective-permute-start.9 = (bf16[2,192,768]{2,1,0:T(8,128)(2,1)S(1)}, bf16[2,192,768]{2,1,0:T(8,128)(2,1)S(1)}, u32[]{:S(2)}, u32[]{:S(2)}) collective-permute-start(bf16[2,192,768]{2,1,0:T(8,128)(2,1)S(1)} %get-tuple-element.284.refs_11_), channel_id=1, source_target_pairs={{0,16},{4,20},{8,24},{12,28},{16,0},{20,4},{24,8},{28,12},{1,17},{... | collective-permute-start | bytes 1769480 | tf_op jit(solution)/shard_map/ppermute | solution.py:36
  447.2 0.8 copy-start.22
  447.2 34.1 %collective-permute-start.10 = (bf16[2,192,768]{2,1,0:T(8,128)(2,1)S(1)}, bf16[2,192,768]{2,1,0:T(8,128)(2,1)S(1)}, u32[]{:S(2)}, u32[]{:S(2)}) collective-permute-start(bf16[2,192,768]{2,1,0:T(8,128)(2,1)S(1)} %get-tuple-element.282.refs_10_), channel_id=1, source_target_pairs={{0,8},{4,12},{8,0},{12,4},{16,24},{20,28},{24,16},{28,20},{1,9},{5... | collective-permute-start | bytes 1769480 | tf_op jit(solution)/shard_map/ppermute | solution.py:36
  480.9 0.7 copy-start.46
  481.0 0.8 copy-start.47
  481.0 1.2 copy-start.42
  481.2 1.2 copy-start.44
  481.2 1.4 copy-start.45
  540.6 2.1 copy-start.11
  540.6 2.4 copy-start.23
  542.8 1.1 copy-start.21
  544.1 4.8 copy-start.28
  544.1 5.4 copy-start.32
  544.1 6.0 %copy-start.38 = (f32[2,256]{1,0:T(2,128)S(1)}, f32[2,256]{1,0:T(2,128)}, u32[]{:S(2)}) copy-start(f32[2,256]{1,0:T(2,128)} %get-tuple-element.246) | copy-start | bytes 6148
  544.1 6.6 %copy-start.37 = (f32[2,768]{1,0:T(2,128)S(1)}, f32[2,768]{1,0:T(2,128)}, u32[]{:S(2)}) copy-start(f32[2,768]{1,0:T(2,128)} %get-tuple-element.247) | copy-start | bytes 18436
  544.1 8.6 %copy-start.18 = (f32[192,768]{1,0:T(8,128)S(1)}, f32[192,768]{1,0:T(8,128)}, u32[]{:S(2)}) copy-start(f32[192,768]{1,0:T(8,128)} %get-tuple-element.249) | copy-start | bytes 1769476
  544.1 8.6 %copy-start.19 = (f32[192,768]{1,0:T(8,128)S(1)}, f32[192,768]{1,0:T(8,128)}, u32[]{:S(2)}) copy-start(f32[192,768]{1,0:T(8,128)} %get-tuple-element.250) | copy-start | bytes 1769476
  547.4 6.5 %copy-start.4 = (bf16[512,1536]{1,0:T(8,128)(2,1)S(1)}, bf16[512,1536]{1,0:T(8,128)(2,1)}, u32[]{:S(2)}) copy-start(bf16[512,1536]{1,0:T(8,128)(2,1)} %get-tuple-element.315) | copy-start | bytes 4718596
  553.9 1.1 copy-start.36

commit v4 on v3

--- a/solution.py
+++ b/solution.py
@@ -9,6 +9,7 @@
 
 CONV = 4
 LAYERS = 2
+OUT_ORDER = (0, 1, 2)
 Z_ORDER = (1, 2, 0)
 EPS = 1e-05
 F32 = jnp.float32
@@ -85,9 +86,9 @@
 
 
 def own_rows(x):
-    for bit in bits_of("head"):
-        x = take(x.reshape((2, x.shape[0] // 2) + x.shape[1:]), 0, my_bit("head", bit))
-    return x
+    rank = lax.axis_index("head")
+    quarter = x.shape[0] // 4
+    return lax.dynamic_slice_in_dim(x, ((rank % 2) * 2 + rank // 2) * quarter, quarter, 0)
 
 
 def carry_scan(state, decay, reverse):
@@ -179,8 +180,8 @@
     return jnp.sum(jnp.where(lanes == h, values, 0.0), axis=1, keepdims=True)
 
 
-def fwd_mix_body(size, nx, wzx, wbc, wdt, tapx, tapbc, dtb, lograte, aux, segrow,
-                 gate, ux, ubc, krs, pdt, steps_o, cum_o, cT, gram, mixed_o, entry_o, state, dec, decl,
+def fwd_mix_body(size, nx, wx, wbc, wdt, tapx, tapbc, dtb, lograte, aux, segrow,
+                 ux, ubc, krs, pdt, steps_o, cum_o, cT, gram, mixed_o, entry_o, state, dec, decl,
                  us, usbc):
     p = pl.program_id(0)
     tokens = aux.shape[1]
@@ -214,8 +215,7 @@
         decl[...] = jnp.broadcast_to(jnp.exp(cum[tokens - 1 : tokens, :]) * keeps, (8, LANE))
         dec[...] = jnp.exp(jnp.broadcast_to(cT[0:16, tokens - 1 : tokens], (16, LANE))) * keeps
 
-    gate[...] = bdot(nx[pl.ds(HALO, tokens), :], wzx[0], NN).astype(BF16)
-    u = bdot(nx[...], wzx[1], NN).astype(BF16)
+    u = bdot(nx[...], wx[...], NN).astype(BF16)
     ux[...] = u
     us[...] = u.astype(F32)
     m = mix_taps(us, tapx, aux, LANE)
@@ -232,12 +232,13 @@
     state[...] = dot3(vd * tail, krs[:, :states], TN)
 
 
-def fwd_inside_body(stages_of, size, mixed, steps, cum, cT, gram, skip, state, dec, ypart, enter, cb, *rest):
+def fwd_inside_body(stages_of, size, nx, wz, mixed, steps, cum, cT, gram, skip, state, dec, ypart, enter, gate, cb, *rest):
     p = pl.program_id(0)
     tokens = mixed.shape[0]
     stages = stages_of(state, dec, enter, *rest)
     for k, stage in enumerate(stages[:-1]):
         pl.when(p == k)(stage)
+    gate[...] = bdot(nx[pl.ds(HALO, tokens), :], wz[...], NN).astype(BF16)
     lanes = lax.broadcasted_iota(jnp.int32, (tokens, LANE), 1)
     half = lanes < size
     h0 = p * (LANE // size)
@@ -275,12 +276,15 @@
     return pl.BlockSpec(shape, lambda p: (0,) * n)
 
 
-def cols(rows):
-    return pl.BlockSpec((rows, LANE), lambda p: (0, p))
-
-
-def rowsb(width):
-    return pl.BlockSpec((LANE, width), lambda p: (p, 0))
+WIDE = 2 * LANE
+
+
+def cols(rows, width=LANE):
+    return pl.BlockSpec((rows, width), lambda p: (0, p))
+
+
+def rowsb(width, rows=LANE):
+    return pl.BlockSpec((rows, width), lambda p: (p, 0))
 
 
 def fwd_gate_body(ypart, entry, gate, krs, enter, y, carr, gated, sq, sqacc):
@@ -293,14 +297,15 @@
     z = gate[...].astype(F32)
     g = yy * (z * sig(z))
     gated[...] = g
+    gg = g[:, :LANE] * g[:, :LANE] + g[:, LANE:] * g[:, LANE:]
 
     @pl.when(p == 0)
     def _():
-        sqacc[...] = g * g
+        sqacc[...] = gg
 
     @pl.when(p > 0)
     def _():
-        sqacc[...] += g * g
+        sqacc[...] += gg
 
     @pl.when(p == pl.num_programs(0) - 1)
     def _():
@@ -315,11 +320,12 @@
     sil = z * s
     yy = y[...]
     gated = yy * sil
-    r2 = r2b[...]
+    twice = lambda v: jnp.concatenate([v, v], axis=1)
+    r2 = twice(r2b[...])
     gr = gated * r2
     ggate[...] = jnp.sum(gs * gr, axis=0, keepdims=True)
     scaled_o[...] = (gr * gain[...]).astype(BF16)
-    gg = r2 * gain[...] * gs - gated * krb[...]
+    gg = r2 * gain[...] * gs - gated * twice(krb[...])
     gy = gg * sil
     gy_o[...] = gy
     gz_o[...] = (gg * yy * (s * (1.0 + z * (1.0 - s)))).astype(BF16)
@@ -328,13 +334,62 @@
     qloc[...] = bdot(gy * entry[...], krs[:, states:], TN)
 
 
-def bwd_local_body(stages_of, size, gy_r, mixed, krs, cum, steps, cT, gram, entry, enter, segc, segrow, qloc, dec,
-                   dvd, dd_o, rowT, dkr, later, cb, db, gramT, dgT, vb, gk, *rest):
+def wgrad_into(blocks, bit, off, lhs, rhs, away, keep, lt):
+    tokens = rhs[0].shape[0]
+    mine = (lax.axis_index("seq") // bit) % 2
+    block = lt.shape[0] // blocks
+    half = blocks // 2
+    turned = jnp.transpose(lhs[pl.ds(off, tokens), :])
+    for at in range(blocks):
+        first = (at // bit) % 2 != mine
+        k = at // (2 * bit) * bit + at % bit
+        place = jnp.where(first, k, half + k) * block
+        lt[pl.ds(pl.multiple_of(place, 16), block), :] = turned[at * block : (at + 1) * block]
+    for dst, base in ((away, 0), (keep, half * block)):
+        c = 0
+        for r in rhs:
+            w = r.shape[1]
+            out = bdot(lt[pl.ds(base, half * block), :], r[...], NN).astype(BF16)
+            dst[:, :, c : c + w] = out.reshape(half, block, w)
+            c += w
+
+
+def wgrad_body(blocks, bit, off, n_rhs, lhs, *refs):
+    wgrad_into(blocks, bit, off, lhs, refs[:n_rhs], *refs[n_rhs:])
+
+
+def halve(dst, got, keep, stride, want):
+    for k in range(dst.shape[0]):
+        at = (k // stride) * 2 * stride + want * stride + k % stride
+        dst[k] = (keep[at].astype(F32) + got[at].astype(F32)).astype(dst.dtype)
+
+
+def fold_body(bit, stride, got, keep, away, kept):
+    me = (lax.axis_index("seq") // bit) % 2
+    halve(away, got, keep, stride, 1 - me)
+    halve(kept, got, keep, stride, me)
+
+
+def bwd_local_body(stages_of, size, blocks, bits, folds, gy_r, mixed, krs, cum, steps, cT, gram, entry, enter, segc, segrow, qloc, dec, *refs):
     p = pl.program_id(0)
-    stages = stages_of(qloc, dec, later, *rest)
+    n = len(folds)
+    gb, scaled, nx, gz = refs[:4]
+    pairs, refs = refs[4 : 4 + 2 * n], refs[4 + 2 * n :]
+    dvd, dd_o, rowT, dkr, later, out_away, out_keep, z_away, z_keep = refs[:9]
+    halved, refs = refs[9 : 9 + 2 * n], refs[9 + 2 * n :]
+    cb, db, gramT, dgT, vb, gk, lt = refs[:7]
+    stages = stages_of(qloc, dec, later, *refs[7:])
     for k, stage in enumerate(stages[:-1]):
         pl.when(p == k)(stage)
     tokens = gy_r.shape[0]
+
+    def beside(k, fn):
+        pl.when(p == k)(fn)
+
+    beside(1, lambda: wgrad_into(blocks, bits[0], gb.shape[0] - tokens, gb, [scaled], out_away, out_keep, lt))
+    beside(2, lambda: wgrad_into(blocks, bits[1], nx.shape[0] - tokens, nx, [gz], z_away, z_keep, lt))
+    for i, (bit, stride) in enumerate(folds):
+        beside((0, 3, 4)[i], partial(fold_body, bit, stride, *pairs[2 * i : 2 * i + 2], *halved[2 * i : 2 * i + 2]))
     states = krs.shape[1] // 2
     lanes = lax.broadcasted_iota(jnp.int32, (tokens, LANE), 1)
     half = lanes < size
@@ -606,7 +661,7 @@
             dec, dec, part, part, pltpu.SemaphoreType.DMA((2 * n + 1,)), pltpu.SemaphoreType.DMA((2 * n + 1,))]
 
 
-def head_core(tokens, part, middle, nx, off, side, tx0, rx0, tx1, rx1, acc, ssem, rsem, me, core_at, y_at):
+def head_core(tokens, part, middle, nx, off, side, tx0, rx0, tx1, rx1, acc, ssem, rsem, me, core_at, y_at, gather=True):
     quarter = tokens // 4
     sub = quarter // SUBS
     c = me % 2
@@ -643,10 +698,17 @@
         first[SUBS + s].wait_recv()
         second[s].wait_recv()
         total = acc[pl.ds(pl.multiple_of(own_y + s * sub, sub), sub), :] + rx0[1, s].astype(F32) + rx1[s].astype(F32)
+        if not gather:
+            nx[pl.ds(s * sub, sub), :] = middle(s, sub, total)
+            continue
         rows = pl.ds(pl.multiple_of(off + own + s * sub, 16), sub)
         nx[rows, :] = middle(s, sub, total)
         to_y.append(go(nx.at[rows, :], nx.at[rows, :], y_at))
         to_core.append(go(nx.at[rows, :], nx.at[rows, :], core_at))
+    if not gather:
+        for copy in sends:
+            copy.wait_send()
+        return
     if side is not None:
         srows = pl.ds(pl.multiple_of((c * 2 + y) * 8, 8), 8)
         to_y.append(go(side.at[srows, :], side.at[srows, :], y_at))
@@ -754,7 +816,7 @@
             pltpu.SemaphoreType.DMA((HEAD_COPIES,)), pltpu.SemaphoreType.DMA((HEAD_COPIES,))]
 
 
-def head_bwd_body(l, tokens, gz, gu, small, wzx_all, wsmall_all, h_own, gain_all, g_own, branch,
+def head_bwd_body(l, gather, tokens, gz, gu, small, wzx_all, wsmall_all, h_own, gain_all, g_own, branch,
                   gb, g_new, ggain, side, tx0, rx0, tx1, rx1, acc, krc, ssem, rsem, wzx, wsem):
     load = pltpu.make_async_copy(wzx_all.at[l], wzx, wsem.at[0])
     load.start()
@@ -786,11 +848,13 @@
         krc[rows, :] = jnp.broadcast_to(jnp.sum(low.astype(F32) * branch[rows, :], axis=1, keepdims=True), (sub, LANE))
         if s == SUBS - 1:
             mine = pl.ds(pl.multiple_of(((me % 2) * 2 + me // 2) * 8, 8), 8)
+            if not gather:
+                side[...] = jnp.zeros_like(side)
             side[mine, :] = jnp.transpose(krc[...])[0:8, :]
         return low
 
     load.wait()
-    head_core(tokens, part, middle, gb, 0, side, tx0, rx0, tx1, rx1, acc, ssem, rsem, me, core_at, y_at)
+    head_core(tokens, part, middle, gb, 0, side, tx0, rx0, tx1, rx1, acc, ssem, rsem, me, core_at, y_at, gather)
 
 
 def maps_bwd_body(l, tokens, dkr, ubc, taps_all, aux, gdt, gtail, gm8, tapx_all,
@@ -819,7 +883,7 @@
     def _():
         ahead_x.start()
     low, high = dkr[:, :LANE], dkr[:, LANE:]
-    ytx[...] = jnp.where(y == 0, high, low)
+    ytx[...] = jnp.where(y == 0, high, low).astype(BF16)
     one = send(ytx, yrx, (sems.at[0], semr.at[0]), y_at)
     tile = pl.ds(pl.multiple_of(y * LANE, LANE), LANE)
     us[...] = ubc[:, tile].astype(F32)
@@ -828,7 +892,7 @@
     s = sig(m)
     slope = s * (1.0 + m * (1.0 - s))
     one.wait()
-    ctx[...] = jnp.where(y == 0, low, high) + yrx[...]
+    ctx[...] = jnp.where(y == 0, low, high) + yrx[...].astype(F32)
     two = send(ctx, crx, (sems.at[1], semr.at[1]), core_at)
     two.wait()
     gm = (ctx[...] + crx[...]) * slope
@@ -897,10 +961,8 @@
         stride = 1 << (len(self.left) - 1 - self.left.index(bit))
         self.left.remove(bit)
         me = (lax.axis_index("seq") // bit) % 2
-        for dst, want in ((away, 1 - me), (kept, me)):
-            for k in range(dst.shape[0]):
-                at = (k // stride) * 2 * stride + want * stride + k % stride
-                dst[k] = (keep[at].astype(F32) + got[at].astype(F32)).astype(dst.dtype)
+        halve(away, got, keep, stride, 1 - me)
+        halve(kept, got, keep, stride, me)
         where = {"seq": flip(lax.axis_index("seq"), bit)}
         k = len(self.steps)
         self.copy = send(away, came, (self.ssem.at[k], self.rsem.at[k]), where)
@@ -912,7 +974,10 @@
     pairs = refs[: 2 * jobs_n]
     ins = refs[2 * jobs_n : 2 * jobs_n + 6 * parts]
     rest = refs[2 * jobs_n + 6 * parts :]
+    low, rest = rest[0], rest[1:]
     outs, rest = rest[:jobs_n], rest[jobs_n:]
+    grad, rest = rest[0], rest[1:]
+    gsend, grecv, rest = rest[-2], rest[-1], rest[:-2]
     conv_x, conv_bc, ggate, gskip, gvec, ggain = rest[:6]
     stage, rx, hx, ssem, rsem = rest[6:11]
     rest = list(rest[11:])
@@ -927,7 +992,17 @@
     steps = [("head", b) for b in bits_of("head")] + [("seq", b) for b in bits_of("seq")]
     wheres = [{axis: flip(lax.axis_index(axis), b)} for axis, b in steps]
     greet(wheres)
-    for job in jobs:
+    jobs[0].advance()
+    quarter = low.shape[0]
+    spot = lambda c, y: pl.ds(pl.multiple_of((c * 2 + y) * quarter, quarter), quarter)
+    c, y = me % 2, me // 2
+    grad[spot(c, y), :] = low[...]
+    core_at, y_at = wheres[0], wheres[1]
+    here = grad.at[spot(c, y), :]
+    there = grad.at[spot(c, 1 - y), :]
+    over_y = send(here, here, (gsend.at[0], grecv.at[0]), y_at)
+    over_core = send(here, here, (gsend.at[1], grecv.at[1]), core_at)
+    for job in jobs[1:]:
         job.advance()
     stage[...] = jnp.zeros_like(stage)
     for l in range(parts):
@@ -959,6 +1034,8 @@
                         job.advance()
             copy.wait()
             stage[...] += rx[i - heads]
+    over_y.wait_recv()
+    onward = send(there, there, (gsend.at[2], grecv.at[2]), core_at)
     for _ in range(longest + 1):
         for job in jobs:
             if job.copy is not None and (job.steps or job.out is not None):
@@ -966,6 +1043,10 @@
                 job.advance()
                 if done:
                     job.out = None
+    over_core.wait_recv()
+    onward.wait_recv()
+    for copy in (over_y, over_core, onward):
+        copy.wait_send()
     for l in range(parts):
         conv_x[l] = stage[l, 0 : CONV + 1, :]
         ggate[l : l + 1, :] = stage[l, 5:6, :]
@@ -984,12 +1065,16 @@
 def of_layer(l, shape, steps=False):
     n = len(shape) - 1
     if steps:
-        return pl.BlockSpec((None,) + shape[1:-1] + (LANE,), lambda p: (l,) + (0,) * (n - 1) + (p,))
+        return pl.BlockSpec((None,) + shape[1:-1] + (LANE if steps is True else steps,), lambda p: (l,) + (0,) * (n - 1) + (p,))
     return pl.BlockSpec((None,) + shape[1:], lambda *p: (l,) + (0,) * n)
 
 
+def projection(l, which, d):
+    return pl.BlockSpec((None, None, d, LANE), lambda p: (l, which, 0, p))
+
+
 def rows_of_layer(l, shape):
-    return pl.BlockSpec((None, LANE, shape[2]), lambda p: (l, p, 0))
+    return pl.BlockSpec((None, WIDE, shape[2]), lambda p: (l, p, 0))
 
 
 def kcall(body, args, specs, us, after=(), cid=None, **kw):
@@ -1014,17 +1099,17 @@
     inner = q["conv_x"].shape[2]
     two = q["w_bc"].shape[2]
     args = [nx, q["w_zx"], q["w_bc"], q["w_dt"], q["conv_x"], q["conv_bc"], q["dt_bias"], q["a_log"], aux, segrow]
-    specs = [full(nx.shape), of_layer(l, q["w_zx"].shape, True), of_layer(l, q["w_bc"].shape), of_layer(l, q["w_dt"].shape),
+    specs = [full(nx.shape), projection(l, 1, d), of_layer(l, q["w_bc"].shape), of_layer(l, q["w_dt"].shape),
              of_layer(l, q["conv_x"].shape, True), of_layer(l, q["conv_bc"].shape), of_layer(l, q["dt_bias"].shape),
              of_layer(l, q["a_log"].shape), full(aux.shape), full(segrow.shape)]
     return kcall(
         partial(fwd_mix_body, size), args, specs, 12,
         name="fwd_mix",
         grid=(inner // LANE,),
-        out_specs=[cols(tokens), cols(ext), full((ext, two)), full((tokens, two)), full((tokens, LANE)), full((tokens, LANE)),
+        out_specs=[cols(ext), full((ext, two)), full((tokens, two)), full((tokens, LANE)), full((tokens, LANE)),
                    full((tokens, LANE)), full((LANE, tokens)), full((tokens, tokens)), cols(tokens),
                    cols(tokens), rowsb(two // 2), full((16, LANE)), full((8, LANE))],
-        out_shape=[S((tokens, inner), BF16), S((ext, inner), BF16), S((ext, two), BF16), S((tokens, two), F32),
+        out_shape=[S((ext, inner), BF16), S((ext, two), BF16), S((tokens, two), F32),
                    S((tokens, LANE), BF16), S((tokens, LANE), F32), S((tokens, LANE), F32), S((LANE, tokens), F32),
                    S((tokens, tokens), F32), S((tokens, inner), F32), S((tokens, inner), F32),
                    S((inner, two // 2), F32), S((16, LANE), F32), S((8, LANE), F32)],
@@ -1032,19 +1117,19 @@
     )
 
 
-def fwd_inside(l, heads, size, mixed, steps, cum, cT, gram, q, state, dec, cid):
+def fwd_inside(l, heads, size, nx, mixed, steps, cum, cT, gram, q, state, dec, cid):
     tokens, inner = mixed.shape
     rows, states = state.shape
     bits = bits_of("seq")
     return kcall(
         partial(fwd_inside_body, partial(carry_stages, bits, False, heads, size), size),
-        [mixed, steps, cum, cT, gram, q["skip"], state, dec],
-        [cols(tokens), full(steps.shape), full(cum.shape), full(cT.shape), full(gram.shape), of_layer(l, q["skip"].shape, True),
+        [nx, q["w_zx"], mixed, steps, cum, cT, gram, q["skip"], state, dec],
+        [full(nx.shape), projection(l, 0, nx.shape[1]), cols(tokens), full(steps.shape), full(cum.shape), full(cT.shape), full(gram.shape), of_layer(l, q["skip"].shape, True),
          full(state.shape), full(dec.shape)], 28, (), cid,
         name="fwd_inside",
         grid=(inner // LANE,),
-        out_specs=[cols(tokens), full((rows, states))],
-        out_shape=[S((tokens, inner), F32), S((rows, states), F32)],
+        out_specs=[cols(tokens), full((rows, states)), cols(tokens)],
+        out_shape=[S((tokens, inner), F32), S((rows, states), F32), S((tokens, inner), BF16)],
         scratch_shapes=[pltpu.VMEM((2, tokens, LANE), F32)] + carry_scratch(len(bits), rows, states, F32),
     )
 
@@ -1053,10 +1138,10 @@
     tokens, inner = ypart.shape
     return kcall(
         fwd_gate_body, [ypart, entry, gate, krs, enter],
-        [cols(tokens), cols(tokens), cols(tokens), full(krs.shape), rowsb(enter.shape[1])], 7,
+        [cols(tokens, WIDE), cols(tokens, WIDE), cols(tokens, WIDE), full(krs.shape), rowsb(enter.shape[1], WIDE)], 7,
         name="fwd_gate",
-        grid=(inner // LANE,),
-        out_specs=[cols(tokens), cols(tokens), cols(tokens), full((8, tokens))],
+        grid=(inner // WIDE,),
+        out_specs=[cols(tokens, WIDE), cols(tokens, WIDE), cols(tokens, WIDE), full((8, tokens))],
         out_shape=[S((tokens, inner), F32)] * 3 + [S((8, tokens), F32)],
         scratch_shapes=[pltpu.VMEM((tokens, LANE), F32)],
     )
@@ -1067,35 +1152,50 @@
     states = krs.shape[1] // 2
     return kcall(
         bwd_gate_body, [gb, q["w_out"], gate, y, mixed, entry, krs, r2b, krb, q["gate_gain"]],
-        [full(gb.shape), rows_of_layer(l, q["w_out"].shape), cols(tokens), cols(tokens), cols(tokens), cols(tokens), full(krs.shape),
-         full(r2b.shape), full(krb.shape), of_layer(l, q["gate_gain"].shape, True)], 9,
+        [full(gb.shape), rows_of_layer(l, q["w_out"].shape), cols(tokens, WIDE), cols(tokens, WIDE), cols(tokens, WIDE), cols(tokens, WIDE), full(krs.shape),
+         full(r2b.shape), full(krb.shape), of_layer(l, q["gate_gain"].shape, WIDE)], 9,
         name="bwd_gate",
-        grid=(inner // LANE,),
-        out_specs=[cols(tokens), cols(tokens), cols(tokens), rowsb(states), cols(1), cols(1)],
+        grid=(inner // WIDE,),
+        out_specs=[cols(tokens, WIDE), cols(tokens, WIDE), cols(tokens, WIDE), rowsb(states, WIDE), cols(1, WIDE), cols(1, WIDE)],
         out_shape=[S((tokens, inner), F32), S((tokens, inner), BF16), S((tokens, inner), BF16), S((inner, states), F32),
                    S((1, inner), F32), S((1, inner), F32)],
     )
 
 
-def bwd_local(heads, size, gy, mixed, krs, cum, steps, cT, gram, entry, enter, aux, segrow, qloc, dec, cid, after):
+def bwd_local(heads, size, gy, mixed, krs, cum, steps, cT, gram, entry, enter, aux, segrow, qloc, dec, cid, gb, scaled, nx, gz, under_way, also):
     tokens, inner = gy.shape
+    d = gb.shape[1]
     two = krs.shape[1]
     rows, states = qloc.shape
     bits = bits_of("seq")
-    return kcall(
-        partial(bwd_local_body, partial(carry_stages, bits, True, heads, size), size),
-        [gy, mixed, krs, cum, steps, cT, gram, entry, enter, aux, segrow, qloc, dec],
+    blocks = lax.axis_size("seq")
+    part = (blocks // 2, d // blocks, inner)
+    out, z = Halving(OUT_ORDER), Halving(Z_ORDER)
+    folds = [p.plan() for p in under_way]
+    pairs = [x for p in under_way for x in (p.got, p.keep)]
+    shapes = [(p.keep.shape[0] // 2,) + p.keep.shape[1:] for p in under_way for _ in range(2)]
+    got = kcall(
+        partial(bwd_local_body, partial(carry_stages, bits, True, heads, size), size, blocks, (out.order[0], z.order[0]), folds),
+        [gy, mixed, krs, cum, steps, cT, gram, entry, enter, aux, segrow, qloc, dec, gb, scaled, nx, gz] + pairs,
         [cols(tokens), cols(tokens), full(krs.shape), full(cum.shape), full(steps.shape), full(cT.shape), full(gram.shape),
          cols(tokens), rowsb(two // 2), pl.BlockSpec((None, tokens, LANE), lambda p: (5, 0, 0)), full(segrow.shape),
-         full(qloc.shape), full(dec.shape)], 20, after, cid,
+         full(qloc.shape), full(dec.shape), full(gb.shape), full(scaled.shape), full(nx.shape), full(gz.shape)]
+        + [full(x.shape) for x in pairs], 24, [p.got for p in also], cid,
         name="bwd_local",
         grid=(inner // LANE,),
-        out_specs=[cols(tokens), full((tokens, LANE)), full((LANE, tokens)), full((tokens, two)), full((rows, states))],
-        out_shape=[S((tokens, inner), F32), S((tokens, LANE), F32), S((LANE, tokens), F32), S((tokens, two), F32), S((rows, states), F32)],
+        out_specs=[cols(tokens), full((tokens, LANE)), full((LANE, tokens)), full((tokens, two)), full((rows, states))]
+        + [full(part)] * 4 + [full(x) for x in shapes],
+        out_shape=[S((tokens, inner), F32), S((tokens, LANE), F32), S((LANE, tokens), F32), S((tokens, two), F32), S((rows, states), F32)]
+        + [S(part, BF16)] * 4 + [S(x, BF16) for x in shapes],
         scratch_shapes=[pltpu.VMEM((tokens, LANE), F32), pltpu.VMEM((tokens, LANE), F32), pltpu.VMEM((tokens, tokens), F32),
-                        pltpu.VMEM((tokens, tokens), F32), pltpu.VMEM((tokens, LANE), BF16), pltpu.VMEM((tokens, LANE), BF16)]
+                        pltpu.VMEM((tokens, tokens), F32), pltpu.VMEM((tokens, LANE), BF16), pltpu.VMEM((tokens, LANE), BF16),
+                        pltpu.VMEM((d, tokens), BF16)]
         + carry_scratch(len(bits), rows, states, BF16),
     )
+    out.away, out.keep, z.away, z.keep = got[5:9]
+    for i, p in enumerate(under_way):
+        p.away, p.keep = got[9 + 2 * i : 11 + 2 * i]
+    return got[:5], out, z
 
 
 def bwd_carry(l, size, gy, dvd, mixed, carr, entry, krs, cum, steps, pdt, q, ux, aux, later, enter, dd, rowT, dkr, decl, after):
@@ -1139,11 +1239,11 @@
     tokens = gz.shape[0]
     d = h_own.shape[1]
     return kcall(
-        partial(head_bwd_body, l, tokens), [gz, gu, small, q["w_zx"], q["w_small"], h_own, q["gain"], g_own, branch],
+        partial(head_bwd_body, l, l > 0, tokens), [gz, gu, small, q["w_zx"], q["w_small"], h_own, q["gain"], g_own, branch],
         [VM, VM, VM, pl.BlockSpec(memory_space=pl.ANY), VM, VM, VM, VM, VM], 29, after, cid,
         name="head_bwd",
         out_specs=[VM] * 4,
-        out_shape=[S((tokens, d), BF16), S((tokens // 4, d), F32), S((1, d), F32), S((32, LANE), F32)],
+        out_shape=[S((tokens if l > 0 else tokens // 4, d), BF16), S((tokens // 4, d), F32), S((1, d), F32), S((32, LANE), F32)],
         scratch_shapes=head_scratch(tokens, d) + [pltpu.VMEM(q["w_zx"].shape[1:], BF16), pltpu.SemaphoreType.DMA((1,))],
     )
 
@@ -1158,14 +1258,15 @@
         name="maps_bwd",
         out_specs=[VM] * 3,
         out_shape=[S((tokens, LANE), BF16), S((8, LANE), F32), S((16, inner), BF16)],
-        scratch_shapes=[tile, tile, tile, tile, tile, pltpu.VMEM((tokens + HALO, LANE), F32), pltpu.VMEM((tokens + 8, LANE), F32),
+        scratch_shapes=[pltpu.VMEM((tokens, LANE), BF16)] * 2 + [tile, tile, tile, pltpu.VMEM((tokens + HALO, LANE), F32), pltpu.VMEM((tokens + 8, LANE), F32),
                         pltpu.VMEM((8, inner), F32), pltpu.VMEM((8, LANE), F32), pltpu.VMEM((8, LANE), F32),
                         pltpu.SemaphoreType.DMA((4,)), pltpu.SemaphoreType.DMA((4,))],
     )
 
 
-def tail(sums, smalls, inner, d, cid):
+def tail(sums, smalls, low, inner, cid):
     parts = len(smalls)
+    quarter, d = low.shape
     plan = [(left, steps) for _, _, left, steps in sums]
     heads, n = len(bits_of("head")), len(bits_of("seq"))
     arrays, scratch, outs = [], [], []
@@ -1179,35 +1280,15 @@
             scratch += [buf, pltpu.VMEM((blocks, block, width), F32), buf]
         scratch += [pltpu.SemaphoreType.DMA((max(len(steps), 1),))] * 2
     return kcall(
-        partial(tail_body, parts, plan), arrays + [x for part in smalls for x in part], [VM] * (2 * len(sums) + 6 * parts), 45, (), cid,
+        partial(tail_body, parts, plan), arrays + [x for part in smalls for x in part] + [low], [VM] * (2 * len(sums) + 6 * parts + 1), 45, (), cid,
         name="tail",
-        out_specs=[VM] * (len(sums) + 6),
-        out_shape=outs + [S((parts, CONV + 1, inner), F32), S((parts, CONV + 1, 2 * LANE), F32), S((parts, inner), F32), S((parts, inner), F32),
+        out_specs=[VM] * (len(sums) + 7),
+        out_shape=outs + [S((4 * quarter, d), BF16), S((parts, CONV + 1, inner), F32), S((parts, CONV + 1, 2 * LANE), F32), S((parts, inner), F32), S((parts, inner), F32),
                           S((parts, 2 * LANE), F32), S((parts, d), F32)],
         scratch_shapes=[pltpu.VMEM((parts, 16, inner), F32), pltpu.VMEM((n, parts, 16, inner), F32), pltpu.VMEM((heads, parts, 8, inner), F32),
-                        pltpu.SemaphoreType.DMA((heads + n,)), pltpu.SemaphoreType.DMA((heads + n,))] + scratch,
+                        pltpu.SemaphoreType.DMA((heads + n,)), pltpu.SemaphoreType.DMA((heads + n,))] + scratch
+        + [pltpu.SemaphoreType.DMA((3,)), pltpu.SemaphoreType.DMA((3,))],
     )
-
-
-def wgrad_body(blocks, bit, off, n_rhs, lhs, *refs):
-    rhs, (away, keep, lt) = refs[:n_rhs], refs[n_rhs:]
-    tokens = rhs[0].shape[0]
-    lt[...] = jnp.transpose(lhs[pl.ds(off, tokens), :])
-    mine = (lax.axis_index("seq") // bit) % 2
-    block = lt.shape[0] // blocks
-
-    def one(k, carry):
-        for dst, want in ((away, 1 - mine), (keep, mine)):
-            at = (k // bit) * (2 * bit) + want * bit + lax.rem(k, bit)
-            rows = lt[pl.ds(pl.multiple_of(at * block, 16), block), :]
-            c = 0
-            for r in rhs:
-                w = r.shape[1]
-                dst[k, :, c : c + w] = bdot(rows, r[...], NN).astype(BF16)
-                c += w
-        return carry
-
-    lax.fori_loop(0, blocks // 2, one, 0)
 
 
 def wgrad(lhs, rhs, bit, after=()):
@@ -1226,42 +1307,35 @@
 
 
 class Halving:
-    def __init__(self, lhs, rhs, order, after=()):
+    def __init__(self, order):
         bits = bits_of("seq")
         self.order = [bits[i % len(bits)] for i in order] + [b for i, b in enumerate(bits) if i not in order]
-        self.left = [b for b in reversed(bits)]
-        self.away, self.keep = wgrad(lhs, rhs, self.order[0], after)
-        self.left.remove(self.order[0])
+        self.left = [b for b in reversed(bits) if b != self.order[0]]
         self.step = 0
-        self.got = None
+        self.got = self.away = self.keep = None
+
+    def plan(self):
+        bit = self.order[self.step]
+        stride = 1 << (len(self.left) - 1 - self.left.index(bit))
+        self.left.remove(bit)
+        return bit, stride
 
     def go(self):
         self.got = swap(self.away, "seq", self.order[self.step])
         self.step += 1
-        return self.got
 
     def rest(self):
-        shape = (-1,) + self.keep.shape[-2:]
-        return self.got.reshape(shape), self.keep.reshape(shape), tuple(self.left), tuple(self.order[self.step :])
-
-    def fold(self):
-        total = self.keep.astype(F32) + self.got.astype(F32)
-        if self.step == len(self.order):
-            self.total = total[0] if total.ndim == 3 else total
-            return self.total
-        bit = self.order[self.step]
-        axis = self.left.index(bit)
-        view = total.reshape((2,) * len(self.left) + total.shape[-2:])
-        me = my_bit("seq", bit)
-        pick = lambda i: take(view, axis, i).astype(BF16).reshape((-1,) + total.shape[-2:])
-        self.away, self.keep = pick(1 - me), pick(me)
-        self.left.remove(bit)
-
-    def finish(self):
-        while self.step < len(self.order):
-            self.go()
-            self.fold()
-        return self.total
+        return self.got, self.keep, tuple(self.left), tuple(self.order[self.step :])
+
+    def fold(self, after=()):
+        bit, stride = self.plan()
+        blocks, block, width = self.keep.shape
+        self.away, self.keep = kcall(
+            partial(fold_body, bit, stride), [self.got, self.keep], [VM] * 2, 2, after,
+            name="fold",
+            out_specs=[VM] * 2,
+            out_shape=[S((blocks // 2, block, width), BF16)] * 2,
+        )
 
 
 def pad_lanes(x, to=LANE):
@@ -1270,8 +1344,8 @@
 
 def forward_layer(nx, h_own, extra, q, aux, segrow, layer):
     heads, size, inner = q["heads"], q["size"], q["inner"]
-    (gate, ux, ubc, krs, pdt, steps, cum, cT, gram, mixed, entry, state, dec, decl) = fwd_mix(layer, size, nx, q, aux, segrow)
-    ypart, enter = fwd_inside(layer, heads, size, mixed, steps, cum, cT, gram, q, state, dec, layer)
+    (ux, ubc, krs, pdt, steps, cum, cT, gram, mixed, entry, state, dec, decl) = fwd_mix(layer, size, nx, q, aux, segrow)
+    ypart, enter, gate = fwd_inside(layer, heads, size, nx, mixed, steps, cum, cT, gram, q, state, dec, layer)
     y, carr, gated, sq = fwd_gate(ypart, entry, gate, krs, enter)
     width = inner * lax.axis_size("head")
     nx_next, h_new, branch, r2b, side = head_fwd(layer, gated, sq, q, h_own, extra, layer == LAYERS - 1, width, LAYERS + layer)
@@ -1311,7 +1385,7 @@
              w_small=w_small, conv_x=conv_x, conv_bc=conv_bc, dt_bias=pad_lanes(dt_bias[:, None, :]), a_log=pad_lanes(a_log[:, None, :]),
              skip=jnp.repeat(skip_d, size, axis=1)[:, None, :], gate_gain=gate_gain[:, None, :], w_out=w_out)
     h = hidden_in.astype(F32)
-    h_own = own_rows(h)
+    h_own = own_rows(hidden_in).astype(F32)
     cot_own = own_rows(cot)
     normed = (h * lax.rsqrt(jnp.mean(h * h, axis=1, keepdims=True) + EPS) * norm_gain[0][None]).astype(BF16)
     nx = jnp.concatenate([shift(normed[tokens - HALO :], "seq", 1), normed], 0)
@@ -1329,37 +1403,39 @@
     for l in reversed(range(LAYERS)):
         s = stored[l]
         gy, gz, scaled, qloc, ggate, gskip = backward_gate(gb, side, s, q, l)
-        dvd, dd, rowT, dkr, later = bwd_local(heads, size, gy, s["mixed"], s["krs"], s["cum"], s["steps"], s["cT"], s["gram"], s["entry"], s["enter"],
-                                              aux, segrow, qloc, s["dec"], 2 * LAYERS + l, [p.got for p in pending])
-        for p in pending:
-            p.fold()
+        (dvd, dd, rowT, dkr, later), out, z = bwd_local(
+            heads, size, gy, s["mixed"], s["krs"], s["cum"], s["steps"], s["cT"], s["gram"], s["entry"], s["enter"], aux, segrow, qloc,
+            s["dec"], 2 * LAYERS + l, gb, scaled, s["nx"], gz, pending[:2], pending[2:])
+        for p in pending[:2]:
             p.go()
-        out = Halving(gb, [scaled], (0, 1, 2), after=[later])
-        z = Halving(s["nx"], [gz], Z_ORDER, after=[later])
         out.go()
         z.go()
         gm8, gu, gtail, gtaps_x, gdt, gvec, dkr = bwd_carry(
             l, size, gy, dvd, s["mixed"], s["carr"], s["entry"], s["krs"], s["cum"], s["steps"], s["pdt"], q, s["ux"], aux, later, s["enter"],
-            dd, rowT, dkr, s["decl"], [out.away, z.away])
+            dd, rowT, dkr, s["decl"], ())
         small, gtaps_bc, gtail = maps_bwd(l, dkr, s["ubc"], q, aux, gdt, gtail, gm8, 3 * LAYERS + l)
         gu = lax.dynamic_update_slice(gu, gtail, (tokens - 16, 0))
-        x = Halving(s["nx"], [gu, small], (0, 1, 2))
+        x = Halving((0, 1, 2))
+        x.away, x.keep = wgrad(s["nx"], [gu, small], x.order[0])
         x.go()
         out.fold()
         z.fold()
         z.go()
         out.go()
+        if pending:
+            pending[2].fold()
+            pending[2].go()
         before = stored[max(l - 1, 0)]["branch"]
-        gb, g_own, g_gain, side = head_bwd(l, gz, gu, small, q, s["h_own"], g_own, before, 4 * LAYERS + l, after=[x.away, out.away, z.away])
+        gb, g_own, g_gain, side = head_bwd(l, gz, gu, small, q, s["h_own"], g_own, before, 4 * LAYERS + l, after=[p.away for p in [x, out, z] + pending[2:]])
         smalls[l] = (gtaps_x, ggate, gskip, gvec, gtaps_bc, g_gain)
         pending = [out, z, x]
         sums[l] = pending
-    grad_in = gb.astype(F32)
     under_way = [p for l in range(LAYERS) for p in reversed(sums[l])]
-    done = tail([p.rest() for p in under_way], smalls, inner, norm_gain.shape[1], 5 * LAYERS)
+    done = tail([p.rest() for p in under_way], smalls, gb, inner, 5 * LAYERS)
     for p, total in zip(under_way, done):
         p.total = total
-    g_conv_x, g_conv_bc, g_gate, g_skip, g_vec, g_gain = done[len(under_way) :]
+    grad_in, g_conv_x, g_conv_bc, g_gate, g_skip, g_vec, g_gain = done[len(under_way) :]
+    grad_in = grad_in.astype(F32)
     g_w_zx = jnp.stack([jnp.stack([z.total, x.total[:, :inner]], 1) for _, z, x in sums], 0)
     g_small = jnp.stack([x.total[:, inner:] for _, _, x in sums], 0)
     g_w_bc = jnp.where(even, g_small[:, :, : LANE // 2], g_small[:, :, LANE // 2 :])

time: 566 us -> 537 us (0.949)
  Pallas kernels: 469 us -> 443 us
  local copies, waits for them, and re-layouts: 45.2 us -> 39 us
  waiting for transfers between devices: 0.27 us -> 6.02 us
    pallas_call x25 -> x26, Pallas kernels: 469 us -> 443 us  [kcall(): pl.pallas_call(wrapped, in_specs=list(specs) + [pl.BlockSpec(memory_space...]
    ppermute x13, waiting for transfers between devices: 0.26 us -> 6.02 us  [swap(): return lax.ppermute(x, axis, [(i, i ^ bit) for i in range(n)])]
    unnamed x107 -> x89, local copies, waits for them, and re-layouts: 24 us -> 25 us
  transfers between devices with their start and end apart: 14 -> 14, of which waited for: 1 -> 3; matrix products, arithmetic and copies ran while one was open for 7% -> 5% of each run, Pallas kernels for 32% -> 33%
where the time goes in v4:
time: 537 us; the launch traced here: 528 us
  Pallas kernels  443 us (82%)
  local copies, waits for them, and re-layouts  39 us (7%)
  other arithmetic  19.5 us (4%)
  starting transfers between devices  18.8 us (4%)
  waiting for transfers between devices  6.02 us (1%)
    pallas_call x26, Pallas kernels, kcall(): pl.pallas_call(wrapped, in_specs=list(specs) + [pl.BlockSpec(memory_space...  443 us
    unnamed x89, local copies, waits for them, and re-layouts  25 us
    ppermute x13, starting transfers between devices, swap(): return lax.ppermute(x, axis, [(i, i ^ bit) for i in range(n)])  14 us
  transfers between devices with their start and end apart: 14, of which 3 were waited for; matrix products, arithmetic and copies ran while one was open for 5% of the time, Pallas kernels for 33%

profile of v4, /device:TPU:0, one launch (start us, length us, event | category | flops | bytes accessed | tf_op | source)
XLA Modules:
  0.0 528.2 jit_solution(13968046358308139286)
XLA Ops:
  0.7 1.9 fusion
  2.6 0.7 slice_reduce_fusion
  3.8 1.1 copy-done.1
  4.9 4.8 collective-permute-start
  10.9 1.0 dynamic-slice_convert_fusion.refs_4_.refs_5_
  12.0 2.1 fusion.15
  14.2 3.0 select_select_fusion
  17.1 1.4 fusion.11
  22.8 8.7 %copy.70 = bf16[2,1536,2,768]{3,1,2,0:T(8,128)(2,1)} copy(bf16[2,1536,2,768]{3,2,1,0:T(2,128)(2,1)} %param.18) | data formatting | bytes 18874368 | tf_op args[4]
  31.5 1.3 pad_maximum_fusion.1.refs_0_.refs_15_
  32.8 1.6 broadcast_in_dim.35.refs_8_.refs_9_.refs_14_.refs_3_
  34.4 15.3 %fwd_mix.2 = (bf16[528,768]{1,0:T(8,128)(2,1)}, bf16[528,256]{1,0:T(8,128)(2,1)}, f32[512,256]{1,0:T(8,128)}, bf16[512,128]{1,0:T(8,128)(2,1)}, f32[512,128]{1,0...) custom-call(bf16[528,1536]{1,0:T(8,128)(2,1)} %pad_maximum_fusion.1., ...), custom_call_target="tpu_custom_call" | custom-call | flops 12000000000 | bytes 36000000 | tf_op jit(solution)/shard_map/fwd_mix/pallas_call | solution.py:1087
  49.7 30.4 %fwd_inside.2 = (f32[512,768]{1,0:T(8,128)}, f32[768,128]{1,0:T(8,128)}, bf16[512,768]{1,0:T(8,128)(2,1)}) custom-call(bf16[528,1536]{1,0:T(8,128)(2,1)} %pad_maximum_fusion.1.refs_0_.refs_15_, bf16[2,2,1536,768]{3,2,1,0:T(8,128)(2,1)} %bitcast.42, f32[512,768]{1,0:T(8,128)} %get-tuple-element.147.refs_2_.refs_4_.refs_1_, ...), custom_call_target="tpu_custom_call" | custom-call | flops 28000000000 | bytes 84000000 | tf_op jit(solution)/shard_map/fwd_inside/pallas_call | solution.py:1087
  80.2 6.3 %fwd_gate.2 = (f32[512,768]{1,0:T(8,128)}, f32[512,768]{1,0:T(8,128)}, f32[512,768]{1,0:T(8,128)}, f32[8,512]{1,0:T(8,128)}) custom-call(f32[512,768]{1,0:T(8,128)} %get-tuple-element.154.refs_0_, f32[512,768]{1,0:T(8,128)} %get-tuple-element.155.refs_1_.refs_5_.refs_7_.refs_4_, bf16[512,768]{1,0:T(8,128)(2,1)} %get-tuple-element.156.refs_2_, ...), custom_call_target="tpu_custom_call" | custom-call | flops 7000000000 | bytes 21000000 | tf_op jit(solution)/shard_map/fwd_gate/pallas_call | solution.py:1087
  86.5 41.2 %head_fwd.1 = (bf16[528,1536]{1,0:T(8,128)(2,1)}, f32[128,1536]{1,0:T(8,128)}, f32[128,1536]{1,0:T(8,128)}, f32[512,128]{1,0:T(8,128)}, f32[32,128]{1,0:T(8,128)}) custom-call(f32[512,768]{1,0:T(8,128)} %get-tuple-element.159.refs_0_, f32[8,512]{1,0:T(8,128)} %get-tuple-element.160.refs_1_, f32[2,1,768]{2,1,0:T(1,128)} %broadcast_in_dim.37.refs_2_.refs_9_, ...), custom_call_target="tpu_custom_call" | custom-call | flops 30000001024 | bytes 90000000 | tf_op jit(solution)/shard_map/head_fwd/pallas_call | solution.py:1087
  127.7 15.5 %fwd_mix.3 = (bf16[528,768]{1,0:T(8,128)(2,1)}, bf16[528,256]{1,0:T(8,128)(2,1)}, f32[512,256]{1,0:T(8,128)}, bf16[512,128]{1,0:T(8,128)(2,1)}, f32[512,128]{1,0...) custom-call(bf16[528,1536]{1,0:T(8,128)(2,1)} %get-tuple-element.161, ...), custom_call_target="tpu_custom_call" | custom-call | flops 12000000000 | bytes 36000000 | tf_op jit(solution)/shard_map/fwd_mix/pallas_call | solution.py:1087
  143.2 33.3 %fwd_inside.3 = (f32[512,768]{1,0:T(8,128)}, f32[768,128]{1,0:T(8,128)}, bf16[512,768]{1,0:T(8,128)(2,1)}) custom-call(bf16[528,1536]{1,0:T(8,128)(2,1)} %get-tuple-element.161.refs_0_.refs_15_, bf16[2,2,1536,768]{3,2,1,0:T(8,128)(2,1)} %bitcast.44, f32[512,768]{1,0:T(8,128)} %get-tuple-element.162.refs_2_.refs_4_.refs_1_, ...), custom_call_target="tpu_custom_call" | custom-call | flops 28000000000 | bytes 84000000 | tf_op jit(solution)/shard_map/fwd_inside/pallas_call | solution.py:1087
  176.5 6.3 %fwd_gate.3 = (f32[512,768]{1,0:T(8,128)}, f32[512,768]{1,0:T(8,128)}, f32[512,768]{1,0:T(8,128)}, f32[8,512]{1,0:T(8,128)}) custom-call(f32[512,768]{1,0:T(8,128)} %get-tuple-element.169.refs_0_, f32[512,768]{1,0:T(8,128)} %get-tuple-element.170.refs_1_.refs_5_.refs_7_.refs_4_, bf16[512,768]{1,0:T(8,128)(2,1)} %get-tuple-element.171.refs_2_, ...), custom_call_target="tpu_custom_call" | custom-call | flops 7000000000 | bytes 21000000 | tf_op jit(solution)/shard_map/fwd_gate/pallas_call | solution.py:1087
  182.8 29.7 %head_fwd_last.1 = (bf16[512,1536]{1,0:T(8,128)(2,1)}, f32[128,1536]{1,0:T(8,128)}, f32[128,1536]{1,0:T(8,128)}, f32[512,128]{1,0:T(8,128)}, f32[32,128]{1,0:T(8,128)}) custom-call(f32[512,768]{1,0:T(8,128)} %get-tuple-element.174.refs_0_, f32[8,512]{1,0:T(8,128)} %get-tuple-element.175.refs_1_, f32[2,1,768]{2,1,0:T(1,128)} %broadcast_in_dim.37.refs_2_.refs_9_, ...), custom_call_target="tpu_custom_call" | custom-call | flops 30000001024 | bytes 90000000 | tf_op jit(solution)/shard_map/head_fwd_last/pallas_call | solution.py:1087
  213.2 1.8 multiply_multiply_fusion.1.refs_8_
  215.0 8.1 %bwd_gate.2 = (f32[512,768]{1,0:T(8,128)}, bf16[512,768]{1,0:T(8,128)(2,1)}, bf16[512,768]{1,0:T(8,128)(2,1)}, f32[768,128]{1,0:T(8,128)}, f32[1,768]{1,0:T(1,128)}, /*index=5*/f32[1,768]{1,0:T(1,128)}) custom-call(bf16[512,1536]{1,0:T(8,128)(2,1)} %refs_13_.3, bf16[2,768,1536]{2,1,0:T(8,128)(2,1)} %refs_1_.3, bf16[512,768]{1,0:T(8,128)(2,1)} %get-tuple-element.171.refs_2_, ...), custom_call_target="tpu_custom_call" | custom-call | flops 8999999488 | bytes 27000000 | tf_op jit(solution)/shard_map/bwd_gate/pallas_call | solution.py:1087
  223.1 26.0 %bwd_local.2 = (f32[512,768]{1,0:T(8,128)}, f32[512,128]{1,0:T(8,128)}, f32[128,512]{1,0:T(8,128)}, f32[512,256]{1,0:T(8,128)}, f32[768,128]{1,0:T(8,128)}, /*in...) custom-call(f32[512,768]{1,0:T(8,128)} %get-tuple-element.182.refs_0, ...), custom_call_target="tpu_custom_call" | custom-call | flops 24000000000 | bytes 72000000 | tf_op jit(solution)/shard_map/bwd_local/pallas_call | solution.py:1087
  249.1 1.2 collective-permute-start.1
  250.3 12.0 %bwd_carry.2 = (f32[8,768]{1,0:T(8,128)}, bf16[512,768]{1,0:T(8,128)(2,1)}, f32[16,768]{1,0:T(8,128)}, f32[8,768]{1,0:T(8,128)}, bf16[512,128]{1,0:T(8,128)(2,1)}, /*index=5*/f32[8,128]{1,0:T(8,128)}, f32[512,256]{1,0:T(8,128)}) custom-call(f32[512,768]{1,0:T(8,128)} %get-tuple-element.182.refs_0_, f32[512,768]{1,0:T(8,128)} %get-tuple-element.185.refs_1_, ...), custom_call_target="tpu_custom_call" | custom-call | flops 11000000512 | bytes 33000000 | tf_op jit(solution)/shard_map/bwd_carry/pallas_call | solution.py:1087
  262.3 15.8 %maps_bwd.2 = (bf16[512,128]{1,0:T(8,128)(2,1)}, f32[8,128]{1,0:T(8,128)}, bf16[16,768]{1,0:T(8,128)(2,1)}) custom-call(f32[512,256]{1,0:T(8,128)} %get-tuple-element.195.refs_0_, bf16[528,256]{1,0:T(8,128)(2,1)} %get-tuple-element.196.refs_1_, f32[2,5,256]{2,1,0:T(8,128)} %copy.51.refs_5_.refs_2_, ...), custom_call_target="tpu_custom_call" | custom-call | flops 14000000000 | bytes 42000000 | tf_op jit(solution)/shard_map/maps_bwd/pallas_call | solution.py:1087
  278.1 1.3 constant_dynamic-update-slice_fusion.1.refs_1_
  279.4 4.8 wgrad.2
  284.2 2.7 collective-permute-start.5
  286.9 1.0 copy-done.31
  287.9 2.9 fold.5
  290.8 1.0 copy-done.29
  291.8 2.9 fold.6
  295.0 29.8 %head_bwd.2 = (bf16[512,1536]{1,0:T(8,128)(2,1)}, f32[128,1536]{1,0:T(8,128)}, f32[1,1536]{1,0:T(1,128)}, f32[32,128]{1,0:T(8,128)}) custom-call(bf16[512,768]{1,0:T(8,128)(2,1)} %get-tuple-element.181.refs_16_.refs_0_, bf16[512,768]{1,0:T(8,128)(2,1)} %constant_dynamic-update-slice_fusion.1.refs_1_, bf16[512,128]{1,0:T(8,128)(2,1)} %get-tuple-element.201.refs_2_, ...), custom_call_target="tpu_custom_call" | custom-call | flops 28999999488 | bytes 87000000 | tf_op jit(solution)/shard_map/head_bwd/pallas_call | solution.py:1087
  325.6 0.8 multiply_multiply_fusion.refs_8_
  326.4 8.2 %bwd_gate.3 = (f32[512,768]{1,0:T(8,128)}, bf16[512,768]{1,0:T(8,128)(2,1)}, bf16[512,768]{1,0:T(8,128)(2,1)}, f32[768,128]{1,0:T(8,128)}, f32[1,768]{1,0:T(1,128)}, /*index=5*/f32[1,768]{1,0:T(1,128)}) custom-call(bf16[512,1536]{1,0:T(8,128)(2,1)} %get-tuple-element.210.refs_0_.refs_13_, bf16[2,768,1536]{2,1,0:T(8,128)(2,1)} %refs_1_.3, ...), custom_call_target="tpu_custom_call" | custom-call | flops 8999999488 | bytes 27000000 | tf_op jit(solution)/shard_map/bwd_gate/pallas_call | solution.py:1087
  334.7 1.1 copy-done.27
  335.8 3.0 fold.9
  338.8 2.0 collective-permute-start.11
  340.9 0.8 copy-done.34
  341.9 32.5 %bwd_local.3 = (f32[512,768]{1,0:T(8,128)}, f32[512,128]{1,0:T(8,128)}, f32[128,512]{1,0:T(8,128)}, f32[512,256]{1,0:T(8,128)}, f32[768,128]{1,0:T(8,128)}, /*in...) custom-call(f32[512,768]{1,0:T(8,128)} %get-tuple-element.214.refs_0, ...), custom_call_target="tpu_custom_call" | custom-call | flops 24000000000 | bytes 72000000 | tf_op jit(solution)/shard_map/bwd_local/pallas_call | solution.py:1087
  374.8 2.6 collective-permute-start.7
  377.4 1.3 collective-permute-start.9
  378.7 12.0 %bwd_carry.3 = (f32[8,768]{1,0:T(8,128)}, bf16[512,768]{1,0:T(8,128)(2,1)}, f32[16,768]{1,0:T(8,128)}, f32[8,768]{1,0:T(8,128)}, bf16[512,128]{1,0:T(8,128)(2,1)}, /*index=5*/f32[8,128]{1,0:T(8,128)}, f32[512,256]{1,0:T(8,128)}) custom-call(f32[512,768]{1,0:T(8,128)} %get-tuple-element.214.refs_0_, f32[512,768]{1,0:T(8,128)} %get-tuple-element.220.refs_1_, ...), custom_call_target="tpu_custom_call" | custom-call | flops 11000000512 | bytes 33000000 | tf_op jit(solution)/shard_map/bwd_carry/pallas_call | solution.py:1087
  390.7 19.0 %maps_bwd.3 = (bf16[512,128]{1,0:T(8,128)(2,1)}, f32[8,128]{1,0:T(8,128)}, bf16[16,768]{1,0:T(8,128)(2,1)}) custom-call(f32[512,256]{1,0:T(8,128)} %get-tuple-element.230.refs_0_, bf16[528,256]{1,0:T(8,128)(2,1)} %get-tuple-element.231.refs_1_, f32[2,5,256]{2,1,0:T(8,128)} %copy.51.refs_5_.refs_2_, ...), custom_call_target="tpu_custom_call" | custom-call | flops 14000000000 | bytes 42000000 | tf_op jit(solution)/shard_map/maps_bwd/pallas_call | solution.py:1087
  409.7 1.4 constant_dynamic-update-slice_fusion.refs_1_
  411.1 4.8 wgrad.3
  415.8 2.5 collective-permute-start.6
  418.3 2.8 fold.7
  422.2 2.8 fold.8
  425.5 19.4 %head_bwd.3 = (bf16[128,1536]{1,0:T(8,128)(2,1)}, f32[128,1536]{1,0:T(8,128)}, f32[1,1536]{1,0:T(1,128)}, f32[32,128]{1,0:T(8,128)}) custom-call(bf16[512,768]{1,0:T(8,128)(2,1)} %get-tuple-element.217.refs_16_.refs_0_, bf16[512,768]{1,0:T(8,128)(2,1)} %constant_dynamic-update-slice_fusion.refs_1_, bf16[512,128]{1,0:T(8,128)(2,1)} %get-tuple-element.236.refs_2_, ...), custom_call_target="tpu_custom_call" | custom-call | flops 28999999488 | bytes 87000000 | tf_op jit(solution)/shard_map/head_bwd/pallas_call | solution.py:1087
  445.0 2.1 collective-permute-done.6.refs_0_
  447.7 3.3 collective-permute-done.10.refs_4_
  451.0 0.8 copy-done.35
  451.9 58.5 %tail.1 = (f32[192,896]{1,0:T(8,128)}, f32[192,768]{1,0:T(8,128)}, f32[192,768]{1,0:T(8,128)}, f32[192,896]{1,0:T(8,128)}, f32[192,768]{1,0:T(8,128)}, /*index=5...) custom-call(bf16[4,192,896]{2,1,0:T(8,128)(2,1)} %copy-done.26, ...), custom_call_target="tpu_custom_call" | custom-call | flops 44999999488 | bytes 135000000 | tf_op jit(solution)/shard_map/tail/pallas_call | solution.py:1087
  510.4 1.0 slice_bitcast_fusion.3
  511.4 1.2 slice_bitcast_fusion.1
  512.5 0.9 slice_bitcast_fusion.2
  516.7 3.2 copy.64
  519.9 0.8 copy.65
  520.7 0.7 copy.66
  521.4 2.1 convert_element_type.33
  523.5 1.4 constant_dynamic-slice_fusion
  524.9 1.1 pad_maximum_fusion.2
  526.0 1.1 copy.75
  (122 shorter events, 14.4 us)
Async XLA Ops:
  0.6 2.7 copy-start
  3.3 6.5 %copy-start.18 = (s32[512]{0:T(512)S(1)}, s32[512]{0:T(512)}, u32[]{:S(2)}) copy-start(s32[512]{0:T(512)} %param.15) | copy-start | bytes 6148
  3.3 7.1 %copy-start.11 = (bf16[2,1536,12]{1,0,2:T(2,128)(2,1)S(1)}, bf16[2,1536,12]{1,0,2:T(2,128)(2,1)}, u32[]{:S(2)}) copy-start(bf16[2,1536,12]{1,0,2:T(2,128)(2,1)} %param.20) | copy-start | bytes 221188
  3.8 1.1 copy-start.1
  4.9 26.6 %collective-permute-start = (bf16[16,1536]{1,0:T(8,128)(2,1)S(1)}, bf16[16,1536]{1,0:T(8,128)(2,1)S(1)}, u32[]{:S(2)}, u32[]{:S(2)}) collective-permute-start(bf16[16,1536]{1,0:T(8,128)(2,1)S(1)} %slice.84), channel_id=1, source_target_pairs={{0,4},{4,8},{8,12},{12,16},{16,20},{20,24},{24,28},{1,5},{5,9},{9,... | collective-permute-start | bytes 147464 | tf_op jit(solution)/shard_map/ppermute | solution.py:42
  9.8 21.7 %copy-start.15 = (f32[512]{0:T(512)}, f32[512]{0:T(512)S(1)}, u32[]{:S(2)}) copy-start(f32[512]{0:T(512)S(1)} %convert_element_type.30) | copy-start | bytes 6148
  14.1 4.4 copy-start.14
  14.1 5.0 copy-start.24
  14.1 5.5 %copy-start.25 = (f32[2,12]{1,0:T(2,128)S(1)}, f32[2,12]{1,0:T(2,128)}, u32[]{:S(2)}) copy-start(f32[2,12]{1,0:T(2,128)} %param.24) | copy-start | bytes 292
  14.1 6.1 %copy-start.19 = (f32[2,768]{1,0:T(2,128)S(1)}, f32[2,768]{1,0:T(2,128)}, u32[]{:S(2)}) copy-start(f32[2,768]{1,0:T(2,128)} %param.26) | copy-start | bytes 18436
  14.1 6.7 %copy-start.17 = (f32[2,5,256]{2,0,1:T(2,128)S(1)}, f32[2,5,256]{2,0,1:T(2,128)}, u32[]{:S(2)}) copy-start(f32[2,5,256]{2,0,1:T(2,128)} %param.22) | copy-start | bytes 30724
  14.1 7.3 %copy-start.23 = (f32[2,12]{1,0:T(2,128)S(1)}, f32[2,12]{1,0:T(2,128)}, u32[]{:S(2)}) copy-start(f32[2,12]{1,0:T(2,128)} %param.25) | copy-start | bytes 292
  14.2 8.0 %copy-start.13 = (f32[2,5,768]{2,0,1:T(2,128)S(1)}, f32[2,5,768]{2,0,1:T(2,128)}, u32[]{:S(2)}) copy-start(f32[2,5,768]{2,0,1:T(2,128)} %param.21) | copy-start | bytes 92164
  22.8 8.7 %copy-start.2 = (bf16[512,1536]{1,0:T(8,128)(2,1)S(1)}, bf16[512,1536]{1,0:T(8,128)(2,1)}, u32[]{:S(2)}) copy-start(bf16[512,1536]{1,0:T(8,128)(2,1)} %copy-done.1) | copy-start | bytes 4718596
  249.1 37.8 %collective-permute-start.1 = (bf16[4,192,768]{2,1,0:T(8,128)(2,1)}, bf16[4,192,768]{2,1,0:T(8,128)(2,1)S(1)}, u32[]{:S(2)}, u32[]{:S(2)}) collective-permute-start(bf16[4,192,768]{2,1,0:T(8,128)(2,1)} %get-tuple-element.204), channel_id=1, source_target_pairs={{0,4},{4,0},{8,12},{12,8},{16,20},{20,16},{24,28},{28,24},{1,5},{5... | collective-permute-start | bytes 3538952 | tf_op jit(solution)/shard_map/ppermute | solution.py:37
  250.3 40.5 %collective-permute-start.2 = (bf16[4,192,768]{2,1,0:T(8,128)(2,1)}, bf16[4,192,768]{2,1,0:T(8,128)(2,1)S(1)}, u32[]{:S(2)}, u32[]{:S(2)}) collective-permute-start(bf16[4,192,768]{2,1,0:T(8,128)(2,1)} %get-tuple-element.207), channel_id=1, source_target_pairs={{0,8},{4,12},{8,0},{12,4},{16,24},{20,28},{24,16},{28,20},{1,9},{5... | collective-permute-start | bytes 3538952 | tf_op jit(solution)/shard_map/ppermute | solution.py:37
  284.2 50.5 %collective-permute-start.5 = (bf16[4,192,896]{2,1,0:T(8,128)(2,1)}, bf16[4,192,896]{2,1,0:T(8,128)(2,1)S(1)}, u32[]{:S(2)}, u32[]{:S(2)}) collective-permute-start(bf16[4,192,896]{2,1,0:T(8,128)(2,1)} %get-tuple-element.203.refs_9_), channel_id=1, source_target_pairs={{0,4},{4,0},{8,12},{12,8},{16,20},{20,16},{24,28},{28,24},{1,5},{5... | collective-permute-start | bytes 4128776 | tf_op jit(solution)/shard_map/ppermute | solution.py:37
  286.9 1.0 copy-start.31
  290.8 50.1 %collective-permute-start.3 = (bf16[2,192,768]{2,1,0:T(8,128)(2,1)}, bf16[2,192,768]{2,1,0:T(8,128)(2,1)S(1)}, u32[]{:S(2)}, u32[]{:S(2)}) collective-permute-start(bf16[2,192,768]{2,1,0:T(8,128)(2,1)} %get-tuple-element.206.refs_10_), channel_id=1, source_target_pairs={{0,8},{4,12},{8,0},{12,4},{16,24},{20,28},{24,16},{28,20},{1,9},{5... | collective-permute-start | bytes 1769480 | tf_op jit(solution)/shard_map/ppermute | solution.py:37
  290.8 1.0 copy-start.29
  294.6 46.2 %collective-permute-start.4 = (bf16[2,192,768]{2,1,0:T(8,128)(2,1)}, bf16[2,192,768]{2,1,0:T(8,128)(2,1)S(1)}, u32[]{:S(2)}, u32[]{:S(2)}) collective-permute-start(bf16[2,192,768]{2,1,0:T(8,128)(2,1)} %get-tuple-element.209.refs_11_), channel_id=1, source_target_pairs={{0,16},{4,20},{8,24},{12,28},{16,0},{20,4},{24,8},{28,12},{1,17},{... | collective-permute-start | bytes 1769480 | tf_op jit(solution)/shard_map/ppermute | solution.py:37
  295.0 30.5 %copy-start.10 = (f32[512,128]{1,0:T(8,128)S(1)}, f32[512,128]{1,0:T(8,128)}, u32[]{:S(2)}) copy-start(f32[512,128]{1,0:T(8,128)} %get-tuple-element.212.refs_7_) | copy-start | bytes 786436
  334.6 1.1 copy-start.27
  338.8 86.2 %collective-permute-start.11 = (bf16[2,192,896]{2,1,0:T(8,128)(2,1)}, bf16[2,192,896]{2,1,0:T(8,128)(2,1)S(1)}, u32[]{:S(2)}, u32[]{:S(2)}) collective-permute-start(bf16[2,192,896]{2,1,0:T(8,128)(2,1)} %get-tuple-element.248.refs_12_), channel_id=1, source_target_pairs={{0,8},{4,12},{8,0},{12,4},{16,24},{20,28},{24,16},{28,20},{1,9},{5... | collective-permute-start | bytes 2064392 | tf_op jit(solution)/shard_map/ppermute | solution.py:37
  340.9 0.8 copy-start.34
  340.9 1.0 copy-start.36
  374.4 70.6 %collective-permute-start.12 = (bf16[1,192,768]{2,1,0:T(8,128)(2,1)}, bf16[1,192,768]{2,1,0:T(8,128)(2,1)S(1)}, u32[]{:S(2)}, u32[]{:S(2)}) collective-permute-start(bf16[1,192,768]{2,1,0:T(8,128)(2,1)} %get-tuple-element.250), channel_id=1, source_target_pairs={{0,4},{4,0},{8,12},{12,8},{16,20},{20,16},{24,28},{28,24},{1,5},{5... | collective-permute-start | bytes 884744 | tf_op jit(solution)/shard_map/ppermute | solution.py:37
  374.8 70.2 %collective-permute-start.13 = (bf16[1,192,768]{2,1,0:T(8,128)(2,1)}, bf16[1,192,768]{2,1,0:T(8,128)(2,1)S(1)}, u32[]{:S(2)}, u32[]{:S(2)}) collective-permute-start(bf16[1,192,768]{2,1,0:T(8,128)(2,1)} %get-tuple-element.252), channel_id=1, source_target_pairs={{0,16},{4,20},{8,24},{12,28},{16,0},{20,4},{24,8},{28,12},{1,17},{... | collective-permute-start | bytes 884744 | tf_op jit(solution)/shard_map/ppermute | solution.py:37
  374.8 41.1 %collective-permute-start.7 = (bf16[4,192,768]{2,1,0:T(8,128)(2,1)}, bf16[4,192,768]{2,1,0:T(8,128)(2,1)S(1)}, u32[]{:S(2)}, u32[]{:S(2)}) collective-permute-start(bf16[4,192,768]{2,1,0:T(8,128)(2,1)} %get-tuple-element.239), channel_id=1, source_target_pairs={{0,8},{4,12},{8,0},{12,4},{16,24},{20,28},{24,16},{28,20},{1,9},{5... | collective-permute-start | bytes 3538952 | tf_op jit(solution)/shard_map/ppermute | solution.py:37
  377.4 43.8 %collective-permute-start.9 = (bf16[4,192,768]{2,1,0:T(8,128)(2,1)}, bf16[4,192,768]{2,1,0:T(8,128)(2,1)S(1)}, u32[]{:S(2)}, u32[]{:S(2)}) collective-permute-start(bf16[4,192,768]{2,1,0:T(8,128)(2,1)} %get-tuple-element.243), channel_id=1, source_target_pairs={{0,4},{4,0},{8,12},{12,8},{16,20},{20,16},{24,28},{28,24},{1,5},{5... | collective-permute-start | bytes 3538952 | tf_op jit(solution)/shard_map/ppermute | solution.py:37
  415.8 2.5 copy-start.30
  415.8 31.3 %collective-permute-start.6 = (bf16[4,192,896]{2,1,0:T(8,128)(2,1)}, bf16[4,192,896]{2,1,0:T(8,128)(2,1)S(1)}, u32[]{:S(2)}, u32[]{:S(2)}) collective-permute-start(bf16[4,192,896]{2,1,0:T(8,128)(2,1)} %get-tuple-element.237.refs_9_), channel_id=1, source_target_pairs={{0,4},{4,0},{8,12},{12,8},{16,20},{20,16},{24,28},{28,24},{1,5},{5... | collective-permute-start | bytes 4128776 | tf_op jit(solution)/shard_map/ppermute | solution.py:37
  421.2 1.0 copy-start.28
  421.2 26.6 %collective-permute-start.8 = (bf16[2,192,768]{2,1,0:T(8,128)(2,1)}, bf16[2,192,768]{2,1,0:T(8,128)(2,1)S(1)}, u32[]{:S(2)}, u32[]{:S(2)}) collective-permute-start(bf16[2,192,768]{2,1,0:T(8,128)(2,1)} %get-tuple-element.241.refs_11_), channel_id=1, source_target_pairs={{0,16},{4,20},{8,24},{12,28},{16,0},{20,4},{24,8},{28,12},{1,17},{... | collective-permute-start | bytes 1769480 | tf_op jit(solution)/shard_map/ppermute | solution.py:37
  425.0 19.9 %copy-start.32 = (bf16[2,192,896]{2,1,0:T(8,128)(2,1)}, bf16[2,192,896]{2,1,0:T(8,128)(2,1)S(1)}, u32[]{:S(2)}) copy-start(bf16[2,192,896]{2,1,0:T(8,128)(2,1)S(1)} %collective-permute-done.11.refs_6_) | copy-start | bytes 2064388
  425.0 26.0 %collective-permute-start.10 = (bf16[2,192,768]{2,1,0:T(8,128)(2,1)}, bf16[2,192,768]{2,1,0:T(8,128)(2,1)S(1)}, u32[]{:S(2)}, u32[]{:S(2)}) collective-permute-start(bf16[2,192,768]{2,1,0:T(8,128)(2,1)} %get-tuple-element.245.refs_10_), channel_id=1, source_target_pairs={{0,8},{4,12},{8,0},{12,4},{16,24},{20,28},{24,16},{28,20},{1,9},{5... | collective-permute-start | bytes 1769480 | tf_op jit(solution)/shard_map/ppermute | solution.py:37
  445.0 6.0 %copy-start.37 = (bf16[1,192,768]{2,1,0:T(8,128)(2,1)}, bf16[1,192,768]{2,1,0:T(8,128)(2,1)S(1)}, u32[]{:S(2)}) copy-start(bf16[1,192,768]{2,1,0:T(8,128)(2,1)S(1)} %collective-permute-done.12.refs_8_) | copy-start | bytes 884740
  445.0 6.0 %copy-start.38 = (bf16[1,192,768]{2,1,0:T(8,128)(2,1)}, bf16[1,192,768]{2,1,0:T(8,128)(2,1)S(1)}, u32[]{:S(2)}) copy-start(bf16[1,192,768]{2,1,0:T(8,128)(2,1)S(1)} %collective-permute-done.13.refs_10_) | copy-start | bytes 884740
  447.2 3.9 copy-start.26
  447.7 3.3 copy-start.33
  451.0 0.8 copy-start.35
  510.3 3.1 copy-start.5
  511.3 2.4 copy-start.22
  511.3 3.0 copy-start.16
  511.3 3.6 copy-start.21
  511.3 4.3 copy-start.12
  511.4 4.9 copy-start.9
  513.5 2.9 copy-start.8
  516.6 4.7 copy-start.4
  521.4 3.5 copy-start.6
  521.4 3.5 copy-start.7
  523.5 2.5 copy-start.3
  526.0 1.1 copy-start.20

commit v5 on v4

--- a/solution.py
+++ b/solution.py
@@ -180,8 +180,8 @@
     return jnp.sum(jnp.where(lanes == h, values, 0.0), axis=1, keepdims=True)
 
 
-def fwd_mix_body(size, nx, wx, wbc, wdt, tapx, tapbc, dtb, lograte, aux, segrow,
-                 ux, ubc, krs, pdt, steps_o, cum_o, cT, gram, mixed_o, entry_o, state, dec, decl,
+def fwd_mix_body(size, nx, wx, wbc, wdt, tapx, tapbc, dtb, lograte, aux,
+                 ux, ubc, krs, pdt, steps_o, cum_o, cT, mixed_o, entry_o, state, dec, decl,
                  us, usbc):
     p = pl.program_id(0)
     tokens = aux.shape[1]
@@ -197,12 +197,8 @@
         m = mix_taps(usbc, tapbc, aux, 2 * states)
         act = m * sig(m)
         krs[...] = act
-        g = dot3(act[:, states:], act[:, :states], NT)
         ii = lax.broadcasted_iota(jnp.int32, (tokens, tokens), 0)
         jj = lax.broadcasted_iota(jnp.int32, (tokens, tokens), 1)
-        segc = jnp.concatenate([aux[5]] * (tokens // LANE), axis=1)
-        keep = (ii >= jj) & (segc == segrow[...])
-        gram[...] = jnp.where(keep, g, 0.0)
         pd = bdot(nx[pl.ds(HALO, tokens), :], wdt[...], NN).astype(BF16)
         pdt[...] = pd
         st = softplus(pd.astype(F32) + dtb[...])
@@ -232,13 +228,22 @@
     state[...] = dot3(vd * tail, krs[:, :states], TN)
 
 
-def fwd_inside_body(stages_of, size, nx, wz, mixed, steps, cum, cT, gram, skip, state, dec, ypart, enter, gate, cb, *rest):
+def fwd_inside_body(stages_of, size, nx, wz, mixed, steps, cum, cT, krs, segc, segrow, skip, state, dec, ypart, enter, gate, gram, cb, *rest):
     p = pl.program_id(0)
     tokens = mixed.shape[0]
     stages = stages_of(state, dec, enter, *rest)
     for k, stage in enumerate(stages[:-1]):
         pl.when(p == k)(stage)
     gate[...] = bdot(nx[pl.ds(HALO, tokens), :], wz[...], NN).astype(BF16)
+    states = krs.shape[1] // 2
+
+    @pl.when(p == 0)
+    def _():
+        ii = lax.broadcasted_iota(jnp.int32, (tokens, tokens), 0)
+        jj = lax.broadcasted_iota(jnp.int32, (tokens, tokens), 1)
+        segs = jnp.concatenate([segc[...]] * (tokens // LANE), axis=1)
+        gram[...] = jnp.where((ii >= jj) & (segs == segrow[...]), dot3(krs[:, states:], krs[:, :states], NT), 0.0)
+
     lanes = lax.broadcasted_iota(jnp.int32, (tokens, LANE), 1)
     half = lanes < size
     h0 = p * (LANE // size)
@@ -312,7 +317,15 @@
         sq[...] = jnp.broadcast_to(jnp.sum(jnp.transpose(sqacc[...]), axis=0, keepdims=True), sq.shape)
 
 
-def bwd_gate_body(gb, wout, gate, y, mixed, entry, krs, r2b, krb, gain, gy_o, gz_o, scaled_o, qloc, ggate, gskip):
+def bwd_gate_body(width, gb, wout, gate, y, mixed, entry, krs, r2b, side, gain, gy_o, gz_o, scaled_o, qloc, ggate, gskip, krb):
+    @pl.when(pl.program_id(0) == 0)
+    def _():
+        quarter = r2b.shape[0] // 4
+        for k in range(4):
+            here = pl.ds(k * quarter, quarter)
+            r = r2b[here, :]
+            krb[here, :] = jnp.transpose(jnp.broadcast_to(side[8 * k : 8 * k + 1, :], (quarter, LANE))) * (r * r * (1.0 / width))
+
     states = krs.shape[1] // 2
     gs = bdot(gb[...], wout[...], NT)
     z = gate[...].astype(F32)
@@ -1093,43 +1106,44 @@
     )(*args, *after)
 
 
-def fwd_mix(l, size, nx, q, aux, segrow):
+def fwd_mix(l, size, nx, q, aux):
     tokens = aux.shape[1]
     ext, d = nx.shape
     inner = q["conv_x"].shape[2]
     two = q["w_bc"].shape[2]
-    args = [nx, q["w_zx"], q["w_bc"], q["w_dt"], q["conv_x"], q["conv_bc"], q["dt_bias"], q["a_log"], aux, segrow]
+    args = [nx, q["w_zx"], q["w_bc"], q["w_dt"], q["conv_x"], q["conv_bc"], q["dt_bias"], q["a_log"], aux]
     specs = [full(nx.shape), projection(l, 1, d), of_layer(l, q["w_bc"].shape), of_layer(l, q["w_dt"].shape),
              of_layer(l, q["conv_x"].shape, True), of_layer(l, q["conv_bc"].shape), of_layer(l, q["dt_bias"].shape),
-             of_layer(l, q["a_log"].shape), full(aux.shape), full(segrow.shape)]
+             of_layer(l, q["a_log"].shape), full(aux.shape)]
     return kcall(
         partial(fwd_mix_body, size), args, specs, 12,
         name="fwd_mix",
         grid=(inner // LANE,),
         out_specs=[cols(ext), full((ext, two)), full((tokens, two)), full((tokens, LANE)), full((tokens, LANE)),
-                   full((tokens, LANE)), full((LANE, tokens)), full((tokens, tokens)), cols(tokens),
+                   full((tokens, LANE)), full((LANE, tokens)), cols(tokens),
                    cols(tokens), rowsb(two // 2), full((16, LANE)), full((8, LANE))],
         out_shape=[S((ext, inner), BF16), S((ext, two), BF16), S((tokens, two), F32),
                    S((tokens, LANE), BF16), S((tokens, LANE), F32), S((tokens, LANE), F32), S((LANE, tokens), F32),
-                   S((tokens, tokens), F32), S((tokens, inner), F32), S((tokens, inner), F32),
+                   S((tokens, inner), F32), S((tokens, inner), F32),
                    S((inner, two // 2), F32), S((16, LANE), F32), S((8, LANE), F32)],
         scratch_shapes=[pltpu.VMEM((ext, LANE), F32), pltpu.VMEM((ext, two), F32)],
     )
 
 
-def fwd_inside(l, heads, size, nx, mixed, steps, cum, cT, gram, q, state, dec, cid):
+def fwd_inside(l, heads, size, nx, mixed, steps, cum, cT, krs, aux, segrow, q, state, dec, cid):
     tokens, inner = mixed.shape
     rows, states = state.shape
     bits = bits_of("seq")
     return kcall(
         partial(fwd_inside_body, partial(carry_stages, bits, False, heads, size), size),
-        [nx, q["w_zx"], mixed, steps, cum, cT, gram, q["skip"], state, dec],
-        [full(nx.shape), projection(l, 0, nx.shape[1]), cols(tokens), full(steps.shape), full(cum.shape), full(cT.shape), full(gram.shape), of_layer(l, q["skip"].shape, True),
+        [nx, q["w_zx"], mixed, steps, cum, cT, krs, aux, segrow, q["skip"], state, dec],
+        [full(nx.shape), projection(l, 0, nx.shape[1]), cols(tokens), full(steps.shape), full(cum.shape), full(cT.shape), full(krs.shape),
+         pl.BlockSpec((None, tokens, LANE), lambda p: (5, 0, 0)), full(segrow.shape), of_layer(l, q["skip"].shape, True),
          full(state.shape), full(dec.shape)], 28, (), cid,
         name="fwd_inside",
         grid=(inner // LANE,),
-        out_specs=[cols(tokens), full((rows, states)), cols(tokens)],
-        out_shape=[S((tokens, inner), F32), S((rows, states), F32), S((tokens, inner), BF16)],
+        out_specs=[cols(tokens), full((rows, states)), cols(tokens), full((tokens, tokens))],
+        out_shape=[S((tokens, inner), F32), S((rows, states), F32), S((tokens, inner), BF16), S((tokens, tokens), F32)],
         scratch_shapes=[pltpu.VMEM((2, tokens, LANE), F32)] + carry_scratch(len(bits), rows, states, F32),
     )
 
@@ -1147,18 +1161,19 @@
     )
 
 
-def bwd_gate(l, gb, q, gate, y, mixed, entry, krs, r2b, krb):
+def bwd_gate(l, gb, q, gate, y, mixed, entry, krs, r2b, side, width):
     tokens, inner = y.shape
     states = krs.shape[1] // 2
     return kcall(
-        bwd_gate_body, [gb, q["w_out"], gate, y, mixed, entry, krs, r2b, krb, q["gate_gain"]],
+        partial(bwd_gate_body, width), [gb, q["w_out"], gate, y, mixed, entry, krs, r2b, side, q["gate_gain"]],
         [full(gb.shape), rows_of_layer(l, q["w_out"].shape), cols(tokens, WIDE), cols(tokens, WIDE), cols(tokens, WIDE), cols(tokens, WIDE), full(krs.shape),
-         full(r2b.shape), full(krb.shape), of_layer(l, q["gate_gain"].shape, WIDE)], 9,
+         full(r2b.shape), full(side.shape), of_layer(l, q["gate_gain"].shape, WIDE)], 9,
         name="bwd_gate",
         grid=(inner // WIDE,),
         out_specs=[cols(tokens, WIDE), cols(tokens, WIDE), cols(tokens, WIDE), rowsb(states, WIDE), cols(1, WIDE), cols(1, WIDE)],
         out_shape=[S((tokens, inner), F32), S((tokens, inner), BF16), S((tokens, inner), BF16), S((inner, states), F32),
                    S((1, inner), F32), S((1, inner), F32)],
+        scratch_shapes=[pltpu.VMEM((tokens, LANE), F32)],
     )
 
 
@@ -1327,15 +1342,15 @@
     def rest(self):
         return self.got, self.keep, tuple(self.left), tuple(self.order[self.step :])
 
-    def fold(self, after=()):
+    def fold(self):
         bit, stride = self.plan()
+        me = my_bit("seq", bit)
         blocks, block, width = self.keep.shape
-        self.away, self.keep = kcall(
-            partial(fold_body, bit, stride), [self.got, self.keep], [VM] * 2, 2, after,
-            name="fold",
-            out_specs=[VM] * 2,
-            out_shape=[S((blocks // 2, block, width), BF16)] * 2,
-        )
+        view = lambda v: v.reshape(blocks // (2 * stride), 2, stride, block, width)
+        keep, got = view(self.keep), view(self.got)
+        pick = lambda v, i: take(v, 1, i).astype(F32)
+        both = [(pick(keep, i) + pick(got, i)).astype(BF16).reshape(blocks // 2, block, width) for i in (1 - me, me)]
+        self.away, self.keep = both
 
 
 def pad_lanes(x, to=LANE):
@@ -1344,8 +1359,8 @@
 
 def forward_layer(nx, h_own, extra, q, aux, segrow, layer):
     heads, size, inner = q["heads"], q["size"], q["inner"]
-    (ux, ubc, krs, pdt, steps, cum, cT, gram, mixed, entry, state, dec, decl) = fwd_mix(layer, size, nx, q, aux, segrow)
-    ypart, enter, gate = fwd_inside(layer, heads, size, nx, mixed, steps, cum, cT, gram, q, state, dec, layer)
+    (ux, ubc, krs, pdt, steps, cum, cT, mixed, entry, state, dec, decl) = fwd_mix(layer, size, nx, q, aux)
+    ypart, enter, gate, gram = fwd_inside(layer, heads, size, nx, mixed, steps, cum, cT, krs, aux, segrow, q, state, dec, layer)
     y, carr, gated, sq = fwd_gate(ypart, entry, gate, krs, enter)
     width = inner * lax.axis_size("head")
     nx_next, h_new, branch, r2b, side = head_fwd(layer, gated, sq, q, h_own, extra, layer == LAYERS - 1, width, LAYERS + layer)
@@ -1355,12 +1370,8 @@
 
 
 def backward_gate(gb, side, s, q, layer):
-    tokens = gb.shape[0]
     width = q["inner"] * lax.axis_size("head")
-    kr = side.reshape(4, 8, LANE)[:, 0, :].reshape(tokens)
-    r2b = s["r2b"]
-    krb = r2b * r2b * (kr[:, None] / width)
-    return bwd_gate(layer, gb, q, s["gate"], s["y"], s["mixed"], s["entry"], s["krs"], r2b, krb)
+    return bwd_gate(layer, gb, q, s["gate"], s["y"], s["mixed"], s["entry"], s["krs"], s["r2b"], side, width)
 
 
 def local(hidden_in, seg, cot, norm_gain, w_zx, w_bc, w_dt, conv_x, conv_bc, dt_bias, a_log, skip_d, gate_gain, w_out):
@@ -1403,16 +1414,23 @@
     for l in reversed(range(LAYERS)):
         s = stored[l]
         gy, gz, scaled, qloc, ggate, gskip = backward_gate(gb, side, s, q, l)
+        if pending:
+            pending[2].fold()
+            pending[2].go()
         (dvd, dd, rowT, dkr, later), out, z = bwd_local(
             heads, size, gy, s["mixed"], s["krs"], s["cum"], s["steps"], s["cT"], s["gram"], s["entry"], s["enter"], aux, segrow, qloc,
-            s["dec"], 2 * LAYERS + l, gb, scaled, s["nx"], gz, pending[:2], pending[2:])
+            s["dec"], 2 * LAYERS + l, gb, scaled, s["nx"], gz, pending[:2], ())
+        if pending:
+            pending[2].keep, _ = lax.optimization_barrier((pending[2].keep, later))
+            pending[2].fold()
+            pending[2].go()
         for p in pending[:2]:
             p.go()
         out.go()
         z.go()
         gm8, gu, gtail, gtaps_x, gdt, gvec, dkr = bwd_carry(
             l, size, gy, dvd, s["mixed"], s["carr"], s["entry"], s["krs"], s["cum"], s["steps"], s["pdt"], q, s["ux"], aux, later, s["enter"],
-            dd, rowT, dkr, s["decl"], ())
+            dd, rowT, dkr, s["decl"], [p.away for p in pending[2:]])
         small, gtaps_bc, gtail = maps_bwd(l, dkr, s["ubc"], q, aux, gdt, gtail, gm8, 3 * LAYERS + l)
         gu = lax.dynamic_update_slice(gu, gtail, (tokens - 16, 0))
         x = Halving((0, 1, 2))
@@ -1422,11 +1440,8 @@
         z.fold()
         z.go()
         out.go()
-        if pending:
-            pending[2].fold()
-            pending[2].go()
         before = stored[max(l - 1, 0)]["branch"]
-        gb, g_own, g_gain, side = head_bwd(l, gz, gu, small, q, s["h_own"], g_own, before, 4 * LAYERS + l, after=[p.away for p in [x, out, z] + pending[2:]])
+        gb, g_own, g_gain, side = head_bwd(l, gz, gu, small, q, s["h_own"], g_own, before, 4 * LAYERS + l, after=[p.away for p in [x, out, z]])
         smalls[l] = (gtaps_x, ggate, gskip, gvec, gtaps_bc, g_gain)
         pending = [out, z, x]
         sums[l] = pending

time: 537 us -> 516 us (0.961)
  Pallas kernels: 443 us -> 417 us
  starting transfers between devices: 18.8 us -> 26.8 us
    pallas_call x26 -> x21, Pallas kernels: 443 us -> 417 us  [kcall(): pl.pallas_call(wrapped, in_specs=list(specs) + [pl.BlockSpec(memory_space...]
    ppermute x13 -> x14, starting transfers between devices: 14 us -> 21.8 us  [swap(): return lax.ppermute(x, axis, [(i, i ^ bit) for i in range(n)])]
    convert_element_type x0 -> x6, other arithmetic: none -> 5.8 us  [fold(): (pick(keep, i) + pick(got, i)).astype(BF16)]
    unnamed x89 -> x99, local copies, waits for them, and re-layouts: 25 us -> 23.3 us
  transfers between devices with their start and end apart: 14 -> 15, of which waited for: 3 -> 3; matrix products, arithmetic and copies ran while one was open for 5% -> 6% of each run, Pallas kernels for 33% -> 31%
where the time goes in v5:
time: 516 us; the launch traced here: 508 us
  Pallas kernels  417 us (81%)
  local copies, waits for them, and re-layouts  36.5 us (7%)
  starting transfers between devices  26.8 us (5%)
  other arithmetic  20 us (4%)
  waiting for transfers between devices  6.12 us (1%)
    pallas_call x21, Pallas kernels, kcall(): pl.pallas_call(wrapped, in_specs=list(specs) + [pl.BlockSpec(memory_space...  417 us
    unnamed x99, local copies, waits for them, and re-layouts  23.3 us
    ppermute x14, starting transfers between devices, swap(): return lax.ppermute(x, axis, [(i, i ^ bit) for i in range(n)])  21.8 us
  transfers between devices with their start and end apart: 15, of which 3 were waited for; matrix products, arithmetic and copies ran while one was open for 6% of the time, Pallas kernels for 31%

profile of v5, /device:TPU:0, one launch (start us, length us, event | category | flops | bytes accessed | tf_op | source)
XLA Modules:
  0.0 507.9 jit_solution(6827169929517839505)
XLA Ops:
  0.7 0.8 slice_reduce_fusion
  1.5 1.8 fusion
  3.8 1.1 copy-done.1
  4.9 5.0 collective-permute-start
  11.1 1.0 dynamic-slice_convert_fusion.refs_4_.refs_5_
  12.2 2.2 fusion.25
  14.4 1.8 select_select_fusion
  16.1 1.4 fusion.21
  18.2 8.7 %copy.94 = bf16[2,1536,2,768]{3,1,2,0:T(8,128)(2,1)} copy(bf16[2,1536,2,768]{3,2,1,0:T(2,128)(2,1)} %param.18) | data formatting | bytes 18874368 | tf_op args[4]
  29.3 0.7 broadcast_in_dim_reshape.4.refs_9_.refs_11_
  30.6 1.3 pad_maximum_fusion.1.refs_0_.refs_15_
  31.9 1.6 broadcast_in_dim.35.refs_8_.refs_7_.refs_9_.refs_14_.refs_3_
  33.5 14.3 %fwd_mix.2 = (bf16[528,768]{1,0:T(8,128)(2,1)}, bf16[528,256]{1,0:T(8,128)(2,1)}, f32[512,256]{1,0:T(8,128)}, bf16[512,128]{1,0:T(8,128)(2,1)}, f32[512,128]{1,0...) custom-call(bf16[528,1536]{1,0:T(8,128)(2,1)} %pad_maximum_fusion.1., ...), custom_call_target="tpu_custom_call" | custom-call | flops 12000000000 | bytes 36000000 | tf_op jit(solution)/shard_map/fwd_mix/pallas_call | solution.py:1100
  47.8 30.6 %fwd_inside.2 = (f32[512,768]{1,0:T(8,128)}, f32[768,128]{1,0:T(8,128)}, bf16[512,768]{1,0:T(8,128)(2,1)}, f32[512,512]{1,0:T(8,128)}) custom-call(bf16[528,1536]{1,0:T(8,128)(2,1)} %pad_maximum_fusion.1.refs_0_.refs_15_, bf16[2,2,1536,768]{3,2,1,0:T(8,128)(2,1)} %bitcast.92, f32[512,768]{1,0:T(8,128)} %get-tuple-element.138.refs_2_.refs_4_.refs_1_, ...), custom_call_target="tpu_custom_call" | custom-call | flops 28000000000 | bytes 84000000 | tf_op jit(solution)/shard_map/fwd_inside/pallas_call | solution.py:1100
  78.4 6.3 %fwd_gate.2 = (f32[512,768]{1,0:T(8,128)}, f32[512,768]{1,0:T(8,128)}, f32[512,768]{1,0:T(8,128)}, f32[8,512]{1,0:T(8,128)}) custom-call(f32[512,768]{1,0:T(8,128)} %get-tuple-element.145.refs_0_, f32[512,768]{1,0:T(8,128)} %get-tuple-element.146.refs_1_.refs_5_.refs_7_.refs_4_, bf16[512,768]{1,0:T(8,128)(2,1)} %get-tuple-element.147.refs_2_, ...), custom_call_target="tpu_custom_call" | custom-call | flops 7000000000 | bytes 21000000 | tf_op jit(solution)/shard_map/fwd_gate/pallas_call | solution.py:1100
  84.7 41.2 %head_fwd.1 = (bf16[528,1536]{1,0:T(8,128)(2,1)}, f32[128,1536]{1,0:T(8,128)}, f32[128,1536]{1,0:T(8,128)}, f32[512,128]{1,0:T(8,128)}, f32[32,128]{1,0:T(8,128)}) custom-call(f32[512,768]{1,0:T(8,128)} %get-tuple-element.149.refs_0_, f32[8,512]{1,0:T(8,128)} %get-tuple-element.150.refs_1_, f32[2,1,768]{2,1,0:T(1,128)} %broadcast_in_dim.37.refs_2_.refs_9_, ...), custom_call_target="tpu_custom_call" | custom-call | flops 30000001024 | bytes 90000000 | tf_op jit(solution)/shard_map/head_fwd/pallas_call | solution.py:1100
  125.9 14.3 %fwd_mix.3 = (bf16[528,768]{1,0:T(8,128)(2,1)}, bf16[528,256]{1,0:T(8,128)(2,1)}, f32[512,256]{1,0:T(8,128)}, bf16[512,128]{1,0:T(8,128)(2,1)}, f32[512,128]{1,0...) custom-call(bf16[528,1536]{1,0:T(8,128)(2,1)} %get-tuple-element.151, ...), custom_call_target="tpu_custom_call" | custom-call | flops 12000000000 | bytes 36000000 | tf_op jit(solution)/shard_map/fwd_mix/pallas_call | solution.py:1100
  140.2 33.5 %fwd_inside.3 = (f32[512,768]{1,0:T(8,128)}, f32[768,128]{1,0:T(8,128)}, bf16[512,768]{1,0:T(8,128)(2,1)}, f32[512,512]{1,0:T(8,128)}) custom-call(bf16[528,1536]{1,0:T(8,128)(2,1)} %get-tuple-element.151.refs_0_.refs_15_, bf16[2,2,1536,768]{3,2,1,0:T(8,128)(2,1)} %bitcast.94, f32[512,768]{1,0:T(8,128)} %get-tuple-element.152.refs_2_.refs_4_.refs_1_, ...), custom_call_target="tpu_custom_call" | custom-call | flops 28000000000 | bytes 84000000 | tf_op jit(solution)/shard_map/fwd_inside/pallas_call | solution.py:1100
  173.8 6.3 %fwd_gate.3 = (f32[512,768]{1,0:T(8,128)}, f32[512,768]{1,0:T(8,128)}, f32[512,768]{1,0:T(8,128)}, f32[8,512]{1,0:T(8,128)}) custom-call(f32[512,768]{1,0:T(8,128)} %get-tuple-element.159.refs_0_, f32[512,768]{1,0:T(8,128)} %get-tuple-element.160.refs_1_.refs_5_.refs_7_.refs_4_, bf16[512,768]{1,0:T(8,128)(2,1)} %get-tuple-element.161.refs_2_, ...), custom_call_target="tpu_custom_call" | custom-call | flops 7000000000 | bytes 21000000 | tf_op jit(solution)/shard_map/fwd_gate/pallas_call | solution.py:1100
  180.1 29.6 %head_fwd_last.1 = (bf16[512,1536]{1,0:T(8,128)(2,1)}, f32[128,1536]{1,0:T(8,128)}, f32[128,1536]{1,0:T(8,128)}, f32[512,128]{1,0:T(8,128)}, f32[32,128]{1,0:T(8,128)}) custom-call(f32[512,768]{1,0:T(8,128)} %get-tuple-element.163.refs_0_, f32[8,512]{1,0:T(8,128)} %get-tuple-element.164.refs_1_, f32[2,1,768]{2,1,0:T(1,128)} %broadcast_in_dim.37.refs_2_.refs_9_, ...), custom_call_target="tpu_custom_call" | custom-call | flops 30000001024 | bytes 90000000 | tf_op jit(solution)/shard_map/head_fwd_last/pallas_call | solution.py:1100
  209.7 8.1 %bwd_gate.2 = (f32[512,768]{1,0:T(8,128)}, bf16[512,768]{1,0:T(8,128)(2,1)}, bf16[512,768]{1,0:T(8,128)(2,1)}, f32[768,128]{1,0:T(8,128)}, f32[1,768]{1,0:T(1,128)}, /*index=5*/f32[1,768]{1,0:T(1,128)}) custom-call(bf16[512,1536]{1,0:T(8,128)(2,1)} %refs_13_.3, bf16[2,768,1536]{2,1,0:T(8,128)(2,1)} %refs_1_.3, bf16[512,768]{1,0:T(8,128)(2,1)} %get-tuple-element.161.refs_2_, ...), custom_call_target="tpu_custom_call" | custom-call | flops 8999999488 | bytes 27000000 | tf_op jit(solution)/shard_map/bwd_gate/pallas_call | solution.py:1100
  217.9 26.3 %bwd_local.2 = (f32[512,768]{1,0:T(8,128)}, f32[512,128]{1,0:T(8,128)}, f32[128,512]{1,0:T(8,128)}, f32[512,256]{1,0:T(8,128)}, f32[768,128]{1,0:T(8,128)}, /*in...) custom-call(f32[512,768]{1,0:T(8,128)} %get-tuple-element.171.refs_0, ...), custom_call_target="tpu_custom_call" | custom-call | flops 24000000000 | bytes 72000000 | tf_op jit(solution)/shard_map/bwd_local/pallas_call | solution.py:1100
  244.1 0.9 collective-permute-start.1
  245.0 12.0 %bwd_carry.2 = (f32[8,768]{1,0:T(8,128)}, bf16[512,768]{1,0:T(8,128)(2,1)}, f32[16,768]{1,0:T(8,128)}, f32[8,768]{1,0:T(8,128)}, bf16[512,128]{1,0:T(8,128)(2,1)}, /*index=5*/f32[8,128]{1,0:T(8,128)}, f32[512,256]{1,0:T(8,128)}) custom-call(f32[512,768]{1,0:T(8,128)} %get-tuple-element.171.refs_0_, f32[512,768]{1,0:T(8,128)} %get-tuple-element.175.refs_1_, ...), custom_call_target="tpu_custom_call" | custom-call | flops 11000000512 | bytes 33000000 | tf_op jit(solution)/shard_map/bwd_carry/pallas_call | solution.py:1100
  257.1 16.1 %maps_bwd.2 = (bf16[512,128]{1,0:T(8,128)(2,1)}, f32[8,128]{1,0:T(8,128)}, bf16[16,768]{1,0:T(8,128)(2,1)}) custom-call(f32[512,256]{1,0:T(8,128)} %get-tuple-element.185.refs_0_, bf16[528,256]{1,0:T(8,128)(2,1)} %get-tuple-element.186.refs_1_, f32[2,5,256]{2,1,0:T(8,128)} %copy.51.refs_5_.refs_2_, ...), custom_call_target="tpu_custom_call" | custom-call | flops 14000000000 | bytes 42000000 | tf_op jit(solution)/shard_map/maps_bwd/pallas_call | solution.py:1100
  273.1 1.3 constant_dynamic-update-slice_fusion.1.refs_1_
  274.5 4.9 wgrad.2
  279.4 2.4 collective-permute-start.5
  281.7 1.2 fusion.7
  283.2 1.2 fusion.8
  284.4 0.7 collective-permute-start.4
  285.2 29.7 %head_bwd.2 = (bf16[512,1536]{1,0:T(8,128)(2,1)}, f32[128,1536]{1,0:T(8,128)}, f32[1,1536]{1,0:T(1,128)}, f32[32,128]{1,0:T(8,128)}) custom-call(bf16[512,768]{1,0:T(8,128)(2,1)} %get-tuple-element.170.refs_16_.refs_0_, bf16[512,768]{1,0:T(8,128)(2,1)} %constant_dynamic-update-slice_fusion.1.refs_1_, bf16[512,128]{1,0:T(8,128)(2,1)} %get-tuple-element.191.refs_2_, ...), custom_call_target="tpu_custom_call" | custom-call | flops 28999999488 | bytes 87000000 | tf_op jit(solution)/shard_map/head_bwd/pallas_call | solution.py:1100
  314.9 8.4 %bwd_gate.3 = (f32[512,768]{1,0:T(8,128)}, bf16[512,768]{1,0:T(8,128)(2,1)}, bf16[512,768]{1,0:T(8,128)(2,1)}, f32[768,128]{1,0:T(8,128)}, f32[1,768]{1,0:T(1,128)}, /*index=5*/f32[1,768]{1,0:T(1,128)}) custom-call(bf16[512,1536]{1,0:T(8,128)(2,1)} %get-tuple-element.198.refs_0_.refs_13_, bf16[2,768,1536]{2,1,0:T(8,128)(2,1)} %refs_1_.3, ...), custom_call_target="tpu_custom_call" | custom-call | flops 8999999488 | bytes 27000000 | tf_op jit(solution)/shard_map/bwd_gate/pallas_call | solution.py:1100
  323.7 1.9 collective-permute-start.6
  325.6 0.8 copy-done.39
  326.6 32.0 %bwd_local.3 = (f32[512,768]{1,0:T(8,128)}, f32[512,128]{1,0:T(8,128)}, f32[128,512]{1,0:T(8,128)}, f32[512,256]{1,0:T(8,128)}, f32[768,128]{1,0:T(8,128)}, /*in...) custom-call(f32[512,768]{1,0:T(8,128)} %get-tuple-element.202.refs_0, ...), custom_call_target="tpu_custom_call" | custom-call | flops 24000000000 | bytes 72000000 | tf_op jit(solution)/shard_map/bwd_local/pallas_call | solution.py:1100
  359.0 1.7 collective-permute-start.13
  360.7 2.2 collective-permute-start.14
  363.0 0.9 add_convert_fusion.10
  363.9 0.7 collective-permute-start.12
  364.6 12.0 %bwd_carry.3 = (f32[8,768]{1,0:T(8,128)}, bf16[512,768]{1,0:T(8,128)(2,1)}, f32[16,768]{1,0:T(8,128)}, f32[8,768]{1,0:T(8,128)}, bf16[512,128]{1,0:T(8,128)(2,1)}, /*index=5*/f32[8,128]{1,0:T(8,128)}, f32[512,256]{1,0:T(8,128)}) custom-call(f32[512,768]{1,0:T(8,128)} %get-tuple-element.202.refs_0_, f32[512,768]{1,0:T(8,128)} %get-tuple-element.207.refs_1_, ...), custom_call_target="tpu_custom_call" | custom-call | flops 11000000512 | bytes 33000000 | tf_op jit(solution)/shard_map/bwd_carry/pallas_call | solution.py:1100
  376.6 16.6 %maps_bwd.3 = (bf16[512,128]{1,0:T(8,128)(2,1)}, f32[8,128]{1,0:T(8,128)}, bf16[16,768]{1,0:T(8,128)(2,1)}) custom-call(f32[512,256]{1,0:T(8,128)} %get-tuple-element.219.refs_0_, bf16[528,256]{1,0:T(8,128)(2,1)} %get-tuple-element.220.refs_1_, f32[2,5,256]{2,1,0:T(8,128)} %copy.51.refs_5_.refs_2_, ...), custom_call_target="tpu_custom_call" | custom-call | flops 14000000000 | bytes 42000000 | tf_op jit(solution)/shard_map/maps_bwd/pallas_call | solution.py:1100
  393.3 1.4 constant_dynamic-update-slice_fusion.refs_1_
  394.6 4.8 wgrad.3
  399.5 7.4 %collective-permute-start.7 = (bf16[4,192,896]{2,1,0:T(8,128)(2,1)}, bf16[4,192,896]{2,1,0:T(8,128)(2,1)S(1)}, u32[]{:S(2)}, u32[]{:S(2)}) collective-permute-start(bf16[4,192,896]{2,1,0:T(8,128)(2,1)} %get-tuple-element.226.refs_9_), channel_id=1, source_target_pairs={{0,4},{4,0},{8,12},{12,8},{16,20},{20,16},{24,28},{28,24},{1,5},{5... | collective-permute-start | bytes 4128776 | tf_op jit(solution)/shard_map/ppermute | solution.py:37
  406.9 1.1 fusion.10
  408.0 3.4 collective-permute-start.9
  411.4 1.1 fusion.12
  412.6 0.7 copy-done.18
  413.3 19.5 %head_bwd.3 = (bf16[128,1536]{1,0:T(8,128)(2,1)}, f32[128,1536]{1,0:T(8,128)}, f32[1,1536]{1,0:T(1,128)}, f32[32,128]{1,0:T(8,128)}) custom-call(bf16[512,768]{1,0:T(8,128)(2,1)} %get-tuple-element.206.refs_16_.refs_0_, bf16[512,768]{1,0:T(8,128)(2,1)} %constant_dynamic-update-slice_fusion.refs_1_, bf16[512,128]{1,0:T(8,128)(2,1)} %get-tuple-element.225.refs_2_, ...), custom_call_target="tpu_custom_call" | custom-call | flops 28999999488 | bytes 87000000 | tf_op jit(solution)/shard_map/head_bwd/pallas_call | solution.py:1100
  433.4 1.0 collective-permute-done.9.refs_2_
  434.4 4.6 collective-permute-done.11.refs_4_
  439.0 0.8 copy-done.38
  439.8 50.1 %tail.1 = (f32[192,896]{1,0:T(8,128)}, f32[192,768]{1,0:T(8,128)}, f32[192,768]{1,0:T(8,128)}, f32[192,896]{1,0:T(8,128)}, f32[192,768]{1,0:T(8,128)}, /*index=5...) custom-call(bf16[4,192,896]{2,1,0:T(8,128)(2,1)} %copy-done.36, ...), custom_call_target="tpu_custom_call" | custom-call | flops 44999999488 | bytes 135000000 | tf_op jit(solution)/shard_map/tail/pallas_call | solution.py:1100
  489.9 1.2 slice_bitcast_fusion.1
  491.1 1.0 slice_bitcast_fusion.3
  492.6 2.1 convert_element_type.345
  494.8 1.0 copy-done.16
  496.0 3.2 copy.76
  499.3 0.8 copy.77
  500.0 0.7 copy.78
  503.3 1.3 constant_dynamic-slice_fusion
  504.6 1.1 pad_maximum_fusion.2
  505.7 1.1 copy.99
  (131 shorter events, 11.3 us)
Async XLA Ops:
  0.6 2.7 copy-start
  3.3 6.6 %copy-start.21 = (bf16[2,1536,12]{1,0,2:T(2,128)(2,1)S(1)}, bf16[2,1536,12]{1,0,2:T(2,128)(2,1)}, u32[]{:S(2)}) copy-start(bf16[2,1536,12]{1,0,2:T(2,128)(2,1)} %param.20) | copy-start | bytes 221188
  3.8 1.1 copy-start.1
  4.9 5.6 %copy-start.28 = (s32[512]{0:T(512)S(1)}, s32[512]{0:T(512)}, u32[]{:S(2)}) copy-start(s32[512]{0:T(512)} %param.15) | copy-start | bytes 6148
  4.9 25.7 %collective-permute-start = (bf16[16,1536]{1,0:T(8,128)(2,1)S(1)}, bf16[16,1536]{1,0:T(8,128)(2,1)S(1)}, u32[]{:S(2)}, u32[]{:S(2)}) collective-permute-start(bf16[16,1536]{1,0:T(8,128)(2,1)S(1)} %slice.76), channel_id=1, source_target_pairs={{0,4},{4,8},{8,12},{12,16},{16,20},{20,24},{24,28},{1,5},{5,9},{9,... | collective-permute-start | bytes 147464 | tf_op jit(solution)/shard_map/ppermute | solution.py:42
  10.5 20.1 %copy-start.25 = (f32[512]{0:T(512)}, f32[512]{0:T(512)S(1)}, u32[]{:S(2)}) copy-start(f32[512]{0:T(512)S(1)} %convert_element_type.296) | copy-start | bytes 6148
  12.2 2.2 copy-start.19
  14.4 3.1 copy-start.24
  18.1 8.8 %copy-start.23 = (f32[2,5,768]{2,0,1:T(2,128)S(1)}, f32[2,5,768]{2,0,1:T(2,128)}, u32[]{:S(2)}) copy-start(f32[2,5,768]{2,0,1:T(2,128)} %param.21) | copy-start | bytes 92164
  18.1 9.4 %copy-start.27 = (f32[2,5,256]{2,0,1:T(2,128)S(1)}, f32[2,5,256]{2,0,1:T(2,128)}, u32[]{:S(2)}) copy-start(f32[2,5,256]{2,0,1:T(2,128)} %param.22) | copy-start | bytes 30724
  18.1 10.0 %copy-start.34 = (f32[2,12]{1,0:T(2,128)S(1)}, f32[2,12]{1,0:T(2,128)}, u32[]{:S(2)}) copy-start(f32[2,12]{1,0:T(2,128)} %param.23) | copy-start | bytes 292
  18.1 10.6 %copy-start.35 = (f32[2,12]{1,0:T(2,128)S(1)}, f32[2,12]{1,0:T(2,128)}, u32[]{:S(2)}) copy-start(f32[2,12]{1,0:T(2,128)} %param.24) | copy-start | bytes 292
  18.1 11.1 %copy-start.33 = (f32[2,12]{1,0:T(2,128)S(1)}, f32[2,12]{1,0:T(2,128)}, u32[]{:S(2)}) copy-start(f32[2,12]{1,0:T(2,128)} %param.25) | copy-start | bytes 292
  18.1 11.9 %copy-start.29 = (f32[2,768]{1,0:T(2,128)S(1)}, f32[2,768]{1,0:T(2,128)}, u32[]{:S(2)}) copy-start(f32[2,768]{1,0:T(2,128)} %param.26) | copy-start | bytes 18436
  18.2 12.5 %copy-start.2 = (bf16[512,1536]{1,0:T(8,128)(2,1)S(1)}, bf16[512,1536]{1,0:T(8,128)(2,1)}, u32[]{:S(2)}) copy-start(bf16[512,1536]{1,0:T(8,128)(2,1)} %copy-done.1) | copy-start | bytes 4718596
  244.1 37.6 %collective-permute-start.1 = (bf16[4,192,768]{2,1,0:T(8,128)(2,1)}, bf16[4,192,768]{2,1,0:T(8,128)(2,1)S(1)}, u32[]{:S(2)}, u32[]{:S(2)}) collective-permute-start(bf16[4,192,768]{2,1,0:T(8,128)(2,1)} %get-tuple-element.195), channel_id=1, source_target_pairs={{0,4},{4,0},{8,12},{12,8},{16,20},{20,16},{24,28},{28,24},{1,5},{5... | collective-permute-start | bytes 3538952 | tf_op jit(solution)/shard_map/ppermute | solution.py:37
  245.0 37.9 %collective-permute-start.2 = (bf16[4,192,768]{2,1,0:T(8,128)(2,1)}, bf16[4,192,768]{2,1,0:T(8,128)(2,1)S(1)}, u32[]{:S(2)}, u32[]{:S(2)}) collective-permute-start(bf16[4,192,768]{2,1,0:T(8,128)(2,1)} %get-tuple-element.197), channel_id=1, source_target_pairs={{0,8},{4,12},{8,0},{12,4},{16,24},{20,28},{24,16},{28,20},{1,9},{5... | collective-permute-start | bytes 3538952 | tf_op jit(solution)/shard_map/ppermute | solution.py:37
  274.5 7.3 %copy-start.9 = (bf16[4,192,768]{2,1,0:T(8,128)(2,1)S(1)}, bf16[4,192,768]{2,1,0:T(8,128)(2,1)}, u32[]{:S(2)}) copy-start(bf16[4,192,768]{2,1,0:T(8,128)(2,1)} %get-tuple-element.194) | copy-start | bytes 3538948
  279.4 44.0 %collective-permute-start.5 = (bf16[4,192,896]{2,1,0:T(8,128)(2,1)}, bf16[4,192,896]{2,1,0:T(8,128)(2,1)S(1)}, u32[]{:S(2)}, u32[]{:S(2)}) collective-permute-start(bf16[4,192,896]{2,1,0:T(8,128)(2,1)} %get-tuple-element.193.refs_9_), channel_id=1, source_target_pairs={{0,4},{4,0},{8,12},{12,8},{16,20},{20,16},{24,28},{28,24},{1,5},{5... | collective-permute-start | bytes 4128776 | tf_op jit(solution)/shard_map/ppermute | solution.py:37
  281.7 1.4 copy-start.8
  282.9 1.5 copy-start.13
  282.9 42.7 %collective-permute-start.3 = (bf16[2,192,768]{2,1,0:T(8,128)(2,1)S(1)}, bf16[2,192,768]{2,1,0:T(8,128)(2,1)S(1)}, u32[]{:S(2)}, u32[]{:S(2)}) collective-permute-start(bf16[2,192,768]{2,1,0:T(8,128)(2,1)S(1)} %get-tuple-element.300.refs_10_), channel_id=1, source_target_pairs={{0,8},{4,12},{8,0},{12,4},{16,24},{20,28},{24,16},{28,20},{1,9},{5... | collective-permute-start | bytes 1769480 | tf_op jit(solution)/shard_map/ppermute | solution.py:37
  284.4 0.8 copy-start.15
  284.4 41.2 %collective-permute-start.4 = (bf16[2,192,768]{2,1,0:T(8,128)(2,1)S(1)}, bf16[2,192,768]{2,1,0:T(8,128)(2,1)S(1)}, u32[]{:S(2)}, u32[]{:S(2)}) collective-permute-start(bf16[2,192,768]{2,1,0:T(8,128)(2,1)S(1)} %get-tuple-element.298.refs_11_), channel_id=1, source_target_pairs={{0,16},{4,20},{8,24},{12,28},{16,0},{20,4},{24,8},{28,12},{1,17},{... | collective-permute-start | bytes 1769480 | tf_op jit(solution)/shard_map/ppermute | solution.py:37
  314.9 8.4 %copy-start.5 = (bf16[4,192,896]{2,1,0:T(8,128)(2,1)S(1)}, bf16[4,192,896]{2,1,0:T(8,128)(2,1)}, u32[]{:S(2)}) copy-start(bf16[4,192,896]{2,1,0:T(8,128)(2,1)} %get-tuple-element.216) | copy-start | bytes 4128772
  323.7 39.2 %collective-permute-start.6 = (bf16[2,192,896]{2,1,0:T(8,128)(2,1)S(1)}, bf16[2,192,896]{2,1,0:T(8,128)(2,1)S(1)}, u32[]{:S(2)}, u32[]{:S(2)}) collective-permute-start(bf16[2,192,896]{2,1,0:T(8,128)(2,1)S(1)} %get-tuple-element.292), channel_id=1, source_target_pairs={{0,8},{4,12},{8,0},{12,4},{16,24},{20,28},{24,16},{28,20},{1,9},{5... | collective-permute-start | bytes 2064392 | tf_op jit(solution)/shard_map/ppermute | solution.py:37
  325.6 0.8 copy-start.39
  325.6 1.0 copy-start.40
  358.6 40.9 %collective-permute-start.8 = (bf16[4,192,768]{2,1,0:T(8,128)(2,1)}, bf16[4,192,768]{2,1,0:T(8,128)(2,1)S(1)}, u32[]{:S(2)}, u32[]{:S(2)}) collective-permute-start(bf16[4,192,768]{2,1,0:T(8,128)(2,1)} %get-tuple-element.229), channel_id=1, source_target_pairs={{0,8},{4,12},{8,0},{12,4},{16,24},{20,28},{24,16},{28,20},{1,9},{5... | collective-permute-start | bytes 3538952 | tf_op jit(solution)/shard_map/ppermute | solution.py:37
  358.6 49.3 %collective-permute-start.10 = (bf16[4,192,768]{2,1,0:T(8,128)(2,1)}, bf16[4,192,768]{2,1,0:T(8,128)(2,1)S(1)}, u32[]{:S(2)}, u32[]{:S(2)}) collective-permute-start(bf16[4,192,768]{2,1,0:T(8,128)(2,1)} %get-tuple-element.231), channel_id=1, source_target_pairs={{0,4},{4,0},{8,12},{12,8},{16,20},{20,16},{24,28},{28,24},{1,5},{5... | collective-permute-start | bytes 3538952 | tf_op jit(solution)/shard_map/ppermute | solution.py:37
  359.0 53.5 %collective-permute-start.13 = (bf16[1,192,768]{2,1,0:T(8,128)(2,1)}, bf16[1,192,768]{2,1,0:T(8,128)(2,1)S(1)}, u32[]{:S(2)}, u32[]{:S(2)}) collective-permute-start(bf16[1,192,768]{2,1,0:T(8,128)(2,1)} %get-tuple-element.232), channel_id=1, source_target_pairs={{0,4},{4,0},{8,12},{12,8},{16,20},{20,16},{24,28},{28,24},{1,5},{5... | collective-permute-start | bytes 884744 | tf_op jit(solution)/shard_map/ppermute | solution.py:37
  360.7 72.1 %collective-permute-start.14 = (bf16[1,192,768]{2,1,0:T(8,128)(2,1)}, bf16[1,192,768]{2,1,0:T(8,128)(2,1)S(1)}, u32[]{:S(2)}, u32[]{:S(2)}) collective-permute-start(bf16[1,192,768]{2,1,0:T(8,128)(2,1)} %get-tuple-element.234), channel_id=1, source_target_pairs={{0,16},{4,20},{8,24},{12,28},{16,0},{20,4},{24,8},{28,12},{1,17},{... | collective-permute-start | bytes 884744 | tf_op jit(solution)/shard_map/ppermute | solution.py:37
  363.9 0.7 copy-start.20
  363.9 69.0 %collective-permute-start.12 = (bf16[1,192,896]{2,1,0:T(8,128)(2,1)S(1)}, bf16[1,192,896]{2,1,0:T(8,128)(2,1)S(1)}, u32[]{:S(2)}, u32[]{:S(2)}) collective-permute-start(bf16[1,192,896]{2,1,0:T(8,128)(2,1)S(1)} %get-tuple-element.302.refs_21_), channel_id=1, source_target_pairs={{0,16},{4,20},{8,24},{12,28},{16,0},{20,4},{24,8},{28,12},{1,17},{... | collective-permute-start | bytes 1032200 | tf_op jit(solution)/shard_map/ppermute | solution.py:37
  394.6 12.2 %copy-start.7 = (bf16[4,192,768]{2,1,0:T(8,128)(2,1)S(1)}, bf16[4,192,768]{2,1,0:T(8,128)(2,1)}, u32[]{:S(2)}) copy-start(bf16[4,192,768]{2,1,0:T(8,128)(2,1)} %get-tuple-element.228) | copy-start | bytes 3538948
  399.5 33.9 %collective-permute-start.7 = (bf16[4,192,896]{2,1,0:T(8,128)(2,1)}, bf16[4,192,896]{2,1,0:T(8,128)(2,1)S(1)}, u32[]{:S(2)}, u32[]{:S(2)}) collective-permute-start(bf16[4,192,896]{2,1,0:T(8,128)(2,1)} %get-tuple-element.226.refs_9_), channel_id=1, source_target_pairs={{0,4},{4,0},{8,12},{12,8},{16,20},{20,16},{24,28},{28,24},{1,5},{5... | collective-permute-start | bytes 4128776 | tf_op jit(solution)/shard_map/ppermute | solution.py:37
  406.9 4.5 copy-start.6
  407.9 4.5 copy-start.14
  408.0 26.4 %collective-permute-start.9 = (bf16[2,192,768]{2,1,0:T(8,128)(2,1)S(1)}, bf16[2,192,768]{2,1,0:T(8,128)(2,1)S(1)}, u32[]{:S(2)}, u32[]{:S(2)}) collective-permute-start(bf16[2,192,768]{2,1,0:T(8,128)(2,1)S(1)} %get-tuple-element.296.refs_11_), channel_id=1, source_target_pairs={{0,16},{4,20},{8,24},{12,28},{16,0},{20,4},{24,8},{28,12},{1,17},{... | collective-permute-start | bytes 1769480 | tf_op jit(solution)/shard_map/ppermute | solution.py:37
  412.5 0.8 copy-start.18
  412.5 20.3 %copy-start.42 = (bf16[1,192,768]{2,1,0:T(8,128)(2,1)}, bf16[1,192,768]{2,1,0:T(8,128)(2,1)S(1)}, u32[]{:S(2)}) copy-start(bf16[1,192,768]{2,1,0:T(8,128)(2,1)S(1)} %collective-permute-done.13.refs_8_) | copy-start | bytes 884740
  412.5 26.5 %collective-permute-start.11 = (bf16[2,192,768]{2,1,0:T(8,128)(2,1)S(1)}, bf16[2,192,768]{2,1,0:T(8,128)(2,1)S(1)}, u32[]{:S(2)}, u32[]{:S(2)}) collective-permute-start(bf16[2,192,768]{2,1,0:T(8,128)(2,1)S(1)} %get-tuple-element.294.refs_10_), channel_id=1, source_target_pairs={{0,8},{4,12},{8,0},{12,4},{16,24},{20,28},{24,16},{28,20},{1,9},{5... | collective-permute-start | bytes 1769480 | tf_op jit(solution)/shard_map/ppermute | solution.py:37
  432.8 6.1 %copy-start.43 = (bf16[1,192,768]{2,1,0:T(8,128)(2,1)}, bf16[1,192,768]{2,1,0:T(8,128)(2,1)S(1)}, u32[]{:S(2)}) copy-start(bf16[1,192,768]{2,1,0:T(8,128)(2,1)S(1)} %collective-permute-done.14.refs_10_) | copy-start | bytes 884740
  432.8 6.1 %copy-start.41 = (bf16[1,192,896]{2,1,0:T(8,128)(2,1)}, bf16[1,192,896]{2,1,0:T(8,128)(2,1)S(1)}, u32[]{:S(2)}) copy-start(bf16[1,192,896]{2,1,0:T(8,128)(2,1)S(1)} %collective-permute-done.12.refs_6_) | copy-start | bytes 1032196
  433.4 5.6 %copy-start.36 = (bf16[4,192,896]{2,1,0:T(8,128)(2,1)}, bf16[4,192,896]{2,1,0:T(8,128)(2,1)S(1)}, u32[]{:S(2)}) copy-start(bf16[4,192,896]{2,1,0:T(8,128)(2,1)S(1)} %collective-permute-done.7.refs_0_) | copy-start | bytes 4128772
  434.4 4.6 copy-start.37
  439.0 0.8 copy-start.38
  489.9 2.2 copy-start.10
  491.1 1.5 copy-start.4
  492.6 2.1 copy-start.17
  494.7 1.1 copy-start.16
  496.0 4.8 copy-start.22
  496.0 5.4 %copy-start.26 = (f32[2,5,256]{2,1,0:T(8,128)S(1)}, f32[2,5,256]{2,1,0:T(8,128)}, u32[]{:S(2)}) copy-start(f32[2,5,256]{2,1,0:T(8,128)} %get-tuple-element.283) | copy-start | bytes 30724
  496.0 6.0 %copy-start.32 = (f32[2,256]{1,0:T(2,128)S(1)}, f32[2,256]{1,0:T(2,128)}, u32[]{:S(2)}) copy-start(f32[2,256]{1,0:T(2,128)} %get-tuple-element.258) | copy-start | bytes 6148
  496.0 6.6 %copy-start.31 = (f32[2,768]{1,0:T(2,128)S(1)}, f32[2,768]{1,0:T(2,128)}, u32[]{:S(2)}) copy-start(f32[2,768]{1,0:T(2,128)} %get-tuple-element.259) | copy-start | bytes 18436
  496.0 8.6 %copy-start.11 = (f32[192,768]{1,0:T(8,128)S(1)}, f32[192,768]{1,0:T(8,128)}, u32[]{:S(2)}) copy-start(f32[192,768]{1,0:T(8,128)} %get-tuple-element.261) | copy-start | bytes 1769476
  496.0 8.6 %copy-start.12 = (f32[192,768]{1,0:T(8,128)S(1)}, f32[192,768]{1,0:T(8,128)}, u32[]{:S(2)}) copy-start(f32[192,768]{1,0:T(8,128)} %get-tuple-element.262) | copy-start | bytes 1769476
  500.0 5.7 %copy-start.3 = (bf16[512,1536]{1,0:T(8,128)(2,1)S(1)}, bf16[512,1536]{1,0:T(8,128)(2,1)}, u32[]{:S(2)}) copy-start(bf16[512,1536]{1,0:T(8,128)(2,1)} %get-tuple-element.329) | copy-start | bytes 4718596
  505.7 1.1 copy-start.30

commit v6 on v5

--- a/solution.py
+++ b/solution.py
@@ -1161,13 +1161,13 @@
     )
 
 
-def bwd_gate(l, gb, q, gate, y, mixed, entry, krs, r2b, side, width):
+def bwd_gate(l, gb, q, gate, y, mixed, entry, krs, r2b, side, width, after):
     tokens, inner = y.shape
     states = krs.shape[1] // 2
     return kcall(
         partial(bwd_gate_body, width), [gb, q["w_out"], gate, y, mixed, entry, krs, r2b, side, q["gate_gain"]],
         [full(gb.shape), rows_of_layer(l, q["w_out"].shape), cols(tokens, WIDE), cols(tokens, WIDE), cols(tokens, WIDE), cols(tokens, WIDE), full(krs.shape),
-         full(r2b.shape), full(side.shape), of_layer(l, q["gate_gain"].shape, WIDE)], 9,
+         full(r2b.shape), full(side.shape), of_layer(l, q["gate_gain"].shape, WIDE)], 9, after,
         name="bwd_gate",
         grid=(inner // WIDE,),
         out_specs=[cols(tokens, WIDE), cols(tokens, WIDE), cols(tokens, WIDE), rowsb(states, WIDE), cols(1, WIDE), cols(1, WIDE)],
@@ -1369,9 +1369,9 @@
     return nx_next, h_new, side, stored
 
 
-def backward_gate(gb, side, s, q, layer):
+def backward_gate(gb, side, s, q, layer, after):
     width = q["inner"] * lax.axis_size("head")
-    return bwd_gate(layer, gb, q, s["gate"], s["y"], s["mixed"], s["entry"], s["krs"], s["r2b"], side, width)
+    return bwd_gate(layer, gb, q, s["gate"], s["y"], s["mixed"], s["entry"], s["krs"], s["r2b"], side, width, after)
 
 
 def local(hidden_in, seg, cot, norm_gain, w_zx, w_bc, w_dt, conv_x, conv_bc, dt_bias, a_log, skip_d, gate_gain, w_out):
@@ -1413,10 +1413,10 @@
     pending = []
     for l in reversed(range(LAYERS)):
         s = stored[l]
-        gy, gz, scaled, qloc, ggate, gskip = backward_gate(gb, side, s, q, l)
         if pending:
             pending[2].fold()
             pending[2].go()
+        gy, gz, scaled, qloc, ggate, gskip = backward_gate(gb, side, s, q, l, [p.away for p in pending[2:]])
         (dvd, dd, rowT, dkr, later), out, z = bwd_local(
             heads, size, gy, s["mixed"], s["krs"], s["cum"], s["steps"], s["cT"], s["gram"], s["entry"], s["enter"], aux, segrow, qloc,
             s["dec"], 2 * LAYERS + l, gb, scaled, s["nx"], gz, pending[:2], ())

time: 516 us -> 510 us (0.988)
    unnamed x99 -> x101, local copies, waits for them, and re-layouts: 23.3 us -> 23.8 us
  transfers between devices with their start and end apart: 15 -> 15, of which waited for: 3 -> 2; matrix products, arithmetic and copies ran while one was open for 6% -> 6% of each run, Pallas kernels for 31% -> 30%
where the time goes in v6:
time: 510 us; the launch traced here: 501 us
  Pallas kernels  412 us (81%)
  local copies, waits for them, and re-layouts  37.1 us (7%)
  starting transfers between devices  25.1 us (5%)
  other arithmetic  20 us (4%)
  waiting for transfers between devices  5.32 us (1%)
    pallas_call x21, Pallas kernels, kcall(): pl.pallas_call(wrapped, in_specs=list(specs) + [pl.BlockSpec(memory_space...  412 us
    unnamed x101, local copies, waits for them, and re-layouts  23.8 us
    ppermute x14, starting transfers between devices, swap(): return lax.ppermute(x, axis, [(i, i ^ bit) for i in range(n)])  20.2 us
  transfers between devices with their start and end apart: 15, of which 2 were waited for; matrix products, arithmetic and copies ran while one was open for 6% of the time, Pallas kernels for 30%

profile of v6, /device:TPU:0, one launch (start us, length us, event | category | flops | bytes accessed | tf_op | source)
XLA Modules:
  0.0 500.8 jit_solution(14147269625598951210)
XLA Ops:
  0.7 0.8 slice_reduce_fusion
  1.5 1.8 fusion
  3.8 1.1 copy-done.1
  4.9 5.0 collective-permute-start
  11.1 1.0 dynamic-slice_convert_fusion.refs_4_.refs_5_
  12.2 2.2 fusion.25
  14.4 1.8 select_select_fusion
  16.2 1.4 fusion.21
  18.2 8.7 %copy.94 = bf16[2,1536,2,768]{3,1,2,0:T(8,128)(2,1)} copy(bf16[2,1536,2,768]{3,2,1,0:T(2,128)(2,1)} %param.18) | data formatting | bytes 18874368 | tf_op args[4]
  29.3 0.7 broadcast_in_dim_reshape.4.refs_9_.refs_11_
  30.7 1.3 pad_maximum_fusion.1.refs_0_.refs_15_
  31.9 1.6 broadcast_in_dim.35.refs_8_.refs_7_.refs_9_.refs_14_.refs_3_
  33.5 14.3 %fwd_mix.2 = (bf16[528,768]{1,0:T(8,128)(2,1)}, bf16[528,256]{1,0:T(8,128)(2,1)}, f32[512,256]{1,0:T(8,128)}, bf16[512,128]{1,0:T(8,128)(2,1)}, f32[512,128]{1,0...) custom-call(bf16[528,1536]{1,0:T(8,128)(2,1)} %pad_maximum_fusion.1., ...), custom_call_target="tpu_custom_call" | custom-call | flops 12000000000 | bytes 36000000 | tf_op jit(solution)/shard_map/fwd_mix/pallas_call | solution.py:1100
  47.8 30.6 %fwd_inside.2 = (f32[512,768]{1,0:T(8,128)}, f32[768,128]{1,0:T(8,128)}, bf16[512,768]{1,0:T(8,128)(2,1)}, f32[512,512]{1,0:T(8,128)}) custom-call(bf16[528,1536]{1,0:T(8,128)(2,1)} %pad_maximum_fusion.1.refs_0_.refs_15_, bf16[2,2,1536,768]{3,2,1,0:T(8,128)(2,1)} %bitcast.92, f32[512,768]{1,0:T(8,128)} %get-tuple-element.138.refs_2_.refs_4_.refs_1_, ...), custom_call_target="tpu_custom_call" | custom-call | flops 28000000000 | bytes 84000000 | tf_op jit(solution)/shard_map/fwd_inside/pallas_call | solution.py:1100
  78.4 6.3 %fwd_gate.2 = (f32[512,768]{1,0:T(8,128)}, f32[512,768]{1,0:T(8,128)}, f32[512,768]{1,0:T(8,128)}, f32[8,512]{1,0:T(8,128)}) custom-call(f32[512,768]{1,0:T(8,128)} %get-tuple-element.145.refs_0_, f32[512,768]{1,0:T(8,128)} %get-tuple-element.146.refs_1_.refs_5_.refs_7_.refs_4_, bf16[512,768]{1,0:T(8,128)(2,1)} %get-tuple-element.147.refs_2_, ...), custom_call_target="tpu_custom_call" | custom-call | flops 7000000000 | bytes 21000000 | tf_op jit(solution)/shard_map/fwd_gate/pallas_call | solution.py:1100
  84.7 41.2 %head_fwd.1 = (bf16[528,1536]{1,0:T(8,128)(2,1)}, f32[128,1536]{1,0:T(8,128)}, f32[128,1536]{1,0:T(8,128)}, f32[512,128]{1,0:T(8,128)}, f32[32,128]{1,0:T(8,128)}) custom-call(f32[512,768]{1,0:T(8,128)} %get-tuple-element.149.refs_0_, f32[8,512]{1,0:T(8,128)} %get-tuple-element.150.refs_1_, f32[2,1,768]{2,1,0:T(1,128)} %broadcast_in_dim.37.refs_2_.refs_9_, ...), custom_call_target="tpu_custom_call" | custom-call | flops 30000001024 | bytes 90000000 | tf_op jit(solution)/shard_map/head_fwd/pallas_call | solution.py:1100
  125.9 14.3 %fwd_mix.3 = (bf16[528,768]{1,0:T(8,128)(2,1)}, bf16[528,256]{1,0:T(8,128)(2,1)}, f32[512,256]{1,0:T(8,128)}, bf16[512,128]{1,0:T(8,128)(2,1)}, f32[512,128]{1,0...) custom-call(bf16[528,1536]{1,0:T(8,128)(2,1)} %get-tuple-element.151, ...), custom_call_target="tpu_custom_call" | custom-call | flops 12000000000 | bytes 36000000 | tf_op jit(solution)/shard_map/fwd_mix/pallas_call | solution.py:1100
  140.2 33.5 %fwd_inside.3 = (f32[512,768]{1,0:T(8,128)}, f32[768,128]{1,0:T(8,128)}, bf16[512,768]{1,0:T(8,128)(2,1)}, f32[512,512]{1,0:T(8,128)}) custom-call(bf16[528,1536]{1,0:T(8,128)(2,1)} %get-tuple-element.151.refs_0_.refs_15_, bf16[2,2,1536,768]{3,2,1,0:T(8,128)(2,1)} %bitcast.94, f32[512,768]{1,0:T(8,128)} %get-tuple-element.152.refs_2_.refs_4_.refs_1_, ...), custom_call_target="tpu_custom_call" | custom-call | flops 28000000000 | bytes 84000000 | tf_op jit(solution)/shard_map/fwd_inside/pallas_call | solution.py:1100
  173.7 6.3 %fwd_gate.3 = (f32[512,768]{1,0:T(8,128)}, f32[512,768]{1,0:T(8,128)}, f32[512,768]{1,0:T(8,128)}, f32[8,512]{1,0:T(8,128)}) custom-call(f32[512,768]{1,0:T(8,128)} %get-tuple-element.159.refs_0_, f32[512,768]{1,0:T(8,128)} %get-tuple-element.160.refs_1_.refs_5_.refs_7_.refs_4_, bf16[512,768]{1,0:T(8,128)(2,1)} %get-tuple-element.161.refs_2_, ...), custom_call_target="tpu_custom_call" | custom-call | flops 7000000000 | bytes 21000000 | tf_op jit(solution)/shard_map/fwd_gate/pallas_call | solution.py:1100
  180.0 29.8 %head_fwd_last.1 = (bf16[512,1536]{1,0:T(8,128)(2,1)}, f32[128,1536]{1,0:T(8,128)}, f32[128,1536]{1,0:T(8,128)}, f32[512,128]{1,0:T(8,128)}, f32[32,128]{1,0:T(8,128)}) custom-call(f32[512,768]{1,0:T(8,128)} %get-tuple-element.163.refs_0_, f32[8,512]{1,0:T(8,128)} %get-tuple-element.164.refs_1_, f32[2,1,768]{2,1,0:T(1,128)} %broadcast_in_dim.37.refs_2_.refs_9_, ...), custom_call_target="tpu_custom_call" | custom-call | flops 30000001024 | bytes 90000000 | tf_op jit(solution)/shard_map/head_fwd_last/pallas_call | solution.py:1100
  209.8 8.1 %bwd_gate.2 = (f32[512,768]{1,0:T(8,128)}, bf16[512,768]{1,0:T(8,128)(2,1)}, bf16[512,768]{1,0:T(8,128)(2,1)}, f32[768,128]{1,0:T(8,128)}, f32[1,768]{1,0:T(1,128)}, /*index=5*/f32[1,768]{1,0:T(1,128)}) custom-call(bf16[512,1536]{1,0:T(8,128)(2,1)} %refs_13_.3, bf16[2,768,1536]{2,1,0:T(8,128)(2,1)} %refs_1_.3, bf16[512,768]{1,0:T(8,128)(2,1)} %get-tuple-element.161.refs_2_, ...), custom_call_target="tpu_custom_call" | custom-call | flops 8999999488 | bytes 27000000 | tf_op jit(solution)/shard_map/bwd_gate/pallas_call | solution.py:1100
  217.9 26.1 %bwd_local.2 = (f32[512,768]{1,0:T(8,128)}, f32[512,128]{1,0:T(8,128)}, f32[128,512]{1,0:T(8,128)}, f32[512,256]{1,0:T(8,128)}, f32[768,128]{1,0:T(8,128)}, /*in...) custom-call(f32[512,768]{1,0:T(8,128)} %get-tuple-element.171.refs_0, ...), custom_call_target="tpu_custom_call" | custom-call | flops 24000000000 | bytes 72000000 | tf_op jit(solution)/shard_map/bwd_local/pallas_call | solution.py:1100
  244.0 1.2 collective-permute-start.1
  245.2 12.0 %bwd_carry.2 = (f32[8,768]{1,0:T(8,128)}, bf16[512,768]{1,0:T(8,128)(2,1)}, f32[16,768]{1,0:T(8,128)}, f32[8,768]{1,0:T(8,128)}, bf16[512,128]{1,0:T(8,128)(2,1)}, /*index=5*/f32[8,128]{1,0:T(8,128)}, f32[512,256]{1,0:T(8,128)}) custom-call(f32[512,768]{1,0:T(8,128)} %get-tuple-element.171.refs_0_, f32[512,768]{1,0:T(8,128)} %get-tuple-element.175.refs_1_, ...), custom_call_target="tpu_custom_call" | custom-call | flops 11000000512 | bytes 33000000 | tf_op jit(solution)/shard_map/bwd_carry/pallas_call | solution.py:1100
  257.2 16.1 %maps_bwd.2 = (bf16[512,128]{1,0:T(8,128)(2,1)}, f32[8,128]{1,0:T(8,128)}, bf16[16,768]{1,0:T(8,128)(2,1)}) custom-call(f32[512,256]{1,0:T(8,128)} %get-tuple-element.185.refs_0_, bf16[528,256]{1,0:T(8,128)(2,1)} %get-tuple-element.186.refs_1_, f32[2,5,256]{2,1,0:T(8,128)} %copy.51.refs_5_.refs_2_, ...), custom_call_target="tpu_custom_call" | custom-call | flops 14000000000 | bytes 42000000 | tf_op jit(solution)/shard_map/maps_bwd/pallas_call | solution.py:1100
  273.3 1.3 constant_dynamic-update-slice_fusion.1.refs_1_
  274.7 4.9 wgrad.2
  279.5 1.9 collective-permute-start.3
  281.5 1.2 fusion.7
  282.9 1.1 fusion.8
  284.9 29.9 %head_bwd.2 = (bf16[512,1536]{1,0:T(8,128)(2,1)}, f32[128,1536]{1,0:T(8,128)}, f32[1,1536]{1,0:T(1,128)}, f32[32,128]{1,0:T(8,128)}) custom-call(bf16[512,768]{1,0:T(8,128)(2,1)} %get-tuple-element.170.refs_16_.refs_0_, bf16[512,768]{1,0:T(8,128)(2,1)} %constant_dynamic-update-slice_fusion.1.refs_1_, bf16[512,128]{1,0:T(8,128)(2,1)} %get-tuple-element.191.refs_2_, ...), custom_call_target="tpu_custom_call" | custom-call | flops 28999999488 | bytes 87000000 | tf_op jit(solution)/shard_map/head_bwd/pallas_call | solution.py:1100
  315.2 1.9 collective-permute-start.6
  317.0 8.3 %bwd_gate.3 = (f32[512,768]{1,0:T(8,128)}, bf16[512,768]{1,0:T(8,128)(2,1)}, bf16[512,768]{1,0:T(8,128)(2,1)}, f32[768,128]{1,0:T(8,128)}, f32[1,768]{1,0:T(1,128)}, /*index=5*/f32[1,768]{1,0:T(1,128)}) custom-call(bf16[512,1536]{1,0:T(8,128)(2,1)} %get-tuple-element.198.refs_0_.refs_13_, bf16[2,768,1536]{2,1,0:T(8,128)(2,1)} %refs_1_.3, ...), custom_call_target="tpu_custom_call" | custom-call | flops 8999999488 | bytes 27000000 | tf_op jit(solution)/shard_map/bwd_gate/pallas_call | solution.py:1100
  325.4 0.8 copy-done.40
  326.3 26.9 %bwd_local.3 = (f32[512,768]{1,0:T(8,128)}, f32[512,128]{1,0:T(8,128)}, f32[128,512]{1,0:T(8,128)}, f32[512,256]{1,0:T(8,128)}, f32[768,128]{1,0:T(8,128)}, /*in...) custom-call(f32[512,768]{1,0:T(8,128)} %get-tuple-element.203.refs_0, ...), custom_call_target="tpu_custom_call" | custom-call | flops 24000000000 | bytes 72000000 | tf_op jit(solution)/shard_map/bwd_local/pallas_call | solution.py:1100
  353.3 1.1 collective-permute-start.10
  354.5 1.0 collective-permute-start.13
  355.4 2.2 collective-permute-start.14
  357.6 0.9 add_convert_fusion.10
  358.5 0.7 collective-permute-start.12
  359.3 12.0 %bwd_carry.3 = (f32[8,768]{1,0:T(8,128)}, bf16[512,768]{1,0:T(8,128)(2,1)}, f32[16,768]{1,0:T(8,128)}, f32[8,768]{1,0:T(8,128)}, bf16[512,128]{1,0:T(8,128)(2,1)}, /*index=5*/f32[8,128]{1,0:T(8,128)}, f32[512,256]{1,0:T(8,128)}) custom-call(f32[512,768]{1,0:T(8,128)} %get-tuple-element.203.refs_0_, f32[512,768]{1,0:T(8,128)} %get-tuple-element.208.refs_1_, ...), custom_call_target="tpu_custom_call" | custom-call | flops 11000000512 | bytes 33000000 | tf_op jit(solution)/shard_map/bwd_carry/pallas_call | solution.py:1100
  371.4 16.6 %maps_bwd.3 = (bf16[512,128]{1,0:T(8,128)(2,1)}, f32[8,128]{1,0:T(8,128)}, bf16[16,768]{1,0:T(8,128)(2,1)}) custom-call(f32[512,256]{1,0:T(8,128)} %get-tuple-element.219.refs_0_, bf16[528,256]{1,0:T(8,128)(2,1)} %get-tuple-element.220.refs_1_, f32[2,5,256]{2,1,0:T(8,128)} %copy.51.refs_5_.refs_2_, ...), custom_call_target="tpu_custom_call" | custom-call | flops 14000000000 | bytes 42000000 | tf_op jit(solution)/shard_map/maps_bwd/pallas_call | solution.py:1100
  388.0 1.4 constant_dynamic-update-slice_fusion.refs_1_
  389.4 4.8 wgrad.3
  394.2 8.2 %collective-permute-start.7 = (bf16[4,192,896]{2,1,0:T(8,128)(2,1)}, bf16[4,192,896]{2,1,0:T(8,128)(2,1)S(1)}, u32[]{:S(2)}, u32[]{:S(2)}) collective-permute-start(bf16[4,192,896]{2,1,0:T(8,128)(2,1)} %get-tuple-element.226.refs_9_), channel_id=1, source_target_pairs={{0,4},{4,0},{8,12},{12,8},{16,20},{20,16},{24,28},{28,24},{1,5},{5... | collective-permute-start | bytes 4128776 | tf_op jit(solution)/shard_map/ppermute | solution.py:37
  402.4 1.1 fusion.10
  403.5 1.6 collective-permute-start.9
  405.1 1.1 fusion.12
  406.3 0.7 copy-done.19
  407.0 19.5 %head_bwd.3 = (bf16[128,1536]{1,0:T(8,128)(2,1)}, f32[128,1536]{1,0:T(8,128)}, f32[1,1536]{1,0:T(1,128)}, f32[32,128]{1,0:T(8,128)}) custom-call(bf16[512,768]{1,0:T(8,128)(2,1)} %get-tuple-element.207.refs_16_.refs_0_, bf16[512,768]{1,0:T(8,128)(2,1)} %constant_dynamic-update-slice_fusion.refs_1_, bf16[512,128]{1,0:T(8,128)(2,1)} %get-tuple-element.225.refs_2_, ...), custom_call_target="tpu_custom_call" | custom-call | flops 28999999488 | bytes 87000000 | tf_op jit(solution)/shard_map/head_bwd/pallas_call | solution.py:1100
  426.6 3.2 collective-permute-done.7.refs_0_
  429.8 2.1 collective-permute-done.11.refs_4_
  431.9 0.8 copy-done.39
  432.7 50.2 %tail.1 = (f32[192,896]{1,0:T(8,128)}, f32[192,768]{1,0:T(8,128)}, f32[192,768]{1,0:T(8,128)}, f32[192,896]{1,0:T(8,128)}, f32[192,768]{1,0:T(8,128)}, /*index=5...) custom-call(bf16[4,192,896]{2,1,0:T(8,128)(2,1)} %copy-done.37, ...), custom_call_target="tpu_custom_call" | custom-call | flops 44999999488 | bytes 135000000 | tf_op jit(solution)/shard_map/tail/pallas_call | solution.py:1100
  482.8 1.2 slice_bitcast_fusion.1
  484.0 1.0 slice_bitcast_fusion.3
  485.5 2.1 convert_element_type.345
  487.7 1.0 copy-done.17
  488.9 3.2 copy.76
  492.2 0.8 copy.77
  492.9 0.7 copy.78
  496.2 1.3 constant_dynamic-slice_fusion
  497.5 1.1 pad_maximum_fusion.2
  498.6 1.1 copy.99
  (133 shorter events, 11.1 us)
Async XLA Ops:
  0.6 2.7 copy-start
  3.3 6.6 %copy-start.22 = (bf16[2,1536,12]{1,0,2:T(2,128)(2,1)S(1)}, bf16[2,1536,12]{1,0,2:T(2,128)(2,1)}, u32[]{:S(2)}) copy-start(bf16[2,1536,12]{1,0,2:T(2,128)(2,1)} %param.20) | copy-start | bytes 221188
  3.8 1.1 copy-start.1
  4.9 5.6 %copy-start.29 = (s32[512]{0:T(512)S(1)}, s32[512]{0:T(512)}, u32[]{:S(2)}) copy-start(s32[512]{0:T(512)} %param.15) | copy-start | bytes 6148
  4.9 25.7 %collective-permute-start = (bf16[16,1536]{1,0:T(8,128)(2,1)S(1)}, bf16[16,1536]{1,0:T(8,128)(2,1)S(1)}, u32[]{:S(2)}, u32[]{:S(2)}) collective-permute-start(bf16[16,1536]{1,0:T(8,128)(2,1)S(1)} %slice.76), channel_id=1, source_target_pairs={{0,4},{4,8},{8,12},{12,16},{16,20},{20,24},{24,28},{1,5},{5,9},{9,... | collective-permute-start | bytes 147464 | tf_op jit(solution)/shard_map/ppermute | solution.py:42
  10.5 20.1 %copy-start.26 = (f32[512]{0:T(512)}, f32[512]{0:T(512)S(1)}, u32[]{:S(2)}) copy-start(f32[512]{0:T(512)S(1)} %convert_element_type.296) | copy-start | bytes 6148
  12.2 2.2 copy-start.20
  14.4 3.2 copy-start.25
  18.2 8.7 %copy-start.24 = (f32[2,5,768]{2,0,1:T(2,128)S(1)}, f32[2,5,768]{2,0,1:T(2,128)}, u32[]{:S(2)}) copy-start(f32[2,5,768]{2,0,1:T(2,128)} %param.21) | copy-start | bytes 92164
  18.2 9.4 %copy-start.28 = (f32[2,5,256]{2,0,1:T(2,128)S(1)}, f32[2,5,256]{2,0,1:T(2,128)}, u32[]{:S(2)}) copy-start(f32[2,5,256]{2,0,1:T(2,128)} %param.22) | copy-start | bytes 30724
  18.2 10.0 %copy-start.35 = (f32[2,12]{1,0:T(2,128)S(1)}, f32[2,12]{1,0:T(2,128)}, u32[]{:S(2)}) copy-start(f32[2,12]{1,0:T(2,128)} %param.23) | copy-start | bytes 292
  18.2 10.5 %copy-start.36 = (f32[2,12]{1,0:T(2,128)S(1)}, f32[2,12]{1,0:T(2,128)}, u32[]{:S(2)}) copy-start(f32[2,12]{1,0:T(2,128)} %param.24) | copy-start | bytes 292
  18.2 11.1 %copy-start.34 = (f32[2,12]{1,0:T(2,128)S(1)}, f32[2,12]{1,0:T(2,128)}, u32[]{:S(2)}) copy-start(f32[2,12]{1,0:T(2,128)} %param.25) | copy-start | bytes 292
  18.2 11.8 %copy-start.30 = (f32[2,768]{1,0:T(2,128)S(1)}, f32[2,768]{1,0:T(2,128)}, u32[]{:S(2)}) copy-start(f32[2,768]{1,0:T(2,128)} %param.26) | copy-start | bytes 18436
  18.2 12.5 %copy-start.2 = (bf16[512,1536]{1,0:T(8,128)(2,1)S(1)}, bf16[512,1536]{1,0:T(8,128)(2,1)}, u32[]{:S(2)}) copy-start(bf16[512,1536]{1,0:T(8,128)(2,1)} %copy-done.1) | copy-start | bytes 4718596
  244.0 37.5 %collective-permute-start.1 = (bf16[4,192,768]{2,1,0:T(8,128)(2,1)}, bf16[4,192,768]{2,1,0:T(8,128)(2,1)S(1)}, u32[]{:S(2)}, u32[]{:S(2)}) collective-permute-start(bf16[4,192,768]{2,1,0:T(8,128)(2,1)} %get-tuple-element.195), channel_id=1, source_target_pairs={{0,4},{4,0},{8,12},{12,8},{16,20},{20,16},{24,28},{28,24},{1,5},{5... | collective-permute-start | bytes 3538952 | tf_op jit(solution)/shard_map/ppermute | solution.py:37
  245.2 37.5 %collective-permute-start.2 = (bf16[4,192,768]{2,1,0:T(8,128)(2,1)}, bf16[4,192,768]{2,1,0:T(8,128)(2,1)S(1)}, u32[]{:S(2)}, u32[]{:S(2)}) collective-permute-start(bf16[4,192,768]{2,1,0:T(8,128)(2,1)} %get-tuple-element.197), channel_id=1, source_target_pairs={{0,8},{4,12},{8,0},{12,4},{16,24},{20,28},{24,16},{28,20},{1,9},{5... | collective-permute-start | bytes 3538952 | tf_op jit(solution)/shard_map/ppermute | solution.py:37
  274.7 6.8 %copy-start.9 = (bf16[4,192,768]{2,1,0:T(8,128)(2,1)S(1)}, bf16[4,192,768]{2,1,0:T(8,128)(2,1)}, u32[]{:S(2)}) copy-start(bf16[4,192,768]{2,1,0:T(8,128)(2,1)} %get-tuple-element.194) | copy-start | bytes 3538948
  279.5 35.2 %collective-permute-start.3 = (bf16[4,192,896]{2,1,0:T(8,128)(2,1)}, bf16[4,192,896]{2,1,0:T(8,128)(2,1)S(1)}, u32[]{:S(2)}, u32[]{:S(2)}) collective-permute-start(bf16[4,192,896]{2,1,0:T(8,128)(2,1)} %get-tuple-element.193.refs_9_), channel_id=1, source_target_pairs={{0,4},{4,0},{8,12},{12,8},{16,20},{20,16},{24,28},{28,24},{1,5},{5... | collective-permute-start | bytes 4128776 | tf_op jit(solution)/shard_map/ppermute | solution.py:37
  281.5 1.4 copy-start.8
  282.7 1.4 copy-start.14
  282.7 42.7 %collective-permute-start.4 = (bf16[2,192,768]{2,1,0:T(8,128)(2,1)S(1)}, bf16[2,192,768]{2,1,0:T(8,128)(2,1)S(1)}, u32[]{:S(2)}, u32[]{:S(2)}) collective-permute-start(bf16[2,192,768]{2,1,0:T(8,128)(2,1)S(1)} %get-tuple-element.300.refs_10_), channel_id=1, source_target_pairs={{0,8},{4,12},{8,0},{12,4},{16,24},{20,28},{24,16},{28,20},{1,9},{5... | collective-permute-start | bytes 1769480 | tf_op jit(solution)/shard_map/ppermute | solution.py:37
  284.0 0.8 copy-start.16
  284.0 41.3 %collective-permute-start.5 = (bf16[2,192,768]{2,1,0:T(8,128)(2,1)S(1)}, bf16[2,192,768]{2,1,0:T(8,128)(2,1)S(1)}, u32[]{:S(2)}, u32[]{:S(2)}) collective-permute-start(bf16[2,192,768]{2,1,0:T(8,128)(2,1)S(1)} %get-tuple-element.298.refs_11_), channel_id=1, source_target_pairs={{0,16},{4,20},{8,24},{12,28},{16,0},{20,4},{24,8},{28,12},{1,17},{... | collective-permute-start | bytes 1769480 | tf_op jit(solution)/shard_map/ppermute | solution.py:37
  284.9 29.9 %copy-start.5 = (bf16[4,192,896]{2,1,0:T(8,128)(2,1)S(1)}, bf16[4,192,896]{2,1,0:T(8,128)(2,1)}, u32[]{:S(2)}) copy-start(bf16[4,192,896]{2,1,0:T(8,128)(2,1)} %get-tuple-element.202) | copy-start | bytes 4128772
  315.2 1.9 copy-start.11
  315.2 42.5 %collective-permute-start.6 = (bf16[2,192,896]{2,1,0:T(8,128)(2,1)S(1)}, bf16[2,192,896]{2,1,0:T(8,128)(2,1)S(1)}, u32[]{:S(2)}, u32[]{:S(2)}) collective-permute-start(bf16[2,192,896]{2,1,0:T(8,128)(2,1)S(1)} %get-tuple-element.292.refs_10_), channel_id=1, source_target_pairs={{0,8},{4,12},{8,0},{12,4},{16,24},{20,28},{24,16},{28,20},{1,9},{5... | collective-permute-start | bytes 2064392 | tf_op jit(solution)/shard_map/ppermute | solution.py:37
  325.3 0.8 copy-start.40
  325.3 1.0 copy-start.41
  353.2 41.0 %collective-permute-start.8 = (bf16[4,192,768]{2,1,0:T(8,128)(2,1)}, bf16[4,192,768]{2,1,0:T(8,128)(2,1)S(1)}, u32[]{:S(2)}, u32[]{:S(2)}) collective-permute-start(bf16[4,192,768]{2,1,0:T(8,128)(2,1)} %get-tuple-element.229), channel_id=1, source_target_pairs={{0,8},{4,12},{8,0},{12,4},{16,24},{20,28},{24,16},{28,20},{1,9},{5... | collective-permute-start | bytes 3538952 | tf_op jit(solution)/shard_map/ppermute | solution.py:37
  353.3 50.2 %collective-permute-start.10 = (bf16[4,192,768]{2,1,0:T(8,128)(2,1)}, bf16[4,192,768]{2,1,0:T(8,128)(2,1)S(1)}, u32[]{:S(2)}, u32[]{:S(2)}) collective-permute-start(bf16[4,192,768]{2,1,0:T(8,128)(2,1)} %get-tuple-element.231), channel_id=1, source_target_pairs={{0,4},{4,0},{8,12},{12,8},{16,20},{20,16},{24,28},{28,24},{1,5},{5... | collective-permute-start | bytes 3538952 | tf_op jit(solution)/shard_map/ppermute | solution.py:37
  354.5 51.7 %collective-permute-start.13 = (bf16[1,192,768]{2,1,0:T(8,128)(2,1)}, bf16[1,192,768]{2,1,0:T(8,128)(2,1)S(1)}, u32[]{:S(2)}, u32[]{:S(2)}) collective-permute-start(bf16[1,192,768]{2,1,0:T(8,128)(2,1)} %get-tuple-element.232), channel_id=1, source_target_pairs={{0,4},{4,0},{8,12},{12,8},{16,20},{20,16},{24,28},{28,24},{1,5},{5... | collective-permute-start | bytes 884744 | tf_op jit(solution)/shard_map/ppermute | solution.py:37
  355.4 71.1 %collective-permute-start.14 = (bf16[1,192,768]{2,1,0:T(8,128)(2,1)}, bf16[1,192,768]{2,1,0:T(8,128)(2,1)S(1)}, u32[]{:S(2)}, u32[]{:S(2)}) collective-permute-start(bf16[1,192,768]{2,1,0:T(8,128)(2,1)} %get-tuple-element.234), channel_id=1, source_target_pairs={{0,16},{4,20},{8,24},{12,28},{16,0},{20,4},{24,8},{28,12},{1,17},{... | collective-permute-start | bytes 884744 | tf_op jit(solution)/shard_map/ppermute | solution.py:37
  358.5 0.8 copy-start.21
  358.5 68.0 %collective-permute-start.12 = (bf16[1,192,896]{2,1,0:T(8,128)(2,1)S(1)}, bf16[1,192,896]{2,1,0:T(8,128)(2,1)S(1)}, u32[]{:S(2)}, u32[]{:S(2)}) collective-permute-start(bf16[1,192,896]{2,1,0:T(8,128)(2,1)S(1)} %get-tuple-element.302.refs_21_), channel_id=1, source_target_pairs={{0,16},{4,20},{8,24},{12,28},{16,0},{20,4},{24,8},{28,12},{1,17},{... | collective-permute-start | bytes 1032200 | tf_op jit(solution)/shard_map/ppermute | solution.py:37
  389.4 13.0 %copy-start.7 = (bf16[4,192,768]{2,1,0:T(8,128)(2,1)S(1)}, bf16[4,192,768]{2,1,0:T(8,128)(2,1)}, u32[]{:S(2)}) copy-start(bf16[4,192,768]{2,1,0:T(8,128)(2,1)} %get-tuple-element.228) | copy-start | bytes 3538948
  394.2 35.6 %collective-permute-start.7 = (bf16[4,192,896]{2,1,0:T(8,128)(2,1)}, bf16[4,192,896]{2,1,0:T(8,128)(2,1)S(1)}, u32[]{:S(2)}, u32[]{:S(2)}) collective-permute-start(bf16[4,192,896]{2,1,0:T(8,128)(2,1)} %get-tuple-element.226.refs_9_), channel_id=1, source_target_pairs={{0,4},{4,0},{8,12},{12,8},{16,20},{20,16},{24,28},{28,24},{1,5},{5... | collective-permute-start | bytes 4128776 | tf_op jit(solution)/shard_map/ppermute | solution.py:37
  402.4 2.7 copy-start.6
  403.5 2.7 copy-start.15
  403.5 26.3 %collective-permute-start.9 = (bf16[2,192,768]{2,1,0:T(8,128)(2,1)S(1)}, bf16[2,192,768]{2,1,0:T(8,128)(2,1)S(1)}, u32[]{:S(2)}, u32[]{:S(2)}) collective-permute-start(bf16[2,192,768]{2,1,0:T(8,128)(2,1)S(1)} %get-tuple-element.296.refs_11_), channel_id=1, source_target_pairs={{0,16},{4,20},{8,24},{12,28},{16,0},{20,4},{24,8},{28,12},{1,17},{... | collective-permute-start | bytes 1769480 | tf_op jit(solution)/shard_map/ppermute | solution.py:37
  406.2 0.8 copy-start.19
  406.2 20.3 %copy-start.43 = (bf16[1,192,768]{2,1,0:T(8,128)(2,1)}, bf16[1,192,768]{2,1,0:T(8,128)(2,1)S(1)}, u32[]{:S(2)}) copy-start(bf16[1,192,768]{2,1,0:T(8,128)(2,1)S(1)} %collective-permute-done.13.refs_8_) | copy-start | bytes 884740
  406.2 25.7 %collective-permute-start.11 = (bf16[2,192,768]{2,1,0:T(8,128)(2,1)S(1)}, bf16[2,192,768]{2,1,0:T(8,128)(2,1)S(1)}, u32[]{:S(2)}, u32[]{:S(2)}) collective-permute-start(bf16[2,192,768]{2,1,0:T(8,128)(2,1)S(1)} %get-tuple-element.294.refs_10_), channel_id=1, source_target_pairs={{0,8},{4,12},{8,0},{12,4},{16,24},{20,28},{24,16},{28,20},{1,9},{5... | collective-permute-start | bytes 1769480 | tf_op jit(solution)/shard_map/ppermute | solution.py:37
  426.5 5.3 %copy-start.44 = (bf16[1,192,768]{2,1,0:T(8,128)(2,1)}, bf16[1,192,768]{2,1,0:T(8,128)(2,1)S(1)}, u32[]{:S(2)}) copy-start(bf16[1,192,768]{2,1,0:T(8,128)(2,1)S(1)} %collective-permute-done.14.refs_10_) | copy-start | bytes 884740
  426.6 5.3 %copy-start.42 = (bf16[1,192,896]{2,1,0:T(8,128)(2,1)}, bf16[1,192,896]{2,1,0:T(8,128)(2,1)S(1)}, u32[]{:S(2)}) copy-start(bf16[1,192,896]{2,1,0:T(8,128)(2,1)S(1)} %collective-permute-done.12.refs_6_) | copy-start | bytes 1032196
  429.8 2.1 copy-start.37
  429.8 2.1 copy-start.38
  431.9 0.8 copy-start.39
  482.8 2.2 copy-start.10
  484.0 1.5 copy-start.4
  485.5 2.1 copy-start.18
  487.6 1.1 copy-start.17
  488.9 4.8 copy-start.23
  488.9 5.4 %copy-start.27 = (f32[2,5,256]{2,1,0:T(8,128)S(1)}, f32[2,5,256]{2,1,0:T(8,128)}, u32[]{:S(2)}) copy-start(f32[2,5,256]{2,1,0:T(8,128)} %get-tuple-element.283) | copy-start | bytes 30724
  488.9 6.0 %copy-start.33 = (f32[2,256]{1,0:T(2,128)S(1)}, f32[2,256]{1,0:T(2,128)}, u32[]{:S(2)}) copy-start(f32[2,256]{1,0:T(2,128)} %get-tuple-element.258) | copy-start | bytes 6148
  488.9 6.6 %copy-start.32 = (f32[2,768]{1,0:T(2,128)S(1)}, f32[2,768]{1,0:T(2,128)}, u32[]{:S(2)}) copy-start(f32[2,768]{1,0:T(2,128)} %get-tuple-element.259) | copy-start | bytes 18436
  488.9 8.6 %copy-start.12 = (f32[192,768]{1,0:T(8,128)S(1)}, f32[192,768]{1,0:T(8,128)}, u32[]{:S(2)}) copy-start(f32[192,768]{1,0:T(8,128)} %get-tuple-element.261) | copy-start | bytes 1769476
  488.9 8.6 %copy-start.13 = (f32[192,768]{1,0:T(8,128)S(1)}, f32[192,768]{1,0:T(8,128)}, u32[]{:S(2)}) copy-start(f32[192,768]{1,0:T(8,128)} %get-tuple-element.262) | copy-start | bytes 1769476
  492.9 5.7 %copy-start.3 = (bf16[512,1536]{1,0:T(8,128)(2,1)S(1)}, bf16[512,1536]{1,0:T(8,128)(2,1)}, u32[]{:S(2)}) copy-start(bf16[512,1536]{1,0:T(8,128)(2,1)} %get-tuple-element.329) | copy-start | bytes 4718596
  498.6 1.1 copy-start.31
